TPU v7x, 32 devices: a whole 2x2x4 slice. The times are simulated.
32 devices in a mesh: dp: 4 (over z), mp: 8 (over y, x, core).
Axes of the slice: x: 2, y: 2, z: 4, core: 2. Of those that a mesh axis runs over, the one named last changes fastest.
Arguments:
- inputs: bfloat16 [8, 1024, 2048], P('dp'), may hold values from -6 to 6
- positions: int32 [8, 1024], P('dp'), may hold values from 0 to 1023, as said below
- cotangent: bfloat16 [8, 1024, 2048], P('dp'), may hold values from -6 to 6
- w_attend_in: float32 [2048, 3, 2048], P('dp', None, 'mp'), may hold values from -0.125 to 0.125
- w_attend_out: float32 [2048, 2048], P('dp', 'mp'), may hold values from -1.5 to 1.5
- w_expand: float32 [2048, 2, 5632], P('dp', None, 'mp'), may hold values from -0.125 to 0.125
- w_reduce: float32 [2048, 5632], P('dp', 'mp'), may hold values from -0.078125 to 0.078125
- norm_params: float32 [2, 2048], replicated, may hold values from -0.8 to 1.2, as said below
- attend_bias: float32 [3, 2048], P(None, 'mp'), may hold values from -3 to 3
- moment_attend_in: float32 [2048, 3, 2048], P('dp', None, 'mp'), may hold values from -640 to 640
- moment_attend_out: float32 [2048, 2048], P('dp', 'mp'), may hold values from -56 to 56
- moment_expand: float32 [2048, 2, 5632], P('dp', None, 'mp'), may hold values from -160 to 160
- moment_reduce: float32 [2048, 5632], P('dp', 'mp'), may hold values from -320 to 320
- moment_norm: float32 [2, 2048], replicated, may hold values from -1024 to 1024
- moment_bias: float32 [3, 2048], P(None, 'mp'), may hold values from -512 to 512
- average_attend_in: float32 [2048, 3, 2048], P('dp', None, 'mp'), may hold values from -0.125 to 0.125
- average_attend_out: float32 [2048, 2048], P('dp', 'mp'), may hold values from -1.5 to 1.5
- average_expand: float32 [2048, 2, 5632], P('dp', None, 'mp'), may hold values from -0.125 to 0.125
- average_reduce: float32 [2048, 5632], P('dp', 'mp'), may hold values from -0.078125 to 0.078125
- average_norm: float32 [2, 2048], replicated, may hold values from -0.8 to 1.2, as said below
- average_bias: float32 [3, 2048], P(None, 'mp'), may hold values from -3 to 3
Outputs:
- output: bfloat16 [8, 1024, 2048], P('dp')
- input_grad: float32 [8, 1024, 2048], P('dp')
- grad_attend_in: float32 [2048, 3, 2048], P('dp', None, 'mp')
- grad_attend_out: float32 [2048, 2048], P('dp', 'mp')
- grad_expand: float32 [2048, 2, 5632], P('dp', None, 'mp')
- grad_reduce: float32 [2048, 5632], P('dp', 'mp')
- grad_norm: float32 [2, 2048], replicated
- grad_bias: float32 [3, 2048], P(None, 'mp')
- new_attend_in: float32 [2048, 3, 2048], P('dp', None, 'mp')
- new_attend_out: float32 [2048, 2048], P('dp', 'mp')
- new_expand: float32 [2048, 2, 5632], P('dp', None, 'mp')
- new_reduce: float32 [2048, 5632], P('dp', 'mp')
- new_norm: float32 [2, 2048], replicated
- new_bias: float32 [3, 2048], P(None, 'mp')
- new_moment_attend_in: float32 [2048, 3, 2048], P('dp', None, 'mp')
- new_moment_attend_out: float32 [2048, 2048], P('dp', 'mp')
- new_moment_expand: float32 [2048, 2, 5632], P('dp', None, 'mp')
- new_moment_reduce: float32 [2048, 5632], P('dp', 'mp')
- new_moment_norm: float32 [2, 2048], replicated
- new_moment_bias: float32 [3, 2048], P(None, 'mp')
- new_average_attend_in: float32 [2048, 3, 2048], P('dp', None, 'mp')
- new_average_attend_out: float32 [2048, 2048], P('dp', 'mp')
- new_average_expand: float32 [2048, 2, 5632], P('dp', None, 'mp')
- new_average_reduce: float32 [2048, 5632], P('dp', 'mp')
- new_average_norm: float32 [2, 2048], replicated
- new_average_bias: float32 [3, 2048], P(None, 'mp')
Inputs may be any that keep to these rules, and one draw needn't show every extreme that they name: `positions`: A position counts the tokens since the start of its document in the sequence; every sequence starts a document at its first token, the first sequence of the batch is one whole document, and in the others further documents begin at random places. `norm_params`: row 0 lies near one, row 1 near zero. `average_norm`: row 0 lies near one, row 1 near zero.
All inputs are finite; a program needn't handle non-finite values.
Results may differ from a plain program's by a relative error of at most 0.012.
Values may be sent and summed in bfloat16 or wider, within the bound.
No kernel may reach another device: no remote copies, remote signals or barrier semaphores. Data moves between devices by JAX's collectives and lax.ppermute only.
A program may use at most 256 MiB of HBM per device.

v0:
```python
import math

import jax
import jax.numpy as jnp
from jax import lax
from jax.sharding import PartitionSpec as P

HD = 64
ROT = 16
FF = 5632


epsilon = 1e-05
decay_moment = 0.9
decay_average = 0.9
masked_score = -1e30


def rotate(values, cosine, sine):
    half = cosine.shape[-1]
    first = values[..., :half]
    second = values[..., half : 2 * half]
    return jnp.concatenate(
        [first * cosine - second * sine, second * cosine + first * sine, values[..., 2 * half :]],
        axis=-1,
    )


def rotate_back(grads, cosine, sine):
    half = cosine.shape[-1]
    first = grads[..., :half]
    second = grads[..., half : 2 * half]
    return jnp.concatenate(
        [first * cosine + second * sine, second * cosine - first * sine, grads[..., 2 * half :]],
        axis=-1,
    )


def advance(weight, grad, moment, average, rate):
    moment_new = decay_moment * moment + grad
    weight_new = weight - rate * (grad + decay_moment * moment_new)
    average_new = decay_average * average + (1.0 - decay_average) * weight_new
    return (weight_new, moment_new, average_new)


def contract_rows(left, right):
    return lax.dot_general(
        left, right, (((0,), (0,)), ((), ())), preferred_element_type=jnp.float32
    )


def contract_cols(left, right):
    return lax.dot_general(
        left, right, (((1,), (1,)), ((), ())), preferred_element_type=jnp.float32
    )


def body(
    inputs,
    positions,
    cotangent,
    w_attend_in,
    w_attend_out,
    w_expand,
    w_reduce,
    norm_params,
    attend_bias,
    moment_attend_in,
    moment_attend_out,
    moment_expand,
    moment_reduce,
    moment_norm,
    moment_bias,
    average_attend_in,
    average_attend_out,
    average_expand,
    average_reduce,
    average_norm,
    average_bias,
):
    batch, length, width = inputs.shape
    rows = batch * length
    cols_local = attend_bias.shape[1]
    heads_local = cols_local // HD
    hidden_local = w_expand.shape[2]
    scale = HD ** (-0.5)
    replicas = lax.axis_size("dp")
    in_low, out_low, expand_low, reduce_low = (
        lax.all_gather(w_attend_in.astype(jnp.bfloat16), "dp", axis=0, tiled=True),
        lax.all_gather(w_attend_out.astype(jnp.bfloat16), "dp", axis=0, tiled=True),
        lax.all_gather(w_expand.astype(jnp.bfloat16), "dp", axis=0, tiled=True),
        lax.all_gather(w_reduce.astype(jnp.bfloat16), "dp", axis=0, tiled=True),
    )
    in_flat = in_low.reshape(width, 3 * cols_local)
    expand_flat = expand_low.reshape(width, 2 * hidden_local)
    tokens = inputs.reshape(rows, width).astype(jnp.float32)
    centre = jnp.mean(tokens, axis=-1, keepdims=True)
    centred = tokens - centre
    inv_dev = lax.rsqrt(jnp.mean(centred * centred, axis=-1, keepdims=True) + epsilon)
    normal = centred * inv_dev
    gain = norm_params[0]
    hidden = (normal * gain + norm_params[1]).astype(jnp.bfloat16)
    mixed = jnp.dot(hidden, in_flat, preferred_element_type=jnp.float32) + attend_bias.reshape(
        3 * cols_local
    )
    mixed = mixed.reshape(rows, 3, heads_local, HD)
    half = ROT // 2
    frequency = 10000.0 ** (-(jnp.arange(half, dtype=jnp.float32) * 2.0 / ROT))
    angles = positions.reshape(rows).astype(jnp.float32)[:, None] * frequency[None, :]
    cosine = jnp.cos(angles)[:, None, :]
    sine = jnp.sin(angles)[:, None, :]
    head_shape = (batch, length, heads_local, HD)
    queries = rotate(mixed[:, 0], cosine, sine).astype(jnp.bfloat16).reshape(head_shape)
    keys = rotate(mixed[:, 1], cosine, sine).astype(jnp.bfloat16).reshape(head_shape)
    values = mixed[:, 2].astype(jnp.bfloat16).reshape(head_shape)
    block = min(512, length)
    count = length // block
    starts = jnp.arange(count, dtype=jnp.int32) * block
    block_rows = jnp.arange(block, dtype=jnp.int32)
    columns = jnp.arange(length, dtype=jnp.int32)

    def scores_of(start):
        query_block = lax.dynamic_slice_in_dim(queries, start, block, 1)
        scores = (
            jnp.einsum("bqhd,bkhd->bhqk", query_block, keys, preferred_element_type=jnp.float32)
            * scale
        )
        allowed = columns[None, :] <= (start + block_rows)[:, None]
        return (query_block, jnp.where(allowed, scores, masked_score))

    def forward_block(start):
        query_block, scores = scores_of(start)
        top = jnp.max(scores, axis=-1, keepdims=True)
        weights = jnp.exp(scores - top)
        total = jnp.sum(weights, axis=-1, keepdims=True)
        probs = (weights / total).astype(jnp.bfloat16)
        context_block = jnp.einsum(
            "bhqk,bkhd->bqhd", probs, values, preferred_element_type=jnp.float32
        )
        return (context_block.astype(jnp.bfloat16), (top + jnp.log(total))[..., 0])

    context_blocks, logsums = lax.map(forward_block, starts)
    context = jnp.moveaxis(context_blocks, 0, 1).reshape(rows, cols_local)
    attended = contract_cols(context, out_low)
    gates = jnp.dot(hidden, expand_flat, preferred_element_type=jnp.float32).reshape(
        rows, 2, hidden_local
    )
    gate = gates[:, 0]
    upper = gates[:, 1]
    sigmoid = jax.nn.sigmoid(gate)
    swish = gate * sigmoid
    active = (swish * upper).astype(jnp.bfloat16)
    expanded = contract_cols(active, reduce_low)
    partial_rows = attended + expanded
    summed = lax.psum(partial_rows, "mp")
    output = (tokens + summed).astype(jnp.bfloat16).reshape(batch, length, width)
    cot_rows = cotangent.reshape(rows, width)
    context_grad = jnp.dot(cot_rows, out_low, preferred_element_type=jnp.float32).astype(
        jnp.bfloat16
    )
    grad_out_local = contract_rows(cot_rows, context)
    active_grad = jnp.dot(cot_rows, reduce_low, preferred_element_type=jnp.float32)
    grad_reduce_local = contract_rows(cot_rows, active)
    gate_grad = active_grad * upper * sigmoid * (1.0 + gate * (1.0 - sigmoid))
    upper_grad = active_grad * swish
    gates_grad = (
        jnp.stack([gate_grad, upper_grad], axis=1)
        .astype(jnp.bfloat16)
        .reshape(rows, 2 * hidden_local)
    )
    context_heads = context_grad.reshape(head_shape)

    def backward_block(carry, block_inputs):
        key_total, value_total = carry
        start, logsum = block_inputs
        query_block, scores = scores_of(start)
        probs = jnp.exp(scores - logsum[..., None])
        grad_block = lax.dynamic_slice_in_dim(context_heads, start, block, 1)
        prob_grads = jnp.einsum(
            "bqhd,bkhd->bhqk", grad_block, values, preferred_element_type=jnp.float32
        )
        middle = jnp.sum(probs * prob_grads, axis=-1, keepdims=True)
        score_grads = (probs * (prob_grads - middle)).astype(jnp.bfloat16)
        query_grads = (
            jnp.einsum("bhqk,bkhd->bqhd", score_grads, keys, preferred_element_type=jnp.float32)
            * scale
        )
        key_total = (
            key_total
            + jnp.einsum(
                "bhqk,bqhd->bkhd", score_grads, query_block, preferred_element_type=jnp.float32
            )
            * scale
        )
        value_total = value_total + jnp.einsum(
            "bhqk,bqhd->bkhd",
            probs.astype(jnp.bfloat16),
            grad_block,
            preferred_element_type=jnp.float32,
        )
        return ((key_total, value_total), query_grads)

    empty = jnp.zeros(head_shape, jnp.float32)
    (key_grads, value_grads), query_parts = lax.scan(
        backward_block, (empty, empty), (starts, logsums)
    )
    query_grads = jnp.moveaxis(query_parts, 0, 1).reshape(rows, heads_local, HD)
    mixed_grad = (
        jnp.stack(
            [
                rotate_back(query_grads, cosine, sine),
                rotate_back(key_grads.reshape(rows, heads_local, HD), cosine, sine),
                value_grads.reshape(rows, heads_local, HD),
            ],
            axis=1,
        )
        .astype(jnp.bfloat16)
        .reshape(rows, 3 * cols_local)
    )
    bias_grad = jnp.sum(mixed_grad.astype(jnp.float32), axis=0).reshape(3, cols_local)
    grad_in_local = contract_rows(hidden, mixed_grad)
    grad_expand_local = contract_rows(hidden, gates_grad)
    hidden_part = contract_cols(mixed_grad, in_flat) + contract_cols(gates_grad, expand_flat)
    hidden_grad = lax.psum(hidden_part, "mp")
    scaled = hidden_grad * gain
    back = inv_dev * (
        scaled
        - jnp.mean(scaled, axis=-1, keepdims=True)
        - normal * jnp.mean(scaled * normal, axis=-1, keepdims=True)
    )
    input_rows_grad = cot_rows.astype(jnp.float32) + back
    norm_grad = jnp.stack([jnp.sum(hidden_grad * normal, axis=0), jnp.sum(hidden_grad, axis=0)])
    input_grad = input_rows_grad.reshape(batch, length, width)
    norm_grad, bias_grad = lax.psum((norm_grad, bias_grad), "dp")
    grad_in, grad_out, grad_expand, grad_reduce = (
        lax.psum_scatter(
            grad_in_local.reshape(width, 3, cols_local), "dp", scatter_dimension=0, tiled=True
        ),
        lax.psum_scatter(grad_out_local, "dp", scatter_dimension=0, tiled=True),
        lax.psum_scatter(
            grad_expand_local.reshape(width, 2, hidden_local), "dp", scatter_dimension=0, tiled=True
        ),
        lax.psum_scatter(grad_reduce_local, "dp", scatter_dimension=0, tiled=True),
    )
    total_tokens = rows * replicas
    new_in, moment_in_new, average_in_new = advance(
        w_attend_in,
        grad_in,
        moment_attend_in,
        average_attend_in,
        0.5 / math.sqrt(width * total_tokens),
    )
    new_out, moment_out_new, average_out_new = advance(
        w_attend_out,
        grad_out,
        moment_attend_out,
        average_attend_out,
        1.8 / math.sqrt(width * batch * replicas),
    )
    new_expand, moment_expand_new, average_expand_new = advance(
        w_expand, grad_expand, moment_expand, average_expand, 1.6 / math.sqrt(width * total_tokens)
    )
    new_reduce, moment_reduce_new, average_reduce_new = advance(
        w_reduce, grad_reduce, moment_reduce, average_reduce, 0.77 / math.sqrt(FF * total_tokens)
    )
    new_norm, moment_norm_new, average_norm_new = advance(
        norm_params, norm_grad, moment_norm, average_norm, 0.06 / math.sqrt(total_tokens)
    )
    new_bias, moment_bias_new, average_bias_new = advance(
        attend_bias, bias_grad, moment_bias, average_bias, 0.25 / math.sqrt(total_tokens)
    )
    return (
        output,
        input_grad,
        grad_in,
        grad_out,
        grad_expand,
        grad_reduce,
        norm_grad,
        bias_grad,
        new_in,
        new_out,
        new_expand,
        new_reduce,
        new_norm,
        new_bias,
        moment_in_new,
        moment_out_new,
        moment_expand_new,
        moment_reduce_new,
        moment_norm_new,
        moment_bias_new,
        average_in_new,
        average_out_new,
        average_expand_new,
        average_reduce_new,
        average_norm_new,
        average_bias_new,
    )


def solution(mesh):
    placed = (
        P("dp", None, None),
        P("dp", None),
        P("dp", None, None),
        P("dp", None, "mp"),
        P("dp", "mp"),
        P("dp", None, "mp"),
        P("dp", "mp"),
        P(),
        P(None, "mp"),
        P("dp", None, "mp"),
        P("dp", "mp"),
        P("dp", None, "mp"),
        P("dp", "mp"),
        P(),
        P(None, "mp"),
        P("dp", None, "mp"),
        P("dp", "mp"),
        P("dp", None, "mp"),
        P("dp", "mp"),
        P(),
        P(None, "mp"),
    )
    return jax.shard_map(
        body,
        mesh=mesh,
        in_specs=placed,
        out_specs=(
            P("dp", None, None),
            P("dp", None, None),
            P("dp", None, "mp"),
            P("dp", "mp"),
            P("dp", None, "mp"),
            P("dp", "mp"),
            P(),
            P(None, "mp"),
            P("dp", None, "mp"),
            P("dp", "mp"),
            P("dp", None, "mp"),
            P("dp", "mp"),
            P(),
            P(None, "mp"),
            P("dp", None, "mp"),
            P("dp", "mp"),
            P("dp", None, "mp"),
            P("dp", "mp"),
            P(),
            P(None, "mp"),
            P("dp", None, "mp"),
            P("dp", "mp"),
            P("dp", None, "mp"),
            P("dp", "mp"),
            P(),
            P(None, "mp"),
        ),
        check_vma=False,
    )
```

profile of v0, /device:TPU:0, one launch (start us, length us, event | category | flops | bytes accessed | tf_op | source)
XLA Modules:
  0.0 1258.4 jit_solution(3881992986400815910)
XLA Ops:
  7.3 3.2 convert_element_type.122
  12.6 4.7 convert_reduce_fusion
  18.4 2.3 fusion.41
  22.0 5.4 fusion.44
  27.3 92.8 %all-gather.9.cloned.1.call-done = bf16[2048,2,704]{0,2,1:T(8,128)(2,1)} async-done(((bf16[512,2,704]{0,2,1:T(8,128)(2,1)}), bf16[2048,2,704]{0,2,1:T(8,128)(2,1)}) %all-gather.9.cloned.1.call-update) | async-done | bytes 5767184 | tf_op jit(solution)/shard_map/all_gather | solution.py:91
  120.1 16.3 %fusion.57 = f32[2048,2,704]{0,2,1:T(8,128)S(1)} fusion(bf16[2048,2048,1]{1,0,2:T(8,128)(2,1)} %bitcast.237, bf16[2048,2,704]{0,2,1:T(8,128)(2,1)} %all-gather.9.cloned.1.call-done), kind=kOutput, calls=%fused_computation.75 | convolution fusion | flops 11811160064 | bytes 25690112 | tf_op jit(solution)/shard_map/dot_general | solution.py:145
  136.4 4.3 copy-done.40
  140.7 10.2 convolution_bitcast_fusion
  151.9 6.0 convolution_convert_fusion
  159.0 2.3 copy.64
  161.3 52.3 %all-gather.5.cloned.1.call-done = bf16[2048,3,256]{0,2,1:T(8,128)(2,1)} async-done(((bf16[512,3,256]{0,2,1:T(8,128)(2,1)}), bf16[2048,3,256]{0,2,1:T(8,128)(2,1)}) %all-gather.5.cloned.1.call-update) | async-done | bytes 3145744 | tf_op jit(solution)/shard_map/all_gather | solution.py:89
  213.6 10.1 broadcast_add_fusion
  230.4 2.6 convert_element_type.120
  233.0 2.5 copy.59
  235.5 81.8 %reduce-scatter.11.cloned.1.call-done = f32[512,704]{0,1:T(8,128)} async-done(((f32[2048,704]{0,1:T(8,128)}), f32[512,704]{0,1:T(8,128)}) %reduce-scatter.11.cloned.1.call-update) | async-done | bytes 1441808 | tf_op jit(solution)/shard_map/reduce_scatter | solution.py:243
  317.3 6.0 multiply_add_fusion.4
  323.4 35.2 %while.28 = (s32[]{:T(128)}, bf16[2,2,512,4,64]{2,4,3,1,0:T(8,128)(2,1)}, f32[2,2,4,512]{3,2,1,0:T(4,128)S(1)}, s32[2]{0:T(128)S(1)}, bf16[2,1024,4,64]{1,3,2,0:...) while((s32[]{:T(128)}, ...), condition=%wide.region_5.6_spmd.clone, body=%wide.region_2.5_spmd.clone.sunk | while | flops 1124856320 | bytes 59904700 | solution.py:142
  327.3 3.6 fusion.123
  331.0 4.4 fusion.124
  335.4 5.8 fusion.125
  344.7 3.7 fusion.123
  348.4 4.4 fusion.124
  352.8 5.8 fusion.125
  358.6 3.3 copy.60
  361.9 2.6 reshape.348
  364.5 7.4 convolution_bitcast_fusion.1
  372.0 123.2 %while.29 = (s32[]{:T(128)}, f32[2,1024,4,64]{1,3,2,0:T(8,128)}, f32[2,1024,4,64]{1,3,2,0:T(8,128)}, f32[2,2,512,4,64]{2,4,3,1,0:T(8,128)}, s32[2]{0:T(128)S(1)}...) while((s32[]{:T(128)}, f32[2,1024,4,64]{1,3,2,0:T(8,128)}, ...), condition=%wide.region_9.10_spmd.clone, body=%wide.region_7.9_spmd.clone.sunk | while | flops 2750673408 | bytes 205640048 | solution.py:204
  374.7 8.6 fusion.135
  384.4 12.8 %multiply_reduce_fusion.3 = (f32[2,4,512]{2,1,0:T(4,128)S(1)}, f32[2,4,512,1024]{3,2,1,0:T(8,128)}) fusion(f32[2,4,512,1024]{3,2,1,0:T(8,128)} %fusion.135, f32[2,4,512]{2,1,0:T(4,128)S(1)} %dynamic-slice_bitcast_fusion.2, pred[512,1024]{1,0:T(8,128)(4,1)S(1)} %iota_compare_fusion.5, bf16[2,1024,4,64]{1,3,2,0:T(8,128)(2,1)S(1)} %copy-done.4, ...), kind=kOutput, calls=%fused_computation.22.clone.1 | convolution fusion | flops 557838336 | bytes 35684356 | tf_op jit(solution)/shard_map/while/body/eval_jaxpr/bqhd,bkhd->bhqk/dot_general | solution.py:179
  397.3 15.5 %multiply_convert_fusion.4 = bf16[2,4,512,1024]{3,2,1,0:T(8,128)(2,1)} fusion(f32[2,4,512,1024]{3,2,1,0:T(8,128)} %get-tuple-element.483, f32[2,4,512,1024]{3,2,1,0:T(8,128)} %fusion.135, f32[2,4,512]{2,1,0:T(4,128)S(1)} %get-tuple-element.484, f32[2,4,512]{2,1,0:T(4,128)S(1)} %dynamic-slice_bitcast_fusion.2, pred[512,1024]{1,0:T(8,128)(4,1)S(1)} %iota_compare_fusion.5), kind=kLoop, calls=%fused_computation.21.clone.1 | loop fusion | flops 25165824 | bytes 42500096 | tf_op jit(solution)/shard_map/while/body/eval_jaxpr/convert_element_type | solution.py:183
  412.7 6.6 bitcast_add_fusion.6
  419.6 2.7 fusion.136
  423.6 9.7 bitcast_add_fusion.7
  435.8 8.6 fusion.135
  445.5 12.8 %multiply_reduce_fusion.3 = (f32[2,4,512]{2,1,0:T(4,128)S(1)}, f32[2,4,512,1024]{3,2,1,0:T(8,128)}) fusion(f32[2,4,512,1024]{3,2,1,0:T(8,128)} %fusion.135, f32[2,4,512]{2,1,0:T(4,128)S(1)} %dynamic-slice_bitcast_fusion.2, pred[512,1024]{1,0:T(8,128)(4,1)S(1)} %iota_compare_fusion.5, bf16[2,1024,4,64]{1,3,2,0:T(8,128)(2,1)S(1)} %copy-done.4, ...), kind=kOutput, calls=%fused_computation.22.clone.1 | convolution fusion | flops 557838336 | bytes 35684356 | tf_op jit(solution)/shard_map/while/body/eval_jaxpr/bqhd,bkhd->bhqk/dot_general | solution.py:179
  458.4 15.1 %multiply_convert_fusion.4 = bf16[2,4,512,1024]{3,2,1,0:T(8,128)(2,1)} fusion(f32[2,4,512,1024]{3,2,1,0:T(8,128)} %get-tuple-element.483, f32[2,4,512,1024]{3,2,1,0:T(8,128)} %fusion.135, f32[2,4,512]{2,1,0:T(4,128)S(1)} %get-tuple-element.484, f32[2,4,512]{2,1,0:T(4,128)S(1)} %dynamic-slice_bitcast_fusion.2, pred[512,1024]{1,0:T(8,128)(4,1)S(1)} %iota_compare_fusion.5), kind=kLoop, calls=%fused_computation.21.clone.1 | loop fusion | flops 25165824 | bytes 42500096 | tf_op jit(solution)/shard_map/while/body/eval_jaxpr/convert_element_type | solution.py:183
  473.5 7.1 bitcast_add_fusion.6
  480.8 2.7 fusion.136
  484.8 10.2 bitcast_add_fusion.7
  495.2 4.7 copy.66
  499.9 4.0 reshape.353
  504.2 2.3 slice.92
  507.5 3.2 copy.68
  517.1 10.9 fusion.78
  528.1 1.8 copy-done.13
  529.9 12.5 fusion.77
  542.4 10.9 fusion.67
  553.4 8.7 convolution_add_fusion
  562.0 13.8 %fusion.62 = (bf16[2048,1,704]{0,2,1:T(8,128)(2,1)S(1)}, bf16[2048,1,704]{0,2,1:T(8,128)(2,1)S(1)}) fusion(f32[2048,2,704]{0,2,1:T(8,128)} %copy-done.40, bf16[2048,2048]{1,0:T(8,128)(2,1)} %bitcast.235, bf16[2048,704]{0,1:T(8,128)(2,1)} %all-gather.11.cloned.1.call-done), kind=kOutput, calls=%fused_computation.82 | convolution fusion | flops 5924323328 | bytes 28573696 | tf_op jit(solution)/shard_map/dot_general | solution.py:162
  577.4 20.3 %bitcast_add_fusion.2 = f32[2048,2048]{1,0:T(8,128)} fusion(f32[2048,2048]{1,0:T(8,128)} %fusion.77, bf16[2048,2,704]{0,2,1:T(8,128)(2,1)} %all-gather.9.cloned.1.call-done, bf16[2048,1,704]{0,2,1:T(8,128)(2,1)S(1)} %get-tuple-element.342, bf16[2048,1,704]{0,2,1:T(8,128)(2,1)S(1)} %get-tuple-element.341), kind=kOutput, calls=%fused_computation.47 | convolution fusion | flops 11818237952 | bytes 45088768 | tf_op jit(solution)/shard_map/dot_general | solution.py:53
  597.7 18.1 %fusion.55 = f32[2048,2,704]{0,2,1:T(8,128)} fusion(bf16[2048,2048,1]{1,0,2:T(8,128)(2,1)} %bitcast.240, bf16[2048,1,704]{0,2,1:T(8,128)(2,1)} %copy-done.41, bf16[2048,1,704]{0,2,1:T(8,128)(2,1)S(1)} %get-tuple-element.341), kind=kOutput, calls=%fused_computation.73 | convolution fusion | flops 11822694400 | bytes 25690112 | tf_op jit(solution)/shard_map/dot_general | solution.py:47
  618.4 2.0 copy.72
  620.6 2.6 multiply_add_fusion.6
  623.2 2.0 copy.74
  625.2 2.0 copy.75
  627.3 2.0 copy.76
  630.3 9.3 reduce-scatter.5.cloned.1.call-done
  639.6 5.0 multiply_add_fusion.2
  644.6 399.8 %all-reduce.4.cloned.1.call-done = (f32[2048,2048]{1,0:T(8,128)}, f32[2048,2048]{1,0:T(8,128)}) async-done(((f32[2048,2048]{1,0:T(8,128)}, f32[2048,2048]{1,0:T(8,128)}), (f32[2048,2048]{1,0:T(8,128)}, f32[2048,2048]{1,0:T(8,128)})) %all-reduce.4.cloned.1.call-update) | async-done | bytes 33554448 | tf_op jit(solution)/shard_map/psum | solution.py:155
  1044.5 11.9 fusion.54
  1056.4 20.1 %all-reduce.1 = (f32[2,2048]{1,0:T(2,128)S(1)}, f32[3,256]{1,0:T(4,128)S(1)}) all-reduce(f32[2,2048]{1,0:T(2,128)S(1)} %pad_maximum_fusion.2, f32[3,256]{1,0:T(4,128)S(1)} %reshape.356), channel_id=1, replica_groups=mesh['dp'=4,'mp'=8] {'dp'}, use_global_device_ids=true, to_apply=%region_19.20 | all-reduce | flops 4864 | bytes 38912 | tf_op jit(solution)/shard_map/psum | solution.py:234
  1077.9 26.8 %fusion.53 = (f32[2048,2048]{1,0:T(8,128)}, bf16[2048,2048]{1,0:T(8,128)(2,1)}) fusion(bf16[2,1024,2048]{2,1,0:T(8,128)(2,1)} %param.25, f32[2048,2048]{1,0:T(8,128)} %get-tuple-element.315, f32[2048]{0:T(1024)S(1)} %broadcast_multiply_fusion, f32[2048]{0:T(1024)S(1)} %get-tuple-element.371, f32[2048]{0:T(1024)S(1)} %broadcast_multiply_fusion.1, ...), kind=kLoop, calls=%fused_computation.66 | loop fusion | flops 50331648 | bytes 75538432 | tf_op jit(solution)/shard_map/add | solution.py:231
  1104.7 138.7 %reduce-scatter.9.cloned.1.call-done = f32[512,2,704]{0,2,1:T(8,128)} async-done(((f32[2048,2,704]{0,2,1:T(8,128)}), f32[512,2,704]{0,2,1:T(8,128)}) %reduce-scatter.9.cloned.1.call-update) | async-done | bytes 2883600 | tf_op jit(solution)/shard_map/reduce_scatter | solution.py:240
  1243.4 8.2 multiply_add_fusion
  (181 shorter events, 37.1 us)
Async XLA Ops:
  7.2 3.4 copy-start.17
  7.2 4.2 copy-start.9
  7.2 112.9 %all-gather.9.cloned.1.call-start = ((), (), s32[]{:S(2)}) async-start(), calls=%async_computation.6 | async-start | bytes 7208960 | tf_op jit(solution)/shard_map/all_gather | solution.py:91
  10.5 141.4 %all-gather.7.cloned.1.call-start = ((), (), s32[]{:S(2)}) async-start(), calls=%async_computation.5 | async-start | bytes 1310720 | tf_op jit(solution)/shard_map/all_gather | solution.py:90
  11.3 202.3 %all-gather.5.cloned.1.call-start = ((), (), s32[]{:S(2)}) async-start(), calls=%async_computation.4 | async-start | bytes 3932160 | tf_op jit(solution)/shard_map/all_gather | solution.py:89
  12.6 304.7 %reduce-scatter.11.cloned.1.call-start = ((), (), s32[]{:S(2)}) async-start(), calls=%async_computation.11 | async-start | bytes 7208960 | tf_op jit(solution)/shard_map/reduce_scatter | solution.py:243
  12.6 5.8 copy-start.1
  17.3 4.0 copy-start.26
  21.4 0.6 copy-start.24
  136.4 4.3 copy-start.40
  150.8 0.7 copy-start.34
  150.8 0.7 copy-start.36
  150.9 391.5 %all-gather.11.cloned.1.call-start = ((), (), s32[]{:S(2)}) async-start(), calls=%async_computation.7 | async-start | bytes 3604480 | tf_op jit(solution)/shard_map/all_gather | solution.py:92
  151.9 73.4 %copy-start.20 = (f32[2048,8]{0,1:T(8,128)}, f32[2048,8]{0,1:T(8,128)S(1)}, u32[]{:S(2)}) copy-start(f32[2048,8]{0,1:T(8,128)S(1)} %get-tuple-element.363) | copy-start | bytes 196612
  151.9 73.4 %copy-start.22 = (f32[2048,8]{0,1:T(8,128)}, f32[2048,8]{0,1:T(8,128)S(1)}, u32[]{:S(2)}) copy-start(f32[2048,8]{0,1:T(8,128)S(1)} %get-tuple-element.364) | copy-start | bytes 196612
  323.3 297.2 %reduce-scatter.7.cloned.1.call-start = ((), (), s32[]{:S(2)}) async-start(), calls=%async_computation.9 | async-start | bytes 2621440 | tf_op jit(solution)/shard_map/reduce_scatter | solution.py:239
  331.0 4.4 copy-start.3
  348.4 4.4 copy-start.3
  371.9 267.7 %reduce-scatter.5.cloned.1.call-start = ((), (), s32[]{:S(2)}) async-start(), calls=%async_computation.8 | async-start | bytes 7864320 | tf_op jit(solution)/shard_map/reduce_scatter | solution.py:236
  374.7 9.7 copy-start.4
  374.7 9.7 copy-start.5
  412.7 6.6 copy-start
  412.7 6.8 copy-start.15
  419.3 4.3 copy-start.6
  422.2 1.3 copy-start.16
  435.8 9.7 copy-start.4
  435.8 9.7 copy-start.5
  473.5 7.1 copy-start
  473.5 7.4 copy-start.15
  480.6 4.2 copy-start.6
  483.5 1.3 copy-start.16
  495.2 8.7 copy-start.2
  503.9 7.6 copy-start.21
  503.9 7.6 copy-start.23
  504.2 2.3 copy-start.11
  515.4 1.7 copy-start.12
  528.0 1.9 copy-start.13
  528.0 516.4 %all-reduce.4.cloned.1.call-start = ((), (), s32[]{:S(2)}) async-start(), calls=%async_computation.12 | async-start | bytes 67108864 | tf_op jit(solution)/shard_map/psum | solution.py:155
  542.4 11.0 copy-start.8
  542.4 11.0 copy-start.19
  575.8 1.6 copy-start.41
  597.7 645.7 %reduce-scatter.9.cloned.1.call-start = ((), (), s32[]{:S(2)}) async-start(), calls=%async_computation.10 | async-start | bytes 14417920 | tf_op jit(solution)/shard_map/reduce_scatter | solution.py:240
  615.8 1.0 copy-start.18
  615.8 4.6 copy-start.28
  615.8 4.6 copy-start.29
  615.8 4.6 copy-start.30
  616.9 22.7 %copy-start.10 = (f32[512,3,256]{2,0,1:T(8,128)S(1)}, f32[512,3,256]{2,0,1:T(8,128)}, u32[]{:S(2)}) copy-start(f32[512,3,256]{2,0,1:T(8,128)} %param.28) | copy-start | bytes 4718596
  620.6 8.7 copy-start.14
  630.3 414.2 %copy-start.25 = (f32[1,2048]{1,0:T(1,128)S(1)}, f32[1,2048]{1,0:T(1,128)}, u32[]{:S(2)}) copy-start(f32[1,2048]{1,0:T(1,128)} %copy-done.24) | copy-start | bytes 24580
  1044.4 32.1 %copy-start.35 = (f32[3,256]{1,0:T(4,128)S(1)}, f32[3,256]{1,0:T(4,128)}, u32[]{:S(2)}) copy-start(f32[3,256]{1,0:T(4,128)} %param.33) | copy-start | bytes 9220
  1044.4 32.1 %copy-start.37 = (f32[3,256]{1,0:T(4,128)S(1)}, f32[3,256]{1,0:T(4,128)}, u32[]{:S(2)}) copy-start(f32[3,256]{1,0:T(4,128)} %param.45) | copy-start | bytes 9220
  1044.5 32.2 %copy-start.38 = (f32[3,256]{1,0:T(4,128)S(1)}, f32[3,256]{1,0:T(4,128)}, u32[]{:S(2)}) copy-start(f32[3,256]{1,0:T(4,128)} %param.39) | copy-start | bytes 9220
  1044.5 32.8 %copy-start.27 = (f32[2,2048]{1,0:T(2,128)S(1)}, f32[2,2048]{1,0:T(2,128)}, u32[]{:S(2)}) copy-start(f32[2,2048]{1,0:T(2,128)} %param.32) | copy-start | bytes 49156
  1044.5 32.8 %copy-start.31 = (f32[2,2048]{1,0:T(2,128)S(1)}, f32[2,2048]{1,0:T(2,128)}, u32[]{:S(2)}) copy-start(f32[2,2048]{1,0:T(2,128)} %param.44) | copy-start | bytes 49156
  1044.5 32.7 %copy-start.32 = (f32[2,2048]{1,0:T(2,128)S(1)}, f32[2,2048]{1,0:T(2,128)}, u32[]{:S(2)}) copy-start(f32[2,2048]{1,0:T(2,128)} %param.38) | copy-start | bytes 49156
  1076.6 28.2 %copy-start.33 = (f32[2,2048]{1,0:T(2,128)}, f32[2,2048]{1,0:T(2,128)S(1)}, u32[]{:S(2)}) copy-start(f32[2,2048]{1,0:T(2,128)S(1)} %get-tuple-element.316) | copy-start | bytes 49156
  1076.6 28.2 %copy-start.39 = (f32[3,256]{1,0:T(4,128)}, f32[3,256]{1,0:T(4,128)S(1)}, u32[]{:S(2)}) copy-start(f32[3,256]{1,0:T(4,128)S(1)} %get-tuple-element.317) | copy-start | bytes 9220
  1077.9 165.5 %copy-start.7 = (f32[512,2,704]{0,2,1:T(8,128)S(1)}, f32[512,2,704]{0,2,1:T(8,128)}, u32[]{:S(2)}) copy-start(f32[512,2,704]{0,2,1:T(8,128)} %param.30) | copy-start | bytes 8650756
Sparse Core Ops, SparseCore 0:
  10.7 109.3 all-gather.8
  122.2 26.1 all-gather.6
  150.6 62.9 all-gather.4
  216.3 100.9 reduce-scatter.10
  323.4 59.6 all-gather.10
  385.3 42.4 reduce-scatter.6
  528.1 111.4 reduce-scatter.4
  644.8 399.6 all-reduce.3
  1047.4 195.9 reduce-scatter.8
where the time goes:
time: 1260 us
  waiting for transfers between devices  775 us (62%)
  matrix products  246 us (20%)
  other arithmetic  130 us (10%)
  local copies, waits for them, and re-layouts  63.7 us (5%)
  blocking collectives  20.1 us (2%)
  between operations  14.7 us (1%)
    psum x1, waiting for transfers between devices, body(): summed = lax.psum(partial_rows, 'mp')  400 us
    reduce_scatter x1, waiting for transfers between devices, body(): lax.psum_scatter(grad_expand_local.reshape(width, 2, hidden_local), 'dp',...  139 us
    all_gather x1, waiting for transfers between devices, body(): lax.all_gather(w_expand.astype(jnp.bfloat16), 'dp', axis=0, tiled=True)  92.8 us
    reduce_scatter x1, waiting for transfers between devices, body(): lax.psum_scatter(grad_reduce_local, 'dp', scatter_dimension=0, tiled=True)  81.8 us
    dot_general x4, matrix products, contract_cols(): lax.dot_general(left, right, (((1,), (1,)), ((), ())), preferred_element_...  52.4 us
    all_gather x1, waiting for transfers between devices, body(): lax.all_gather(w_attend_in.astype(jnp.bfloat16), 'dp', axis=0, tiled=True)  52.3 us
    dot_general x4, matrix products, contract_rows(): lax.dot_general(left, right, (((0,), (0,)), ((), ())), preferred_element_...  46.6 us
    convert_element_type x2, other arithmetic, backward_block(): score_grads = (probs * (prob_grads - middle)).astype(jnp.bfloat16)  30.6 us
  transfers between devices with their start and end apart: 9, of which 6 were waited for; matrix products, arithmetic and copies ran while one was open for 32% of the time, Pallas kernels for 0%

commit v1 on v0

v1 whole, which is shorter than its diff:
```python
import functools
import math

import jax
import jax.numpy as jnp
from jax import lax
from jax.experimental import pallas as pl
from jax.experimental.pallas import tpu as pltpu
from jax.sharding import PartitionSpec as P

HD = 64
ROT = 16
FF = 5632

epsilon = 1e-05
decay_moment = 0.9
decay_average = 0.9
masked_score = -1e30

low = jnp.bfloat16
full = jnp.float32
vmem_limit = 60 << 20


def dot_nt(left, right):
    return lax.dot_general(left, right, (((1,), (1,)), ((), ())), preferred_element_type=full)


def dot_nn(left, right):
    return lax.dot_general(left, right, (((1,), (0,)), ((), ())), preferred_element_type=full)


def dot_tn(left, right):
    return lax.dot_general(left, right, (((0,), (0,)), ((), ())), preferred_element_type=full)


def params(**more):
    return pltpu.CompilerParams(vmem_limit_bytes=vmem_limit, **more)


def cost(flops, moved, trans=0):
    return pl.CostEstimate(flops=int(flops), bytes_accessed=int(moved), transcendentals=int(trans))


def shape(dims, kind):
    return jax.ShapeDtypeStruct(dims, kind)


def advance(weight, grad, moment, average, rate):
    moment_new = decay_moment * moment + grad
    weight_new = weight - rate * (grad + decay_moment * moment_new)
    average_new = decay_average * average + (1.0 - decay_average) * weight_new
    return (weight_new, moment_new, average_new)


def gather_hops(shard):
    n = lax.axis_size("dp")
    rights, lefts = [], []
    right = left = shard
    for k in range(1, n):
        right = lax.ppermute(right, "dp", [(a, a + 1) for a in range(k - 1, n - 1)])
        left = lax.ppermute(left, "dp", [(a, a - 1) for a in range(1, n - k + 1)])
        right, left = yield right, left
        yield
        rights.append(right)
        lefts.append(left)
    yield [shard] + rights + lefts


def scatter_hops(slots):
    n = lax.axis_size("dp")
    right = left = None
    for k in range(1, n):
        to_right, to_left = slots[n - k], slots[k]
        if k > 1:
            to_right = (to_right.astype(full) + right.astype(full)).astype(low)
            to_left = (to_left.astype(full) + left.astype(full)).astype(low)
        right = lax.ppermute(to_right, "dp", [(a, a + 1) for a in range(k)])
        left = lax.ppermute(to_left, "dp", [(a, a - 1) for a in range(n - 1, n - 1 - k, -1)])
        right, left = yield right, left
        yield
    yield slots[0] + right.astype(full) + left.astype(full)


def swap(value, mask, axis="mp"):
    n = lax.axis_size(axis)
    return lax.ppermute(value, axis, [(a, a ^ mask) for a in range(n)])


def small_sum(value, axis):
    n = lax.axis_size(axis)
    if n & (n - 1):
        return lax.psum(value, axis)
    mask = 1
    while mask < n:
        value = value + swap(value, mask, axis)
        mask *= 2
    return value


def norm_kernel(x_ref, p_ref, o_ref):
    x = x_ref[...].astype(full)
    centred = x - jnp.mean(x, axis=-1, keepdims=True)
    inv = lax.rsqrt(jnp.mean(centred * centred, axis=-1, keepdims=True) + epsilon)
    o_ref[...] = (centred * inv * p_ref[0:1] + p_ref[1:2]).astype(low)


def layer_norm(rows, norm_params):
    count, width = rows.shape
    block = min(256, count)
    return pl.pallas_call(
        norm_kernel,
        grid=(count // block,),
        in_specs=[
            pl.BlockSpec((block, width), lambda i: (i, 0)),
            pl.BlockSpec((2, width), lambda i: (0, 0)),
        ],
        out_specs=pl.BlockSpec((block, width), lambda i: (i, 0)),
        out_shape=shape((count, width), low),
        compiler_params=params(),
        cost_estimate=cost(8 * count * width, 4 * count * width),
        name="layer_norm",
    )(rows, norm_params)


def fetch(n, me, pieces, target_of, sems, action):
    def run(source, index, sem):
        copy = pltpu.make_async_copy(source, target_of(index), sem)
        if action == "start":
            copy.start()
        else:
            copy.wait()

    if len(pieces) == 1:
        for j in range(n):
            run(pieces[0].at[j], j, sems.at[j])
        return
    run(pieces[0], me, sems.at[0])
    for k in range(1, n):

        @pl.when(me >= k)
        def _(k=k):
            run(pieces[k], me - k, sems.at[k])

        @pl.when(me + k < n)
        def _(k=k):
            run(pieces[n - 1 + k], me + k, sems.at[n - 1 + k])


def gates_of(w_ref, h, c):
    units = w_ref.shape[1]
    both = dot_nt(w_ref[0:2].reshape(2 * units, w_ref.shape[2]), h)
    gate, upper = both[:units], both[units:]
    active_grad = dot_nt(w_ref[2], c)
    sigmoid = jax.nn.sigmoid(gate)
    swish = gate * sigmoid
    active = (swish * upper).astype(low)
    gate_grad = active_grad * upper * sigmoid * (1.0 + gate * (1.0 - sigmoid))
    return active, jnp.concatenate([gate_grad, active_grad * swish], axis=0).astype(low)


def add_grads(acc, step, active, gates_grad, h, c):
    units = active.shape[0]

    @pl.when(step == 0)
    def _():
        acc[: 2 * units] = dot_nn(gates_grad, h)
        acc[2 * units :] = dot_nn(active, c)

    @pl.when(step > 0)
    def _():
        acc[: 2 * units] += dot_nn(gates_grad, h)
        acc[2 * units :] += dot_nn(active, c)


def store_grads(n, acc, out_ref):
    piece = out_ref.shape[2]
    for j in range(n):
        out_ref[j] = acc[:, j * piece : (j + 1) * piece].astype(low)


def wide_target(w_ref, piece):
    return lambda index: w_ref.at[:, :, pl.ds(pl.multiple_of(index * piece, piece), piece)]


def feed_kernel(n, count, steps, me_ref, *refs):
    pieces = refs[:count]
    h_ref, c_ref, act_ref, grad_ref, w_ref, out_ref, acc, sems = refs[count:]
    step = pl.program_id(0)
    target_of = wide_target(w_ref, out_ref.shape[2])

    @pl.when(step == 0)
    def _():
        fetch(n, me_ref[0], pieces, target_of, sems, "start")
        fetch(n, me_ref[0], pieces, target_of, sems, "wait")

    h = h_ref[...]
    c = c_ref[...]
    active, gates_grad = gates_of(w_ref, h, c)
    act_ref[...] = active
    grad_ref[...] = gates_grad
    add_grads(acc, step, active, gates_grad, h, c)

    @pl.when(step == steps - 1)
    def _():
        store_grads(n, acc, out_ref)


def feed_chunk(n, me, pieces, hidden, cot):
    rows, width = hidden.shape
    units, piece = pieces[0].shape[-2:]
    count = len(pieces)
    block = min(512, rows)
    steps = rows // block
    row_spec = pl.BlockSpec((block, width), lambda i, m: (i, 0))
    return pl.pallas_call(
        functools.partial(feed_kernel, n, count, steps),
        grid_spec=pltpu.PrefetchScalarGridSpec(
            num_scalar_prefetch=1,
            grid=(steps,),
            in_specs=[pl.BlockSpec(memory_space=pl.ANY)] * count + [row_spec, row_spec],
            out_specs=[
                pl.BlockSpec((units, block), lambda i, m: (0, i)),
                pl.BlockSpec((2 * units, block), lambda i, m: (0, i)),
                pl.BlockSpec((3, units, width), lambda i, m: (0, 0, 0)),
                pl.BlockSpec((n, 3 * units, piece), lambda i, m: (0, 0, 0)),
            ],
            scratch_shapes=[
                pltpu.VMEM((3 * units, width), full),
                pltpu.SemaphoreType.DMA((2 * n - 1,)),
            ],
        ),
        out_shape=[
            shape((units, rows), low),
            shape((2 * units, rows), low),
            shape((3, units, width), low),
            shape((n, 3 * units, piece), low),
        ],
        compiler_params=params(),
        cost_estimate=cost(
            12 * rows * width * units, 4 * rows * width + 20 * units * width, rows * units
        ),
        name="feed_chunk",
    )(me, *pieces, hidden, cot)


def last_kernel(n, count, split, info_ref, *refs):
    pieces = refs[:count]
    h_ref, c_ref, hid_ref, out_ref = refs[count : count + 4]
    w_ref, sems = refs[-2:]
    act_ref, grad_ref = refs[-4:-2]
    parts = refs[count + 4 : -4]
    target_of = wide_target(w_ref, w_ref.shape[2] // n)
    step = pl.program_id(0)

    @pl.when(step == 0)
    def _():
        fetch(n, info_ref[3], pieces, target_of, sems, "start")
        fetch(n, info_ref[3], pieces, target_of, sems, "wait")

    active, gates_grad = gates_of(w_ref, h_ref[...], c_ref[...])
    act_ref[...] = active
    grad_ref[...] = gates_grad
    joined = w_ref[0:2].reshape(gates_grad.shape[0], w_ref.shape[2])
    hid = (hid_ref[...].astype(full) + dot_tn(gates_grad, joined)).astype(low)
    out = (out_ref[...].astype(full) + dot_tn(active, w_ref[2])).astype(low)
    if not split:
        parts[0][...] = hid
        parts[1][...] = out
        return
    sub = hid.shape[0] // 4
    high = jnp.where(step % 2 == 0, info_ref[1], info_ref[2])
    small = jnp.where(step % 2 == 0, info_ref[2], info_ref[1])
    for half in range(2):

        @pl.when(step // 2 == half)
        def _(half=half):
            for ref, value in ((parts[2 * half], hid), (parts[2 * half + 1], out)):
                for i in range(4):
                    at = ((i // 2) ^ high) * 2 + ((i % 2) ^ small)
                    place = pl.ds(pl.multiple_of(at * sub, sub), sub)
                    ref[place, :] = value[i * sub : (i + 1) * sub]


def feed_last(n, info, split, pieces, hidden, cot, hid_early, out_early):
    rows, width = hidden.shape
    units = pieces[0].shape[-2]
    count = len(pieces)
    if split:
        block, steps = rows // 4, 4
        place = lambda i, m: (m[0] ^ (1 - i // 2)) * 2 + i % 2
        part_specs = [pl.BlockSpec((block, width), lambda i, m: (jnp.minimum(i, 1), 0))] * 2
        part_specs += [pl.BlockSpec((block, width), lambda i, m: (jnp.maximum(i, 2) - 2, 0))] * 2
        part_shapes = [shape((rows // 2, width), low)] * 4
    else:
        block = min(256, rows)
        steps = rows // block
        place = lambda i, m: i
        part_specs = [pl.BlockSpec((block, width), lambda i, m: (i, 0))] * 2
        part_shapes = [shape((rows, width), low)] * 2
    row_spec = pl.BlockSpec((block, width), lambda i, m: (place(i, m), 0))
    return pl.pallas_call(
        functools.partial(last_kernel, n, count, split),
        grid_spec=pltpu.PrefetchScalarGridSpec(
            num_scalar_prefetch=1,
            grid=(steps,),
            in_specs=[pl.BlockSpec(memory_space=pl.ANY)] * count + [row_spec] * 4,
            out_specs=part_specs
            + [
                pl.BlockSpec((units, block), lambda i, m: (0, place(i, m))),
                pl.BlockSpec((2 * units, block), lambda i, m: (0, place(i, m))),
            ],
            scratch_shapes=[
                pltpu.VMEM((3, units, width), low),
                pltpu.SemaphoreType.DMA((2 * n - 1,)),
            ],
        ),
        out_shape=part_shapes + [shape((units, rows), low), shape((2 * units, rows), low)],
        compiler_params=params(),
        cost_estimate=cost(12 * rows * width * units, 12 * rows * width, rows * units),
        name="feed_last",
    )(info, *pieces, hidden, cot, hid_early, out_early)


def feed_grads_kernel(n, steps, h_ref, c_ref, act_ref, grad_ref, out_ref, acc):
    step = pl.program_id(0)
    add_grads(acc, step, act_ref[...], grad_ref[...], h_ref[...], c_ref[...])

    @pl.when(step == steps - 1)
    def _():
        store_grads(n, acc, out_ref)


def feed_grads(n, hidden, cot, active, gates_grad):
    rows, width = hidden.shape
    units = active.shape[0]
    piece = width // n
    block = min(512, rows)
    steps = rows // block
    row_spec = pl.BlockSpec((block, width), lambda i: (i, 0))
    return pl.pallas_call(
        functools.partial(feed_grads_kernel, n, steps),
        grid=(steps,),
        in_specs=[
            row_spec,
            row_spec,
            pl.BlockSpec((units, block), lambda i: (0, i)),
            pl.BlockSpec((2 * units, block), lambda i: (0, i)),
        ],
        out_specs=pl.BlockSpec((n, 3 * units, piece), lambda i: (0, 0, 0)),
        out_shape=shape((n, 3 * units, piece), low),
        scratch_shapes=[pltpu.VMEM((3 * units, width), full)],
        compiler_params=params(),
        cost_estimate=cost(6 * rows * width * units, 4 * rows * width + 12 * units * width),
        name="feed_grads",
    )(hidden, cot, active, gates_grad)


def turn(values, cosine, sine, half):
    cols = values.shape[1]
    lane = lax.broadcasted_iota(jnp.int32, (1, cols), 1) % HD
    other = jnp.where(
        lane < half, pltpu.roll(values, cols - half, 1), pltpu.roll(values, half, 1)
    )
    repeat = cols // cosine.shape[1]
    if repeat > 1:
        cosine = jnp.concatenate([cosine] * repeat, axis=1)
        sine = jnp.concatenate([sine] * repeat, axis=1)
    return values * cosine + other * sine


def project_kernel(n, count, me_ref, *refs):
    pieces = refs[:count]
    h_ref, c_ref, cos_ref, sin_ref, bias_ref, q_ref, k_ref, v_ref, o_ref, w_ref, sems = refs[
        count:
    ]
    piece = pieces[0].shape[-2]

    def target_of(index):
        return w_ref.at[:, pl.ds(pl.multiple_of(index * piece, piece), piece), :]

    @pl.when(pl.program_id(0) == 0)
    def _():
        fetch(n, me_ref[0], pieces, target_of, sems, "start")
        fetch(n, me_ref[0], pieces, target_of, sems, "wait")

    h = h_ref[...]
    cosine, sine = cos_ref[...], sin_ref[...]
    half = ROT // 2
    q_ref[...] = turn(dot_nn(h, w_ref[0]) + bias_ref[0:1], cosine, sine, half).astype(low)
    k_ref[...] = turn(dot_nn(h, w_ref[1]) + bias_ref[1:2], cosine, sine, half).astype(low)
    v_ref[...] = (dot_nn(h, w_ref[2]) + bias_ref[2:3]).astype(low)
    o_ref[...] = dot_nn(c_ref[...], w_ref[3]).astype(low)


def project(n, me, pieces, hidden, cot, cosine, sine, bias):
    rows, width = hidden.shape
    piece, cols = pieces[0].shape[-2:]
    count = len(pieces)
    block = min(512, rows)
    row_spec = pl.BlockSpec((block, width), lambda i, m: (i, 0))
    angle_spec = pl.BlockSpec((block, 128), lambda i, m: (i, 0))
    out_spec = pl.BlockSpec((block, cols), lambda i, m: (i, 0))
    return pl.pallas_call(
        functools.partial(project_kernel, n, count),
        grid_spec=pltpu.PrefetchScalarGridSpec(
            num_scalar_prefetch=1,
            grid=(rows // block,),
            in_specs=[pl.BlockSpec(memory_space=pl.ANY)] * count
            + [row_spec, row_spec, angle_spec, angle_spec]
            + [pl.BlockSpec((3, cols), lambda i, m: (0, 0))],
            out_specs=[out_spec] * 4 + [pl.BlockSpec((4, width, cols), lambda i, m: (0, 0, 0))],
            scratch_shapes=[pltpu.SemaphoreType.DMA((2 * n - 1,))],
        ),
        out_shape=[shape((rows, cols), low)] * 4 + [shape((4, width, cols), low)],
        compiler_params=params(),
        cost_estimate=cost(8 * rows * width * cols, 4 * rows * width + 16 * width * cols),
        name="project",
    )(me, *pieces, hidden, cot, cosine, sine, bias)


def attend_kernel(block, q_ref, k_ref, v_ref, o_ref, cos_ref, sin_ref, ctx_ref, mg_ref, bias_ref, dq, dk, dv):
    length, lanes = q_ref.shape
    scale = HD ** (-0.5)
    for head in range(lanes // HD):
        cols = slice(head * HD, (head + 1) * HD)
        for i in range(length // block):
            rows = slice(i * block, (i + 1) * block)
            end = (i + 1) * block
            q = q_ref[rows, cols]
            o = o_ref[rows, cols]
            k = k_ref[:end, cols]
            v = v_ref[:end, cols]
            scores = dot_nt(q, k) * scale
            row = i * block + lax.broadcasted_iota(jnp.int32, (block, end), 0)
            col = lax.broadcasted_iota(jnp.int32, (block, end), 1)
            scores = jnp.where(col <= row, scores, masked_score)
            top = jnp.max(scores, axis=-1, keepdims=True)
            weights = jnp.exp(scores - top)
            probs = weights * (1.0 / jnp.sum(weights, axis=-1, keepdims=True))
            probs_low = probs.astype(low)
            ctx_ref[rows, cols] = dot_nn(probs_low, v).astype(low)
            prob_grads = dot_nt(o, v)
            middle = jnp.sum(probs * prob_grads, axis=-1, keepdims=True)
            score_grads = (probs * (prob_grads - middle)).astype(low)
            dq[rows, cols] = dot_nn(score_grads, k) * scale
            key_part = dot_tn(score_grads, q) * scale
            value_part = dot_tn(probs_low, o)
            if i == 0:
                dk[:end, cols] = key_part
                dv[:end, cols] = value_part
                if end < length:
                    dk[end:, cols] = jnp.zeros((length - end, HD), full)
                    dv[end:, cols] = jnp.zeros((length - end, HD), full)
            else:
                dk[:end, cols] += key_part
                dv[:end, cols] += value_part
    cosine, sine = cos_ref[...], -sin_ref[...]
    half = ROT // 2
    sums = []
    for part, grads in enumerate(
        (turn(dq[...], cosine, sine, half), turn(dk[...], cosine, sine, half), dv[...])
    ):
        rounded = grads.astype(low)
        mg_ref[part] = rounded
        sums.append(jnp.sum(rounded.astype(full), axis=0, keepdims=True))
    total = jnp.concatenate(sums, axis=0)

    @pl.when(pl.program_id(1) == 0)
    def _():
        bias_ref[...] = total

    @pl.when(pl.program_id(1) > 0)
    def _():
        bias_ref[...] += total


def attend(batch, q, k, v, o, cosine, sine):
    rows, cols = q.shape
    length = rows // batch
    lanes = 128
    spec = pl.BlockSpec((length, lanes), lambda p, b: (b, p))
    angle_spec = pl.BlockSpec((length, 128), lambda p, b: (b, 0))
    return pl.pallas_call(
        functools.partial(attend_kernel, min(512, length)),
        grid=(cols // lanes, batch),
        in_specs=[spec] * 4 + [angle_spec] * 2,
        out_specs=[
            spec,
            pl.BlockSpec((3, length, lanes), lambda p, b: (0, b, p)),
            pl.BlockSpec((3, lanes), lambda p, b: (0, p)),
        ],
        out_shape=[
            shape((rows, cols), low),
            shape((3, rows, cols), low),
            shape((3, cols), full),
        ],
        scratch_shapes=[pltpu.VMEM((length, lanes), full)] * 3,
        compiler_params=params(),
        cost_estimate=cost(
            40 * rows * length * cols, 20 * rows * cols, rows * length * cols // HD
        ),
        name="attend",
    )(q, k, v, o, cosine, sine)


def attend_grads_kernel(n, me_ref, h_ref, c_ref, mg_ref, ctx_ref, *refs):
    own_ref, *slot_refs = refs[:n]
    wide = refs[n]
    step = pl.program_id(0)
    cols = ctx_ref.shape[1]

    @pl.when(step == 0)
    def _():
        for part in range(3):
            wide[:, part * cols : (part + 1) * cols] = mg_ref[part]

    grad = dot_tn(h_ref[...], wide[...])
    grads = [grad[:, part * cols : (part + 1) * cols] for part in range(3)]
    grads.append(dot_tn(c_ref[...], ctx_ref[...]))
    for j in range(n):

        @pl.when(step == j)
        def _(j=j):
            for part in range(4):
                if j == 0:
                    own_ref[part] = grads[part]
                else:
                    slot_refs[j - 1][part] = grads[part].astype(low)


def attend_grads(n, me, hidden, cot, mixed_grad, context):
    rows, width = hidden.shape
    cols = context.shape[1]
    piece = width // n
    whole3 = pl.BlockSpec((4, piece, cols), lambda i, m: (0, 0, 0))
    cut_spec = pl.BlockSpec((rows, piece), lambda i, m: (0, lax.rem(m[0] + i, n)))
    return pl.pallas_call(
        functools.partial(attend_grads_kernel, n),
        grid_spec=pltpu.PrefetchScalarGridSpec(
            num_scalar_prefetch=1,
            grid=(n,),
            in_specs=[
                cut_spec,
                cut_spec,
                pl.BlockSpec((3, rows, cols), lambda i, m: (0, 0, 0)),
                pl.BlockSpec((rows, cols), lambda i, m: (0, 0)),
            ],
            out_specs=[whole3] * n,
            scratch_shapes=[pltpu.VMEM((rows, 3 * cols), low)],
        ),
        out_shape=[shape((4, piece, cols), full)] + [shape((4, piece, cols), low)] * (n - 1),
        compiler_params=params(),
        cost_estimate=cost(8 * rows * width * cols, 4 * rows * width + 16 * width * cols),
        name="attend_grads",
    )(me, hidden, cot, mixed_grad, context)


def early_kernel(ctx_ref, mg_ref, act_ref, grad_ref, wa_ref, wf_ref, hid_ref, out_ref):
    hid = dot_nt(mg_ref[0], wa_ref[0]) + dot_nt(mg_ref[1], wa_ref[1]) + dot_nt(mg_ref[2], wa_ref[2])
    hid += dot_tn(grad_ref[...], wf_ref[0:2].reshape(grad_ref.shape[0], wf_ref.shape[2]))
    hid_ref[...] = hid.astype(low)
    out_ref[...] = (dot_nt(ctx_ref[...], wa_ref[3]) + dot_tn(act_ref[...], wf_ref[2])).astype(low)


def early_parts(context, mixed_grad, active, gates_grad, w_attend, w_feed):
    rows, cols = context.shape
    units, width = w_feed.shape[1:]
    block = min(256, rows)
    out_spec = pl.BlockSpec((block, width), lambda i: (i, 0))
    return pl.pallas_call(
        early_kernel,
        grid=(rows // block,),
        in_specs=[
            pl.BlockSpec((block, cols), lambda i: (i, 0)),
            pl.BlockSpec((3, block, cols), lambda i: (0, i, 0)),
            pl.BlockSpec((units, block), lambda i: (0, i)),
            pl.BlockSpec((2 * units, block), lambda i: (0, i)),
            pl.BlockSpec((4, width, cols), lambda i: (0, 0, 0)),
            pl.BlockSpec((3, units, width), lambda i: (0, 0, 0)),
        ],
        out_specs=[out_spec, out_spec],
        out_shape=[shape((rows, width), low)] * 2,
        compiler_params=params(),
        cost_estimate=cost(
            2 * rows * width * (4 * cols + 3 * units),
            4 * rows * width + 2 * (rows + width) * (4 * cols + 3 * units),
        ),
        name="early_parts",
    )(context, mixed_grad, active, gates_grad, w_attend, w_feed)


def sixteenth(which, m):
    return m[0] * 8 + (m[1] * 2 + m[2] if which == 0 else 4 + m[2] * 2 + m[1])


def back_kernel(info_ref, *refs):
    p_ref = refs[6]
    sums_ref = refs[9]
    total = 0.0
    for x_ref, near_ref, far_ref, back_ref in zip(refs[0:2], refs[2:4], refs[4:6], refs[7:9]):
        x = x_ref[...].astype(full)
        centred = x - jnp.mean(x, axis=-1, keepdims=True)
        inv = lax.rsqrt(jnp.mean(centred * centred, axis=-1, keepdims=True) + epsilon)
        normal = centred * inv
        grad = near_ref[...].astype(full) + far_ref[...].astype(full)
        scaled = grad * p_ref[0:1]
        back = inv * (
            scaled
            - jnp.mean(scaled, axis=-1, keepdims=True)
            - normal * jnp.mean(scaled * normal, axis=-1, keepdims=True)
        )
        back_ref[...] = back.astype(low)
        total += jnp.concatenate(
            [jnp.sum(grad * normal, axis=0, keepdims=True), jnp.sum(grad, axis=0, keepdims=True)],
            axis=0,
        )
    sums_ref[...] = total


def back_rows(info, rows, near, far, norm_params):
    count, width = near[0].shape
    spec = pl.BlockSpec((count, width), lambda i, m: (0, 0))
    pair = pl.BlockSpec((2, width), lambda i, m: (0, 0))
    return pl.pallas_call(
        back_kernel,
        grid_spec=pltpu.PrefetchScalarGridSpec(
            num_scalar_prefetch=1,
            grid=(1,),
            in_specs=[
                pl.BlockSpec((count, width), lambda i, m: (sixteenth(0, m), 0)),
                pl.BlockSpec((count, width), lambda i, m: (sixteenth(1, m), 0)),
            ]
            + [spec] * 4
            + [pair],
            out_specs=[spec, spec, pair],
        ),
        out_shape=[shape((count, width), low)] * 2 + [shape((2, width), full)],
        compiler_params=params(),
        cost_estimate=cost(40 * count * width, 16 * count * width),
        name="back_rows",
    )(info, rows, rows, *near, *far, norm_params)


def add_kernel(info_ref, *refs):
    for x_ref, near_ref, far_ref, out_ref in zip(refs[0:2], refs[2:4], refs[4:6], refs[6:8]):
        total = x_ref[...].astype(full) + near_ref[...].astype(full) + far_ref[...].astype(full)
        out_ref[...] = total.astype(low)


def add_rows(info, rows, near, far):
    count, width = near[0].shape
    spec = pl.BlockSpec((count, width), lambda i, m: (0, 0))
    return pl.pallas_call(
        add_kernel,
        grid_spec=pltpu.PrefetchScalarGridSpec(
            num_scalar_prefetch=1,
            grid=(1,),
            in_specs=[
                pl.BlockSpec((count, width), lambda i, m: (sixteenth(0, m), 0)),
                pl.BlockSpec((count, width), lambda i, m: (sixteenth(1, m), 0)),
            ]
            + [spec] * 4,
            out_specs=[spec, spec],
        ),
        out_shape=[shape((count, width), low)] * 2,
        compiler_params=params(),
        cost_estimate=cost(4 * count * width, 16 * count * width),
        name="add_rows",
    )(info, rows, rows, *near, *far)


def pack_kernel(info_ref, *refs):
    pieces, out_ref, sems = refs[:8], refs[8], refs[9]
    block = pieces[0].shape[0]
    x, y = info_ref[1], info_ref[2]
    copies = []
    for i, piece in enumerate(pieces):
        high, small = (i // 2) % 2, i % 2
        if i < 4:
            at = (x ^ high) * 2 + (y ^ small)
        else:
            at = 4 + (y ^ high) * 2 + (x ^ small)
        place = out_ref.at[pl.ds(pl.multiple_of(at * block, block), block), :]
        copies.append(pltpu.make_async_copy(piece, place, sems.at[i]))
    for copy in copies:
        copy.start()
    for copy in copies:
        copy.wait()


def pack_rows(info, pieces):
    block, width = pieces[0].shape
    return pl.pallas_call(
        pack_kernel,
        grid_spec=pltpu.PrefetchScalarGridSpec(
            num_scalar_prefetch=1,
            grid=(1,),
            in_specs=[pl.BlockSpec((block, width), lambda i, m: (0, 0))] * 8,
            out_specs=pl.BlockSpec(memory_space=pl.ANY),
            scratch_shapes=[pltpu.SemaphoreType.DMA((8,))],
        ),
        out_shape=shape((8 * block, width), low),
        compiler_params=params(),
        cost_estimate=cost(0, 32 * block * width),
        name="pack_rows",
    )(info, *pieces)


def finish_kernel(info_ref, *refs):
    own_ref, other_ref, out_ref = refs[-3:]
    mine = (pl.program_id(0) // 4) == info_ref[0]

    def store(value):
        if len(refs) == 4:
            value = refs[0][...].astype(full) + value.astype(full)
        out_ref[...] = value

    @pl.when(mine)
    def _():
        store(own_ref[...])

    @pl.when(jnp.logical_not(mine))
    def _():
        store(other_ref[...])


def finish_rows(info, own, other, cot=None):
    rows, width = 2 * own.shape[0], own.shape[1]
    extra = () if cot is None else (cot,)
    block = rows // 8
    spec = pl.BlockSpec((block, width), lambda i, m: (i, 0))
    edge = lambda i: jnp.where(i < 4, 0, 3)
    return pl.pallas_call(
        finish_kernel,
        grid_spec=pltpu.PrefetchScalarGridSpec(
            num_scalar_prefetch=1,
            grid=(8,),
            in_specs=[spec] * len(extra)
            + [
                pl.BlockSpec((block, width), lambda i, m: (jnp.where(i // 4 == m[0], i % 4, edge(i)), 0)),
                pl.BlockSpec((block, width), lambda i, m: (jnp.where(i // 4 == m[0], edge(i), i % 4), 0)),
            ],
            out_specs=spec,
        ),
        out_shape=shape((rows, width), low if cot is None else full),
        compiler_params=params(),
        cost_estimate=cost(2 * rows * width, 8 * rows * width),
        name="finish_rows",
    )(info, *extra, own, other)


def update_kernel(rates, count, *refs):
    g_ref = refs[0]
    ins = refs[1:7]
    outs = refs[7 + count :]
    for which, rate in enumerate(rates):
        grad = g_ref[:2] if which == 0 else g_ref[2]
        grad = grad.astype(full)
        w, m, a = (ref[...] for ref in ins[3 * which : 3 * which + 3])
        g_out, w_out, m_out, a_out = outs[4 * which : 4 * which + 4]
        g_out[...] = grad
        w_out[...], m_out[...], a_out[...] = advance(w, grad, m, a, rate)


def update_feed(start, grads, states, rates, begun=()):
    _, units, piece = grads.shape
    block = math.gcd(start, units)
    while block > 128 and block % 16 == 0:
        block //= 2
    at = start // block
    pair = pl.BlockSpec((2, block, piece), lambda i: (0, at + i, 0))
    single = pl.BlockSpec((block, piece), lambda i: (at + i, 0))
    total = states[0].shape[1]
    return pl.pallas_call(
        functools.partial(update_kernel, rates, len(begun)),
        grid=(units // block,),
        in_specs=[pl.BlockSpec((3, block, piece), lambda i: (0, i, 0))]
        + [pair] * 3
        + [single] * 3
        + [pl.BlockSpec(memory_space=pl.ANY)] * len(begun),
        out_specs=[pair] * 4 + [single] * 4,
        out_shape=[shape((2, total, piece), full)] * 4 + [shape((total, piece), full)] * 4,
        input_output_aliases={7 + i: i for i in range(len(begun))},
        compiler_params=params(),
        cost_estimate=cost(30 * units * piece, 3 * 30 * units * piece),
        name="update_feed",
    )(grads, *states, *begun)


def body(
    inputs,
    positions,
    cotangent,
    w_attend_in,
    w_attend_out,
    w_expand,
    w_reduce,
    norm_params,
    attend_bias,
    moment_attend_in,
    moment_attend_out,
    moment_expand,
    moment_reduce,
    moment_norm,
    moment_bias,
    average_attend_in,
    average_attend_out,
    average_expand,
    average_reduce,
    average_norm,
    average_bias,
):
    batch, length, width = inputs.shape
    rows = batch * length
    units = w_expand.shape[2]
    n = lax.axis_size("dp")
    group = lax.axis_size("mp")
    me = lax.axis_index("dp").astype(jnp.int32).reshape(1)
    spot = lax.axis_index("mp").astype(jnp.int32)
    info = jnp.stack([spot & 1, (spot >> 1) & 1, (spot >> 2) & 1, me[0]])
    fast = group == 8

    expand_t = jnp.transpose(w_expand, (1, 2, 0))
    reduce_t = jnp.transpose(w_reduce)
    in_t = jnp.transpose(w_attend_in, (1, 0, 2))
    cut = units // 2 // 16 * 16
    shards = [
        jnp.concatenate([expand_t[:, a:b], reduce_t[None, a:b]], axis=0).astype(low)
        for a, b in ((0, cut), (cut, units))
    ]
    attend_shard = jnp.concatenate([in_t, w_attend_out[None]], axis=0).astype(low)
    attend_pieces = [lax.all_gather(attend_shard, "dp")]
    first_shard, _ = lax.optimization_barrier((shards[0], attend_shard))
    first_pieces = [lax.all_gather(first_shard, "dp")]

    tokens = inputs.reshape(rows, width)
    cot = cotangent.reshape(rows, width)
    hidden = layer_norm(tokens, norm_params)

    half = ROT // 2
    lane = jnp.arange(128, dtype=jnp.int32) % HD
    frequency = 10000.0 ** (-((lane % half).astype(full) * 2.0 / ROT))
    angles = positions.reshape(rows).astype(full)[:, None] * frequency[None, :]
    cosine = jnp.where(lane < ROT, jnp.cos(angles), 1.0)
    sine = jnp.where(lane < half, -jnp.sin(angles), jnp.where(lane < ROT, jnp.sin(angles), 0.0))

    q, k, v, o, w_attend = project(n, me, attend_pieces, hidden, cot, cosine, sine, attend_bias)
    context, mixed_grad, bias_part = attend(batch, q, k, v, o, cosine, sine)
    attend_slots = attend_grads(n, me, hidden, cot, mixed_grad, context)
    last_shard, first_piece, attend_slots = lax.optimization_barrier(
        (shards[1], first_pieces[0], attend_slots)
    )
    active, gates_grad, w_feed, first_grads = feed_chunk(n, me, [first_piece], hidden, cot)
    hid_early, out_early = early_parts(context, mixed_grad, active, gates_grad, w_attend, w_feed)
    bias_grad = small_sum(bias_part, "dp")
    gathering, scattering = gather_hops(last_shard), scatter_hops(attend_slots)
    arrived = lax.optimization_barrier((next(gathering), first_grads))
    gathering.send(arrived[0])
    first_grads = arrived[1]
    for k in range(2, n):
        beside = (hid_early, out_early, bias_grad) if k == 2 else ()
        arrived = lax.optimization_barrier((next(gathering), next(scattering), beside))
        gathering.send(arrived[0])
        scattering.send(arrived[1])
        if k == 2:
            hid_early, out_early, bias_grad = arrived[2]
    last_pieces = next(gathering)
    arrived, last_pieces = lax.optimization_barrier((next(scattering), last_pieces))
    scattering.send(arrived)
    attend_grad = next(scattering)

    def scatter(grads):
        return lax.psum_scatter(grads, "dp", scatter_dimension=0, tiled=False)

    first_grads, _ = lax.optimization_barrier((first_grads, last_pieces))
    first_grads = scatter(first_grads)

    if fast:
        other_hid, other_out, own_hid, own_out, active, gates_grad = feed_last(
            n, info, True, last_pieces, hidden, cot, hid_early, out_early
        )
        came_hid, came_out = swap(other_hid, 1), swap(other_out, 1)
        e = rows // 8
        s = e // 2

        def send_rows(own, came):
            own = [own[i * e : (i + 1) * e].astype(full) + came[i * e : (i + 1) * e].astype(full) for i in range(4)]
            to_x, to_y = own[1].astype(low), own[3].astype(low)
            return own, (to_x, to_y), (swap(to_x, 2), swap(to_y, 4))

        def reduce_rows(own, came):
            over_x, over_y = came
            first = own[0] + over_x.astype(full)
            second = own[2] + over_y.astype(full)
            far = [swap(first[s:].astype(low), 4), swap(second[s:].astype(low), 2)]
            return [first[:s].astype(low), second[:s].astype(low)], far

        def spread_rows(first, second):
            first_y, second_x = swap(first, 4), swap(second, 2)
            first_x, second_y = swap(first, 2), swap(second, 4)
            first_xy, second_xy = swap(first_y, 2), swap(second_x, 4)
            return [first, first_y, first_x, first_xy, second, second_x, second_y, second_xy]

        own_hid, sent, came_hid = send_rows(own_hid, came_hid)
        active, gates_grad, _ = lax.optimization_barrier((active, gates_grad, sent))
        last_grads = feed_grads(n, hidden, cot, active, gates_grad)
        came_hid, last_grads, came_out, own_out = lax.optimization_barrier(
            (came_hid, last_grads, came_out, own_out)
        )
        own_out, _, came_out = send_rows(own_out, came_out)
        near, far = reduce_rows(own_hid, came_hid)
        back_a, back_b, norm_part = back_rows(info, tokens, near, far, norm_params)
        near, far = reduce_rows(own_out, came_out)
        out_a, out_b = add_rows(info, tokens, near, far)
        hid_pieces = spread_rows(back_a, back_b)
        hid_pieces[1], hid_pieces[5], out_a, out_b = lax.optimization_barrier(
            (hid_pieces[1], hid_pieces[5], out_a, out_b)
        )
        out_pieces = spread_rows(out_a, out_b)
        norm_grad = small_sum(small_sum(norm_part, "mp"), "dp")
        last_grads = scatter(last_grads)
    else:
        hid_part, out_part, active, gates_grad = feed_last(
            n, info, False, last_pieces, hidden, cot, hid_early, out_early
        )
        last_grads = scatter(feed_grads(n, hidden, cot, active, gates_grad))
        hidden_grad = lax.psum(hid_part, "mp").astype(full)
        summed = lax.psum(out_part, "mp").astype(full)
        values = tokens.astype(full)
        output = (values + summed).astype(low)
        centred = values - jnp.mean(values, axis=-1, keepdims=True)
        inv = lax.rsqrt(jnp.mean(centred * centred, axis=-1, keepdims=True) + epsilon)
        normal = centred * inv
        scaled = hidden_grad * norm_params[0]
        back = inv * (
            scaled
            - jnp.mean(scaled, axis=-1, keepdims=True)
            - normal * jnp.mean(scaled * normal, axis=-1, keepdims=True)
        )
        input_grad = cot.astype(full) + back
        norm_part = jnp.stack([jnp.sum(hidden_grad * normal, axis=0), jnp.sum(hidden_grad, axis=0)])
        norm_grad = small_sum(norm_part, "dp")

    grad_in = jnp.transpose(attend_grad[:3], (1, 0, 2))
    grad_out = attend_grad[3]

    total_tokens = rows * n
    new_in, moment_in_new, average_in_new = advance(
        w_attend_in, grad_in, moment_attend_in, average_attend_in, 0.5 / math.sqrt(width * total_tokens)
    )
    new_out, moment_out_new, average_out_new = advance(
        w_attend_out, grad_out, moment_attend_out, average_attend_out, 1.8 / math.sqrt(width * batch * n)
    )
    rates = (1.6 / math.sqrt(width * total_tokens), 0.77 / math.sqrt(FF * total_tokens))
    states = [jnp.transpose(a, (1, 2, 0)) for a in (w_expand, moment_expand, average_expand)]
    states += [jnp.transpose(a) for a in (w_reduce, moment_reduce, average_reduce)]
    first_grads = first_grads.reshape(3, cut, -1)
    last_grads = last_grads.reshape(3, units - cut, -1)
    begun = update_feed(0, first_grads, states, rates)
    if fast:
        updated = (norm_grad, new_in, new_out, begun)
        hid_pieces, updated = lax.optimization_barrier((hid_pieces, updated))
        norm_grad, new_in, new_out, begun = updated
    done = update_feed(cut, last_grads, states, rates, begun)
    if fast:
        mine_hid = pack_rows(info, hid_pieces)
        mine_out = pack_rows(info, out_pieces)
        input_grad = finish_rows(info, mine_hid, swap(mine_hid, 1), cot)
        other_out, done = lax.optimization_barrier((swap(mine_out, 1), done))
        output = finish_rows(info, mine_out, other_out)
    grad_expand, new_expand, moment_expand_new, average_expand_new = (
        jnp.transpose(a, (2, 0, 1)) for a in done[:4]
    )
    grad_reduce, new_reduce, moment_reduce_new, average_reduce_new = (
        jnp.transpose(a) for a in done[4:]
    )
    input_grad = input_grad.reshape(batch, length, width)
    output = output.reshape(batch, length, width)
    new_norm, moment_norm_new, average_norm_new = advance(
        norm_params, norm_grad, moment_norm, average_norm, 0.06 / math.sqrt(total_tokens)
    )
    new_bias, moment_bias_new, average_bias_new = advance(
        attend_bias, bias_grad, moment_bias, average_bias, 0.25 / math.sqrt(total_tokens)
    )
    return (
        output,
        input_grad,
        grad_in,
        grad_out,
        grad_expand,
        grad_reduce,
        norm_grad,
        bias_grad,
        new_in,
        new_out,
        new_expand,
        new_reduce,
        new_norm,
        new_bias,
        moment_in_new,
        moment_out_new,
        moment_expand_new,
        moment_reduce_new,
        moment_norm_new,
        moment_bias_new,
        average_in_new,
        average_out_new,
        average_expand_new,
        average_reduce_new,
        average_norm_new,
        average_bias_new,
    )


def solution(mesh):
    rows3 = P("dp", None, None)
    in3 = P("dp", None, "mp")
    in2 = P("dp", "mp")
    bias = P(None, "mp")
    states = (in3, in2, in3, in2, P(), bias)
    return jax.shard_map(
        body,
        mesh=mesh,
        in_specs=(rows3, P("dp", None), rows3) + states * 3,
        out_specs=(rows3, rows3) + states * 4,
        check_vma=False,
    )
```

time: 1260 us -> 604 us (0.48)
  waiting for transfers between devices: 775 us -> 233 us
  matrix products: 246 us -> 0 us
  Pallas kernels: 0 us -> 246 us
  other arithmetic: 130 us -> 37.5 us
  local copies, waits for them, and re-layouts: 63.7 us -> 7.6 us
  starting transfers between devices: 0.37 us -> 54.6 us
  blocking collectives: 20.1 us -> 0 us
    psum x1 -> x0, waiting for transfers between devices: 400 us -> none  [body(): summed = lax.psum(partial_rows, 'mp')]
    pallas_call x0 -> x16, Pallas kernels: none -> 246 us  [the longest x1 36.6 us: feed_last(): pl.pallas_call(functools.partial(last_kernel, n, count, split), grid_spec...]
    dot_general x26 -> x0, matrix products: 246 us -> none  [the longest x4 52.4 us: contract_cols(): lax.dot_general(left, right, (((1,), (1,)), ((), ())), preferred_element_...]
    reduce_scatter x4 -> x2, waiting for transfers between devices: 230 us -> 0.02 us  [scatter(): return lax.psum_scatter(grads, 'dp', scatter_dimension=0, tiled=False)]
    ppermute x0 -> x43, waiting for transfers between devices: none -> 159 us  [the longest x31 117 us: swap(): return lax.ppermute(value, axis, [(a, a ^ mask) for a in range(n)])]
    all_gather x4 -> x2, waiting for transfers between devices: 145 us -> 73.9 us  [the longest x1 63 us: body(): attend_pieces = [lax.all_gather(attend_shard, 'dp')]]
    ppermute x0 -> x43, starting transfers between devices: none -> 54.4 us  [the longest x31 25 us: swap(): return lax.ppermute(value, axis, [(a, a ^ mask) for a in range(n)])]
    convert_element_type x5, other arithmetic: 39.9 us -> 8.01 us  [the longest x2 5.76 us: send_rows(): to_x, to_y = (own[1].astype(low), own[3].astype(low))]
  transfers between devices with their start and end apart: 9 -> 47, of which waited for: 6 -> 22; matrix products, arithmetic and copies ran while one was open for 32% -> 6% of each run, Pallas kernels for 0% -> 40%
where the time goes in v1:
time: 604 us; the launch traced here: 594 us
  Pallas kernels  246 us (41%)
  waiting for transfers between devices  233 us (39%)
  starting transfers between devices  54.6 us (9%)
  other arithmetic  37.5 us (6%)
  between operations  15 us (2%)
  local copies, waits for them, and re-layouts  7.6 us (1%)
    ppermute x31, waiting for transfers between devices, swap(): return lax.ppermute(value, axis, [(a, a ^ mask) for a in range(n)])  117 us
    all_gather x1, waiting for transfers between devices, body(): attend_pieces = [lax.all_gather(attend_shard, 'dp')]  63 us
    ppermute x3, waiting for transfers between devices, scatter_hops(): right = lax.ppermute(to_right, 'dp', [(a, a + 1) for a in range(k)])  39.2 us
    pallas_call x1, Pallas kernels, feed_last(): pl.pallas_call(functools.partial(last_kernel, n, count, split), grid_spec...  36.6 us
    pallas_call x1, Pallas kernels, attend(): pl.pallas_call(functools.partial(attend_kernel, min(512, length)), grid=(...  34 us
    pallas_call x1, Pallas kernels, feed_chunk(): pl.pallas_call(functools.partial(feed_kernel, n, count, steps), grid_spec...  29.9 us
    pallas_call x1, Pallas kernels, early_parts(): pl.pallas_call(early_kernel, grid=(rows // block,), in_specs=[pl.BlockSpe...  26.4 us
    ppermute x31, starting transfers between devices, swap(): return lax.ppermute(value, axis, [(a, a ^ mask) for a in range(n)])  25 us
  transfers between devices with their start and end apart: 47, of which 22 were waited for; matrix products, arithmetic and copies ran while one was open for 6% of the time, Pallas kernels for 40%

profile of v1, /device:TPU:0, one launch (start us, length us, event | category | flops | bytes accessed | tf_op | source)
XLA Modules:
  0.0 594.3 jit_solution(13206325262534254889)
XLA Ops:
  8.3 1.5 convert_bitcast_fusion
  11.0 1.6 bitcast_convert_fusion
  14.6 11.2 %layer_norm.1.refs_1_.h_ref.refs_7_ = bf16[2048,2048]{1,0:T(8,128)(2,1)} custom-call(bf16[2048,2048]{1,0:T(8,128)(2,1)} %bitcast.48, f32[2,2048]{1,0:T(2,128)} %refs_6_.1), custom_call_target="tpu_custom_call" | custom-call | flops 33554432 | bytes 16777216 | tf_op jit(solution)/shard_map/layer_norm/pallas_call | solution.py:111
  25.9 5.6 fusion.4
  31.5 63.0 %all-gather.4.cloned.1.call-done.refs_0_ = bf16[4,4,512,256]{3,2,1,0:T(8,128)(2,1)} async-done(((bf16[1,4,512,256]{3,2,1,0:T(8,128)(2,1)}), bf16[4,4,512,256]{3,2,1,0:T(8,128)(2,1)}) %all-gather.4.cloned.1.call-update) | async-done | bytes 4194320 | tf_op jit(solution)/shard_map/all_gather | solution.py:833
  94.5 17.4 %project.1 = (bf16[2048,256]{1,0:T(8,128)(2,1)}, bf16[2048,256]{1,0:T(8,128)(2,1)}, bf16[2048,256]{1,0:T(8,128)(2,1)}, bf16[2048,256]{1,0:T(8,128)(2,1)}, bf16[4,2048,256]{2,1,0:T(8,128)(2,1)}) custom-call(s32[1]{0:T(128)} %bitcast.3.me_ref, bf16[4,4,512,256]{3,2,1,0:T(8,128)(2,1)} %all-gather.4.cloned.1.call-done.refs_0_, ...), custom_call_target="tpu_custom_call" | custom-call | flops 8589934592 | bytes 25165824 | tf_op jit(solution)/shard_map/project/pallas_call | solution.py:404
  112.0 34.0 %attend.1 = (bf16[2048,256]{1,0:T(8,128)(2,1)}, bf16[3,2048,256]{2,1,0:T(8,128)(2,1)}, f32[3,256]{1,0:T(4,128)}) custom-call(bf16[2048,256]{1,0:T(8,128)(2,1)} %get-tuple-element.140.q_ref, bf16[2048,256]{1,0:T(8,128)(2,1)} %get-tuple-element.141.k_ref, bf16[2048,256]{1,0:T(8,128)(2,1)} %get-tuple-element.142.v_ref, ...), custom_call_target="tpu_custom_call" | custom-call | flops 21474836480 | bytes 10485760 | tf_op jit(solution)/shard_map/attend/pallas_call | solution.py:484
  146.2 3.7 collective-permute-done.6
  151.0 16.4 %attend_grads.1 = (f32[4,512,256]{2,1,0:T(8,128)}, bf16[4,512,256]{2,1,0:T(8,128)(2,1)}, bf16[4,512,256]{2,1,0:T(8,128)(2,1)}, bf16[4,512,256]{2,1,0:T(8,128)(2,1)}) custom-call(s32[1]{0:T(128)} %bitcast.3.me_ref, bf16[2048,2048]{1,0:T(8,128)(2,1)} %layer_norm.1.refs_1_.h_ref.refs_7_, bf16[2048,2048]{1,0:T(8,128)(2,1)} %bitcast.63, ...), custom_call_target="tpu_custom_call" | custom-call | flops 8589934592 | bytes 25165824 | tf_op jit(solution)/shard_map/attend_grads/pallas_call | solution.py:538
  167.4 10.9 %all-gather.6.cloned.1.call-done = bf16[12,352,512]{2,1,0:T(8,128)(2,1)} async-done(((bf16[3,352,512]{2,1,0:T(8,128)(2,1)}), bf16[12,352,512]{2,1,0:T(8,128)(2,1)}) %all-gather.6.cloned.1.call-update) | async-done | bytes 4325392 | tf_op jit(solution)/shard_map/all_gather | solution.py:835
  178.3 1.3 collective-permute-start
  181.0 4.6 collective-permute-start.4
  185.6 1.6 collective-permute-start.5
  187.3 29.9 %feed_chunk.1 = (bf16[352,2048]{1,0:T(8,128)(2,1)}, bf16[704,2048]{1,0:T(8,128)(2,1)}, bf16[3,352,2048]{2,1,0:T(8,128)(2,1)}, bf16[4,1056,512]{2,1,0:T(8,128)(2,1)}) custom-call(s32[1]{0:T(128)} %bitcast.3.me_ref, bf16[4,3,352,512]{3,2,1,0:T(8,128)(2,1)} %bitcast.84, bf16[2048,2048]{1,0:T(8,128)(2,1)} %layer_norm.1.refs_1_.h_ref.refs_7_, ...), custom_call_target="tpu_custom_call" | custom-call | flops 17716740096 | bytes 31195136 | tf_op jit(solution)/shard_map/feed_chunk/pallas_call | solution.py:216
  218.2 1.7 collective-permute-start.2
  221.1 26.4 %early_parts.1 = (bf16[2048,2048]{1,0:T(8,128)(2,1)}, bf16[2048,2048]{1,0:T(8,128)(2,1)}) custom-call(bf16[2048,256]{1,0:T(8,128)(2,1)} %get-tuple-element.145.ctx_ref, bf16[3,2048,256]{2,1,0:T(8,128)(2,1)} %get-tuple-element.144.mg_ref, bf16[352,2048]{1,0:T(8,128)(2,1)} %get-tuple-element.157.act_ref, bf16[704,2048]{1,0:T(8,128)(2,1)} %get-tuple-element.158.grad_ref, ...), custom_call_target="tpu_custom_call" | custom-call | flops 17448304640 | bytes 33816576 | tf_op jit(solution)/shard_map/early_parts/pallas_call | solution.py:571
  248.4 1.5 collective-permute-start.9
  249.9 1.7 fusion.1
  251.6 4.8 collective-permute-start.10
  257.1 20.8 %collective-permute-done.10 = bf16[4,512,256]{2,1,0:T(8,128)(2,1)S(1)} collective-permute-done((bf16[4,512,256]{2,1,0:T(8,128)(2,1)S(1)}, bf16[4,512,256]{2,1,0:T(8,128)(2,1)S(1)}, u32[]{:S(2)}, u32[]{:S(2)}) %collective-permute-start.10) | collective-permute-done | bytes 1048608 | tf_op jit(solution)/shard_map/ppermute | solution.py:78
  278.2 8.4 %collective-permute-start.12 = (bf16[4,512,256]{2,1,0:T(8,128)(2,1)S(1)}, bf16[4,512,256]{2,1,0:T(8,128)(2,1)S(1)}, u32[]{:S(2)}, u32[]{:S(2)}) collective-permute-start(bf16[4,512,256]{2,1,0:T(8,128)(2,1)S(1)} %add_convert_fusion.9), channel_id=1, source_target_pairs={{0,8},{8,16},{16,24},{1,9},{9,17},{17,25},{2,10},{10,18},{18,26},{... | collective-permute-start | bytes 3145736 | tf_op jit(solution)/shard_map/ppermute | solution.py:78
  288.3 18.4 %collective-permute-done.12 = bf16[4,512,256]{2,1,0:T(8,128)(2,1)S(1)} collective-permute-done((bf16[4,512,256]{2,1,0:T(8,128)(2,1)S(1)}, bf16[4,512,256]{2,1,0:T(8,128)(2,1)S(1)}, u32[]{:S(2)}, u32[]{:S(2)}) %collective-permute-start.12) | collective-permute-done | bytes 1048608 | tf_op jit(solution)/shard_map/ppermute | solution.py:78
  307.6 3.6 collective-permute-done.13
  311.9 36.6 %feed_last.1 = (bf16[1024,2048]{1,0:T(8,128)(2,1)}, bf16[1024,2048]{1,0:T(8,128)(2,1)}, bf16[1024,2048]{1,0:T(8,128)(2,1)}, bf16[1024,2048]{1,0:T(8,128)(2,1)}, ...) custom-call(s32[4]{0:T(128)} %pad_add_fusion.info_ref, bf16[3,352,512]{2,1,0:T(8,128)(2,1)} %copy-done.8, ...), custom_call_target="tpu_custom_call" | custom-call | flops 17716740096 | bytes 50331648 | tf_op jit(solution)/shard_map/feed_last/pallas_call | solution.py:302
  349.1 12.1 %collective-permute-done.14 = bf16[1024,2048]{1,0:T(8,128)(2,1)S(1)} collective-permute-done((bf16[1024,2048]{1,0:T(8,128)(2,1)}, bf16[1024,2048]{1,0:T(8,128)(2,1)S(1)}, u32[]{:S(2)}, u32[]{:S(2)}) %collective-permute-start.14) | collective-permute-done | bytes 4194336 | tf_op jit(solution)/shard_map/ppermute | solution.py:87
  361.2 3.8 add_convert_fusion.6
  365.0 1.5 collective-permute-start.15
  366.5 1.5 collective-permute-start.16
  368.0 16.3 %feed_grads.1 = bf16[4,1056,512]{2,1,0:T(8,128)(2,1)} custom-call(bf16[2048,2048]{1,0:T(8,128)(2,1)} %layer_norm.1.refs_1_.h_ref.refs_7_, bf16[2048,2048]{1,0:T(8,128)(2,1)} %bitcast.66, bf16[352,2048]{1,0:T(8,128)(2,1)} %get-tuple-element.186.act_ref, bf16[704,2048]{1,0:T(8,128)(2,1)} %get-tuple-element.187.grad_ref), custom_call_target="tpu_custom_call" | custom-call | flops 8858370048 | bytes 25427968 | tf_op jit(solution)/shard_map/feed_grads/pallas_call | solution.py:341
  384.3 6.0 %collective-permute-done.15 = bf16[256,2048]{1,0:T(8,128)(2,1)S(1)} collective-permute-done((bf16[256,2048]{1,0:T(8,128)(2,1)S(1)}, bf16[256,2048]{1,0:T(8,128)(2,1)S(1)}, u32[]{:S(2)}, u32[]{:S(2)}) %collective-permute-start.15) | collective-permute-done | bytes 1048608 | tf_op jit(solution)/shard_map/ppermute | solution.py:87
  391.5 1.9 add_convert_fusion.1
  393.5 1.5 collective-permute-start.23
  395.1 4.4 add_convert_fusion.4
  400.4 17.4 %collective-permute-done.23 = bf16[256,2048]{1,0:T(8,128)(2,1)S(1)} collective-permute-done((bf16[256,2048]{1,0:T(8,128)(2,1)S(1)}, bf16[256,2048]{1,0:T(8,128)(2,1)S(1)}, u32[]{:S(2)}, u32[]{:S(2)}) %collective-permute-start.23) | collective-permute-done | bytes 1048608 | tf_op jit(solution)/shard_map/ppermute | solution.py:87
  417.8 2.7 add_convert_fusion
  420.5 1.5 collective-permute-start.22
  422.8 1.5 collective-permute-start.18
  424.9 10.1 %collective-permute-done.18.refs_4_ = bf16[128,2048]{1,0:T(8,128)(2,1)S(1)} collective-permute-done((bf16[128,2048]{1,0:T(8,128)(2,1)S(1)}, bf16[128,2048]{1,0:T(8,128)(2,1)S(1)}, u32[]{:S(2)}, u32[]{:S(2)}) %collective-permute-start.18) | collective-permute-done | bytes 524320 | tf_op jit(solution)/shard_map/ppermute | solution.py:87
  435.0 20.3 %collective-permute-done.19.refs_5_ = bf16[128,2048]{1,0:T(8,128)(2,1)} collective-permute-done((bf16[128,2048]{1,0:T(8,128)(2,1)S(1)}, bf16[128,2048]{1,0:T(8,128)(2,1)}, u32[]{:S(2)}, u32[]{:S(2)}) %collective-permute-start.19) | collective-permute-done | bytes 524320 | tf_op jit(solution)/shard_map/ppermute | solution.py:87
  455.2 5.3 back_rows.1
  460.6 1.4 collective-permute-start.20
  462.9 1.7 collective-permute-start.25
  464.6 2.1 add_convert_fusion.2
  469.7 1.8 collective-permute-start.38
  471.4 14.2 %collective-permute-done.38 = f32[2,2048]{1,0:T(2,128)S(1)} collective-permute-done((f32[2,2048]{1,0:T(2,128)S(1)}, f32[2,2048]{1,0:T(2,128)S(1)}, u32[]{:S(2)}, u32[]{:S(2)}) %collective-permute-start.38) | collective-permute-done | bytes 16416 | tf_op jit(solution)/shard_map/ppermute | solution.py:87
  486.3 3.2 collective-permute-done.39
  490.0 3.3 collective-permute-done.40
  493.4 1.8 collective-permute-start.33
  496.6 3.9 add_rows.1
  500.6 1.5 collective-permute-start.26
  503.3 1.6 convert_add_fusion.2
  505.1 1.4 multiply_add_fusion.2
  506.5 2.0 collective-permute-done.33.refs_2_
  509.0 1.4 collective-permute-done.35.refs_6_
  510.8 8.9 %collective-permute-done.34.refs_3_ = bf16[128,2048]{1,0:T(8,128)(2,1)} collective-permute-done((bf16[128,2048]{1,0:T(8,128)(2,1)}, bf16[128,2048]{1,0:T(8,128)(2,1)}, u32[]{:S(2)}, u32[]{:S(2)}) %collective-permute-start.34) | collective-permute-done | bytes 524320 | tf_op jit(solution)/shard_map/ppermute | solution.py:87
  520.2 1.4 collective-permute-done.26.refs_1_
  522.0 8.9 %collective-permute-done.29.refs_5_ = bf16[128,2048]{1,0:T(8,128)(2,1)} collective-permute-done((bf16[128,2048]{1,0:T(8,128)(2,1)}, bf16[128,2048]{1,0:T(8,128)(2,1)}, u32[]{:S(2)}, u32[]{:S(2)}) %collective-permute-start.29) | collective-permute-done | bytes 524320 | tf_op jit(solution)/shard_map/ppermute | solution.py:87
  531.5 3.1 multiply_add_fusion
  534.6 7.0 %update_feed.2 = (f32[2,704,512]{2,1,0:T(8,128)}, f32[2,704,512]{2,1,0:T(8,128)}, f32[2,704,512]{2,1,0:T(8,128)}, f32[2,704,512]{2,1,0:T(8,128)}, f32[704,512]{1...) custom-call(bf16[3,352,512]{2,1,0:T(8,128)(2,1)} %bitcast.82, f32[2,704,512]{2,1,0:T(8,128)} %bitcast.53, ...), custom_call_target="tpu_custom_call" | custom-call | flops 5406720 | bytes 16220160 | tf_op jit(solution)/shard_map/update_feed/pallas_call | solution.py:775
  542.4 4.9 pack_rows.3.refs_1_
  548.7 5.0 pack_rows.2.refs_0_
  555.5 14.7 %finish_rows.3 = f32[2048,2048]{1,0:T(8,128)} custom-call(s32[4]{0:T(128)} %pad_add_fusion.info_ref, bf16[2048,2048]{1,0:T(8,128)(2,1)} %bitcast.67, bf16[1024,2048]{1,0:T(8,128)(2,1)} %pack_rows.3.refs_1_, bf16[1024,2048]{1,0:T(8,128)(2,1)} %collective-permute-done.42.refs_2_), custom_call_target="tpu_custom_call" | custom-call | flops 8388608 | bytes 33554432 | tf_op jit(solution)/shard_map/finish_rows/pallas_call | solution.py:734
  570.2 7.0 %update_feed.3 = (f32[2,704,512]{2,1,0:T(8,128)}, f32[2,704,512]{2,1,0:T(8,128)}, f32[2,704,512]{2,1,0:T(8,128)}, f32[2,704,512]{2,1,0:T(8,128)}, f32[704,512]{1...) custom-call(bf16[3,352,512]{2,1,0:T(8,128)(2,1)} %bitcast.81, ...), custom_call_target="tpu_custom_call", output_to_operand_aliasing={{0}: (7, {}), {1}: (8, {}), {2}: (9, {}), {3}: (10, {}), {4... | custom-call | flops 5406720 | bytes 16220160 | tf_op jit(solution)/shard_map/update_feed/pallas_call | solution.py:775
  577.2 10.2 %finish_rows.2 = bf16[2048,2048]{1,0:T(8,128)(2,1)} custom-call(s32[4]{0:T(128)} %pad_add_fusion.info_ref, bf16[1024,2048]{1,0:T(8,128)(2,1)} %pack_rows.2.refs_0_, bf16[1024,2048]{1,0:T(8,128)(2,1)} %collective-permute-done.32.refs_1_), custom_call_target="tpu_custom_call" | custom-call | flops 8388608 | bytes 33554432 | tf_op jit(solution)/shard_map/finish_rows/pallas_call | solution.py:734
  (171 shorter events, 32.2 us)
Async XLA Ops:
  7.2 87.3 %all-gather.4.cloned.1.call-start = ((), (), s32[]{:S(2)}) async-start(), calls=%async_computation.2 | async-start | bytes 5242880 | tf_op jit(solution)/shard_map/all_gather | solution.py:833
  10.9 167.4 %all-gather.6.cloned.1.call-start = ((), (), s32[]{:S(2)}) async-start(), calls=%async_computation.5 | async-start | bytes 5406720 | tf_op jit(solution)/shard_map/all_gather | solution.py:835
  14.5 520.1 %reduce-scatter.5.cloned.1.call-start = ((), (), s32[]{:S(2)}) async-start(), calls=%async_computation.4 | async-start | bytes 5406720 | tf_op jit(solution)/shard_map/reduce_scatter | solution.py:874
  146.0 3.9 collective-permute-start.6
  146.2 33.5 %copy-start.8 = (bf16[3,352,512]{2,1,0:T(8,128)(2,1)}, bf16[3,352,512]{2,1,0:T(8,128)(2,1)S(1)}, u32[]{:S(2)}) copy-start(bf16[3,352,512]{2,1,0:T(8,128)(2,1)S(1)} %pad_maximum_fusion.refs_0_) | copy-start | bytes 3244036
  149.9 17.5 %collective-permute-start.7 = (f32[3,256]{1,0:T(4,128)S(1)}, f32[3,256]{1,0:T(4,128)S(1)}, u32[]{:S(2)}, u32[]{:S(2)}) collective-permute-start(f32[3,256]{1,0:T(4,128)S(1)} %add.141), channel_id=1, source_target_pairs={{0,16},{8,24},{16,0},{24,8},{1,17},{9,25},{17,1},{25,9},{2,18},{10... | collective-permute-start | bytes 9224 | tf_op jit(solution)/shard_map/ppermute | solution.py:87
  167.4 386.8 %copy-start.32 = (f32[3,256]{1,0:T(4,128)}, f32[3,256]{1,0:T(4,128)S(1)}, u32[]{:S(2)}) copy-start(f32[3,256]{1,0:T(4,128)S(1)} %add.142) | copy-start | bytes 9220
  178.3 38.9 %collective-permute-start = (bf16[3,352,512]{2,1,0:T(8,128)(2,1)S(1)}, bf16[3,352,512]{2,1,0:T(8,128)(2,1)S(1)}, u32[]{:S(2)}, u32[]{:S(2)}) collective-permute-start(bf16[3,352,512]{2,1,0:T(8,128)(2,1)S(1)} %pad_maximum_fusion.refs_0_), channel_id=1, source_target_pairs={{0,8},{8,16},{16,24},{1,9},{9,17},{17,25},{2,10},{10,18},{18,26},{... | collective-permute-start | bytes 3244040 | tf_op jit(solution)/shard_map/ppermute | solution.py:61
  179.7 37.5 %collective-permute-start.1 = (bf16[3,352,512]{2,1,0:T(8,128)(2,1)S(1)}, bf16[3,352,512]{2,1,0:T(8,128)(2,1)}, u32[]{:S(2)}, u32[]{:S(2)}) collective-permute-start(bf16[3,352,512]{2,1,0:T(8,128)(2,1)S(1)} %pad_maximum_fusion.refs_0_), channel_id=1, source_target_pairs={{8,0},{16,8},{24,16},{9,1},{17,9},{25,17},{10,2},{18,10},{26,18},{... | collective-permute-start | bytes 3244040 | tf_op jit(solution)/shard_map/ppermute | solution.py:62
  181.0 66.5 %collective-permute-start.4 = (bf16[4,512,256]{2,1,0:T(8,128)(2,1)}, bf16[4,512,256]{2,1,0:T(8,128)(2,1)S(1)}, u32[]{:S(2)}, u32[]{:S(2)}) collective-permute-start(bf16[4,512,256]{2,1,0:T(8,128)(2,1)} %get-tuple-element.156), channel_id=1, source_target_pairs={{0,8},{1,9},{2,10},{3,11},{4,12},{5,13},{6,14},{7,15}} | collective-permute-start | bytes 3145736 | tf_op jit(solution)/shard_map/ppermute | solution.py:78
  185.6 61.9 %collective-permute-start.5 = (bf16[4,512,256]{2,1,0:T(8,128)(2,1)}, bf16[4,512,256]{2,1,0:T(8,128)(2,1)}, u32[]{:S(2)}, u32[]{:S(2)}) collective-permute-start(bf16[4,512,256]{2,1,0:T(8,128)(2,1)} %get-tuple-element.150), channel_id=1, source_target_pairs={{24,16},{25,17},{26,18},{27,19},{28,20},{29,21},{30,22},{31,23}} | collective-permute-start | bytes 3145736 | tf_op jit(solution)/shard_map/ppermute | solution.py:79
  218.2 29.3 %collective-permute-start.2 = (bf16[3,352,512]{2,1,0:T(8,128)(2,1)}, bf16[3,352,512]{2,1,0:T(8,128)(2,1)}, u32[]{:S(2)}, u32[]{:S(2)}) collective-permute-start(bf16[3,352,512]{2,1,0:T(8,128)(2,1)} %copy-done.38), channel_id=1, source_target_pairs={{8,16},{16,24},{9,17},{17,25},{10,18},{18,26},{11,19},{19,27},{12,... | collective-permute-start | bytes 3244040 | tf_op jit(solution)/shard_map/ppermute | solution.py:61
  219.8 27.7 %collective-permute-start.3 = (bf16[3,352,512]{2,1,0:T(8,128)(2,1)}, bf16[3,352,512]{2,1,0:T(8,128)(2,1)}, u32[]{:S(2)}, u32[]{:S(2)}) collective-permute-start(bf16[3,352,512]{2,1,0:T(8,128)(2,1)} %collective-permute-done.1.refs_4_), channel_id=1, source_target_pairs={{8,0},{16,8},{9,1},{17,9},{10,2},{18,10},{11,3},{19,11},{12,4},{20... | collective-permute-start | bytes 3244040 | tf_op jit(solution)/shard_map/ppermute | solution.py:62
  221.1 28.8 %copy-start.11 = (bf16[4,512,256]{2,1,0:T(8,128)(2,1)S(1)}, bf16[4,512,256]{2,1,0:T(8,128)(2,1)}, u32[]{:S(2)}) copy-start(bf16[4,512,256]{2,1,0:T(8,128)(2,1)} %get-tuple-element.166) | copy-start | bytes 3145732
  247.5 30.4 %copy-start.10 = (bf16[4,512,256]{2,1,0:T(8,128)(2,1)S(1)}, bf16[4,512,256]{2,1,0:T(8,128)(2,1)}, u32[]{:S(2)}) copy-start(bf16[4,512,256]{2,1,0:T(8,128)(2,1)} %get-tuple-element.150) | copy-start | bytes 3145732
  247.5 30.4 %collective-permute-start.8 = (bf16[3,352,512]{2,1,0:T(8,128)(2,1)}, bf16[3,352,512]{2,1,0:T(8,128)(2,1)S(1)}, u32[]{:S(2)}, u32[]{:S(2)}) collective-permute-start(bf16[3,352,512]{2,1,0:T(8,128)(2,1)} %collective-permute-done.2.refs_2_), channel_id=1, source_target_pairs={{16,24},{17,25},{18,26},{19,27},{20,28},{21,29},{22,30},{23,31}} | collective-permute-start | bytes 3244040 | tf_op jit(solution)/shard_map/ppermute | solution.py:61
  248.4 29.5 %collective-permute-start.9 = (bf16[3,352,512]{2,1,0:T(8,128)(2,1)}, bf16[3,352,512]{2,1,0:T(8,128)(2,1)S(1)}, u32[]{:S(2)}, u32[]{:S(2)}) collective-permute-start(bf16[3,352,512]{2,1,0:T(8,128)(2,1)} %collective-permute-done.3.refs_5_), channel_id=1, source_target_pairs={{8,0},{9,1},{10,2},{11,3},{12,4},{13,5},{14,6},{15,7}} | collective-permute-start | bytes 3244040 | tf_op jit(solution)/shard_map/ppermute | solution.py:62
  251.6 35.1 %copy-start.9 = (bf16[4,512,256]{2,1,0:T(8,128)(2,1)S(1)}, bf16[4,512,256]{2,1,0:T(8,128)(2,1)}, u32[]{:S(2)}) copy-start(bf16[4,512,256]{2,1,0:T(8,128)(2,1)} %get-tuple-element.156) | copy-start | bytes 3145732
  251.6 26.3 %collective-permute-start.10 = (bf16[4,512,256]{2,1,0:T(8,128)(2,1)S(1)}, bf16[4,512,256]{2,1,0:T(8,128)(2,1)S(1)}, u32[]{:S(2)}, u32[]{:S(2)}) collective-permute-start(bf16[4,512,256]{2,1,0:T(8,128)(2,1)S(1)} %get-tuple-element.285), channel_id=1, source_target_pairs={{0,8},{8,16},{1,9},{9,17},{2,10},{10,18},{3,11},{11,19},{4,12},{12... | collective-permute-start | bytes 3145736 | tf_op jit(solution)/shard_map/ppermute | solution.py:78
  256.4 21.5 %collective-permute-start.11 = (bf16[4,512,256]{2,1,0:T(8,128)(2,1)S(1)}, bf16[4,512,256]{2,1,0:T(8,128)(2,1)S(1)}, u32[]{:S(2)}, u32[]{:S(2)}) collective-permute-start(bf16[4,512,256]{2,1,0:T(8,128)(2,1)S(1)} %get-tuple-element.284), channel_id=1, source_target_pairs={{24,16},{16,8},{25,17},{17,9},{26,18},{18,10},{27,19},{19,11},{28,... | collective-permute-start | bytes 3145736 | tf_op jit(solution)/shard_map/ppermute | solution.py:79
  277.9 9.1 %copy-start.39 = (bf16[3,352,512]{2,1,0:T(8,128)(2,1)}, bf16[3,352,512]{2,1,0:T(8,128)(2,1)S(1)}, u32[]{:S(2)}) copy-start(bf16[3,352,512]{2,1,0:T(8,128)(2,1)S(1)} %collective-permute-done.8.refs_3_) | copy-start | bytes 3244036
  277.9 9.1 %copy-start.40 = (bf16[3,352,512]{2,1,0:T(8,128)(2,1)}, bf16[3,352,512]{2,1,0:T(8,128)(2,1)S(1)}, u32[]{:S(2)}) copy-start(bf16[3,352,512]{2,1,0:T(8,128)(2,1)S(1)} %collective-permute-done.9.refs_6_) | copy-start | bytes 3244036
  278.2 28.4 %collective-permute-start.12 = (bf16[4,512,256]{2,1,0:T(8,128)(2,1)S(1)}, bf16[4,512,256]{2,1,0:T(8,128)(2,1)S(1)}, u32[]{:S(2)}, u32[]{:S(2)}) collective-permute-start(bf16[4,512,256]{2,1,0:T(8,128)(2,1)S(1)} %add_convert_fusion.9), channel_id=1, source_target_pairs={{0,8},{8,16},{16,24},{1,9},{9,17},{17,25},{2,10},{10,18},{18,26},{... | collective-permute-start | bytes 3145736 | tf_op jit(solution)/shard_map/ppermute | solution.py:78
  287.0 24.3 %collective-permute-start.13 = (bf16[4,512,256]{2,1,0:T(8,128)(2,1)S(1)}, bf16[4,512,256]{2,1,0:T(8,128)(2,1)}, u32[]{:S(2)}, u32[]{:S(2)}) collective-permute-start(bf16[4,512,256]{2,1,0:T(8,128)(2,1)S(1)} %add_convert_fusion.8), channel_id=1, source_target_pairs={{24,16},{16,8},{8,0},{25,17},{17,9},{9,1},{26,18},{18,10},{10,2},{... | collective-permute-start | bytes 3145736 | tf_op jit(solution)/shard_map/ppermute | solution.py:79
  311.3 258.9 %reduce-scatter.3.cloned.1.call-start = ((), (), s32[]{:S(2)}) async-start(), calls=%async_computation.3 | async-start | bytes 5406720 | tf_op jit(solution)/shard_map/reduce_scatter | solution.py:874
  348.5 12.6 %collective-permute-start.14 = (bf16[1024,2048]{1,0:T(8,128)(2,1)}, bf16[1024,2048]{1,0:T(8,128)(2,1)S(1)}, u32[]{:S(2)}, u32[]{:S(2)}) collective-permute-start(bf16[1024,2048]{1,0:T(8,128)(2,1)} %get-tuple-element.183), channel_id=1, source_target_pairs={{0,1},{1,0},{2,3},{3,2},{4,5},{5,4},{6,7},{7,6},{8,9},{9,8},{10,11... | collective-permute-start | bytes 12582920 | tf_op jit(solution)/shard_map/ppermute | solution.py:87
  348.6 35.6 %collective-permute-start.17 = (bf16[1024,2048]{1,0:T(8,128)(2,1)}, bf16[1024,2048]{1,0:T(8,128)(2,1)}, u32[]{:S(2)}, u32[]{:S(2)}) collective-permute-start(bf16[1024,2048]{1,0:T(8,128)(2,1)} %get-tuple-element.188), channel_id=1, source_target_pairs={{0,1},{1,0},{2,3},{3,2},{4,5},{5,4},{6,7},{7,6},{8,9},{9,8},{10,11... | collective-permute-start | bytes 12582920 | tf_op jit(solution)/shard_map/ppermute | solution.py:87
  365.0 25.3 %collective-permute-start.15 = (bf16[256,2048]{1,0:T(8,128)(2,1)S(1)}, bf16[256,2048]{1,0:T(8,128)(2,1)S(1)}, u32[]{:S(2)}, u32[]{:S(2)}) collective-permute-start(bf16[256,2048]{1,0:T(8,128)(2,1)S(1)} %get-tuple-element.273), channel_id=1, source_target_pairs={{0,2},{1,3},{2,0},{3,1},{4,6},{5,7},{6,4},{7,5},{8,10},{9,11},{10,... | collective-permute-start | bytes 3145736 | tf_op jit(solution)/shard_map/ppermute | solution.py:87
  366.5 25.0 %collective-permute-start.16 = (bf16[256,2048]{1,0:T(8,128)(2,1)S(1)}, bf16[256,2048]{1,0:T(8,128)(2,1)}, u32[]{:S(2)}, u32[]{:S(2)}) collective-permute-start(bf16[256,2048]{1,0:T(8,128)(2,1)S(1)} %get-tuple-element.272), channel_id=1, source_target_pairs={{0,4},{1,5},{2,6},{3,7},{4,0},{5,1},{6,2},{7,3},{8,12},{9,13},{10,... | collective-permute-start | bytes 3145736 | tf_op jit(solution)/shard_map/ppermute | solution.py:87
  393.5 24.3 %collective-permute-start.23 = (bf16[256,2048]{1,0:T(8,128)(2,1)S(1)}, bf16[256,2048]{1,0:T(8,128)(2,1)S(1)}, u32[]{:S(2)}, u32[]{:S(2)}) collective-permute-start(bf16[256,2048]{1,0:T(8,128)(2,1)S(1)} %add_convert_fusion.1), channel_id=1, source_target_pairs={{0,4},{1,5},{2,6},{3,7},{4,0},{5,1},{6,2},{7,3},{8,12},{9,13},{10,... | collective-permute-start | bytes 3145736 | tf_op jit(solution)/shard_map/ppermute | solution.py:87
  395.0 22.7 %copy-start.2 = (bf16[1024,2048]{1,0:T(8,128)(2,1)S(1)}, bf16[1024,2048]{1,0:T(8,128)(2,1)}, u32[]{:S(2)}) copy-start(bf16[1024,2048]{1,0:T(8,128)(2,1)} %get-tuple-element.194) | copy-start | bytes 12582916
  420.5 44.1 %collective-permute-start.22 = (bf16[256,2048]{1,0:T(8,128)(2,1)S(1)}, bf16[256,2048]{1,0:T(8,128)(2,1)S(1)}, u32[]{:S(2)}, u32[]{:S(2)}) collective-permute-start(bf16[256,2048]{1,0:T(8,128)(2,1)S(1)} %get-tuple-element.269), channel_id=1, source_target_pairs={{0,2},{1,3},{2,0},{3,1},{4,6},{5,7},{6,4},{7,5},{8,10},{9,11},{10,... | collective-permute-start | bytes 3145736 | tf_op jit(solution)/shard_map/ppermute | solution.py:87
  422.8 12.1 %collective-permute-start.18 = (bf16[128,2048]{1,0:T(8,128)(2,1)S(1)}, bf16[128,2048]{1,0:T(8,128)(2,1)S(1)}, u32[]{:S(2)}, u32[]{:S(2)}) collective-permute-start(bf16[128,2048]{1,0:T(8,128)(2,1)S(1)} %get-tuple-element.282), channel_id=1, source_target_pairs={{0,4},{1,5},{2,6},{3,7},{4,0},{5,1},{6,2},{7,3},{8,12},{9,13},{10,... | collective-permute-start | bytes 1572872 | tf_op jit(solution)/shard_map/ppermute | solution.py:87
  424.3 30.9 %collective-permute-start.19 = (bf16[128,2048]{1,0:T(8,128)(2,1)S(1)}, bf16[128,2048]{1,0:T(8,128)(2,1)}, u32[]{:S(2)}, u32[]{:S(2)}) collective-permute-start(bf16[128,2048]{1,0:T(8,128)(2,1)S(1)} %get-tuple-element.280), channel_id=1, source_target_pairs={{0,2},{1,3},{2,0},{3,1},{4,6},{5,7},{6,4},{7,5},{8,10},{9,11},{10,... | collective-permute-start | bytes 1572872 | tf_op jit(solution)/shard_map/ppermute | solution.py:87
  435.0 20.3 %copy-start.24 = (bf16[128,2048]{1,0:T(8,128)(2,1)}, bf16[128,2048]{1,0:T(8,128)(2,1)S(1)}, u32[]{:S(2)}) copy-start(bf16[128,2048]{1,0:T(8,128)(2,1)S(1)} %collective-permute-done.18.refs_4_) | copy-start | bytes 1572868
  460.6 32.8 %collective-permute-start.20 = (bf16[128,2048]{1,0:T(8,128)(2,1)}, bf16[128,2048]{1,0:T(8,128)(2,1)}, u32[]{:S(2)}, u32[]{:S(2)}) collective-permute-start(bf16[128,2048]{1,0:T(8,128)(2,1)} %get-tuple-element.234.refs_0_), channel_id=1, source_target_pairs={{0,4},{1,5},{2,6},{3,7},{4,0},{5,1},{6,2},{7,3},{8,12},{9,13},{10,... | collective-permute-start | bytes 1572872 | tf_op jit(solution)/shard_map/ppermute | solution.py:87
  462.9 32.4 %collective-permute-start.25 = (bf16[128,2048]{1,0:T(8,128)(2,1)S(1)}, bf16[128,2048]{1,0:T(8,128)(2,1)S(1)}, u32[]{:S(2)}, u32[]{:S(2)}) collective-permute-start(bf16[128,2048]{1,0:T(8,128)(2,1)S(1)} %get-tuple-element.276), channel_id=1, source_target_pairs={{0,2},{1,3},{2,0},{3,1},{4,6},{5,7},{6,4},{7,5},{8,10},{9,11},{10,... | collective-permute-start | bytes 1572872 | tf_op jit(solution)/shard_map/ppermute | solution.py:87
  466.8 26.6 %copy-start.15 = (bf16[128,2048]{1,0:T(8,128)(2,1)S(1)}, bf16[128,2048]{1,0:T(8,128)(2,1)}, u32[]{:S(2)}) copy-start(bf16[128,2048]{1,0:T(8,128)(2,1)} %get-tuple-element.234.refs_0_) | copy-start | bytes 1572868
  467.6 28.1 %collective-permute-start.24 = (bf16[128,2048]{1,0:T(8,128)(2,1)S(1)}, bf16[128,2048]{1,0:T(8,128)(2,1)S(1)}, u32[]{:S(2)}, u32[]{:S(2)}) collective-permute-start(bf16[128,2048]{1,0:T(8,128)(2,1)S(1)} %get-tuple-element.278), channel_id=1, source_target_pairs={{0,4},{1,5},{2,6},{3,7},{4,0},{5,1},{6,2},{7,3},{8,12},{9,13},{10,... | collective-permute-start | bytes 1572872 | tf_op jit(solution)/shard_map/ppermute | solution.py:87
  468.1 32.4 %collective-permute-start.21 = (bf16[128,2048]{1,0:T(8,128)(2,1)}, bf16[128,2048]{1,0:T(8,128)(2,1)}, u32[]{:S(2)}, u32[]{:S(2)}) collective-permute-start(bf16[128,2048]{1,0:T(8,128)(2,1)} %get-tuple-element.238.refs_4_), channel_id=1, source_target_pairs={{0,2},{1,3},{2,0},{3,1},{4,6},{5,7},{6,4},{7,5},{8,10},{9,11},{10,... | collective-permute-start | bytes 1572872 | tf_op jit(solution)/shard_map/ppermute | solution.py:87
  468.5 1.2 collective-permute-start.37
  469.7 16.0 %collective-permute-start.38 = (f32[2,2048]{1,0:T(2,128)S(1)}, f32[2,2048]{1,0:T(2,128)S(1)}, u32[]{:S(2)}, u32[]{:S(2)}) collective-permute-start(f32[2,2048]{1,0:T(2,128)S(1)} %add.159), channel_id=1, source_target_pairs={{0,2},{1,3},{2,0},{3,1},{4,6},{5,7},{6,4},{7,5},{8,10},{9,11},{10,... | collective-permute-start | bytes 49160 | tf_op jit(solution)/shard_map/ppermute | solution.py:87
  485.7 3.8 collective-permute-start.39
  489.5 3.8 collective-permute-start.40
  493.3 8.8 %collective-permute-start.41 = (f32[2,2048]{1,0:T(2,128)S(1)}, f32[2,2048]{1,0:T(2,128)S(1)}, u32[]{:S(2)}, u32[]{:S(2)}) collective-permute-start(f32[2,2048]{1,0:T(2,128)S(1)} %add.162), channel_id=1, source_target_pairs={{0,16},{8,24},{16,0},{24,8},{1,17},{9,25},{17,1},{25,9},{2,18},{10... | collective-permute-start | bytes 49160 | tf_op jit(solution)/shard_map/ppermute | solution.py:87
  493.4 15.0 %collective-permute-start.33 = (bf16[128,2048]{1,0:T(8,128)(2,1)S(1)}, bf16[128,2048]{1,0:T(8,128)(2,1)}, u32[]{:S(2)}, u32[]{:S(2)}) collective-permute-start(bf16[128,2048]{1,0:T(8,128)(2,1)S(1)} %copy-done.15), channel_id=1, source_target_pairs={{0,2},{1,3},{2,0},{3,1},{4,6},{5,7},{6,4},{7,5},{8,10},{9,11},{10,... | collective-permute-start | bytes 1572872 | tf_op jit(solution)/shard_map/ppermute | solution.py:87
  495.2 15.2 %collective-permute-start.35 = (bf16[128,2048]{1,0:T(8,128)(2,1)}, bf16[128,2048]{1,0:T(8,128)(2,1)}, u32[]{:S(2)}, u32[]{:S(2)}) collective-permute-start(bf16[128,2048]{1,0:T(8,128)(2,1)} %get-tuple-element.238.refs_4_), channel_id=1, source_target_pairs={{0,4},{1,5},{2,6},{3,7},{4,0},{5,1},{6,2},{7,3},{8,12},{9,13},{10,... | collective-permute-start | bytes 1572872 | tf_op jit(solution)/shard_map/ppermute | solution.py:87
  495.8 23.9 %collective-permute-start.34 = (bf16[128,2048]{1,0:T(8,128)(2,1)}, bf16[128,2048]{1,0:T(8,128)(2,1)}, u32[]{:S(2)}, u32[]{:S(2)}) collective-permute-start(bf16[128,2048]{1,0:T(8,128)(2,1)} %collective-permute-done.20.refs_1_), channel_id=1, source_target_pairs={{0,2},{1,3},{2,0},{3,1},{4,6},{5,7},{6,4},{7,5},{8,10},{9,11},{10,... | collective-permute-start | bytes 1572872 | tf_op jit(solution)/shard_map/ppermute | solution.py:87
  500.6 21.1 %collective-permute-start.26 = (bf16[128,2048]{1,0:T(8,128)(2,1)}, bf16[128,2048]{1,0:T(8,128)(2,1)}, u32[]{:S(2)}, u32[]{:S(2)}) collective-permute-start(bf16[128,2048]{1,0:T(8,128)(2,1)} %get-tuple-element.198.refs_0_), channel_id=1, source_target_pairs={{0,4},{1,5},{2,6},{3,7},{4,0},{5,1},{6,2},{7,3},{8,12},{9,13},{10,... | collective-permute-start | bytes 1572872 | tf_op jit(solution)/shard_map/ppermute | solution.py:87
  502.1 28.8 %collective-permute-start.29 = (bf16[128,2048]{1,0:T(8,128)(2,1)}, bf16[128,2048]{1,0:T(8,128)(2,1)}, u32[]{:S(2)}, u32[]{:S(2)}) collective-permute-start(bf16[128,2048]{1,0:T(8,128)(2,1)} %get-tuple-element.199.refs_4_), channel_id=1, source_target_pairs={{0,2},{1,3},{2,0},{3,1},{4,6},{5,7},{6,4},{7,5},{8,10},{9,11},{10,... | collective-permute-start | bytes 1572872 | tf_op jit(solution)/shard_map/ppermute | solution.py:87
  503.3 28.1 %copy-start.7 = (f32[512,3,256]{2,0,1:T(8,128)S(1)}, f32[512,3,256]{2,0,1:T(8,128)}, u32[]{:S(2)}) copy-start(f32[512,3,256]{2,0,1:T(8,128)} %param.30) | copy-start | bytes 4718596
  505.0 14.7 %copy-start.17 = (bf16[128,2048]{1,0:T(8,128)(2,1)S(1)}, bf16[128,2048]{1,0:T(8,128)(2,1)}, u32[]{:S(2)}) copy-start(bf16[128,2048]{1,0:T(8,128)(2,1)} %get-tuple-element.199.refs_4_) | copy-start | bytes 1572868
  505.0 26.4 %copy-start.1 = (f32[512,3,256]{2,0,1:T(8,128)S(1)}, f32[512,3,256]{2,0,1:T(8,128)}, u32[]{:S(2)}) copy-start(f32[512,3,256]{2,0,1:T(8,128)} %param.24) | copy-start | bytes 4718596
  505.1 26.4 %copy-start.6 = (f32[512,3,256]{2,0,1:T(8,128)S(1)}, f32[512,3,256]{2,0,1:T(8,128)}, u32[]{:S(2)}) copy-start(f32[512,3,256]{2,0,1:T(8,128)} %param.36) | copy-start | bytes 4718596
  508.5 33.2 %collective-permute-start.36 = (bf16[128,2048]{1,0:T(8,128)(2,1)}, bf16[128,2048]{1,0:T(8,128)(2,1)S(1)}, u32[]{:S(2)}, u32[]{:S(2)}) collective-permute-start(bf16[128,2048]{1,0:T(8,128)(2,1)} %collective-permute-done.21.refs_5_), channel_id=1, source_target_pairs={{0,4},{1,5},{2,6},{3,7},{4,0},{5,1},{6,2},{7,3},{8,12},{9,13},{10,... | collective-permute-start | bytes 1572872 | tf_op jit(solution)/shard_map/ppermute | solution.py:87
  510.4 37.1 %collective-permute-start.27 = (bf16[128,2048]{1,0:T(8,128)(2,1)S(1)}, bf16[128,2048]{1,0:T(8,128)(2,1)S(1)}, u32[]{:S(2)}, u32[]{:S(2)}) collective-permute-start(bf16[128,2048]{1,0:T(8,128)(2,1)S(1)} %copy-done.16), channel_id=1, source_target_pairs={{0,2},{1,3},{2,0},{3,1},{4,6},{5,7},{6,4},{7,5},{8,10},{9,11},{10,... | collective-permute-start | bytes 1572872 | tf_op jit(solution)/shard_map/ppermute | solution.py:87
  519.7 27.8 %collective-permute-start.30 = (bf16[128,2048]{1,0:T(8,128)(2,1)S(1)}, bf16[128,2048]{1,0:T(8,128)(2,1)S(1)}, u32[]{:S(2)}, u32[]{:S(2)}) collective-permute-start(bf16[128,2048]{1,0:T(8,128)(2,1)S(1)} %copy-done.17), channel_id=1, source_target_pairs={{0,4},{1,5},{2,6},{3,7},{4,0},{5,1},{6,2},{7,3},{8,12},{9,13},{10,... | collective-permute-start | bytes 1572872 | tf_op jit(solution)/shard_map/ppermute | solution.py:87
  521.6 25.9 %collective-permute-start.28 = (bf16[128,2048]{1,0:T(8,128)(2,1)}, bf16[128,2048]{1,0:T(8,128)(2,1)S(1)}, u32[]{:S(2)}, u32[]{:S(2)}) collective-permute-start(bf16[128,2048]{1,0:T(8,128)(2,1)} %collective-permute-done.26.refs_1_), channel_id=1, source_target_pairs={{0,2},{1,3},{2,0},{3,1},{4,6},{5,7},{6,4},{7,5},{8,10},{9,11},{10,... | collective-permute-start | bytes 1572872 | tf_op jit(solution)/shard_map/ppermute | solution.py:87
  530.9 17.8 %collective-permute-start.31 = (bf16[128,2048]{1,0:T(8,128)(2,1)}, bf16[128,2048]{1,0:T(8,128)(2,1)}, u32[]{:S(2)}, u32[]{:S(2)}) collective-permute-start(bf16[128,2048]{1,0:T(8,128)(2,1)} %collective-permute-done.29.refs_5_), channel_id=1, source_target_pairs={{0,4},{1,5},{2,6},{3,7},{4,0},{5,1},{6,2},{7,3},{8,12},{9,13},{10,... | collective-permute-start | bytes 1572872 | tf_op jit(solution)/shard_map/ppermute | solution.py:87
  534.6 20.2 %copy-start.28 = (f32[2,2048]{1,0:T(2,128)}, f32[2,2048]{1,0:T(2,128)S(1)}, u32[]{:S(2)}) copy-start(f32[2,2048]{1,0:T(2,128)S(1)} %add.163) | copy-start | bytes 49156
  547.4 7.5 %copy-start.27 = (f32[2,2048]{1,0:T(2,128)S(1)}, f32[2,2048]{1,0:T(2,128)}, u32[]{:S(2)}) copy-start(f32[2,2048]{1,0:T(2,128)} %refs_6_.1) | copy-start | bytes 49156
  547.4 7.4 %copy-start.29 = (f32[2,2048]{1,0:T(2,128)S(1)}, f32[2,2048]{1,0:T(2,128)}, u32[]{:S(2)}) copy-start(f32[2,2048]{1,0:T(2,128)} %param.40) | copy-start | bytes 49156
  547.4 8.1 %collective-permute-start.42 = (bf16[1024,2048]{1,0:T(8,128)(2,1)}, bf16[1024,2048]{1,0:T(8,128)(2,1)}, u32[]{:S(2)}, u32[]{:S(2)}) collective-permute-start(bf16[1024,2048]{1,0:T(8,128)(2,1)} %pack_rows.3.refs_1_), channel_id=1, source_target_pairs={{0,1},{1,0},{2,3},{3,2},{4,5},{5,4},{6,7},{7,6},{8,9},{9,8},{10,11... | collective-permute-start | bytes 12582920 | tf_op jit(solution)/shard_map/ppermute | solution.py:87
  553.7 23.5 %collective-permute-start.32 = (bf16[1024,2048]{1,0:T(8,128)(2,1)}, bf16[1024,2048]{1,0:T(8,128)(2,1)}, u32[]{:S(2)}, u32[]{:S(2)}) collective-permute-start(bf16[1024,2048]{1,0:T(8,128)(2,1)} %pack_rows.2.refs_0_), channel_id=1, source_target_pairs={{0,1},{1,0},{2,3},{3,2},{4,5},{5,4},{6,7},{7,6},{8,9},{9,8},{10,11... | collective-permute-start | bytes 12582920 | tf_op jit(solution)/shard_map/ppermute | solution.py:87
  (24 other events, 82.5 us)
Sparse Core Ops, SparseCore 0:
  11.0 83.4 all-gather.3
  96.7 81.6 all-gather.5
  311.4 77.0 reduce-scatter.4
  395.2 75.7 reduce-scatter.2

commit v2 on v1

--- a/solution.py
+++ b/solution.py
@@ -20,6 +20,7 @@
 low = jnp.bfloat16
 full = jnp.float32
 vmem_limit = 60 << 20
+tail_rows = 16
 
 
 def dot_nt(left, right):
@@ -53,33 +54,31 @@
     return (weight_new, moment_new, average_new)
 
 
-def gather_hops(shard):
+def after(value, *others):
+    return lax.optimization_barrier((value, others))[0]
+
+
+def gather_hop(k, right, left):
     n = lax.axis_size("dp")
-    rights, lefts = [], []
-    right = left = shard
-    for k in range(1, n):
-        right = lax.ppermute(right, "dp", [(a, a + 1) for a in range(k - 1, n - 1)])
-        left = lax.ppermute(left, "dp", [(a, a - 1) for a in range(1, n - k + 1)])
-        right, left = yield right, left
-        yield
-        rights.append(right)
-        lefts.append(left)
-    yield [shard] + rights + lefts
-
-
-def scatter_hops(slots):
+    right = lax.ppermute(right, "dp", [(a, a + 1) for a in range(k - 1, n - 1)])
+    left = lax.ppermute(left, "dp", [(a, a - 1) for a in range(1, n - k + 1)])
+    return right, left
+
+
+def scatter_load(k, slots, right, left):
     n = lax.axis_size("dp")
-    right = left = None
-    for k in range(1, n):
-        to_right, to_left = slots[n - k], slots[k]
-        if k > 1:
-            to_right = (to_right.astype(full) + right.astype(full)).astype(low)
-            to_left = (to_left.astype(full) + left.astype(full)).astype(low)
-        right = lax.ppermute(to_right, "dp", [(a, a + 1) for a in range(k)])
-        left = lax.ppermute(to_left, "dp", [(a, a - 1) for a in range(n - 1, n - 1 - k, -1)])
-        right, left = yield right, left
-        yield
-    yield slots[0] + right.astype(full) + left.astype(full)
+    to_right, to_left = slots[n - k], slots[k]
+    if k > 1:
+        to_right = (to_right.astype(full) + right.astype(full)).astype(low)
+        to_left = (to_left.astype(full) + left.astype(full)).astype(low)
+    return to_right, to_left
+
+
+def scatter_hop(k, to_right, to_left):
+    n = lax.axis_size("dp")
+    right = lax.ppermute(to_right, "dp", [(a, a + 1) for a in range(k)])
+    left = lax.ppermute(to_left, "dp", [(a, a - 1) for a in range(n - 1, n - 1 - k, -1)])
+    return right, left
 
 
 def swap(value, mask, axis="mp"):
@@ -96,6 +95,16 @@
         value = value + swap(value, mask, axis)
         mask *= 2
     return value
+
+
+def join_sums(norm_part, bias_part):
+    cols = bias_part.shape[1]
+    return jnp.concatenate([norm_part.reshape(-1, cols), bias_part])
+
+
+def split_sums(sums, norm_part, bias_part):
+    count = sums.shape[0] - bias_part.shape[0]
+    return sums[:count].reshape(norm_part.shape), sums[count:]
 
 
 def norm_kernel(x_ref, p_ref, o_ref):
@@ -183,62 +192,46 @@
     return lambda index: w_ref.at[:, :, pl.ds(pl.multiple_of(index * piece, piece), piece)]
 
 
-def feed_kernel(n, count, steps, me_ref, *refs):
+def feed_kernel(n, count, me_ref, *refs):
     pieces = refs[:count]
-    h_ref, c_ref, act_ref, grad_ref, w_ref, out_ref, acc, sems = refs[count:]
-    step = pl.program_id(0)
-    target_of = wide_target(w_ref, out_ref.shape[2])
-
-    @pl.when(step == 0)
+    h_ref, c_ref, act_ref, grad_ref, w_ref, sems = refs[count:]
+    target_of = wide_target(w_ref, w_ref.shape[2] // n)
+
+    @pl.when(pl.program_id(0) == 0)
     def _():
         fetch(n, me_ref[0], pieces, target_of, sems, "start")
         fetch(n, me_ref[0], pieces, target_of, sems, "wait")
 
-    h = h_ref[...]
-    c = c_ref[...]
-    active, gates_grad = gates_of(w_ref, h, c)
-    act_ref[...] = active
-    grad_ref[...] = gates_grad
-    add_grads(acc, step, active, gates_grad, h, c)
-
-    @pl.when(step == steps - 1)
-    def _():
-        store_grads(n, acc, out_ref)
+    act_ref[...], grad_ref[...] = gates_of(w_ref, h_ref[...], c_ref[...])
 
 
 def feed_chunk(n, me, pieces, hidden, cot):
     rows, width = hidden.shape
-    units, piece = pieces[0].shape[-2:]
+    units = pieces[0].shape[-2]
     count = len(pieces)
     block = min(512, rows)
-    steps = rows // block
     row_spec = pl.BlockSpec((block, width), lambda i, m: (i, 0))
     return pl.pallas_call(
-        functools.partial(feed_kernel, n, count, steps),
+        functools.partial(feed_kernel, n, count),
         grid_spec=pltpu.PrefetchScalarGridSpec(
             num_scalar_prefetch=1,
-            grid=(steps,),
+            grid=(rows // block,),
             in_specs=[pl.BlockSpec(memory_space=pl.ANY)] * count + [row_spec, row_spec],
             out_specs=[
                 pl.BlockSpec((units, block), lambda i, m: (0, i)),
                 pl.BlockSpec((2 * units, block), lambda i, m: (0, i)),
                 pl.BlockSpec((3, units, width), lambda i, m: (0, 0, 0)),
-                pl.BlockSpec((n, 3 * units, piece), lambda i, m: (0, 0, 0)),
             ],
-            scratch_shapes=[
-                pltpu.VMEM((3 * units, width), full),
-                pltpu.SemaphoreType.DMA((2 * n - 1,)),
-            ],
+            scratch_shapes=[pltpu.SemaphoreType.DMA((2 * n - 1,))],
         ),
         out_shape=[
             shape((units, rows), low),
             shape((2 * units, rows), low),
             shape((3, units, width), low),
-            shape((n, 3 * units, piece), low),
         ],
         compiler_params=params(),
         cost_estimate=cost(
-            12 * rows * width * units, 4 * rows * width + 20 * units * width, rows * units
+            6 * rows * width * units, 4 * rows * width + 12 * units * width, rows * units
         ),
         name="feed_chunk",
     )(me, *pieces, hidden, cot)
@@ -596,7 +589,6 @@
 
 def back_kernel(info_ref, *refs):
     p_ref = refs[6]
-    sums_ref = refs[9]
     total = 0.0
     for x_ref, near_ref, far_ref, back_ref in zip(refs[0:2], refs[2:4], refs[4:6], refs[7:9]):
         x = x_ref[...].astype(full)
@@ -610,12 +602,18 @@
             - jnp.mean(scaled, axis=-1, keepdims=True)
             - normal * jnp.mean(scaled * normal, axis=-1, keepdims=True)
         )
-        back_ref[...] = back.astype(low)
+        back_ref[: x.shape[0]] = back.astype(low)
         total += jnp.concatenate(
             [jnp.sum(grad * normal, axis=0, keepdims=True), jnp.sum(grad, axis=0, keepdims=True)],
             axis=0,
         )
-    sums_ref[...] = total
+    high = total.astype(low)
+    rest = total - high.astype(full)
+    middle = rest.astype(low)
+    small = (rest - middle.astype(full)).astype(low)
+    zeros = jnp.zeros((tail_rows - 6, total.shape[1]), full)
+    terms = [high.astype(full), middle.astype(full), small.astype(full), zeros]
+    refs[7][refs[0].shape[0] :] = jnp.concatenate(terms, axis=0).astype(low)
 
 
 def back_rows(info, rows, near, far, norm_params):
@@ -633,9 +631,9 @@
             ]
             + [spec] * 4
             + [pair],
-            out_specs=[spec, spec, pair],
+            out_specs=[pl.BlockSpec((count + tail_rows, width), lambda i, m: (0, 0)), spec],
         ),
-        out_shape=[shape((count, width), low)] * 2 + [shape((2, width), full)],
+        out_shape=[shape((count + tail_rows, width), low), shape((count, width), low)],
         compiler_params=params(),
         cost_estimate=cost(40 * count * width, 16 * count * width),
         name="back_rows",
@@ -670,19 +668,25 @@
     )(info, rows, rows, *near, *far)
 
 
-def pack_kernel(info_ref, *refs):
+def pack_kernel(block, info_ref, *refs):
     pieces, out_ref, sems = refs[:8], refs[8], refs[9]
-    block = pieces[0].shape[0]
     x, y = info_ref[1], info_ref[2]
     copies = []
+
+    def move(source, at, size):
+        place = out_ref.at[pl.ds(pl.multiple_of(at, 16), size), :]
+        copies.append(pltpu.make_async_copy(source, place, sems.at[len(copies)]))
+
     for i, piece in enumerate(pieces):
         high, small = (i // 2) % 2, i % 2
         if i < 4:
             at = (x ^ high) * 2 + (y ^ small)
         else:
             at = 4 + (y ^ high) * 2 + (x ^ small)
-        place = out_ref.at[pl.ds(pl.multiple_of(at * block, block), block), :]
-        copies.append(pltpu.make_async_copy(piece, place, sems.at[i]))
+        extra = piece.shape[0] - block
+        move(piece.at[pl.ds(0, block), :], at * block, block)
+        if extra:
+            move(piece.at[pl.ds(block, extra), :], 8 * block + at * extra, extra)
     for copy in copies:
         copy.start()
     for copy in copies:
@@ -690,21 +694,50 @@
 
 
 def pack_rows(info, pieces):
-    block, width = pieces[0].shape
-    return pl.pallas_call(
-        pack_kernel,
+    block, width = pieces[-1].shape
+    extra = pieces[0].shape[0] - block
+    return pl.pallas_call(
+        functools.partial(pack_kernel, block),
         grid_spec=pltpu.PrefetchScalarGridSpec(
             num_scalar_prefetch=1,
             grid=(1,),
-            in_specs=[pl.BlockSpec((block, width), lambda i, m: (0, 0))] * 8,
+            in_specs=[pl.BlockSpec(piece.shape, lambda i, m: (0, 0)) for piece in pieces],
             out_specs=pl.BlockSpec(memory_space=pl.ANY),
-            scratch_shapes=[pltpu.SemaphoreType.DMA((8,))],
+            scratch_shapes=[pltpu.SemaphoreType.DMA((12,))],
         ),
-        out_shape=shape((8 * block, width), low),
+        out_shape=shape((8 * block + 4 * extra, width), low),
         compiler_params=params(),
         cost_estimate=cost(0, 32 * block * width),
         name="pack_rows",
     )(info, *pieces)
+
+
+def tail_kernel(own_ref, other_ref, out_ref):
+    def total(ref):
+        values = ref[...].astype(full)
+        sums = 0.0
+        for i in range(4):
+            at = i * tail_rows
+            sums += values[at : at + 2] + values[at + 2 : at + 4] + values[at + 4 : at + 6]
+        return sums
+
+    out_ref[...] = total(own_ref) + total(other_ref)
+
+
+def tail_sums(own, other):
+    count, width = own.shape
+    size = 4 * tail_rows
+    spec = pl.BlockSpec((size, width), lambda i: (count // size - 1, 0))
+    return pl.pallas_call(
+        tail_kernel,
+        grid=(1,),
+        in_specs=[spec, spec],
+        out_specs=pl.BlockSpec((2, width), lambda i: (0, 0)),
+        out_shape=shape((2, width), full),
+        compiler_params=params(),
+        cost_estimate=cost(20 * width, 512 * width),
+        name="tail_sums",
+    )(own, other)
 
 
 def finish_kernel(info_ref, *refs):
@@ -725,8 +758,8 @@
         store(other_ref[...])
 
 
-def finish_rows(info, own, other, cot=None):
-    rows, width = 2 * own.shape[0], own.shape[1]
+def finish_rows(info, rows, own, other, cot=None):
+    width = own.shape[1]
     extra = () if cot is None else (cot,)
     block = rows // 8
     spec = pl.BlockSpec((block, width), lambda i, m: (i, 0))
@@ -851,80 +884,122 @@
     last_shard, first_piece, attend_slots = lax.optimization_barrier(
         (shards[1], first_pieces[0], attend_slots)
     )
-    active, gates_grad, w_feed, first_grads = feed_chunk(n, me, [first_piece], hidden, cot)
-    hid_early, out_early = early_parts(context, mixed_grad, active, gates_grad, w_attend, w_feed)
-    bias_grad = small_sum(bias_part, "dp")
-    gathering, scattering = gather_hops(last_shard), scatter_hops(attend_slots)
-    arrived = lax.optimization_barrier((next(gathering), first_grads))
-    gathering.send(arrived[0])
-    first_grads = arrived[1]
-    for k in range(2, n):
-        beside = (hid_early, out_early, bias_grad) if k == 2 else ()
-        arrived = lax.optimization_barrier((next(gathering), next(scattering), beside))
-        gathering.send(arrived[0])
-        scattering.send(arrived[1])
-        if k == 2:
-            hid_early, out_early, bias_grad = arrived[2]
-    last_pieces = next(gathering)
-    arrived, last_pieces = lax.optimization_barrier((next(scattering), last_pieces))
-    scattering.send(arrived)
-    attend_grad = next(scattering)
+
+    rights, lefts = [last_shard], [last_shard]
+    came, beside = (None, None), None
+    for k in range(1, n):
+        right, left = gather_hop(k, rights[-1], lefts[-1])
+        if k > 1:
+            slots = after(attend_slots, (rights[-1], lefts[-1]))
+            coming = scatter_hop(k - 1, *scatter_load(k - 1, slots, *came))
+        if k == 1:
+            active, gates_grad, w_feed = feed_chunk(n, me, [first_piece], hidden, cot)
+            beside = (active, gates_grad, w_feed)
+        elif k == 2:
+            hid_early, out_early = early_parts(
+                context, mixed_grad, active, gates_grad, w_attend, w_feed
+            )
+            beside = (hid_early, out_early)
+        elif k == 3:
+            first_grads = feed_grads(n, hidden, cot, active, gates_grad)
+            beside = (first_grads,)
+        if k > 1:
+            right, left, came = lax.optimization_barrier((right, left, coming, beside))[:3]
+        else:
+            right, left = lax.optimization_barrier((right, left, beside))[:2]
+        rights.append(right)
+        lefts.append(left)
+    load = scatter_load(n - 1, attend_slots, *came)
+    came = scatter_hop(n - 1, *load)
+    attend_grad = attend_slots[0] + came[0].astype(full) + came[1].astype(full)
+    last_pieces = after([last_shard] + rights[1:] + lefts[1:], load)
 
     def scatter(grads):
         return lax.psum_scatter(grads, "dp", scatter_dimension=0, tiled=False)
 
-    first_grads, _ = lax.optimization_barrier((first_grads, last_pieces))
-    first_grads = scatter(first_grads)
+    first_grads = scatter(first_grads).reshape(3, cut, -1)
+
+    grad_in = jnp.transpose(attend_grad[:3], (1, 0, 2))
+    grad_out = attend_grad[3]
+    total_tokens = rows * n
+    attend_new = advance(
+        w_attend_in, grad_in, moment_attend_in, average_attend_in, 0.5 / math.sqrt(width * total_tokens)
+    ) + advance(
+        w_attend_out, grad_out, moment_attend_out, average_attend_out, 1.8 / math.sqrt(width * batch * n)
+    )
+    rates = (1.6 / math.sqrt(width * total_tokens), 0.77 / math.sqrt(FF * total_tokens))
+    states = [jnp.transpose(a, (1, 2, 0)) for a in (w_expand, moment_expand, average_expand)]
+    states += [jnp.transpose(a) for a in (w_reduce, moment_reduce, average_reduce)]
 
     if fast:
         other_hid, other_out, own_hid, own_out, active, gates_grad = feed_last(
             n, info, True, last_pieces, hidden, cot, hid_early, out_early
         )
-        came_hid, came_out = swap(other_hid, 1), swap(other_out, 1)
         e = rows // 8
         s = e // 2
 
-        def send_rows(own, came):
+        def sum_cores(own, came):
             own = [own[i * e : (i + 1) * e].astype(full) + came[i * e : (i + 1) * e].astype(full) for i in range(4)]
-            to_x, to_y = own[1].astype(low), own[3].astype(low)
-            return own, (to_x, to_y), (swap(to_x, 2), swap(to_y, 4))
-
-        def reduce_rows(own, came):
-            over_x, over_y = came
-            first = own[0] + over_x.astype(full)
-            second = own[2] + over_y.astype(full)
-            far = [swap(first[s:].astype(low), 4), swap(second[s:].astype(low), 2)]
-            return [first[:s].astype(low), second[:s].astype(low)], far
-
-        def spread_rows(first, second):
-            first_y, second_x = swap(first, 4), swap(second, 2)
-            first_x, second_y = swap(first, 2), swap(second, 4)
-            first_xy, second_xy = swap(first_y, 2), swap(second_x, 4)
-            return [first, first_y, first_x, first_xy, second, second_x, second_y, second_xy]
-
-        own_hid, sent, came_hid = send_rows(own_hid, came_hid)
-        active, gates_grad, _ = lax.optimization_barrier((active, gates_grad, sent))
+            return own, (own[1].astype(low), own[3].astype(low))
+
+        def sum_first(own, came):
+            first = own[0] + came[0].astype(full)
+            second = own[2] + came[1].astype(full)
+            near = [first[:s].astype(low), second[:s].astype(low)]
+            return near, (first[s:].astype(low), second[s:].astype(low))
+
+        def both_ways(pair, masks):
+            return [swap(pair[0], masks[0]), swap(pair[1], masks[1])]
+
+        came_hid = swap(other_hid, 1)
+        came_out = swap(after(other_out, came_hid), 1)
+        own_hid, load_hid = sum_cores(own_hid, came_hid)
+        one_hid = both_ways(load_hid, (2, 4))
+        active, gates_grad = after((active, gates_grad), load_hid)
         last_grads = feed_grads(n, hidden, cot, active, gates_grad)
-        came_hid, last_grads, came_out, own_out = lax.optimization_barrier(
-            (came_hid, last_grads, came_out, own_out)
+        own_out, load_out = sum_cores(own_out, came_out)
+        one_hid = after(one_hid, last_grads, load_out)
+        last_grads = scatter(last_grads).reshape(3, units - cut, -1)
+        near_hid, load_hid = sum_first(own_hid, one_hid)
+        two_hid = both_ways(load_hid, (4, 2))
+        load_out = after(load_out, load_hid)
+        one_out = both_ways(load_out, (2, 4))
+        two_hid = after(two_hid, attend_new)
+        back = back_rows(info, tokens, near_hid, two_hid, norm_params)
+        hid_one = both_ways(back, (4, 2))
+        hid_two = both_ways(back, (2, 4))
+        one_out = after(one_out, back)
+        near_out, load_out = sum_first(own_out, one_out)
+        two_out = both_ways(load_out, (4, 2))
+        begun = update_feed(0, after(first_grads, load_out), states, rates)
+        hid_one = after(hid_one, begun)
+        hid_three = both_ways(hid_one, (2, 4))
+        two_out = after(two_out, hid_one)
+        add = add_rows(info, tokens, near_out, two_out)
+        out_one = both_ways(add, (4, 2))
+        out_two = both_ways(add, (2, 4))
+        hid_two, hid_three = after((hid_two, hid_three), add)
+        mine_hid = pack_rows(
+            info, [back[0], hid_one[0], hid_two[0], hid_three[0], back[1], hid_one[1], hid_two[1], hid_three[1]]
         )
-        own_out, _, came_out = send_rows(own_out, came_out)
-        near, far = reduce_rows(own_hid, came_hid)
-        back_a, back_b, norm_part = back_rows(info, tokens, near, far, norm_params)
-        near, far = reduce_rows(own_out, came_out)
-        out_a, out_b = add_rows(info, tokens, near, far)
-        hid_pieces = spread_rows(back_a, back_b)
-        hid_pieces[1], hid_pieces[5], out_a, out_b = lax.optimization_barrier(
-            (hid_pieces[1], hid_pieces[5], out_a, out_b)
+        out_one = after(out_one, mine_hid)
+        out_three = both_ways(out_one, (2, 4))
+        other_hid = after(swap(mine_hid, 1), out_one)
+        norm_part = tail_sums(mine_hid, other_hid)
+        sums = small_sum(join_sums(norm_part, bias_part), "dp")
+        input_grad = finish_rows(info, rows, mine_hid, after(other_hid, norm_part), cot)
+        done = update_feed(cut, after(last_grads, input_grad), states, rates, begun)
+        out_two, out_three = after((out_two, out_three), done)
+        mine_out = pack_rows(
+            info, [add[0], out_one[0], out_two[0], out_three[0], add[1], out_one[1], out_two[1], out_three[1]]
         )
-        out_pieces = spread_rows(out_a, out_b)
-        norm_grad = small_sum(small_sum(norm_part, "mp"), "dp")
-        last_grads = scatter(last_grads)
+        output = finish_rows(info, rows, mine_out, swap(mine_out, 1))
+        norm_grad, bias_grad = split_sums(sums, norm_part, bias_part)
     else:
         hid_part, out_part, active, gates_grad = feed_last(
             n, info, False, last_pieces, hidden, cot, hid_early, out_early
         )
-        last_grads = scatter(feed_grads(n, hidden, cot, active, gates_grad))
+        last_grads = scatter(feed_grads(n, hidden, cot, active, gates_grad)).reshape(3, units - cut, -1)
         hidden_grad = lax.psum(hid_part, "mp").astype(full)
         summed = lax.psum(out_part, "mp").astype(full)
         values = tokens.astype(full)
@@ -940,35 +1015,11 @@
         )
         input_grad = cot.astype(full) + back
         norm_part = jnp.stack([jnp.sum(hidden_grad * normal, axis=0), jnp.sum(hidden_grad, axis=0)])
-        norm_grad = small_sum(norm_part, "dp")
-
-    grad_in = jnp.transpose(attend_grad[:3], (1, 0, 2))
-    grad_out = attend_grad[3]
-
-    total_tokens = rows * n
-    new_in, moment_in_new, average_in_new = advance(
-        w_attend_in, grad_in, moment_attend_in, average_attend_in, 0.5 / math.sqrt(width * total_tokens)
-    )
-    new_out, moment_out_new, average_out_new = advance(
-        w_attend_out, grad_out, moment_attend_out, average_attend_out, 1.8 / math.sqrt(width * batch * n)
-    )
-    rates = (1.6 / math.sqrt(width * total_tokens), 0.77 / math.sqrt(FF * total_tokens))
-    states = [jnp.transpose(a, (1, 2, 0)) for a in (w_expand, moment_expand, average_expand)]
-    states += [jnp.transpose(a) for a in (w_reduce, moment_reduce, average_reduce)]
-    first_grads = first_grads.reshape(3, cut, -1)
-    last_grads = last_grads.reshape(3, units - cut, -1)
-    begun = update_feed(0, first_grads, states, rates)
-    if fast:
-        updated = (norm_grad, new_in, new_out, begun)
-        hid_pieces, updated = lax.optimization_barrier((hid_pieces, updated))
-        norm_grad, new_in, new_out, begun = updated
-    done = update_feed(cut, last_grads, states, rates, begun)
-    if fast:
-        mine_hid = pack_rows(info, hid_pieces)
-        mine_out = pack_rows(info, out_pieces)
-        input_grad = finish_rows(info, mine_hid, swap(mine_hid, 1), cot)
-        other_out, done = lax.optimization_barrier((swap(mine_out, 1), done))
-        output = finish_rows(info, mine_out, other_out)
+        sums = small_sum(join_sums(norm_part, bias_part), "dp")
+        norm_grad, bias_grad = split_sums(sums, norm_part, bias_part)
+        begun = update_feed(0, first_grads, states, rates)
+        done = update_feed(cut, last_grads, states, rates, begun)
+    new_in, moment_in_new, average_in_new, new_out, moment_out_new, average_out_new = attend_new
     grad_expand, new_expand, moment_expand_new, average_expand_new = (
         jnp.transpose(a, (2, 0, 1)) for a in done[:4]
     )

time: 604 us -> 567 us (0.939)
  waiting for transfers between devices: 233 us -> 165 us
  Pallas kernels: 246 us -> 262 us
  other arithmetic: 37.5 us -> 44.5 us
  starting transfers between devices: 54.6 us -> 60.8 us
    ppermute x31 -> x26, waiting for transfers between devices: 117 us -> 69.8 us  [swap(): return lax.ppermute(value, axis, [(a, a ^ mask) for a in range(n)])]
    pallas_call x1 -> x2, Pallas kernels: 16.3 us -> 43.4 us  [feed_grads(): pl.pallas_call(functools.partial(feed_grads_kernel, n, steps), grid=(step...]
    ppermute x12, waiting for transfers between devices: 42.8 us -> 16.6 us  [the longest x3 6.81 us: scatter_hop(): lax.ppermute(to_left, 'dp', [(a, a - 1) for a in range(n - 1, n - 1 - k,...]
    pallas_call x3 -> x4, Pallas kernels: 39.7 us -> 28.5 us  [the longest x1 16.5 us: feed_chunk(): pl.pallas_call(functools.partial(feed_kernel, n, count), grid_spec=pltpu....]
    convert_element_type x5, other arithmetic: 8.01 us -> 15.9 us  [the longest x2 7.77 us: sum_cores(): return (own, (own[1].astype(low), own[3].astype(low)))]
    ppermute x31 -> x26, starting transfers between devices: 25 us -> 28.3 us  [swap(): return lax.ppermute(value, axis, [(a, a ^ mask) for a in range(n)])]
  transfers between devices with their start and end apart: 47 -> 42, of which waited for: 22 -> 15; matrix products, arithmetic and copies ran while one was open for 6% -> 8% of each run, Pallas kernels for 40% -> 44%
where the time goes in v2:
time: 567 us; the launch traced here: 557 us
  Pallas kernels  262 us (46%)
  waiting for transfers between devices  165 us (29%)
  starting transfers between devices  60.8 us (11%)
  other arithmetic  44.5 us (8%)
  between operations  14.8 us (3%)
  local copies, waits for them, and re-layouts  9.74 us (2%)
    ppermute x26, waiting for transfers between devices, swap(): return lax.ppermute(value, axis, [(a, a ^ mask) for a in range(n)])  69.8 us
    all_gather x1, waiting for transfers between devices, body(): attend_pieces = [lax.all_gather(attend_shard, 'dp')]  62.9 us
    pallas_call x2, Pallas kernels, feed_grads(): pl.pallas_call(functools.partial(feed_grads_kernel, n, steps), grid=(step...  43.4 us
    pallas_call x1, Pallas kernels, feed_last(): pl.pallas_call(functools.partial(last_kernel, n, count, split), grid_spec...  36.7 us
    pallas_call x1, Pallas kernels, attend(): pl.pallas_call(functools.partial(attend_kernel, min(512, length)), grid=(...  34 us
    ppermute x26, starting transfers between devices, swap(): return lax.ppermute(value, axis, [(a, a ^ mask) for a in range(n)])  28.3 us
    pallas_call x1, Pallas kernels, early_parts(): pl.pallas_call(early_kernel, grid=(rows // block,), in_specs=[pl.BlockSpe...  26.3 us
    pallas_call x2, Pallas kernels, finish_rows(): pl.pallas_call(finish_kernel, grid_spec=pltpu.PrefetchScalarGridSpec(num_...  24.7 us
  transfers between devices with their start and end apart: 42, of which 15 were waited for; matrix products, arithmetic and copies ran while one was open for 8% of the time, Pallas kernels for 44%

profile of v2, /device:TPU:0, one launch (start us, length us, event | category | flops | bytes accessed | tf_op | source)
XLA Modules:
  0.0 557.0 jit_solution(17960258269844276214)
XLA Ops:
  8.3 1.5 convert_bitcast_fusion
  11.0 1.6 bitcast_convert_fusion
  14.6 11.2 %layer_norm.1.refs_1_.h_ref.refs_7_ = bf16[2048,2048]{1,0:T(8,128)(2,1)} custom-call(bf16[2048,2048]{1,0:T(8,128)(2,1)} %bitcast.48, f32[2,2048]{1,0:T(2,128)} %refs_6_.1), custom_call_target="tpu_custom_call" | custom-call | flops 33554432 | bytes 16777216 | tf_op jit(solution)/shard_map/layer_norm/pallas_call | solution.py:120
  26.0 5.6 %fusion.4 = (f32[2048,128]{1,0:T(8,128)}, f32[2048,128]{1,0:T(8,128)}) fusion(f32[128]{0:T(128)S(1)} %fusion.9, f32[2048]{0:T(1024)S(1)} %bitcast.84, pred[128]{0:T(512)(128)(4,1)S(1)} %get-tuple-element.261, pred[128]{0:T(512)(128)(4,1)S(1)} %get-tuple-element.262), kind=kLoop, calls=%fused_computation.25 | loop fusion | flops 1310720 | bytes 2106112 | tf_op jit(solution)/shard_map/jit(_where)/select_n | solution.py:879
  31.6 62.9 %all-gather.4.cloned.1.call-done.refs_0_ = bf16[4,4,512,256]{3,2,1,0:T(8,128)(2,1)} async-done(((bf16[1,4,512,256]{3,2,1,0:T(8,128)(2,1)}), bf16[4,4,512,256]{3,2,1,0:T(8,128)(2,1)}) %all-gather.4.cloned.1.call-update) | async-done | bytes 4194320 | tf_op jit(solution)/shard_map/all_gather | solution.py:866
  94.5 17.4 %project.1 = (bf16[2048,256]{1,0:T(8,128)(2,1)}, bf16[2048,256]{1,0:T(8,128)(2,1)}, bf16[2048,256]{1,0:T(8,128)(2,1)}, bf16[2048,256]{1,0:T(8,128)(2,1)}, bf16[4,2048,256]{2,1,0:T(8,128)(2,1)}) custom-call(s32[1]{0:T(128)} %bitcast.3.me_ref, bf16[4,4,512,256]{3,2,1,0:T(8,128)(2,1)} %all-gather.4.cloned.1.call-done.refs_0_, ...), custom_call_target="tpu_custom_call" | custom-call | flops 8589934592 | bytes 25165824 | tf_op jit(solution)/shard_map/project/pallas_call | solution.py:397
  112.0 34.0 %attend.1 = (bf16[2048,256]{1,0:T(8,128)(2,1)}, bf16[3,2048,256]{2,1,0:T(8,128)(2,1)}, f32[3,256]{1,0:T(4,128)}) custom-call(bf16[2048,256]{1,0:T(8,128)(2,1)} %get-tuple-element.124.q_ref, bf16[2048,256]{1,0:T(8,128)(2,1)} %get-tuple-element.125.k_ref, bf16[2048,256]{1,0:T(8,128)(2,1)} %get-tuple-element.126.v_ref, ...), custom_call_target="tpu_custom_call" | custom-call | flops 21474836480 | bytes 10485760 | tf_op jit(solution)/shard_map/attend/pallas_call | solution.py:477
  145.9 16.3 %attend_grads.1 = (f32[4,512,256]{2,1,0:T(8,128)}, bf16[4,512,256]{2,1,0:T(8,128)(2,1)}, bf16[4,512,256]{2,1,0:T(8,128)(2,1)}, bf16[4,512,256]{2,1,0:T(8,128)(2,1)}) custom-call(s32[1]{0:T(128)} %bitcast.3.me_ref, bf16[2048,2048]{1,0:T(8,128)(2,1)} %layer_norm.1.refs_1_.h_ref.refs_7_, bf16[2048,2048]{1,0:T(8,128)(2,1)} %bitcast.63, ...), custom_call_target="tpu_custom_call" | custom-call | flops 8589934592 | bytes 25165824 | tf_op jit(solution)/shard_map/attend_grads/pallas_call | solution.py:531
  162.2 15.9 %all-gather.6.cloned.1.call-done = bf16[12,352,512]{2,1,0:T(8,128)(2,1)} async-done(((bf16[3,352,512]{2,1,0:T(8,128)(2,1)}), bf16[12,352,512]{2,1,0:T(8,128)(2,1)}) %all-gather.6.cloned.1.call-update) | async-done | bytes 4325392 | tf_op jit(solution)/shard_map/all_gather | solution.py:868
  178.2 2.4 collective-permute-start
  181.8 16.5 %feed_chunk.1 = (bf16[352,2048]{1,0:T(8,128)(2,1)}, bf16[704,2048]{1,0:T(8,128)(2,1)}, bf16[3,352,2048]{2,1,0:T(8,128)(2,1)}) custom-call(s32[1]{0:T(128)} %bitcast.3.me_ref, bf16[4,3,352,512]{3,2,1,0:T(8,128)(2,1)} %bitcast.85, bf16[2048,2048]{1,0:T(8,128)(2,1)} %layer_norm.1.refs_1_.h_ref.refs_7_, bf16[2048,2048]{1,0:T(8,128)(2,1)} %bitcast.64), custom_call_target="tpu_custom_call" | custom-call | flops 8858370048 | bytes 25427968 | tf_op jit(solution)/shard_map/feed_chunk/pallas_call | solution.py:214
  198.4 4.6 collective-permute-done.refs_1_
  203.0 5.2 collective-permute-done.1.refs_4_
  208.2 1.6 collective-permute-start.2
  211.1 6.0 %collective-permute-start.4 = (bf16[4,512,256]{2,1,0:T(8,128)(2,1)S(1)}, bf16[4,512,256]{2,1,0:T(8,128)(2,1)}, u32[]{:S(2)}, u32[]{:S(2)}) collective-permute-start(bf16[4,512,256]{2,1,0:T(8,128)(2,1)S(1)} %copy-done.9), channel_id=1, source_target_pairs={{0,8},{1,9},{2,10},{3,11},{4,12},{5,13},{6,14},{7,15}} | collective-permute-start | bytes 3145736 | tf_op jit(solution)/shard_map/ppermute | solution.py:79
  217.1 1.6 collective-permute-start.5
  218.8 26.3 %early_parts.1 = (bf16[2048,2048]{1,0:T(8,128)(2,1)}, bf16[2048,2048]{1,0:T(8,128)(2,1)}) custom-call(bf16[2048,256]{1,0:T(8,128)(2,1)} %get-tuple-element.129.ctx_ref, bf16[3,2048,256]{2,1,0:T(8,128)(2,1)} %get-tuple-element.128.mg_ref, bf16[352,2048]{1,0:T(8,128)(2,1)} %get-tuple-element.136.act_ref, bf16[704,2048]{1,0:T(8,128)(2,1)} %get-tuple-element.137.grad_ref, ...), custom_call_target="tpu_custom_call" | custom-call | flops 17448304640 | bytes 33816576 | tf_op jit(solution)/shard_map/early_parts/pallas_call | solution.py:564
  245.1 1.7 collective-permute-start.6
  248.1 3.3 fusion.1
  251.4 6.6 %collective-permute-start.8 = (bf16[4,512,256]{2,1,0:T(8,128)(2,1)}, bf16[4,512,256]{2,1,0:T(8,128)(2,1)}, u32[]{:S(2)}, u32[]{:S(2)}) collective-permute-start(bf16[4,512,256]{2,1,0:T(8,128)(2,1)} %get-tuple-element.256), channel_id=1, source_target_pairs={{0,8},{8,16},{1,9},{9,17},{2,10},{10,18},{3,11},{11,19},{4,12},{12... | collective-permute-start | bytes 3145736 | tf_op jit(solution)/shard_map/ppermute | solution.py:79
  258.0 1.7 collective-permute-start.9
  260.3 27.1 %feed_grads.2 = bf16[4,1056,512]{2,1,0:T(8,128)(2,1)} custom-call(bf16[2048,2048]{1,0:T(8,128)(2,1)} %layer_norm.1.refs_1_.h_ref.refs_7_, bf16[2048,2048]{1,0:T(8,128)(2,1)} %bitcast.65, bf16[352,2048]{1,0:T(8,128)(2,1)} %get-tuple-element.136.act_ref, bf16[704,2048]{1,0:T(8,128)(2,1)} %get-tuple-element.137.grad_ref), custom_call_target="tpu_custom_call" | custom-call | flops 8858370048 | bytes 25427968 | tf_op jit(solution)/shard_map/feed_grads/pallas_call | solution.py:334
  288.7 2.4 add_convert_fusion.9
  291.1 2.4 add_convert_fusion.8
  293.5 36.7 %feed_last.1 = (bf16[1024,2048]{1,0:T(8,128)(2,1)}, bf16[1024,2048]{1,0:T(8,128)(2,1)}, bf16[1024,2048]{1,0:T(8,128)(2,1)}, bf16[1024,2048]{1,0:T(8,128)(2,1)}, ...) custom-call(s32[4]{0:T(128)} %pad_add_fusion.info_ref, bf16[3,352,512]{2,1,0:T(8,128)(2,1)} %copy-done.8, ...), custom_call_target="tpu_custom_call" | custom-call | flops 17716740096 | bytes 50331648 | tf_op jit(solution)/shard_map/feed_last/pallas_call | solution.py:295
  330.3 7.4 %collective-permute-done.10 = bf16[1024,2048]{1,0:T(8,128)(2,1)S(1)} collective-permute-done((bf16[1024,2048]{1,0:T(8,128)(2,1)}, bf16[1024,2048]{1,0:T(8,128)(2,1)S(1)}, u32[]{:S(2)}, u32[]{:S(2)}) %collective-permute-start.10) | collective-permute-done | bytes 4194336 | tf_op jit(solution)/shard_map/ppermute | solution.py:86
  339.1 5.6 %collective-permute-start.18 = (bf16[4,512,256]{2,1,0:T(8,128)(2,1)S(1)}, bf16[4,512,256]{2,1,0:T(8,128)(2,1)}, u32[]{:S(2)}, u32[]{:S(2)}) collective-permute-start(bf16[4,512,256]{2,1,0:T(8,128)(2,1)S(1)} %copy-done.12), channel_id=1, source_target_pairs={{0,8},{8,16},{16,24},{1,9},{9,17},{17,25},{2,10},{10,18},{18,26},{... | collective-permute-start | bytes 3145736 | tf_op jit(solution)/shard_map/ppermute | solution.py:79
  344.7 3.6 add_convert_fusion.4
  348.3 1.8 collective-permute-start.12
  350.1 1.5 collective-permute-start.13
  351.6 16.2 %feed_grads.3 = bf16[4,1056,512]{2,1,0:T(8,128)(2,1)} custom-call(bf16[2048,2048]{1,0:T(8,128)(2,1)} %layer_norm.1.refs_1_.h_ref.refs_7_, bf16[2048,2048]{1,0:T(8,128)(2,1)} %bitcast.67, bf16[352,2048]{1,0:T(8,128)(2,1)} %get-tuple-element.173.act_ref, bf16[704,2048]{1,0:T(8,128)(2,1)} %get-tuple-element.174.grad_ref), custom_call_target="tpu_custom_call" | custom-call | flops 8858370048 | bytes 25427968 | tf_op jit(solution)/shard_map/feed_grads/pallas_call | solution.py:334
  367.9 4.1 add_convert_fusion.6
  372.0 1.5 collective-permute-done.12
  373.5 1.5 collective-permute-done.13
  375.0 3.7 add_convert_fusion.2
  380.6 1.8 collective-permute-start.15
  382.4 6.8 %collective-permute-done.19 = bf16[4,512,256]{2,1,0:T(8,128)(2,1)} collective-permute-done((bf16[4,512,256]{2,1,0:T(8,128)(2,1)S(1)}, bf16[4,512,256]{2,1,0:T(8,128)(2,1)}, u32[]{:S(2)}, u32[]{:S(2)}) %collective-permute-start.19) | collective-permute-done | bytes 1048608 | tf_op jit(solution)/shard_map/ppermute | solution.py:80
  389.2 2.1 convert_add_fusion.2
  391.4 1.4 multiply_add_fusion.2
  392.8 1.5 collective-permute-start.16
  394.3 1.5 collective-permute-start.17
  395.7 3.1 multiply_add_fusion
  398.8 16.8 %collective-permute-done.16.refs_4_ = bf16[128,2048]{1,0:T(8,128)(2,1)S(1)} collective-permute-done((bf16[128,2048]{1,0:T(8,128)(2,1)S(1)}, bf16[128,2048]{1,0:T(8,128)(2,1)S(1)}, u32[]{:S(2)}, u32[]{:S(2)}) %collective-permute-start.16) | collective-permute-done | bytes 524320 | tf_op jit(solution)/shard_map/ppermute | solution.py:86
  416.5 5.5 back_rows.1
  422.0 1.5 collective-permute-start.22
  423.5 1.5 collective-permute-start.26
  425.5 4.2 add_convert_fusion
  432.3 7.0 %update_feed.2 = (f32[2,704,512]{2,1,0:T(8,128)}, f32[2,704,512]{2,1,0:T(8,128)}, f32[2,704,512]{2,1,0:T(8,128)}, f32[2,704,512]{2,1,0:T(8,128)}, f32[704,512]{1...) custom-call(bf16[3,352,512]{2,1,0:T(8,128)(2,1)} %bitcast.83, f32[2,704,512]{2,1,0:T(8,128)} %bitcast.53, ...), custom_call_target="tpu_custom_call" | custom-call | flops 5406720 | bytes 16220160 | tf_op jit(solution)/shard_map/update_feed/pallas_call | solution.py:808
  439.4 8.1 %collective-permute-done.23.refs_5_ = bf16[128,2048]{1,0:T(8,128)(2,1)S(1)} collective-permute-done((bf16[128,2048]{1,0:T(8,128)(2,1)}, bf16[128,2048]{1,0:T(8,128)(2,1)S(1)}, u32[]{:S(2)}, u32[]{:S(2)}) %collective-permute-start.23) | collective-permute-done | bytes 524320 | tf_op jit(solution)/shard_map/ppermute | solution.py:86
  448.3 1.5 collective-permute-start.28
  452.4 19.0 %collective-permute-done.21.refs_5_ = bf16[128,2048]{1,0:T(8,128)(2,1)} collective-permute-done((bf16[128,2048]{1,0:T(8,128)(2,1)}, bf16[128,2048]{1,0:T(8,128)(2,1)}, u32[]{:S(2)}, u32[]{:S(2)}) %collective-permute-start.21) | collective-permute-done | bytes 524320 | tf_op jit(solution)/shard_map/ppermute | solution.py:86
  471.4 3.7 add_rows.1
  476.4 5.2 pack_rows.2.own_ref.refs_1_
  485.9 10.7 %collective-permute-done.24.refs_1_ = bf16[128,2048]{1,0:T(8,128)(2,1)S(1)} collective-permute-done((bf16[128,2048]{1,0:T(8,128)(2,1)S(1)}, bf16[128,2048]{1,0:T(8,128)(2,1)S(1)}, u32[]{:S(2)}, u32[]{:S(2)}) %collective-permute-start.24) | collective-permute-done | bytes 524320 | tf_op jit(solution)/shard_map/ppermute | solution.py:86
  498.6 1.4 collective-permute-start.33
  500.1 1.7 tail_sums.1
  501.8 14.5 %finish_rows.2 = f32[2048,2048]{1,0:T(8,128)} custom-call(s32[4]{0:T(128)} %pad_add_fusion.info_ref, bf16[2048,2048]{1,0:T(8,128)(2,1)} %bitcast.68, bf16[1088,2048]{1,0:T(8,128)(2,1)} %pack_rows.2.own_ref.refs_1_, bf16[1088,2048]{1,0:T(8,128)(2,1)} %collective-permute-done.34.other_ref.refs_2_), custom_call_target="tpu_custom_call" | custom-call | flops 8388608 | bytes 33554432 | tf_op jit(solution)/shard_map/finish_rows/pallas_call | solution.py:767
  516.4 7.0 %update_feed.3 = (f32[2,704,512]{2,1,0:T(8,128)}, f32[2,704,512]{2,1,0:T(8,128)}, f32[2,704,512]{2,1,0:T(8,128)}, f32[2,704,512]{2,1,0:T(8,128)}, f32[704,512]{1...) custom-call(bf16[3,352,512]{2,1,0:T(8,128)(2,1)} %bitcast.82, ...), custom_call_target="tpu_custom_call", output_to_operand_aliasing={{0}: (7, {}), {1}: (8, {}), {2}: (9, {}), {3}: (10, {}), {4... | custom-call | flops 5406720 | bytes 16220160 | tf_op jit(solution)/shard_map/update_feed/pallas_call | solution.py:808
  524.4 5.1 pack_rows.3.refs_0_
  529.7 1.9 collective-permute-start.36
  531.6 2.0 collective-permute-done.36
  533.6 3.2 collective-permute-start.37
  536.8 1.8 collective-permute-done.37
  539.9 10.2 %finish_rows.3 = bf16[2048,2048]{1,0:T(8,128)(2,1)} custom-call(s32[4]{0:T(128)} %pad_add_fusion.info_ref, bf16[1024,2048]{1,0:T(8,128)(2,1)} %pack_rows.3.refs_0_, bf16[1024,2048]{1,0:T(8,128)(2,1)} %collective-permute-done.35.refs_1_), custom_call_target="tpu_custom_call" | custom-call | flops 8388608 | bytes 33554432 | tf_op jit(solution)/shard_map/finish_rows/pallas_call | solution.py:767
  (166 shorter events, 31.0 us)
Async XLA Ops:
  7.2 87.3 %all-gather.4.cloned.1.call-start = ((), (), s32[]{:S(2)}) async-start(), calls=%async_computation.2 | async-start | bytes 5242880 | tf_op jit(solution)/shard_map/all_gather | solution.py:866
  10.9 167.2 %all-gather.6.cloned.1.call-start = ((), (), s32[]{:S(2)}) async-start(), calls=%async_computation.5 | async-start | bytes 5406720 | tf_op jit(solution)/shard_map/all_gather | solution.py:868
  14.5 417.8 %reduce-scatter.3.cloned.1.call-start = ((), (), s32[]{:S(2)}) async-start(), calls=%async_computation.3 | async-start | bytes 5406720 | tf_op jit(solution)/shard_map/reduce_scatter | solution.py:918
  26.0 154.6 %copy-start.8 = (bf16[3,352,512]{2,1,0:T(8,128)(2,1)}, bf16[3,352,512]{2,1,0:T(8,128)(2,1)S(1)}, u32[]{:S(2)}) copy-start(bf16[3,352,512]{2,1,0:T(8,128)(2,1)S(1)} %pad_maximum_fusion.refs_0_) | copy-start | bytes 3244036
  178.1 33.0 %copy-start.9 = (bf16[4,512,256]{2,1,0:T(8,128)(2,1)S(1)}, bf16[4,512,256]{2,1,0:T(8,128)(2,1)}, u32[]{:S(2)}) copy-start(bf16[4,512,256]{2,1,0:T(8,128)(2,1)} %get-tuple-element.145) | copy-start | bytes 3145732
  178.1 39.0 %copy-start.10 = (bf16[4,512,256]{2,1,0:T(8,128)(2,1)S(1)}, bf16[4,512,256]{2,1,0:T(8,128)(2,1)}, u32[]{:S(2)}) copy-start(bf16[4,512,256]{2,1,0:T(8,128)(2,1)} %get-tuple-element.146) | copy-start | bytes 3145732
  178.2 24.8 %collective-permute-start = (bf16[3,352,512]{2,1,0:T(8,128)(2,1)S(1)}, bf16[3,352,512]{2,1,0:T(8,128)(2,1)}, u32[]{:S(2)}, u32[]{:S(2)}) collective-permute-start(bf16[3,352,512]{2,1,0:T(8,128)(2,1)S(1)} %pad_maximum_fusion.refs_0_), channel_id=1, source_target_pairs={{0,8},{8,16},{16,24},{1,9},{9,17},{17,25},{2,10},{10,18},{18,26},{... | collective-permute-start | bytes 3244040 | tf_op jit(solution)/shard_map/ppermute | solution.py:63
  180.6 27.6 %collective-permute-start.1 = (bf16[3,352,512]{2,1,0:T(8,128)(2,1)S(1)}, bf16[3,352,512]{2,1,0:T(8,128)(2,1)}, u32[]{:S(2)}, u32[]{:S(2)}) collective-permute-start(bf16[3,352,512]{2,1,0:T(8,128)(2,1)S(1)} %pad_maximum_fusion.refs_0_), channel_id=1, source_target_pairs={{8,0},{16,8},{24,16},{9,1},{17,9},{25,17},{10,2},{18,10},{26,18},{... | collective-permute-start | bytes 3244040 | tf_op jit(solution)/shard_map/ppermute | solution.py:64
  208.2 36.9 %collective-permute-start.2 = (bf16[3,352,512]{2,1,0:T(8,128)(2,1)}, bf16[3,352,512]{2,1,0:T(8,128)(2,1)}, u32[]{:S(2)}, u32[]{:S(2)}) collective-permute-start(bf16[3,352,512]{2,1,0:T(8,128)(2,1)} %collective-permute-done.refs_1_), channel_id=1, source_target_pairs={{8,16},{16,24},{9,17},{17,25},{10,18},{18,26},{11,19},{19,27},{12,... | collective-permute-start | bytes 3244040 | tf_op jit(solution)/shard_map/ppermute | solution.py:63
  209.8 35.3 %collective-permute-start.3 = (bf16[3,352,512]{2,1,0:T(8,128)(2,1)}, bf16[3,352,512]{2,1,0:T(8,128)(2,1)}, u32[]{:S(2)}, u32[]{:S(2)}) collective-permute-start(bf16[3,352,512]{2,1,0:T(8,128)(2,1)} %collective-permute-done.1.refs_4_), channel_id=1, source_target_pairs={{8,0},{16,8},{9,1},{17,9},{10,2},{18,10},{11,3},{19,11},{12,4},{20... | collective-permute-start | bytes 3244040 | tf_op jit(solution)/shard_map/ppermute | solution.py:64
  211.1 34.0 %collective-permute-start.4 = (bf16[4,512,256]{2,1,0:T(8,128)(2,1)S(1)}, bf16[4,512,256]{2,1,0:T(8,128)(2,1)}, u32[]{:S(2)}, u32[]{:S(2)}) collective-permute-start(bf16[4,512,256]{2,1,0:T(8,128)(2,1)S(1)} %copy-done.9), channel_id=1, source_target_pairs={{0,8},{1,9},{2,10},{3,11},{4,12},{5,13},{6,14},{7,15}} | collective-permute-start | bytes 3145736 | tf_op jit(solution)/shard_map/ppermute | solution.py:79
  217.1 28.0 %collective-permute-start.5 = (bf16[4,512,256]{2,1,0:T(8,128)(2,1)S(1)}, bf16[4,512,256]{2,1,0:T(8,128)(2,1)}, u32[]{:S(2)}, u32[]{:S(2)}) collective-permute-start(bf16[4,512,256]{2,1,0:T(8,128)(2,1)S(1)} %copy-done.10), channel_id=1, source_target_pairs={{24,16},{25,17},{26,18},{27,19},{28,20},{29,21},{30,22},{31,23}} | collective-permute-start | bytes 3145736 | tf_op jit(solution)/shard_map/ppermute | solution.py:80
  218.8 29.3 %copy-start.14 = (bf16[4,512,256]{2,1,0:T(8,128)(2,1)S(1)}, bf16[4,512,256]{2,1,0:T(8,128)(2,1)}, u32[]{:S(2)}) copy-start(bf16[4,512,256]{2,1,0:T(8,128)(2,1)} %get-tuple-element.152) | copy-start | bytes 3145732
  245.1 42.4 %collective-permute-start.6 = (bf16[3,352,512]{2,1,0:T(8,128)(2,1)}, bf16[3,352,512]{2,1,0:T(8,128)(2,1)}, u32[]{:S(2)}, u32[]{:S(2)}) collective-permute-start(bf16[3,352,512]{2,1,0:T(8,128)(2,1)} %collective-permute-done.2.refs_2_), channel_id=1, source_target_pairs={{16,24},{17,25},{18,26},{19,27},{20,28},{21,29},{22,30},{23,31}} | collective-permute-start | bytes 3244040 | tf_op jit(solution)/shard_map/ppermute | solution.py:63
  246.8 40.7 %collective-permute-start.7 = (bf16[3,352,512]{2,1,0:T(8,128)(2,1)}, bf16[3,352,512]{2,1,0:T(8,128)(2,1)}, u32[]{:S(2)}, u32[]{:S(2)}) collective-permute-start(bf16[3,352,512]{2,1,0:T(8,128)(2,1)} %collective-permute-done.3.refs_5_), channel_id=1, source_target_pairs={{8,0},{9,1},{10,2},{11,3},{12,4},{13,5},{14,6},{15,7}} | collective-permute-start | bytes 3244040 | tf_op jit(solution)/shard_map/ppermute | solution.py:64
  251.4 36.1 %collective-permute-start.8 = (bf16[4,512,256]{2,1,0:T(8,128)(2,1)}, bf16[4,512,256]{2,1,0:T(8,128)(2,1)}, u32[]{:S(2)}, u32[]{:S(2)}) collective-permute-start(bf16[4,512,256]{2,1,0:T(8,128)(2,1)} %get-tuple-element.256), channel_id=1, source_target_pairs={{0,8},{8,16},{1,9},{9,17},{2,10},{10,18},{3,11},{11,19},{4,12},{12... | collective-permute-start | bytes 3145736 | tf_op jit(solution)/shard_map/ppermute | solution.py:79
  258.0 29.5 %collective-permute-start.9 = (bf16[4,512,256]{2,1,0:T(8,128)(2,1)}, bf16[4,512,256]{2,1,0:T(8,128)(2,1)}, u32[]{:S(2)}, u32[]{:S(2)}) collective-permute-start(bf16[4,512,256]{2,1,0:T(8,128)(2,1)} %get-tuple-element.255), channel_id=1, source_target_pairs={{24,16},{16,8},{25,17},{17,9},{26,18},{18,10},{27,19},{19,11},{28,... | collective-permute-start | bytes 3145736 | tf_op jit(solution)/shard_map/ppermute | solution.py:80
  287.5 228.9 %reduce-scatter.5.cloned.1.call-start = ((), (), s32[]{:S(2)}) async-start(), calls=%async_computation.4 | async-start | bytes 5406720 | tf_op jit(solution)/shard_map/reduce_scatter | solution.py:918
  293.5 44.3 %copy-start.13 = (bf16[4,512,256]{2,1,0:T(8,128)(2,1)S(1)}, bf16[4,512,256]{2,1,0:T(8,128)(2,1)}, u32[]{:S(2)}) copy-start(bf16[4,512,256]{2,1,0:T(8,128)(2,1)} %add_convert_fusion.8) | copy-start | bytes 3145732
  293.5 45.6 %copy-start.12 = (bf16[4,512,256]{2,1,0:T(8,128)(2,1)S(1)}, bf16[4,512,256]{2,1,0:T(8,128)(2,1)}, u32[]{:S(2)}) copy-start(bf16[4,512,256]{2,1,0:T(8,128)(2,1)} %add_convert_fusion.9) | copy-start | bytes 3145732
  330.2 7.4 %collective-permute-start.10 = (bf16[1024,2048]{1,0:T(8,128)(2,1)}, bf16[1024,2048]{1,0:T(8,128)(2,1)S(1)}, u32[]{:S(2)}, u32[]{:S(2)}) collective-permute-start(bf16[1024,2048]{1,0:T(8,128)(2,1)} %get-tuple-element.168), channel_id=1, source_target_pairs={{0,1},{1,0},{2,3},{3,2},{4,5},{5,4},{6,7},{7,6},{8,9},{9,8},{10,11... | collective-permute-start | bytes 12582920 | tf_op jit(solution)/shard_map/ppermute | solution.py:86
  337.7 10.7 %copy-start.3 = (bf16[1024,2048]{1,0:T(8,128)(2,1)}, bf16[1024,2048]{1,0:T(8,128)(2,1)S(1)}, u32[]{:S(2)}) copy-start(bf16[1024,2048]{1,0:T(8,128)(2,1)S(1)} %collective-permute-done.10) | copy-start | bytes 12582916
  337.7 30.2 %collective-permute-start.11 = (bf16[1024,2048]{1,0:T(8,128)(2,1)}, bf16[1024,2048]{1,0:T(8,128)(2,1)}, u32[]{:S(2)}, u32[]{:S(2)}) collective-permute-start(bf16[1024,2048]{1,0:T(8,128)(2,1)} %get-tuple-element.169), channel_id=1, source_target_pairs={{0,1},{1,0},{2,3},{3,2},{4,5},{5,4},{6,7},{7,6},{8,9},{9,8},{10,11... | collective-permute-start | bytes 12582920 | tf_op jit(solution)/shard_map/ppermute | solution.py:86
  337.8 51.4 %collective-permute-start.19 = (bf16[4,512,256]{2,1,0:T(8,128)(2,1)S(1)}, bf16[4,512,256]{2,1,0:T(8,128)(2,1)}, u32[]{:S(2)}, u32[]{:S(2)}) collective-permute-start(bf16[4,512,256]{2,1,0:T(8,128)(2,1)S(1)} %copy-done.13), channel_id=1, source_target_pairs={{24,16},{16,8},{8,0},{25,17},{17,9},{9,1},{26,18},{18,10},{10,2},{... | collective-permute-start | bytes 3145736 | tf_op jit(solution)/shard_map/ppermute | solution.py:80
  339.1 50.1 %collective-permute-start.18 = (bf16[4,512,256]{2,1,0:T(8,128)(2,1)S(1)}, bf16[4,512,256]{2,1,0:T(8,128)(2,1)}, u32[]{:S(2)}, u32[]{:S(2)}) collective-permute-start(bf16[4,512,256]{2,1,0:T(8,128)(2,1)S(1)} %copy-done.12), channel_id=1, source_target_pairs={{0,8},{8,16},{16,24},{1,9},{9,17},{17,25},{2,10},{10,18},{18,26},{... | collective-permute-start | bytes 3145736 | tf_op jit(solution)/shard_map/ppermute | solution.py:79
  348.3 25.2 %collective-permute-start.12 = (bf16[256,2048]{1,0:T(8,128)(2,1)}, bf16[256,2048]{1,0:T(8,128)(2,1)}, u32[]{:S(2)}, u32[]{:S(2)}) collective-permute-start(bf16[256,2048]{1,0:T(8,128)(2,1)} %get-tuple-element.242), channel_id=1, source_target_pairs={{0,2},{1,3},{2,0},{3,1},{4,6},{5,7},{6,4},{7,5},{8,10},{9,11},{10,... | collective-permute-start | bytes 3145736 | tf_op jit(solution)/shard_map/ppermute | solution.py:86
  350.1 24.9 %collective-permute-start.13 = (bf16[256,2048]{1,0:T(8,128)(2,1)}, bf16[256,2048]{1,0:T(8,128)(2,1)}, u32[]{:S(2)}, u32[]{:S(2)}) collective-permute-start(bf16[256,2048]{1,0:T(8,128)(2,1)} %get-tuple-element.241), channel_id=1, source_target_pairs={{0,4},{1,5},{2,6},{3,7},{4,0},{5,1},{6,2},{7,3},{8,12},{9,13},{10,... | collective-permute-start | bytes 3145736 | tf_op jit(solution)/shard_map/ppermute | solution.py:86
  367.9 7.1 %copy-start.2 = (bf16[1024,2048]{1,0:T(8,128)(2,1)S(1)}, bf16[1024,2048]{1,0:T(8,128)(2,1)}, u32[]{:S(2)}) copy-start(bf16[1024,2048]{1,0:T(8,128)(2,1)} %get-tuple-element.170) | copy-start | bytes 12582916
  378.7 10.5 %copy-start.4 = (f32[4,512,256]{2,1,0:T(8,128)S(1)}, f32[4,512,256]{2,1,0:T(8,128)}, u32[]{:S(2)}) copy-start(f32[4,512,256]{2,1,0:T(8,128)} %get-tuple-element.141) | copy-start | bytes 6291460
  380.5 10.9 %copy-start.5 = (f32[512,256]{1,0:T(8,128)S(1)}, f32[512,256]{1,0:T(8,128)}, u32[]{:S(2)}) copy-start(f32[512,256]{1,0:T(8,128)} %param.25) | copy-start | bytes 1572868
  380.5 10.9 %copy-start.31 = (f32[512,256]{1,0:T(8,128)S(1)}, f32[512,256]{1,0:T(8,128)}, u32[]{:S(2)}) copy-start(f32[512,256]{1,0:T(8,128)} %param.37) | copy-start | bytes 1572868
  380.5 10.9 %copy-start.32 = (f32[512,256]{1,0:T(8,128)S(1)}, f32[512,256]{1,0:T(8,128)}, u32[]{:S(2)}) copy-start(f32[512,256]{1,0:T(8,128)} %param.31) | copy-start | bytes 1572868
  380.5 45.1 %collective-permute-start.14 = (bf16[256,2048]{1,0:T(8,128)(2,1)}, bf16[256,2048]{1,0:T(8,128)(2,1)}, u32[]{:S(2)}, u32[]{:S(2)}) collective-permute-start(bf16[256,2048]{1,0:T(8,128)(2,1)} %get-tuple-element.177), channel_id=1, source_target_pairs={{0,2},{1,3},{2,0},{3,1},{4,6},{5,7},{6,4},{7,5},{8,10},{9,11},{10,... | collective-permute-start | bytes 3145736 | tf_op jit(solution)/shard_map/ppermute | solution.py:86
  380.6 44.9 %collective-permute-start.15 = (bf16[256,2048]{1,0:T(8,128)(2,1)S(1)}, bf16[256,2048]{1,0:T(8,128)(2,1)}, u32[]{:S(2)}, u32[]{:S(2)}) collective-permute-start(bf16[256,2048]{1,0:T(8,128)(2,1)S(1)} %get-tuple-element.178), channel_id=1, source_target_pairs={{0,4},{1,5},{2,6},{3,7},{4,0},{5,1},{6,2},{7,3},{8,12},{9,13},{10,... | collective-permute-start | bytes 3145736 | tf_op jit(solution)/shard_map/ppermute | solution.py:86
  392.8 22.8 %collective-permute-start.16 = (bf16[128,2048]{1,0:T(8,128)(2,1)S(1)}, bf16[128,2048]{1,0:T(8,128)(2,1)S(1)}, u32[]{:S(2)}, u32[]{:S(2)}) collective-permute-start(bf16[128,2048]{1,0:T(8,128)(2,1)S(1)} %get-tuple-element.254), channel_id=1, source_target_pairs={{0,4},{1,5},{2,6},{3,7},{4,0},{5,1},{6,2},{7,3},{8,12},{9,13},{10,... | collective-permute-start | bytes 1572872 | tf_op jit(solution)/shard_map/ppermute | solution.py:86
  394.3 21.3 %collective-permute-start.17 = (bf16[128,2048]{1,0:T(8,128)(2,1)S(1)}, bf16[128,2048]{1,0:T(8,128)(2,1)S(1)}, u32[]{:S(2)}, u32[]{:S(2)}) collective-permute-start(bf16[128,2048]{1,0:T(8,128)(2,1)S(1)} %get-tuple-element.252), channel_id=1, source_target_pairs={{0,2},{1,3},{2,0},{3,1},{4,6},{5,7},{6,4},{7,5},{8,10},{9,11},{10,... | collective-permute-start | bytes 1572872 | tf_op jit(solution)/shard_map/ppermute | solution.py:86
  422.0 25.5 %collective-permute-start.22 = (bf16[144,2048]{1,0:T(8,128)(2,1)}, bf16[144,2048]{1,0:T(8,128)(2,1)S(1)}, u32[]{:S(2)}, u32[]{:S(2)}) collective-permute-start(bf16[144,2048]{1,0:T(8,128)(2,1)} %get-tuple-element.181.refs_0_), channel_id=1, source_target_pairs={{0,4},{1,5},{2,6},{3,7},{4,0},{5,1},{6,2},{7,3},{8,12},{9,13},{10,... | collective-permute-start | bytes 1769480 | tf_op jit(solution)/shard_map/ppermute | solution.py:86
  423.5 51.6 %collective-permute-start.26 = (bf16[144,2048]{1,0:T(8,128)(2,1)}, bf16[144,2048]{1,0:T(8,128)(2,1)S(1)}, u32[]{:S(2)}, u32[]{:S(2)}) collective-permute-start(bf16[144,2048]{1,0:T(8,128)(2,1)} %get-tuple-element.181.refs_0_), channel_id=1, source_target_pairs={{0,2},{1,3},{2,0},{3,1},{4,6},{5,7},{6,4},{7,5},{8,10},{9,11},{10,... | collective-permute-start | bytes 1769480 | tf_op jit(solution)/shard_map/ppermute | solution.py:86
  425.0 22.5 %collective-permute-start.23 = (bf16[128,2048]{1,0:T(8,128)(2,1)}, bf16[128,2048]{1,0:T(8,128)(2,1)S(1)}, u32[]{:S(2)}, u32[]{:S(2)}) collective-permute-start(bf16[128,2048]{1,0:T(8,128)(2,1)} %get-tuple-element.182.refs_4_), channel_id=1, source_target_pairs={{0,2},{1,3},{2,0},{3,1},{4,6},{5,7},{6,4},{7,5},{8,10},{9,11},{10,... | collective-permute-start | bytes 1572872 | tf_op jit(solution)/shard_map/ppermute | solution.py:86
  430.7 20.5 %collective-permute-start.20 = (bf16[128,2048]{1,0:T(8,128)(2,1)S(1)}, bf16[128,2048]{1,0:T(8,128)(2,1)S(1)}, u32[]{:S(2)}, u32[]{:S(2)}) collective-permute-start(bf16[128,2048]{1,0:T(8,128)(2,1)S(1)} %get-tuple-element.249), channel_id=1, source_target_pairs={{0,4},{1,5},{2,6},{3,7},{4,0},{5,1},{6,2},{7,3},{8,12},{9,13},{10,... | collective-permute-start | bytes 1572872 | tf_op jit(solution)/shard_map/ppermute | solution.py:86
  432.3 18.0 %copy-start.18 = (bf16[128,2048]{1,0:T(8,128)(2,1)S(1)}, bf16[128,2048]{1,0:T(8,128)(2,1)}, u32[]{:S(2)}) copy-start(bf16[128,2048]{1,0:T(8,128)(2,1)} %get-tuple-element.182.refs_4_) | copy-start | bytes 1572868
  447.5 27.6 %copy-start.15 = (bf16[144,2048]{1,0:T(8,128)(2,1)}, bf16[144,2048]{1,0:T(8,128)(2,1)S(1)}, u32[]{:S(2)}) copy-start(bf16[144,2048]{1,0:T(8,128)(2,1)S(1)} %collective-permute-done.22.refs_1_) | copy-start | bytes 1769476
  448.3 26.8 %collective-permute-start.28 = (bf16[144,2048]{1,0:T(8,128)(2,1)S(1)}, bf16[144,2048]{1,0:T(8,128)(2,1)S(1)}, u32[]{:S(2)}, u32[]{:S(2)}) collective-permute-start(bf16[144,2048]{1,0:T(8,128)(2,1)S(1)} %collective-permute-done.22.refs_1_), channel_id=1, source_target_pairs={{0,2},{1,3},{2,0},{3,1},{4,6},{5,7},{6,4},{7,5},{8,10},{9,11},{10,... | collective-permute-start | bytes 1769480 | tf_op jit(solution)/shard_map/ppermute | solution.py:86
  449.8 21.6 %collective-permute-start.21 = (bf16[128,2048]{1,0:T(8,128)(2,1)}, bf16[128,2048]{1,0:T(8,128)(2,1)}, u32[]{:S(2)}, u32[]{:S(2)}) collective-permute-start(bf16[128,2048]{1,0:T(8,128)(2,1)} %get-tuple-element.247), channel_id=1, source_target_pairs={{0,2},{1,3},{2,0},{3,1},{4,6},{5,7},{6,4},{7,5},{8,10},{9,11},{10,... | collective-permute-start | bytes 1572872 | tf_op jit(solution)/shard_map/ppermute | solution.py:86
  450.4 24.7 %collective-permute-start.27 = (bf16[128,2048]{1,0:T(8,128)(2,1)S(1)}, bf16[128,2048]{1,0:T(8,128)(2,1)S(1)}, u32[]{:S(2)}, u32[]{:S(2)}) collective-permute-start(bf16[128,2048]{1,0:T(8,128)(2,1)S(1)} %copy-done.18), channel_id=1, source_target_pairs={{0,4},{1,5},{2,6},{3,7},{4,0},{5,1},{6,2},{7,3},{8,12},{9,13},{10,... | collective-permute-start | bytes 1572872 | tf_op jit(solution)/shard_map/ppermute | solution.py:86
  451.2 20.3 %copy-start.26 = (bf16[128,2048]{1,0:T(8,128)(2,1)}, bf16[128,2048]{1,0:T(8,128)(2,1)S(1)}, u32[]{:S(2)}) copy-start(bf16[128,2048]{1,0:T(8,128)(2,1)S(1)} %collective-permute-done.20.refs_4_) | copy-start | bytes 1572868
  451.2 24.0 %collective-permute-start.29 = (bf16[128,2048]{1,0:T(8,128)(2,1)}, bf16[128,2048]{1,0:T(8,128)(2,1)S(1)}, u32[]{:S(2)}, u32[]{:S(2)}) collective-permute-start(bf16[128,2048]{1,0:T(8,128)(2,1)} %copy-done.21), channel_id=1, source_target_pairs={{0,4},{1,5},{2,6},{3,7},{4,0},{5,1},{6,2},{7,3},{8,12},{9,13},{10,... | collective-permute-start | bytes 1572872 | tf_op jit(solution)/shard_map/ppermute | solution.py:86
  481.7 18.4 %collective-permute-start.34 = (bf16[1088,2048]{1,0:T(8,128)(2,1)}, bf16[1088,2048]{1,0:T(8,128)(2,1)}, u32[]{:S(2)}, u32[]{:S(2)}) collective-permute-start(bf16[1088,2048]{1,0:T(8,128)(2,1)} %pack_rows.2.own_ref.refs_1_), channel_id=1, source_target_pairs={{0,1},{1,0},{2,3},{3,2},{4,5},{5,4},{6,7},{7,6},{8,9},{9,8},{10,11... | collective-permute-start | bytes 13369352 | tf_op jit(solution)/shard_map/ppermute | solution.py:86
  481.8 14.8 %collective-permute-start.24 = (bf16[128,2048]{1,0:T(8,128)(2,1)S(1)}, bf16[128,2048]{1,0:T(8,128)(2,1)S(1)}, u32[]{:S(2)}, u32[]{:S(2)}) collective-permute-start(bf16[128,2048]{1,0:T(8,128)(2,1)S(1)} %copy-done.19), channel_id=1, source_target_pairs={{0,4},{1,5},{2,6},{3,7},{4,0},{5,1},{6,2},{7,3},{8,12},{9,13},{10,... | collective-permute-start | bytes 1572872 | tf_op jit(solution)/shard_map/ppermute | solution.py:86
  482.8 14.8 %collective-permute-start.25 = (bf16[128,2048]{1,0:T(8,128)(2,1)S(1)}, bf16[128,2048]{1,0:T(8,128)(2,1)S(1)}, u32[]{:S(2)}, u32[]{:S(2)}) collective-permute-start(bf16[128,2048]{1,0:T(8,128)(2,1)S(1)} %copy-done.20), channel_id=1, source_target_pairs={{0,2},{1,3},{2,0},{3,1},{4,6},{5,7},{6,4},{7,5},{8,10},{9,11},{10,... | collective-permute-start | bytes 1572872 | tf_op jit(solution)/shard_map/ppermute | solution.py:86
  483.9 39.5 %collective-permute-start.30 = (bf16[128,2048]{1,0:T(8,128)(2,1)S(1)}, bf16[128,2048]{1,0:T(8,128)(2,1)S(1)}, u32[]{:S(2)}, u32[]{:S(2)}) collective-permute-start(bf16[128,2048]{1,0:T(8,128)(2,1)S(1)} %copy-done.19), channel_id=1, source_target_pairs={{0,2},{1,3},{2,0},{3,1},{4,6},{5,7},{6,4},{7,5},{8,10},{9,11},{10,... | collective-permute-start | bytes 1572872 | tf_op jit(solution)/shard_map/ppermute | solution.py:86
  484.9 38.5 %collective-permute-start.31 = (bf16[128,2048]{1,0:T(8,128)(2,1)S(1)}, bf16[128,2048]{1,0:T(8,128)(2,1)S(1)}, u32[]{:S(2)}, u32[]{:S(2)}) collective-permute-start(bf16[128,2048]{1,0:T(8,128)(2,1)S(1)} %copy-done.20), channel_id=1, source_target_pairs={{0,4},{1,5},{2,6},{3,7},{4,0},{5,1},{6,2},{7,3},{8,12},{9,13},{10,... | collective-permute-start | bytes 1572872 | tf_op jit(solution)/shard_map/ppermute | solution.py:86
  497.6 25.8 %collective-permute-start.32 = (bf16[128,2048]{1,0:T(8,128)(2,1)S(1)}, bf16[128,2048]{1,0:T(8,128)(2,1)}, u32[]{:S(2)}, u32[]{:S(2)}) collective-permute-start(bf16[128,2048]{1,0:T(8,128)(2,1)S(1)} %collective-permute-done.24.refs_1_), channel_id=1, source_target_pairs={{0,2},{1,3},{2,0},{3,1},{4,6},{5,7},{6,4},{7,5},{8,10},{9,11},{10,... | collective-permute-start | bytes 1572872 | tf_op jit(solution)/shard_map/ppermute | solution.py:86
  498.6 24.8 %collective-permute-start.33 = (bf16[128,2048]{1,0:T(8,128)(2,1)S(1)}, bf16[128,2048]{1,0:T(8,128)(2,1)}, u32[]{:S(2)}, u32[]{:S(2)}) collective-permute-start(bf16[128,2048]{1,0:T(8,128)(2,1)S(1)} %collective-permute-done.25.refs_5_), channel_id=1, source_target_pairs={{0,4},{1,5},{2,6},{3,7},{4,0},{5,1},{6,2},{7,3},{8,12},{9,13},{10,... | collective-permute-start | bytes 1572872 | tf_op jit(solution)/shard_map/ppermute | solution.py:86
  524.4 14.3 %copy-start.40 = (f32[3,256]{1,0:T(4,128)S(1)}, f32[3,256]{1,0:T(4,128)}, u32[]{:S(2)}) copy-start(f32[3,256]{1,0:T(4,128)} %refs_5_.1) | copy-start | bytes 9220
  524.4 14.3 %copy-start.41 = (f32[3,256]{1,0:T(4,128)S(1)}, f32[3,256]{1,0:T(4,128)}, u32[]{:S(2)}) copy-start(f32[3,256]{1,0:T(4,128)} %param.41) | copy-start | bytes 9220
  524.4 14.3 %copy-start.42 = (f32[3,256]{1,0:T(4,128)S(1)}, f32[3,256]{1,0:T(4,128)}, u32[]{:S(2)}) copy-start(f32[3,256]{1,0:T(4,128)} %param.35) | copy-start | bytes 9220
  524.4 14.9 %copy-start.33 = (f32[2,2048]{1,0:T(2,128)S(1)}, f32[2,2048]{1,0:T(2,128)}, u32[]{:S(2)}) copy-start(f32[2,2048]{1,0:T(2,128)} %refs_6_.1) | copy-start | bytes 49156
  524.4 14.9 %copy-start.36 = (f32[2,2048]{1,0:T(2,128)S(1)}, f32[2,2048]{1,0:T(2,128)}, u32[]{:S(2)}) copy-start(f32[2,2048]{1,0:T(2,128)} %param.40) | copy-start | bytes 49156
  524.4 14.9 %copy-start.37 = (f32[2,2048]{1,0:T(2,128)S(1)}, f32[2,2048]{1,0:T(2,128)}, u32[]{:S(2)}) copy-start(f32[2,2048]{1,0:T(2,128)} %param.34) | copy-start | bytes 49156
  529.5 10.4 %collective-permute-start.35 = (bf16[1024,2048]{1,0:T(8,128)(2,1)}, bf16[1024,2048]{1,0:T(8,128)(2,1)}, u32[]{:S(2)}, u32[]{:S(2)}) collective-permute-start(bf16[1024,2048]{1,0:T(8,128)(2,1)} %pack_rows.3.refs_0_), channel_id=1, source_target_pairs={{0,1},{1,0},{2,3},{3,2},{4,5},{5,4},{6,7},{7,6},{8,9},{9,8},{10,11... | collective-permute-start | bytes 12582920 | tf_op jit(solution)/shard_map/ppermute | solution.py:86
  529.7 3.9 collective-permute-start.36
  533.6 5.0 collective-permute-start.37
  538.6 11.4 %copy-start.35 = (f32[2,2048]{1,0:T(2,128)}, f32[2,2048]{1,0:T(2,128)S(1)}, u32[]{:S(2)}) copy-start(f32[2,2048]{1,0:T(2,128)S(1)} %reshape.139) | copy-start | bytes 49156
  (21 other events, 60.1 us)
Sparse Core Ops, SparseCore 0:
  11.0 83.4 all-gather.3
  96.7 81.4 all-gather.5
  287.6 100.2 reduce-scatter.2
  390.0 81.8 reduce-scatter.4

commit v3 on v2

--- a/solution.py
+++ b/solution.py
@@ -58,11 +58,14 @@
     return lax.optimization_barrier((value, others))[0]
 
 
-def gather_hop(k, right, left):
+def gather_hop(k, right, left, me):
     n = lax.axis_size("dp")
-    right = lax.ppermute(right, "dp", [(a, a + 1) for a in range(k - 1, n - 1)])
-    left = lax.ppermute(left, "dp", [(a, a - 1) for a in range(1, n - k + 1)])
-    return right, left
+    to_right = [(a, a + 1) for a in range(k - 1, n - 1)]
+    to_left = [(a, a - 1) for a in range(1, n - k + 1)]
+    if k == n - 1 and n != 3:
+        both = lax.ppermute(jnp.where(me == 1, left, right), "dp", to_right + to_left)
+        return both, both
+    return lax.ppermute(right, "dp", to_right), lax.ppermute(left, "dp", to_left)
 
 
 def scatter_load(k, slots, right, left):
@@ -76,9 +79,12 @@
 
 def scatter_hop(k, to_right, to_left):
     n = lax.axis_size("dp")
-    right = lax.ppermute(to_right, "dp", [(a, a + 1) for a in range(k)])
-    left = lax.ppermute(to_left, "dp", [(a, a - 1) for a in range(n - 1, n - 1 - k, -1)])
-    return right, left
+    rights = [(a, a + 1) for a in range(k)]
+    lefts = [(a, a - 1) for a in range(n - 1, n - 1 - k, -1)]
+    if k == 1 and n != 3:
+        both = lax.ppermute(to_right, "dp", rights + lefts)
+        return both, both
+    return lax.ppermute(to_right, "dp", rights), lax.ppermute(to_left, "dp", lefts)
 
 
 def swap(value, mask, axis="mp"):
@@ -156,16 +162,27 @@
             run(pieces[n - 1 + k], me + k, sems.at[n - 1 + k])
 
 
+def swish_of(both):
+    units = both.shape[0] // 2
+    gate, upper = both[:units], both[units:]
+    sigmoid = jax.nn.sigmoid(gate)
+    return gate, upper, sigmoid, gate * sigmoid
+
+
+def join_gates(w_ref):
+    return w_ref[0:2].reshape(2 * w_ref.shape[1], w_ref.shape[2])
+
+
+def gates_grad_of(both, active_grad):
+    gate, upper, sigmoid, swish = swish_of(both)
+    gate_grad = active_grad * upper * sigmoid * (1.0 + gate * (1.0 - sigmoid))
+    return jnp.concatenate([gate_grad, active_grad * swish], axis=0).astype(low)
+
+
 def gates_of(w_ref, h, c):
-    units = w_ref.shape[1]
-    both = dot_nt(w_ref[0:2].reshape(2 * units, w_ref.shape[2]), h)
-    gate, upper = both[:units], both[units:]
-    active_grad = dot_nt(w_ref[2], c)
-    sigmoid = jax.nn.sigmoid(gate)
-    swish = gate * sigmoid
-    active = (swish * upper).astype(low)
-    gate_grad = active_grad * upper * sigmoid * (1.0 + gate * (1.0 - sigmoid))
-    return active, jnp.concatenate([gate_grad, active_grad * swish], axis=0).astype(low)
+    both = dot_nt(join_gates(w_ref), h)
+    _, upper, _, swish = swish_of(both)
+    return (swish * upper).astype(low), gates_grad_of(both, dot_nt(w_ref[2], c))
 
 
 def add_grads(acc, step, active, gates_grad, h, c):
@@ -237,82 +254,118 @@
     )(me, *pieces, hidden, cot)
 
 
-def last_kernel(n, count, split, info_ref, *refs):
-    pieces = refs[:count]
-    h_ref, c_ref, hid_ref, out_ref = refs[count : count + 4]
-    w_ref, sems = refs[-2:]
-    act_ref, grad_ref = refs[-4:-2]
-    parts = refs[count + 4 : -4]
-    target_of = wide_target(w_ref, w_ref.shape[2] // n)
+def put_part(split, info_ref, parts, value):
+    if not split:
+        parts[0][...] = value
+        return
     step = pl.program_id(0)
-
-    @pl.when(step == 0)
-    def _():
-        fetch(n, info_ref[3], pieces, target_of, sems, "start")
-        fetch(n, info_ref[3], pieces, target_of, sems, "wait")
-
-    active, gates_grad = gates_of(w_ref, h_ref[...], c_ref[...])
-    act_ref[...] = active
-    grad_ref[...] = gates_grad
-    joined = w_ref[0:2].reshape(gates_grad.shape[0], w_ref.shape[2])
-    hid = (hid_ref[...].astype(full) + dot_tn(gates_grad, joined)).astype(low)
-    out = (out_ref[...].astype(full) + dot_tn(active, w_ref[2])).astype(low)
-    if not split:
-        parts[0][...] = hid
-        parts[1][...] = out
-        return
-    sub = hid.shape[0] // 4
+    sub = value.shape[0] // 4
     high = jnp.where(step % 2 == 0, info_ref[1], info_ref[2])
     small = jnp.where(step % 2 == 0, info_ref[2], info_ref[1])
     for half in range(2):
 
         @pl.when(step // 2 == half)
         def _(half=half):
-            for ref, value in ((parts[2 * half], hid), (parts[2 * half + 1], out)):
-                for i in range(4):
-                    at = ((i // 2) ^ high) * 2 + ((i % 2) ^ small)
-                    place = pl.ds(pl.multiple_of(at * sub, sub), sub)
-                    ref[place, :] = value[i * sub : (i + 1) * sub]
-
-
-def feed_last(n, info, split, pieces, hidden, cot, hid_early, out_early):
-    rows, width = hidden.shape
-    units = pieces[0].shape[-2]
-    count = len(pieces)
+            for i in range(4):
+                at = ((i // 2) ^ high) * 2 + ((i % 2) ^ small)
+                place = pl.ds(pl.multiple_of(at * sub, sub), sub)
+                parts[half][place, :] = value[i * sub : (i + 1) * sub]
+
+
+def last_blocks(split, rows, width):
     if split:
         block, steps = rows // 4, 4
         place = lambda i, m: (m[0] ^ (1 - i // 2)) * 2 + i % 2
-        part_specs = [pl.BlockSpec((block, width), lambda i, m: (jnp.minimum(i, 1), 0))] * 2
-        part_specs += [pl.BlockSpec((block, width), lambda i, m: (jnp.maximum(i, 2) - 2, 0))] * 2
-        part_shapes = [shape((rows // 2, width), low)] * 4
+        part_specs = [
+            pl.BlockSpec((block, width), lambda i, m: (jnp.minimum(i, 1), 0)),
+            pl.BlockSpec((block, width), lambda i, m: (jnp.maximum(i, 2) - 2, 0)),
+        ]
+        part_shapes = [shape((rows // 2, width), low)] * 2
     else:
         block = min(256, rows)
         steps = rows // block
         place = lambda i, m: i
-        part_specs = [pl.BlockSpec((block, width), lambda i, m: (i, 0))] * 2
-        part_shapes = [shape((rows, width), low)] * 2
+        part_specs = [pl.BlockSpec((block, width), lambda i, m: (i, 0))]
+        part_shapes = [shape((rows, width), low)]
+    return block, steps, place, part_specs, part_shapes
+
+
+def out_last_kernel(n, count, split, info_ref, *refs):
+    pieces = refs[:count]
+    h_ref, early_ref = refs[count : count + 2]
+    parts = refs[count + 2 : -4]
+    act_ref, both_ref, w_ref, sems = refs[-4:]
+    target_of = wide_target(w_ref, w_ref.shape[2] // n)
+
+    @pl.when(pl.program_id(0) == 0)
+    def _():
+        fetch(n, info_ref[3], pieces, target_of, sems, "start")
+        fetch(n, info_ref[3], pieces, target_of, sems, "wait")
+
+    both = dot_nt(join_gates(w_ref), h_ref[...])
+    both_ref[...] = both
+    _, upper, _, swish = swish_of(both)
+    active = (swish * upper).astype(low)
+    act_ref[...] = active
+    put_part(split, info_ref, parts, (early_ref[...].astype(full) + dot_tn(active, w_ref[2])).astype(low))
+
+
+def out_last(n, info, split, pieces, hidden, early):
+    rows, width = hidden.shape
+    units = pieces[0].shape[-2]
+    count = len(pieces)
+    block, steps, place, part_specs, part_shapes = last_blocks(split, rows, width)
     row_spec = pl.BlockSpec((block, width), lambda i, m: (place(i, m), 0))
     return pl.pallas_call(
-        functools.partial(last_kernel, n, count, split),
+        functools.partial(out_last_kernel, n, count, split),
         grid_spec=pltpu.PrefetchScalarGridSpec(
             num_scalar_prefetch=1,
             grid=(steps,),
-            in_specs=[pl.BlockSpec(memory_space=pl.ANY)] * count + [row_spec] * 4,
+            in_specs=[pl.BlockSpec(memory_space=pl.ANY)] * count + [row_spec] * 2,
             out_specs=part_specs
             + [
                 pl.BlockSpec((units, block), lambda i, m: (0, place(i, m))),
                 pl.BlockSpec((2 * units, block), lambda i, m: (0, place(i, m))),
+                pl.BlockSpec((3, units, width), lambda i, m: (0, 0, 0)),
             ],
-            scratch_shapes=[
-                pltpu.VMEM((3, units, width), low),
-                pltpu.SemaphoreType.DMA((2 * n - 1,)),
-            ],
+            scratch_shapes=[pltpu.SemaphoreType.DMA((2 * n - 1,))],
         ),
-        out_shape=part_shapes + [shape((units, rows), low), shape((2 * units, rows), low)],
-        compiler_params=params(),
-        cost_estimate=cost(12 * rows * width * units, 12 * rows * width, rows * units),
-        name="feed_last",
-    )(info, *pieces, hidden, cot, hid_early, out_early)
+        out_shape=part_shapes
+        + [shape((units, rows), low), shape((2 * units, rows), full), shape((3, units, width), low)],
+        compiler_params=params(),
+        cost_estimate=cost(6 * rows * width * units, 8 * rows * width, rows * units),
+        name="out_last",
+    )(info, *pieces, hidden, early)
+
+
+def hid_last_kernel(split, info_ref, w_ref, both_ref, c_ref, early_ref, *refs):
+    grad_ref = refs[-1]
+    gates_grad = gates_grad_of(both_ref[...], dot_nt(w_ref[2], c_ref[...]))
+    grad_ref[...] = gates_grad
+    hid = early_ref[...].astype(full) + dot_tn(gates_grad, join_gates(w_ref))
+    put_part(split, info_ref, refs[:-1], hid.astype(low))
+
+
+def hid_last(info, split, weights, both, cot, early):
+    rows, width = cot.shape
+    units = weights.shape[1]
+    block, steps, place, part_specs, part_shapes = last_blocks(split, rows, width)
+    row_spec = pl.BlockSpec((block, width), lambda i, m: (place(i, m), 0))
+    both_spec = pl.BlockSpec((2 * units, block), lambda i, m: (0, place(i, m)))
+    return pl.pallas_call(
+        functools.partial(hid_last_kernel, split),
+        grid_spec=pltpu.PrefetchScalarGridSpec(
+            num_scalar_prefetch=1,
+            grid=(steps,),
+            in_specs=[pl.BlockSpec((3, units, width), lambda i, m: (0, 0, 0)), both_spec]
+            + [row_spec] * 2,
+            out_specs=part_specs + [both_spec],
+        ),
+        out_shape=part_shapes + [shape((2 * units, rows), low)],
+        compiler_params=params(),
+        cost_estimate=cost(6 * rows * width * units, 8 * rows * width, rows * units),
+        name="hid_last",
+    )(info, weights, both, cot, early)
 
 
 def feed_grads_kernel(n, steps, h_ref, c_ref, act_ref, grad_ref, out_ref, acc):
@@ -499,7 +552,7 @@
 
 def attend_grads_kernel(n, me_ref, h_ref, c_ref, mg_ref, ctx_ref, *refs):
     own_ref, *slot_refs = refs[:n]
-    wide = refs[n]
+    edge_ref, wide = refs[n:]
     step = pl.program_id(0)
     cols = ctx_ref.shape[1]
 
@@ -520,6 +573,11 @@
                     own_ref[part] = grads[part]
                 else:
                     slot_refs[j - 1][part] = grads[part].astype(low)
+
+    @pl.when(lax.rem(me_ref[0] + step, n) == n - 1 - me_ref[0])
+    def _():
+        for part in range(4):
+            edge_ref[part] = grads[part].astype(low)
 
 
 def attend_grads(n, me, hidden, cot, mixed_grad, context):
@@ -539,48 +597,71 @@
                 pl.BlockSpec((3, rows, cols), lambda i, m: (0, 0, 0)),
                 pl.BlockSpec((rows, cols), lambda i, m: (0, 0)),
             ],
-            out_specs=[whole3] * n,
+            out_specs=[whole3] * (n + 1),
             scratch_shapes=[pltpu.VMEM((rows, 3 * cols), low)],
         ),
-        out_shape=[shape((4, piece, cols), full)] + [shape((4, piece, cols), low)] * (n - 1),
+        out_shape=[shape((4, piece, cols), full)] + [shape((4, piece, cols), low)] * n,
         compiler_params=params(),
         cost_estimate=cost(8 * rows * width * cols, 4 * rows * width + 16 * width * cols),
         name="attend_grads",
     )(me, hidden, cot, mixed_grad, context)
 
 
-def early_kernel(ctx_ref, mg_ref, act_ref, grad_ref, wa_ref, wf_ref, hid_ref, out_ref):
+def heads_kernel(ctx_ref, mg_ref, wa_ref, hid_ref, out_ref):
     hid = dot_nt(mg_ref[0], wa_ref[0]) + dot_nt(mg_ref[1], wa_ref[1]) + dot_nt(mg_ref[2], wa_ref[2])
-    hid += dot_tn(grad_ref[...], wf_ref[0:2].reshape(grad_ref.shape[0], wf_ref.shape[2]))
     hid_ref[...] = hid.astype(low)
-    out_ref[...] = (dot_nt(ctx_ref[...], wa_ref[3]) + dot_tn(act_ref[...], wf_ref[2])).astype(low)
-
-
-def early_parts(context, mixed_grad, active, gates_grad, w_attend, w_feed):
+    out_ref[...] = dot_nt(ctx_ref[...], wa_ref[3]).astype(low)
+
+
+def heads_parts(context, mixed_grad, w_attend):
     rows, cols = context.shape
-    units, width = w_feed.shape[1:]
+    width = w_attend.shape[1]
     block = min(256, rows)
     out_spec = pl.BlockSpec((block, width), lambda i: (i, 0))
     return pl.pallas_call(
-        early_kernel,
+        heads_kernel,
         grid=(rows // block,),
         in_specs=[
             pl.BlockSpec((block, cols), lambda i: (i, 0)),
             pl.BlockSpec((3, block, cols), lambda i: (0, i, 0)),
-            pl.BlockSpec((units, block), lambda i: (0, i)),
-            pl.BlockSpec((2 * units, block), lambda i: (0, i)),
             pl.BlockSpec((4, width, cols), lambda i: (0, 0, 0)),
-            pl.BlockSpec((3, units, width), lambda i: (0, 0, 0)),
         ],
         out_specs=[out_spec, out_spec],
         out_shape=[shape((rows, width), low)] * 2,
         compiler_params=params(),
-        cost_estimate=cost(
-            2 * rows * width * (4 * cols + 3 * units),
-            4 * rows * width + 2 * (rows + width) * (4 * cols + 3 * units),
-        ),
+        cost_estimate=cost(8 * rows * width * cols, 4 * rows * width + 8 * (rows + width) * cols),
+        name="heads_parts",
+    )(context, mixed_grad, w_attend)
+
+
+def early_kernel(act_ref, grad_ref, w_ref, hid_in_ref, out_in_ref, hid_ref, out_ref):
+    hid = hid_in_ref[...].astype(full) + dot_tn(grad_ref[...], join_gates(w_ref))
+    hid_ref[...] = hid.astype(low)
+    out = out_in_ref[...].astype(full) + dot_tn(act_ref[...], w_ref[2])
+    out_ref[...] = out.astype(low)
+
+
+def early_parts(active, gates_grad, w_feed, hid, out):
+    rows, width = hid.shape
+    units = w_feed.shape[1]
+    block = min(256, rows)
+    row_spec = pl.BlockSpec((block, width), lambda i: (i, 0))
+    return pl.pallas_call(
+        early_kernel,
+        grid=(rows // block,),
+        in_specs=[
+            pl.BlockSpec((units, block), lambda i: (0, i)),
+            pl.BlockSpec((2 * units, block), lambda i: (0, i)),
+            pl.BlockSpec((3, units, width), lambda i: (0, 0, 0)),
+            row_spec,
+            row_spec,
+        ],
+        out_specs=[row_spec, row_spec],
+        out_shape=[shape((rows, width), low)] * 2,
+        compiler_params=params(),
+        cost_estimate=cost(6 * rows * width * units, 8 * rows * width + 6 * (rows + width) * units),
         name="early_parts",
-    )(context, mixed_grad, active, gates_grad, w_attend, w_feed)
+    )(active, gates_grad, w_feed, hid, out)
 
 
 def sixteenth(which, m):
@@ -741,46 +822,38 @@
 
 
 def finish_kernel(info_ref, *refs):
-    own_ref, other_ref, out_ref = refs[-3:]
-    mine = (pl.program_id(0) // 4) == info_ref[0]
-
-    def store(value):
-        if len(refs) == 4:
-            value = refs[0][...].astype(full) + value.astype(full)
-        out_ref[...] = value
-
-    @pl.when(mine)
-    def _():
-        store(own_ref[...])
-
-    @pl.when(jnp.logical_not(mine))
-    def _():
-        store(other_ref[...])
-
-
-def finish_rows(info, rows, own, other, cot=None):
-    width = own.shape[1]
-    extra = () if cot is None else (cot,)
+    out_ref = refs[-1]
+    value = refs[0][...]
+    if len(refs) > 2 and refs[1].shape == out_ref.shape:
+        value = refs[1][...].astype(full) + value.astype(full)
+    out_ref[...] = value
+
+
+def finish_rows(info, rows, half, part, cot=None, begun=None):
+    width = part.shape[1]
     block = rows // 8
-    spec = pl.BlockSpec((block, width), lambda i, m: (i, 0))
-    edge = lambda i: jnp.where(i < 4, 0, 3)
+    place = lambda i, m: ((m[0] ^ half) * 4 + i, 0)
+    ins, specs = [part], [pl.BlockSpec((block, width), lambda i, m: (i, 0))]
+    if cot is not None:
+        ins.append(cot)
+        specs.append(pl.BlockSpec((block, width), place))
+    if begun is not None:
+        ins.append(begun)
+        specs.append(pl.BlockSpec(memory_space=pl.ANY))
     return pl.pallas_call(
         finish_kernel,
         grid_spec=pltpu.PrefetchScalarGridSpec(
             num_scalar_prefetch=1,
-            grid=(8,),
-            in_specs=[spec] * len(extra)
-            + [
-                pl.BlockSpec((block, width), lambda i, m: (jnp.where(i // 4 == m[0], i % 4, edge(i)), 0)),
-                pl.BlockSpec((block, width), lambda i, m: (jnp.where(i // 4 == m[0], edge(i), i % 4), 0)),
-            ],
-            out_specs=spec,
+            grid=(4,),
+            in_specs=specs,
+            out_specs=pl.BlockSpec((block, width), place),
         ),
         out_shape=shape((rows, width), low if cot is None else full),
-        compiler_params=params(),
-        cost_estimate=cost(2 * rows * width, 8 * rows * width),
+        input_output_aliases={} if begun is None else {len(ins): 0},
+        compiler_params=params(),
+        cost_estimate=cost(rows * width, 4 * rows * width),
         name="finish_rows",
-    )(info, *extra, own, other)
+    )(info, *ins)
 
 
 def update_kernel(rates, count, *refs):
@@ -880,61 +953,60 @@
 
     q, k, v, o, w_attend = project(n, me, attend_pieces, hidden, cot, cosine, sine, attend_bias)
     context, mixed_grad, bias_part = attend(batch, q, k, v, o, cosine, sine)
-    attend_slots = attend_grads(n, me, hidden, cot, mixed_grad, context)
-    last_shard, first_piece, attend_slots = lax.optimization_barrier(
-        (shards[1], first_pieces[0], attend_slots)
+    *attend_slots, edge = attend_grads(n, me, hidden, cot, mixed_grad, context)
+    hid_early, out_early = heads_parts(context, mixed_grad, w_attend)
+    last_shard, first_piece, attend_slots, edge, hid_early, out_early = lax.optimization_barrier(
+        (shards[1], first_pieces[0], attend_slots, edge, hid_early, out_early)
     )
 
     rights, lefts = [last_shard], [last_shard]
-    came, beside = (None, None), None
+    came = (None, None)
     for k in range(1, n):
-        right, left = gather_hop(k, rights[-1], lefts[-1])
+        right, left = gather_hop(k, rights[-1], lefts[-1], me[0])
         if k > 1:
-            slots = after(attend_slots, (rights[-1], lefts[-1]))
-            coming = scatter_hop(k - 1, *scatter_load(k - 1, slots, *came))
+            if k == 2:
+                load = (after(edge, (rights[-1], lefts[-1])),) * 2
+            else:
+                load = scatter_load(k - 1, attend_slots, *came)
+            coming = scatter_hop(k - 1, *load)
+        beside = ()
         if k == 1:
-            active, gates_grad, w_feed = feed_chunk(n, me, [first_piece], hidden, cot)
-            beside = (active, gates_grad, w_feed)
+            active, gates_grad, w_feed = beside = feed_chunk(n, me, [first_piece], hidden, cot)
         elif k == 2:
-            hid_early, out_early = early_parts(
-                context, mixed_grad, active, gates_grad, w_attend, w_feed
+            hid_early, out_early = beside = early_parts(
+                active, gates_grad, w_feed, hid_early, out_early
             )
-            beside = (hid_early, out_early)
         elif k == 3:
-            first_grads = feed_grads(n, hidden, cot, active, gates_grad)
-            beside = (first_grads,)
+            first_grads = beside = feed_grads(n, hidden, cot, active, gates_grad)
         if k > 1:
-            right, left, came = lax.optimization_barrier((right, left, coming, beside))[:3]
+            (right, left), came = after(((right, left), coming), beside)
         else:
-            right, left = lax.optimization_barrier((right, left, beside))[:2]
+            right, left = after((right, left), beside)
         rights.append(right)
         lefts.append(left)
-    load = scatter_load(n - 1, attend_slots, *came)
-    came = scatter_hop(n - 1, *load)
-    attend_grad = attend_slots[0] + came[0].astype(full) + came[1].astype(full)
-    last_pieces = after([last_shard] + rights[1:] + lefts[1:], load)
+    last_pieces = [last_shard] + rights[1:] + lefts[1:]
 
     def scatter(grads):
         return lax.psum_scatter(grads, "dp", scatter_dimension=0, tiled=False)
 
     first_grads = scatter(first_grads).reshape(3, cut, -1)
 
-    grad_in = jnp.transpose(attend_grad[:3], (1, 0, 2))
-    grad_out = attend_grad[3]
     total_tokens = rows * n
-    attend_new = advance(
-        w_attend_in, grad_in, moment_attend_in, average_attend_in, 0.5 / math.sqrt(width * total_tokens)
-    ) + advance(
-        w_attend_out, grad_out, moment_attend_out, average_attend_out, 1.8 / math.sqrt(width * batch * n)
-    )
+
+    def update_attend(came):
+        grad = attend_slots[0] + came[0].astype(full) + came[1].astype(full)
+        grad_in, grad_out = jnp.transpose(grad[:3], (1, 0, 2)), grad[3]
+        rate_in = 0.5 / math.sqrt(width * total_tokens)
+        rate_out = 1.8 / math.sqrt(width * batch * n)
+        new_in = advance(w_attend_in, grad_in, moment_attend_in, average_attend_in, rate_in)
+        new_out = advance(w_attend_out, grad_out, moment_attend_out, average_attend_out, rate_out)
+        return (grad_in, grad_out) + new_in + new_out
+
     rates = (1.6 / math.sqrt(width * total_tokens), 0.77 / math.sqrt(FF * total_tokens))
     states = [jnp.transpose(a, (1, 2, 0)) for a in (w_expand, moment_expand, average_expand)]
     states += [jnp.transpose(a) for a in (w_reduce, moment_reduce, average_reduce)]
 
     if fast:
-        other_hid, other_out, own_hid, own_out, active, gates_grad = feed_last(
-            n, info, True, last_pieces, hidden, cot, hid_early, out_early
-        )
         e = rows // 8
         s = e // 2
 
@@ -951,54 +1023,65 @@
         def both_ways(pair, masks):
             return [swap(pair[0], masks[0]), swap(pair[1], masks[1])]
 
+        def join(one, first, second, third):
+            pieces = (one, first, second, third)
+            return pack_rows(info, [p[0] for p in pieces] + [p[1] for p in pieces])
+
+        other_out, own_out, active, both, w_last = out_last(
+            n, info, True, last_pieces, hidden, out_early
+        )
+        came_out = swap(other_out, 1)
+        load = scatter_load(n - 1, after(attend_slots, other_out), *came)
+        came_out = after(came_out, load)
+        own_out, load_out = sum_cores(own_out, came_out)
+        one_out = both_ways(load_out, (2, 4))
+        other_hid, own_hid, gates_grad = hid_last(
+            info, True, w_last, after(both, load_out), cot, hid_early
+        )
         came_hid = swap(other_hid, 1)
-        came_out = swap(after(other_out, came_hid), 1)
-        own_hid, load_hid = sum_cores(own_hid, came_hid)
+        near_out, load_out = sum_first(own_out, after(one_out, other_hid))
+        two_out = both_ways(load_out, (4, 2))
+        own_hid, load_hid = sum_cores(own_hid, after(came_hid, load_out))
         one_hid = both_ways(load_hid, (2, 4))
-        active, gates_grad = after((active, gates_grad), load_hid)
-        last_grads = feed_grads(n, hidden, cot, active, gates_grad)
-        own_out, load_out = sum_cores(own_out, came_out)
-        one_hid = after(one_hid, last_grads, load_out)
+        last_grads = feed_grads(n, hidden, cot, after(active, load_hid), gates_grad)
+        two_out = after(two_out, last_grads)
         last_grads = scatter(last_grads).reshape(3, units - cut, -1)
-        near_hid, load_hid = sum_first(own_hid, one_hid)
+        add = add_rows(info, tokens, near_out, two_out)
+        out_one = both_ways(add, (4, 2))
+        out_two = both_ways(add, (2, 4))
+        near_hid, load_hid = sum_first(own_hid, after(one_hid, add))
         two_hid = both_ways(load_hid, (4, 2))
-        load_out = after(load_out, load_hid)
-        one_out = both_ways(load_out, (2, 4))
-        two_hid = after(two_hid, attend_new)
+        came = scatter_hop(n - 1, *after(load, load_hid))
+        out_one = after(out_one, load_hid)
+        out_three = both_ways(out_one, (2, 4))
+        two_hid = after(two_hid, out_one)
         back = back_rows(info, tokens, near_hid, two_hid, norm_params)
         hid_one = both_ways(back, (4, 2))
         hid_two = both_ways(back, (2, 4))
-        one_out = after(one_out, back)
-        near_out, load_out = sum_first(own_out, one_out)
-        two_out = both_ways(load_out, (4, 2))
-        begun = update_feed(0, after(first_grads, load_out), states, rates)
+        begun = update_feed(0, after(first_grads, back), states, rates)
         hid_one = after(hid_one, begun)
         hid_three = both_ways(hid_one, (2, 4))
-        two_out = after(two_out, hid_one)
-        add = add_rows(info, tokens, near_out, two_out)
-        out_one = both_ways(add, (4, 2))
-        out_two = both_ways(add, (2, 4))
-        hid_two, hid_three = after((hid_two, hid_three), add)
-        mine_hid = pack_rows(
-            info, [back[0], hid_one[0], hid_two[0], hid_three[0], back[1], hid_one[1], hid_two[1], hid_three[1]]
-        )
-        out_one = after(out_one, mine_hid)
-        out_three = both_ways(out_one, (2, 4))
-        other_hid = after(swap(mine_hid, 1), out_one)
+        attend_new = update_attend(after(came, hid_one))
+        out_two, out_three = after((out_two, out_three), attend_new)
+        mine_out = join(add, out_one, out_two, out_three)
+        other_out = swap(mine_out, 1)
+        output = finish_rows(info, rows, 0, mine_out)
+        output = finish_rows(info, rows, 1, after(other_out, output), begun=output)
+        done = update_feed(cut, after(last_grads, output), states, rates, begun)
+        hid_two, hid_three = after((hid_two, hid_three), done)
+        mine_hid = join(back, hid_one, hid_two, hid_three)
+        other_hid = swap(mine_hid, 1)
+        input_grad = finish_rows(info, rows, 0, mine_hid, cot)
+        other_hid = after(other_hid, input_grad)
         norm_part = tail_sums(mine_hid, other_hid)
         sums = small_sum(join_sums(norm_part, bias_part), "dp")
-        input_grad = finish_rows(info, rows, mine_hid, after(other_hid, norm_part), cot)
-        done = update_feed(cut, after(last_grads, input_grad), states, rates, begun)
-        out_two, out_three = after((out_two, out_three), done)
-        mine_out = pack_rows(
-            info, [add[0], out_one[0], out_two[0], out_three[0], add[1], out_one[1], out_two[1], out_three[1]]
-        )
-        output = finish_rows(info, rows, mine_out, swap(mine_out, 1))
+        input_grad = finish_rows(info, rows, 1, after(other_hid, norm_part), cot, input_grad)
         norm_grad, bias_grad = split_sums(sums, norm_part, bias_part)
     else:
-        hid_part, out_part, active, gates_grad = feed_last(
-            n, info, False, last_pieces, hidden, cot, hid_early, out_early
-        )
+        out_part, active, both, w_last = out_last(n, info, False, last_pieces, hidden, out_early)
+        hid_part, gates_grad = hid_last(info, False, w_last, both, cot, hid_early)
+        came = scatter_hop(n - 1, *scatter_load(n - 1, attend_slots, *came))
+        attend_new = update_attend(came)
         last_grads = scatter(feed_grads(n, hidden, cot, active, gates_grad)).reshape(3, units - cut, -1)
         hidden_grad = lax.psum(hid_part, "mp").astype(full)
         summed = lax.psum(out_part, "mp").astype(full)
@@ -1019,7 +1102,9 @@
         norm_grad, bias_grad = split_sums(sums, norm_part, bias_part)
         begun = update_feed(0, first_grads, states, rates)
         done = update_feed(cut, last_grads, states, rates, begun)
-    new_in, moment_in_new, average_in_new, new_out, moment_out_new, average_out_new = attend_new
+    grad_in, grad_out = attend_new[:2]
+    new_in, moment_in_new, average_in_new = attend_new[2:5]
+    new_out, moment_out_new, average_out_new = attend_new[5:]
     grad_expand, new_expand, moment_expand_new, average_expand_new = (
         jnp.transpose(a, (2, 0, 1)) for a in done[:4]
     )

time: 567 us -> 568 us (level)
  starting transfers between devices: 60.8 us -> 52.9 us
  other arithmetic: 44.5 us -> 38.1 us
  Pallas kernels: 262 us -> 268 us
    ppermute x12 -> x10, waiting for transfers between devices: 16.6 us -> 49 us  [the longest x2 27.1 us: scatter_hop(): lax.ppermute(to_left, 'dp', lefts)]
    pallas_call x1 -> x3, Pallas kernels: 36.7 us -> 58 us  [the longest x1 22.8 us: out_last(): pl.pallas_call(functools.partial(out_last_kernel, n, count, split), grid_...]
    all_gather x1, waiting for transfers between devices: 15.9 us -> 0.67 us  [body(): first_pieces = [lax.all_gather(first_shard, 'dp')]]
    ppermute x26, waiting for transfers between devices: 69.8 us -> 57.5 us  [swap(): return lax.ppermute(value, axis, [(a, a ^ mask) for a in range(n)])]
    pallas_call x2, Pallas kernels: 43.4 us -> 32.5 us  [feed_grads(): pl.pallas_call(functools.partial(feed_grads_kernel, n, steps), grid=(step...]
    pallas_call x1, Pallas kernels: 26.3 us -> 19.6 us  [early_parts(): pl.pallas_call(early_kernel, grid=(rows // block,), in_specs=[pl.BlockSpe...]
    ppermute x26, starting transfers between devices: 28.3 us -> 22.6 us  [swap(): return lax.ppermute(value, axis, [(a, a ^ mask) for a in range(n)])]
    ppermute x12 -> x10, starting transfers between devices: 32.4 us -> 30.1 us  [the longest x2 11.2 us: scatter_hop(): lax.ppermute(to_right, 'dp', rights)]
  transfers between devices with their start and end apart: 42 -> 40, of which waited for: 15 -> 18; matrix products, arithmetic and copies ran while one was open for 8% -> 7% of each run, Pallas kernels for 44% -> 43%
where the time goes in v3:
time: 568 us; the launch traced here: 557 us
  Pallas kernels  268 us (47%)
  waiting for transfers between devices  170 us (30%)
  starting transfers between devices  52.9 us (9%)
  other arithmetic  38.1 us (7%)
  between operations  14.9 us (3%)
  local copies, waits for them, and re-layouts  13.5 us (2%)
    all_gather x1, waiting for transfers between devices, body(): attend_pieces = [lax.all_gather(attend_shard, 'dp')]  62.9 us
    ppermute x26, waiting for transfers between devices, swap(): return lax.ppermute(value, axis, [(a, a ^ mask) for a in range(n)])  57.5 us
    pallas_call x1, Pallas kernels, attend(): pl.pallas_call(functools.partial(attend_kernel, min(512, length)), grid=(...  33.9 us
    pallas_call x2, Pallas kernels, feed_grads(): pl.pallas_call(functools.partial(feed_grads_kernel, n, steps), grid=(step...  32.5 us
    ppermute x2, waiting for transfers between devices, scatter_hop(): lax.ppermute(to_left, 'dp', lefts)  27.1 us
    pallas_call x4, Pallas kernels, finish_rows(): pl.pallas_call(finish_kernel, grid_spec=pltpu.PrefetchScalarGridSpec(num_...  26.5 us
    pallas_call x1, Pallas kernels, out_last(): pl.pallas_call(functools.partial(out_last_kernel, n, count, split), grid_...  22.8 us
    ppermute x26, starting transfers between devices, swap(): return lax.ppermute(value, axis, [(a, a ^ mask) for a in range(n)])  22.6 us
  transfers between devices with their start and end apart: 40, of which 18 were waited for; matrix products, arithmetic and copies ran while one was open for 7% of the time, Pallas kernels for 43%

profile of v3, /device:TPU:0, one launch (start us, length us, event | category | flops | bytes accessed | tf_op | source)
XLA Modules:
  0.0 557.4 jit_solution(10217196673439289499)
XLA Ops:
  8.3 1.5 convert_bitcast_fusion
  11.0 1.6 bitcast_convert_fusion
  14.6 11.2 %layer_norm.1.refs_1_.h_ref.refs_7_ = bf16[2048,2048]{1,0:T(8,128)(2,1)} custom-call(bf16[2048,2048]{1,0:T(8,128)(2,1)} %bitcast.48, f32[2,2048]{1,0:T(2,128)} %refs_6_.1), custom_call_target="tpu_custom_call" | custom-call | flops 33554432 | bytes 16777216 | tf_op jit(solution)/shard_map/layer_norm/pallas_call | solution.py:126
  26.0 5.6 %fusion.4 = (f32[2048,128]{1,0:T(8,128)}, f32[2048,128]{1,0:T(8,128)}) fusion(f32[128]{0:T(128)S(1)} %fusion.9, f32[2048]{0:T(1024)S(1)} %bitcast.85, pred[128]{0:T(512)(128)(4,1)S(1)} %get-tuple-element.271, pred[128]{0:T(512)(128)(4,1)S(1)} %get-tuple-element.272), kind=kLoop, calls=%fused_computation.26 | loop fusion | flops 1310720 | bytes 2106112 | tf_op jit(solution)/shard_map/jit(_where)/select_n | solution.py:952
  31.6 62.9 %all-gather.4.cloned.1.call-done.refs_0_ = bf16[4,4,512,256]{3,2,1,0:T(8,128)(2,1)} async-done(((bf16[1,4,512,256]{3,2,1,0:T(8,128)(2,1)}), bf16[4,4,512,256]{3,2,1,0:T(8,128)(2,1)}) %all-gather.4.cloned.1.call-update) | async-done | bytes 4194320 | tf_op jit(solution)/shard_map/all_gather | solution.py:939
  94.5 17.4 %project.1 = (bf16[2048,256]{1,0:T(8,128)(2,1)}, bf16[2048,256]{1,0:T(8,128)(2,1)}, bf16[2048,256]{1,0:T(8,128)(2,1)}, bf16[2048,256]{1,0:T(8,128)(2,1)}, bf16[4,2048,256]{2,1,0:T(8,128)(2,1)}) custom-call(s32[1]{0:T(128)} %bitcast.3.me_ref, bf16[4,4,512,256]{3,2,1,0:T(8,128)(2,1)} %all-gather.4.cloned.1.call-done.refs_0_, ...), custom_call_target="tpu_custom_call" | custom-call | flops 8589934592 | bytes 25165824 | tf_op jit(solution)/shard_map/project/pallas_call | solution.py:450
  112.0 33.9 %attend.1 = (bf16[2048,256]{1,0:T(8,128)(2,1)}, bf16[3,2048,256]{2,1,0:T(8,128)(2,1)}, f32[3,256]{1,0:T(4,128)}) custom-call(bf16[2048,256]{1,0:T(8,128)(2,1)} %get-tuple-element.129.q_ref, bf16[2048,256]{1,0:T(8,128)(2,1)} %get-tuple-element.130.k_ref, bf16[2048,256]{1,0:T(8,128)(2,1)} %get-tuple-element.131.v_ref, ...), custom_call_target="tpu_custom_call" | custom-call | flops 21474836480 | bytes 10485760 | tf_op jit(solution)/shard_map/attend/pallas_call | solution.py:530
  145.9 17.0 %attend_grads.1 = (f32[4,512,256]{2,1,0:T(8,128)}, bf16[4,512,256]{2,1,0:T(8,128)(2,1)}, bf16[4,512,256]{2,1,0:T(8,128)(2,1)}, bf16[4,512,256]{2,1,0:T(8,128)(2,1)}, bf16[4,512,256]{2,1,0:T(8,128)(2,1)}) custom-call(s32[1]{0:T(128)} %bitcast.3.me_ref, bf16[2048,2048]{1,0:T(8,128)(2,1)} %layer_norm.1.refs_1_.h_ref.refs_7_, bf16[2048,2048]{1,0:T(8,128)(2,1)} %bitcast.56, ...), custom_call_target="tpu_custom_call" | custom-call | flops 8589934592 | bytes 25165824 | tf_op jit(solution)/shard_map/attend_grads/pallas_call | solution.py:589
  162.9 14.6 %heads_parts.1 = (bf16[2048,2048]{1,0:T(8,128)(2,1)}, bf16[2048,2048]{1,0:T(8,128)(2,1)}) custom-call(bf16[2048,256]{1,0:T(8,128)(2,1)} %get-tuple-element.134.ctx_ref, bf16[3,2048,256]{2,1,0:T(8,128)(2,1)} %get-tuple-element.133.mg_ref, bf16[4,2048,256]{2,1,0:T(8,128)(2,1)} %get-tuple-element.140.wa_ref), custom_call_target="tpu_custom_call" | custom-call | flops 8589934592 | bytes 25165824 | tf_op jit(solution)/shard_map/heads_parts/pallas_call | solution.py:621
  179.4 5.5 collective-permute-start
  185.0 16.5 %feed_chunk.1 = (bf16[352,2048]{1,0:T(8,128)(2,1)}, bf16[704,2048]{1,0:T(8,128)(2,1)}, bf16[3,352,2048]{2,1,0:T(8,128)(2,1)}) custom-call(s32[1]{0:T(128)} %bitcast.3.me_ref, bf16[4,3,352,512]{3,2,1,0:T(8,128)(2,1)} %bitcast.86, bf16[2048,2048]{1,0:T(8,128)(2,1)} %layer_norm.1.refs_1_.h_ref.refs_7_, bf16[2048,2048]{1,0:T(8,128)(2,1)} %bitcast.57), custom_call_target="tpu_custom_call" | custom-call | flops 8858370048 | bytes 25427968 | tf_op jit(solution)/shard_map/feed_chunk/pallas_call | solution.py:231
  201.5 4.3 collective-permute-done.1.refs_4_
  208.9 6.7 %collective-permute-start.4 = (bf16[4,512,256]{2,1,0:T(8,128)(2,1)}, bf16[4,512,256]{2,1,0:T(8,128)(2,1)S(1)}, u32[]{:S(2)}, u32[]{:S(2)}) collective-permute-start(bf16[4,512,256]{2,1,0:T(8,128)(2,1)} %get-tuple-element.151), channel_id=1, source_target_pairs={{0,8},{24,16},{1,9},{25,17},{2,10},{26,18},{3,11},{27,19},{4,12},{... | collective-permute-start | bytes 3145736 | tf_op jit(solution)/shard_map/ppermute | solution.py:85
  215.6 19.6 %early_parts.1 = (bf16[2048,2048]{1,0:T(8,128)(2,1)}, bf16[2048,2048]{1,0:T(8,128)(2,1)}) custom-call(bf16[352,2048]{1,0:T(8,128)(2,1)} %get-tuple-element.145.act_ref, bf16[704,2048]{1,0:T(8,128)(2,1)} %get-tuple-element.146.grad_ref, bf16[3,352,2048]{2,1,0:T(8,128)(2,1)} %get-tuple-element.147.w_ref, bf16[2048,2048]{1,0:T(8,128)(2,1)} %get-tuple-element.152.hid_in_ref, ...), custom_call_target="tpu_custom_call" | custom-call | flops 8858370048 | bytes 42205184 | tf_op jit(solution)/shard_map/early_parts/pallas_call | solution.py:649
  235.2 1.9 collective-permute-done.4
  238.2 1.4 collective-permute-start.5
  239.7 1.6 fusion.1
  242.0 6.2 %collective-permute-start.6 = (bf16[4,512,256]{2,1,0:T(8,128)(2,1)}, bf16[4,512,256]{2,1,0:T(8,128)(2,1)S(1)}, u32[]{:S(2)}, u32[]{:S(2)}) collective-permute-start(bf16[4,512,256]{2,1,0:T(8,128)(2,1)} %get-tuple-element.266), channel_id=1, source_target_pairs={{0,8},{8,16},{1,9},{9,17},{2,10},{10,18},{3,11},{11,19},{4,12},{12... | collective-permute-start | bytes 3145736 | tf_op jit(solution)/shard_map/ppermute | solution.py:87
  248.8 16.2 %feed_grads.2 = bf16[4,1056,512]{2,1,0:T(8,128)(2,1)} custom-call(bf16[2048,2048]{1,0:T(8,128)(2,1)} %layer_norm.1.refs_1_.h_ref.refs_7_, bf16[2048,2048]{1,0:T(8,128)(2,1)} %bitcast.58, bf16[352,2048]{1,0:T(8,128)(2,1)} %get-tuple-element.145.act_ref, bf16[704,2048]{1,0:T(8,128)(2,1)} %get-tuple-element.146.grad_ref), custom_call_target="tpu_custom_call" | custom-call | flops 8858370048 | bytes 25427968 | tf_op jit(solution)/shard_map/feed_grads/pallas_call | solution.py:387
  265.0 3.5 collective-permute-done.6
  268.5 22.8 %out_last.1 = (bf16[1024,2048]{1,0:T(8,128)(2,1)}, bf16[1024,2048]{1,0:T(8,128)(2,1)}, bf16[352,2048]{1,0:T(8,128)(2,1)}, f32[704,2048]{1,0:T(8,128)}, bf16[3,352,2048]{2,1,0:T(8,128)(2,1)}) custom-call(s32[4]{0:T(128)} %pad_add_fusion.info_ref, bf16[3,352,512]{2,1,0:T(8,128)(2,1)} %copy-done.9, bf16[3,352,512]{2,1,0:T(8,128)(2,1)} %collective-permute-done.refs_1_, ...), custom_call_target="tpu_custom_call" | custom-call | flops 8858370048 | bytes 33554432 | tf_op jit(solution)/shard_map/out_last/pallas_call | solution.py:319
  294.1 1.9 add_convert_fusion.8
  296.0 3.0 collective-permute-done.8
  299.0 2.8 add_convert_fusion.6
  301.8 20.6 %hid_last.1 = (bf16[1024,2048]{1,0:T(8,128)(2,1)}, bf16[1024,2048]{1,0:T(8,128)(2,1)}, bf16[704,2048]{1,0:T(8,128)(2,1)}) custom-call(s32[4]{0:T(128)} %pad_add_fusion.info_ref, bf16[3,352,2048]{2,1,0:T(8,128)(2,1)} %get-tuple-element.173.w_ref, f32[704,2048]{1,0:T(8,128)} %get-tuple-element.175.both_ref, bf16[2048,2048]{1,0:T(8,128)(2,1)} %bitcast.59, ...), custom_call_target="tpu_custom_call" | custom-call | flops 8858370048 | bytes 33554432 | tf_op jit(solution)/shard_map/hid_last/pallas_call | solution.py:355
  322.6 1.4 collective-permute-start.10
  324.0 1.5 collective-permute-start.9
  325.5 22.5 %collective-permute-done.10 = bf16[256,2048]{1,0:T(8,128)(2,1)S(1)} collective-permute-done((bf16[256,2048]{1,0:T(8,128)(2,1)S(1)}, bf16[256,2048]{1,0:T(8,128)(2,1)S(1)}, u32[]{:S(2)}, u32[]{:S(2)}) %collective-permute-start.10) | collective-permute-done | bytes 1048608 | tf_op jit(solution)/shard_map/ppermute | solution.py:92
  349.2 3.4 add_convert_fusion.4
  353.7 1.5 collective-permute-start.12
  356.8 2.2 add_convert_fusion.2
  359.1 1.5 collective-permute-start.17
  361.1 16.3 %feed_grads.3 = bf16[4,1056,512]{2,1,0:T(8,128)(2,1)} custom-call(bf16[2048,2048]{1,0:T(8,128)(2,1)} %layer_norm.1.refs_1_.h_ref.refs_7_, bf16[2048,2048]{1,0:T(8,128)(2,1)} %bitcast.60, bf16[352,2048]{1,0:T(8,128)(2,1)} %get-tuple-element.182.act_ref, bf16[704,2048]{1,0:T(8,128)(2,1)} %get-tuple-element.183.grad_ref), custom_call_target="tpu_custom_call" | custom-call | flops 8858370048 | bytes 25427968 | tf_op jit(solution)/shard_map/feed_grads/pallas_call | solution.py:387
  378.2 3.7 add_rows.1
  382.5 1.5 collective-permute-start.15
  384.0 9.9 %collective-permute-done.17 = bf16[256,2048]{1,0:T(8,128)(2,1)} collective-permute-done((bf16[256,2048]{1,0:T(8,128)(2,1)}, bf16[256,2048]{1,0:T(8,128)(2,1)}, u32[]{:S(2)}, u32[]{:S(2)}) %collective-permute-start.17) | collective-permute-done | bytes 1048608 | tf_op jit(solution)/shard_map/ppermute | solution.py:92
  393.9 4.2 add_convert_fusion
  401.1 5.0 collective-permute-start.22
  408.2 3.9 collective-permute-done.25.refs_5_
  412.1 2.3 collective-permute-done.24.refs_4_
  415.1 5.5 back_rows.1
  421.8 1.5 collective-permute-start.18
  423.2 7.2 %update_feed.2 = (f32[2,704,512]{2,1,0:T(8,128)}, f32[2,704,512]{2,1,0:T(8,128)}, f32[2,704,512]{2,1,0:T(8,128)}, f32[2,704,512]{2,1,0:T(8,128)}, f32[704,512]{1...) custom-call(bf16[3,352,512]{2,1,0:T(8,128)(2,1)} %bitcast.84, f32[2,704,512]{2,1,0:T(8,128)} %bitcast.63, ...), custom_call_target="tpu_custom_call" | custom-call | flops 5406720 | bytes 16220160 | tf_op jit(solution)/shard_map/update_feed/pallas_call | solution.py:881
  430.4 6.0 %collective-permute-done.27.refs_5_ = bf16[128,2048]{1,0:T(8,128)(2,1)} collective-permute-done((bf16[128,2048]{1,0:T(8,128)(2,1)}, bf16[128,2048]{1,0:T(8,128)(2,1)}, u32[]{:S(2)}, u32[]{:S(2)}) %collective-permute-start.27) | collective-permute-done | bytes 524320 | tf_op jit(solution)/shard_map/ppermute | solution.py:92
  436.4 1.4 collective-permute-start.19
  438.4 11.2 %collective-permute-done.22 = bf16[4,512,256]{2,1,0:T(8,128)(2,1)} collective-permute-done((bf16[4,512,256]{2,1,0:T(8,128)(2,1)}, bf16[4,512,256]{2,1,0:T(8,128)(2,1)}, u32[]{:S(2)}, u32[]{:S(2)}) %collective-permute-start.22) | collective-permute-done | bytes 1048608 | tf_op jit(solution)/shard_map/ppermute | solution.py:87
  449.5 1.4 collective-permute-start.21
  450.9 27.1 %collective-permute-done.23 = bf16[4,512,256]{2,1,0:T(8,128)(2,1)} collective-permute-done((bf16[4,512,256]{2,1,0:T(8,128)(2,1)S(1)}, bf16[4,512,256]{2,1,0:T(8,128)(2,1)}, u32[]{:S(2)}, u32[]{:S(2)}) %collective-permute-start.23) | collective-permute-done | bytes 1048608 | tf_op jit(solution)/shard_map/ppermute | solution.py:87
  478.0 2.0 convert_add_fusion.2
  480.1 1.4 multiply_add_fusion.2
  482.7 3.1 multiply_add_fusion
  487.0 5.1 pack_rows.2.refs_0_
  492.2 1.5 collective-permute-start.29
  494.3 1.5 collective-permute-start.30
  496.3 5.4 finish_rows.4.refs_1_
  501.7 5.4 finish_rows.5
  507.1 7.0 %update_feed.3 = (f32[2,704,512]{2,1,0:T(8,128)}, f32[2,704,512]{2,1,0:T(8,128)}, f32[2,704,512]{2,1,0:T(8,128)}, f32[2,704,512]{2,1,0:T(8,128)}, f32[704,512]{1...) custom-call(bf16[3,352,512]{2,1,0:T(8,128)(2,1)} %bitcast.83, ...), custom_call_target="tpu_custom_call", output_to_operand_aliasing={{0}: (7, {}), {1}: (8, {}), {2}: (9, {}), {3}: (10, {}), {4... | custom-call | flops 5406720 | bytes 16220160 | tf_op jit(solution)/shard_map/update_feed/pallas_call | solution.py:881
  514.1 5.2 collective-permute-done.32.refs_7_
  521.4 5.1 pack_rows.3.refs_0_.own_ref
  526.6 7.8 %finish_rows.6.refs_2_ = f32[2048,2048]{1,0:T(8,128)} custom-call(s32[4]{0:T(128)} %pad_add_fusion.info_ref, bf16[1088,2048]{1,0:T(8,128)(2,1)} %pack_rows.3.refs_0_.own_ref, bf16[2048,2048]{1,0:T(8,128)(2,1)} %bitcast.61), custom_call_target="tpu_custom_call" | custom-call | flops 4194304 | bytes 16777216 | tf_op jit(solution)/shard_map/finish_rows/pallas_call | solution.py:843
  534.4 1.7 tail_sums.1
  536.9 1.5 collective-permute-start.34
  538.5 2.4 collective-permute-done.34
  541.3 7.8 %finish_rows.7 = f32[2048,2048]{1,0:T(8,128)} custom-call(s32[4]{0:T(128)} %pad_add_fusion.info_ref, bf16[1088,2048]{1,0:T(8,128)(2,1)} %collective-permute-done.33.other_ref.refs_0_, bf16[2048,2048]{1,0:T(8,128)(2,1)} %bitcast.62, f32[2048,2048]{1,0:T(8,128)} %finish_rows.6.refs_2_), custom_call_target="tpu_custom_call", output_to_operand_aliasing={{}: (3, {})} | custom-call | flops 4194304 | bytes 16777216 | tf_op jit(solution)/shard_map/finish_rows/pallas_call | solution.py:843
  (169 shorter events, 36.5 us)
Async XLA Ops:
  7.2 87.3 %all-gather.4.cloned.1.call-start = ((), (), s32[]{:S(2)}) async-start(), calls=%async_computation.2 | async-start | bytes 5242880 | tf_op jit(solution)/shard_map/all_gather | solution.py:939
  10.9 167.2 %all-gather.6.cloned.1.call-start = ((), (), s32[]{:S(2)}) async-start(), calls=%async_computation.5 | async-start | bytes 5406720 | tf_op jit(solution)/shard_map/all_gather | solution.py:941
  14.5 408.7 %reduce-scatter.3.cloned.1.call-start = ((), (), s32[]{:S(2)}) async-start(), calls=%async_computation.3 | async-start | bytes 5406720 | tf_op jit(solution)/shard_map/reduce_scatter | solution.py:990
  26.0 153.5 %copy-start.9 = (bf16[3,352,512]{2,1,0:T(8,128)(2,1)}, bf16[3,352,512]{2,1,0:T(8,128)(2,1)S(1)}, u32[]{:S(2)}) copy-start(bf16[3,352,512]{2,1,0:T(8,128)(2,1)S(1)} %pad_maximum_fusion.refs_0_) | copy-start | bytes 3244036
  178.1 27.6 %collective-permute-start.1 = (bf16[3,352,512]{2,1,0:T(8,128)(2,1)S(1)}, bf16[3,352,512]{2,1,0:T(8,128)(2,1)}, u32[]{:S(2)}, u32[]{:S(2)}) collective-permute-start(bf16[3,352,512]{2,1,0:T(8,128)(2,1)S(1)} %pad_maximum_fusion.refs_0_), channel_id=1, source_target_pairs={{8,0},{16,8},{24,16},{9,1},{17,9},{25,17},{10,2},{18,10},{26,18},{... | collective-permute-start | bytes 3244040 | tf_op jit(solution)/shard_map/ppermute | solution.py:68
  179.4 27.4 %collective-permute-start = (bf16[3,352,512]{2,1,0:T(8,128)(2,1)S(1)}, bf16[3,352,512]{2,1,0:T(8,128)(2,1)}, u32[]{:S(2)}, u32[]{:S(2)}) collective-permute-start(bf16[3,352,512]{2,1,0:T(8,128)(2,1)S(1)} %pad_maximum_fusion.refs_0_), channel_id=1, source_target_pairs={{0,8},{8,16},{16,24},{1,9},{9,17},{17,25},{2,10},{10,18},{18,26},{... | collective-permute-start | bytes 3244040 | tf_op jit(solution)/shard_map/ppermute | solution.py:68
  206.8 30.3 %collective-permute-start.2 = (bf16[3,352,512]{2,1,0:T(8,128)(2,1)}, bf16[3,352,512]{2,1,0:T(8,128)(2,1)S(1)}, u32[]{:S(2)}, u32[]{:S(2)}) collective-permute-start(bf16[3,352,512]{2,1,0:T(8,128)(2,1)} %collective-permute-done.refs_1_), channel_id=1, source_target_pairs={{8,16},{16,24},{9,17},{17,25},{10,18},{18,26},{11,19},{19,27},{12,... | collective-permute-start | bytes 3244040 | tf_op jit(solution)/shard_map/ppermute | solution.py:68
  207.6 29.6 %collective-permute-start.3 = (bf16[3,352,512]{2,1,0:T(8,128)(2,1)}, bf16[3,352,512]{2,1,0:T(8,128)(2,1)S(1)}, u32[]{:S(2)}, u32[]{:S(2)}) collective-permute-start(bf16[3,352,512]{2,1,0:T(8,128)(2,1)} %collective-permute-done.1.refs_4_), channel_id=1, source_target_pairs={{8,0},{16,8},{9,1},{17,9},{10,2},{18,10},{11,3},{19,11},{12,4},{20... | collective-permute-start | bytes 3244040 | tf_op jit(solution)/shard_map/ppermute | solution.py:68
  208.9 28.3 %collective-permute-start.4 = (bf16[4,512,256]{2,1,0:T(8,128)(2,1)}, bf16[4,512,256]{2,1,0:T(8,128)(2,1)S(1)}, u32[]{:S(2)}, u32[]{:S(2)}) collective-permute-start(bf16[4,512,256]{2,1,0:T(8,128)(2,1)} %get-tuple-element.151), channel_id=1, source_target_pairs={{0,8},{24,16},{1,9},{25,17},{2,10},{26,18},{3,11},{27,19},{4,12},{... | collective-permute-start | bytes 3145736 | tf_op jit(solution)/shard_map/ppermute | solution.py:85
  235.2 4.4 copy-start.17
  237.1 4.1 copy-start.10
  237.1 4.1 copy-start.11
  238.2 30.3 %collective-permute-start.5 = (bf16[3,352,512]{2,1,0:T(8,128)(2,1)S(1)}, bf16[3,352,512]{2,1,0:T(8,128)(2,1)}, u32[]{:S(2)}, u32[]{:S(2)}) collective-permute-start(bf16[3,352,512]{2,1,0:T(8,128)(2,1)S(1)} %broadcast_select_fusion), channel_id=1, source_target_pairs={{16,24},{8,0},{17,25},{9,1},{18,26},{10,2},{19,27},{11,3},{20,28},... | collective-permute-start | bytes 3244040 | tf_op jit(solution)/shard_map/ppermute | solution.py:66
  241.3 23.7 %collective-permute-start.7 = (bf16[4,512,256]{2,1,0:T(8,128)(2,1)}, bf16[4,512,256]{2,1,0:T(8,128)(2,1)S(1)}, u32[]{:S(2)}, u32[]{:S(2)}) collective-permute-start(bf16[4,512,256]{2,1,0:T(8,128)(2,1)} %get-tuple-element.265), channel_id=1, source_target_pairs={{24,16},{16,8},{25,17},{17,9},{26,18},{18,10},{27,19},{19,11},{28,... | collective-permute-start | bytes 3145736 | tf_op jit(solution)/shard_map/ppermute | solution.py:87
  242.0 26.5 %collective-permute-start.6 = (bf16[4,512,256]{2,1,0:T(8,128)(2,1)}, bf16[4,512,256]{2,1,0:T(8,128)(2,1)S(1)}, u32[]{:S(2)}, u32[]{:S(2)}) collective-permute-start(bf16[4,512,256]{2,1,0:T(8,128)(2,1)} %get-tuple-element.266), channel_id=1, source_target_pairs={{0,8},{8,16},{1,9},{9,17},{2,10},{10,18},{3,11},{11,19},{4,12},{12... | collective-permute-start | bytes 3145736 | tf_op jit(solution)/shard_map/ppermute | solution.py:87
  265.0 26.4 %copy-start.14 = (bf16[4,512,256]{2,1,0:T(8,128)(2,1)}, bf16[4,512,256]{2,1,0:T(8,128)(2,1)S(1)}, u32[]{:S(2)}) copy-start(bf16[4,512,256]{2,1,0:T(8,128)(2,1)S(1)} %collective-permute-done.7) | copy-start | bytes 3145732
  268.5 22.9 %copy-start.15 = (bf16[4,512,256]{2,1,0:T(8,128)(2,1)}, bf16[4,512,256]{2,1,0:T(8,128)(2,1)S(1)}, u32[]{:S(2)}) copy-start(bf16[4,512,256]{2,1,0:T(8,128)(2,1)S(1)} %collective-permute-done.6) | copy-start | bytes 3145732
  291.4 7.6 %collective-permute-start.8 = (bf16[1024,2048]{1,0:T(8,128)(2,1)}, bf16[1024,2048]{1,0:T(8,128)(2,1)}, u32[]{:S(2)}, u32[]{:S(2)}) collective-permute-start(bf16[1024,2048]{1,0:T(8,128)(2,1)} %get-tuple-element.164), channel_id=1, source_target_pairs={{0,1},{1,0},{2,3},{3,2},{4,5},{5,4},{6,7},{7,6},{8,9},{9,8},{10,11... | collective-permute-start | bytes 12582920 | tf_op jit(solution)/shard_map/ppermute | solution.py:92
  291.5 215.6 %reduce-scatter.5.cloned.1.call-start = ((), (), s32[]{:S(2)}) async-start(), calls=%async_computation.4 | async-start | bytes 5406720 | tf_op jit(solution)/shard_map/reduce_scatter | solution.py:990
  292.9 6.0 %copy-start.4 = (bf16[1024,2048]{1,0:T(8,128)(2,1)S(1)}, bf16[1024,2048]{1,0:T(8,128)(2,1)}, u32[]{:S(2)}) copy-start(bf16[1024,2048]{1,0:T(8,128)(2,1)} %get-tuple-element.163) | copy-start | bytes 12582916
  322.4 34.4 %collective-permute-start.13 = (bf16[1024,2048]{1,0:T(8,128)(2,1)}, bf16[1024,2048]{1,0:T(8,128)(2,1)S(1)}, u32[]{:S(2)}, u32[]{:S(2)}) collective-permute-start(bf16[1024,2048]{1,0:T(8,128)(2,1)} %get-tuple-element.176), channel_id=1, source_target_pairs={{0,1},{1,0},{2,3},{3,2},{4,5},{5,4},{6,7},{7,6},{8,9},{9,8},{10,11... | collective-permute-start | bytes 12582920 | tf_op jit(solution)/shard_map/ppermute | solution.py:92
  322.6 25.4 %collective-permute-start.10 = (bf16[256,2048]{1,0:T(8,128)(2,1)S(1)}, bf16[256,2048]{1,0:T(8,128)(2,1)S(1)}, u32[]{:S(2)}, u32[]{:S(2)}) collective-permute-start(bf16[256,2048]{1,0:T(8,128)(2,1)S(1)} %get-tuple-element.253), channel_id=1, source_target_pairs={{0,4},{1,5},{2,6},{3,7},{4,0},{5,1},{6,2},{7,3},{8,12},{9,13},{10,... | collective-permute-start | bytes 3145736 | tf_op jit(solution)/shard_map/ppermute | solution.py:92
  324.0 25.2 %collective-permute-start.9 = (bf16[256,2048]{1,0:T(8,128)(2,1)S(1)}, bf16[256,2048]{1,0:T(8,128)(2,1)S(1)}, u32[]{:S(2)}, u32[]{:S(2)}) collective-permute-start(bf16[256,2048]{1,0:T(8,128)(2,1)S(1)} %get-tuple-element.254), channel_id=1, source_target_pairs={{0,2},{1,3},{2,0},{3,1},{4,6},{5,7},{6,4},{7,5},{8,10},{9,11},{10,... | collective-permute-start | bytes 3145736 | tf_op jit(solution)/shard_map/ppermute | solution.py:92
  352.6 4.2 copy-start.2
  353.7 23.8 %collective-permute-start.12 = (bf16[128,2048]{1,0:T(8,128)(2,1)}, bf16[128,2048]{1,0:T(8,128)(2,1)S(1)}, u32[]{:S(2)}, u32[]{:S(2)}) collective-permute-start(bf16[128,2048]{1,0:T(8,128)(2,1)} %get-tuple-element.261), channel_id=1, source_target_pairs={{0,2},{1,3},{2,0},{3,1},{4,6},{5,7},{6,4},{7,5},{8,10},{9,11},{10,... | collective-permute-start | bytes 1572872 | tf_op jit(solution)/shard_map/ppermute | solution.py:92
  356.2 21.2 %collective-permute-start.11 = (bf16[128,2048]{1,0:T(8,128)(2,1)}, bf16[128,2048]{1,0:T(8,128)(2,1)}, u32[]{:S(2)}, u32[]{:S(2)}) collective-permute-start(bf16[128,2048]{1,0:T(8,128)(2,1)} %get-tuple-element.263), channel_id=1, source_target_pairs={{0,4},{1,5},{2,6},{3,7},{4,0},{5,1},{6,2},{7,3},{8,12},{9,13},{10,... | collective-permute-start | bytes 1572872 | tf_op jit(solution)/shard_map/ppermute | solution.py:92
  359.1 34.8 %collective-permute-start.17 = (bf16[256,2048]{1,0:T(8,128)(2,1)}, bf16[256,2048]{1,0:T(8,128)(2,1)}, u32[]{:S(2)}, u32[]{:S(2)}) collective-permute-start(bf16[256,2048]{1,0:T(8,128)(2,1)} %get-tuple-element.249), channel_id=1, source_target_pairs={{0,4},{1,5},{2,6},{3,7},{4,0},{5,1},{6,2},{7,3},{8,12},{9,13},{10,... | collective-permute-start | bytes 3145736 | tf_op jit(solution)/shard_map/ppermute | solution.py:92
  360.6 33.3 %collective-permute-start.16 = (bf16[256,2048]{1,0:T(8,128)(2,1)S(1)}, bf16[256,2048]{1,0:T(8,128)(2,1)}, u32[]{:S(2)}, u32[]{:S(2)}) collective-permute-start(bf16[256,2048]{1,0:T(8,128)(2,1)S(1)} %get-tuple-element.250), channel_id=1, source_target_pairs={{0,2},{1,3},{2,0},{3,1},{4,6},{5,7},{6,4},{7,5},{8,10},{9,11},{10,... | collective-permute-start | bytes 3145736 | tf_op jit(solution)/shard_map/ppermute | solution.py:92
  381.9 24.2 %collective-permute-start.14 = (bf16[128,2048]{1,0:T(8,128)(2,1)}, bf16[128,2048]{1,0:T(8,128)(2,1)S(1)}, u32[]{:S(2)}, u32[]{:S(2)}) collective-permute-start(bf16[128,2048]{1,0:T(8,128)(2,1)} %get-tuple-element.186.refs_0_), channel_id=1, source_target_pairs={{0,4},{1,5},{2,6},{3,7},{4,0},{5,1},{6,2},{7,3},{8,12},{9,13},{10,... | collective-permute-start | bytes 1572872 | tf_op jit(solution)/shard_map/ppermute | solution.py:92
  382.5 24.8 %collective-permute-start.15 = (bf16[128,2048]{1,0:T(8,128)(2,1)}, bf16[128,2048]{1,0:T(8,128)(2,1)S(1)}, u32[]{:S(2)}, u32[]{:S(2)}) collective-permute-start(bf16[128,2048]{1,0:T(8,128)(2,1)} %get-tuple-element.187.refs_4_), channel_id=1, source_target_pairs={{0,2},{1,3},{2,0},{3,1},{4,6},{5,7},{6,4},{7,5},{8,10},{9,11},{10,... | collective-permute-start | bytes 1572872 | tf_op jit(solution)/shard_map/ppermute | solution.py:92
  399.0 13.1 %collective-permute-start.25 = (bf16[128,2048]{1,0:T(8,128)(2,1)S(1)}, bf16[128,2048]{1,0:T(8,128)(2,1)S(1)}, u32[]{:S(2)}, u32[]{:S(2)}) collective-permute-start(bf16[128,2048]{1,0:T(8,128)(2,1)S(1)} %get-tuple-element.258), channel_id=1, source_target_pairs={{0,2},{1,3},{2,0},{3,1},{4,6},{5,7},{6,4},{7,5},{8,10},{9,11},{10,... | collective-permute-start | bytes 1572872 | tf_op jit(solution)/shard_map/ppermute | solution.py:92
  400.5 13.9 %collective-permute-start.24 = (bf16[128,2048]{1,0:T(8,128)(2,1)S(1)}, bf16[128,2048]{1,0:T(8,128)(2,1)S(1)}, u32[]{:S(2)}, u32[]{:S(2)}) collective-permute-start(bf16[128,2048]{1,0:T(8,128)(2,1)S(1)} %get-tuple-element.260), channel_id=1, source_target_pairs={{0,4},{1,5},{2,6},{3,7},{4,0},{5,1},{6,2},{7,3},{8,12},{9,13},{10,... | collective-permute-start | bytes 1572872 | tf_op jit(solution)/shard_map/ppermute | solution.py:92
  401.1 48.4 %collective-permute-start.22 = (bf16[4,512,256]{2,1,0:T(8,128)(2,1)}, bf16[4,512,256]{2,1,0:T(8,128)(2,1)}, u32[]{:S(2)}, u32[]{:S(2)}) collective-permute-start(bf16[4,512,256]{2,1,0:T(8,128)(2,1)} %add_convert_fusion.9), channel_id=1, source_target_pairs={{0,8},{8,16},{16,24},{1,9},{9,17},{17,25},{2,10},{10,18},{18,26},{... | collective-permute-start | bytes 3145736 | tf_op jit(solution)/shard_map/ppermute | solution.py:87
  406.1 71.9 %collective-permute-start.23 = (bf16[4,512,256]{2,1,0:T(8,128)(2,1)S(1)}, bf16[4,512,256]{2,1,0:T(8,128)(2,1)}, u32[]{:S(2)}, u32[]{:S(2)}) collective-permute-start(bf16[4,512,256]{2,1,0:T(8,128)(2,1)S(1)} %add_convert_fusion.8), channel_id=1, source_target_pairs={{24,16},{16,8},{8,0},{25,17},{17,9},{9,1},{26,18},{18,10},{10,2},{... | collective-permute-start | bytes 3145736 | tf_op jit(solution)/shard_map/ppermute | solution.py:87
  420.6 17.2 %collective-permute-start.26 = (bf16[144,2048]{1,0:T(8,128)(2,1)}, bf16[144,2048]{1,0:T(8,128)(2,1)S(1)}, u32[]{:S(2)}, u32[]{:S(2)}) collective-permute-start(bf16[144,2048]{1,0:T(8,128)(2,1)} %get-tuple-element.196.refs_0_), channel_id=1, source_target_pairs={{0,4},{1,5},{2,6},{3,7},{4,0},{5,1},{6,2},{7,3},{8,12},{9,13},{10,... | collective-permute-start | bytes 1769480 | tf_op jit(solution)/shard_map/ppermute | solution.py:92
  421.2 15.2 %collective-permute-start.27 = (bf16[128,2048]{1,0:T(8,128)(2,1)}, bf16[128,2048]{1,0:T(8,128)(2,1)}, u32[]{:S(2)}, u32[]{:S(2)}) collective-permute-start(bf16[128,2048]{1,0:T(8,128)(2,1)} %get-tuple-element.197.refs_4_), channel_id=1, source_target_pairs={{0,2},{1,3},{2,0},{3,1},{4,6},{5,7},{6,4},{7,5},{8,10},{9,11},{10,... | collective-permute-start | bytes 1572872 | tf_op jit(solution)/shard_map/ppermute | solution.py:92
  421.8 64.0 %collective-permute-start.18 = (bf16[128,2048]{1,0:T(8,128)(2,1)}, bf16[128,2048]{1,0:T(8,128)(2,1)}, u32[]{:S(2)}, u32[]{:S(2)}) collective-permute-start(bf16[128,2048]{1,0:T(8,128)(2,1)} %get-tuple-element.186.refs_0_), channel_id=1, source_target_pairs={{0,2},{1,3},{2,0},{3,1},{4,6},{5,7},{6,4},{7,5},{8,10},{9,11},{10,... | collective-permute-start | bytes 1572872 | tf_op jit(solution)/shard_map/ppermute | solution.py:92
  423.2 54.7 %copy-start.5 = (f32[4,512,256]{2,1,0:T(8,128)S(1)}, f32[4,512,256]{2,1,0:T(8,128)}, u32[]{:S(2)}) copy-start(f32[4,512,256]{2,1,0:T(8,128)} %get-tuple-element.165) | copy-start | bytes 6291460
  436.4 49.4 %collective-permute-start.19 = (bf16[128,2048]{1,0:T(8,128)(2,1)}, bf16[128,2048]{1,0:T(8,128)(2,1)S(1)}, u32[]{:S(2)}, u32[]{:S(2)}) collective-permute-start(bf16[128,2048]{1,0:T(8,128)(2,1)} %get-tuple-element.187.refs_4_), channel_id=1, source_target_pairs={{0,4},{1,5},{2,6},{3,7},{4,0},{5,1},{6,2},{7,3},{8,12},{9,13},{10,... | collective-permute-start | bytes 1572872 | tf_op jit(solution)/shard_map/ppermute | solution.py:92
  437.8 55.8 %copy-start.21 = (bf16[144,2048]{1,0:T(8,128)(2,1)}, bf16[144,2048]{1,0:T(8,128)(2,1)S(1)}, u32[]{:S(2)}) copy-start(bf16[144,2048]{1,0:T(8,128)(2,1)S(1)} %collective-permute-done.26.refs_1_) | copy-start | bytes 1769476
  437.8 47.9 %collective-permute-start.20 = (bf16[128,2048]{1,0:T(8,128)(2,1)}, bf16[128,2048]{1,0:T(8,128)(2,1)S(1)}, u32[]{:S(2)}, u32[]{:S(2)}) collective-permute-start(bf16[128,2048]{1,0:T(8,128)(2,1)} %copy-done.25), channel_id=1, source_target_pairs={{0,2},{1,3},{2,0},{3,1},{4,6},{5,7},{6,4},{7,5},{8,10},{9,11},{10,... | collective-permute-start | bytes 1572872 | tf_op jit(solution)/shard_map/ppermute | solution.py:92
  438.4 41.6 %copy-start.6 = (f32[512,256]{1,0:T(8,128)S(1)}, f32[512,256]{1,0:T(8,128)}, u32[]{:S(2)}) copy-start(f32[512,256]{1,0:T(8,128)} %param.25) | copy-start | bytes 1572868
  438.4 41.6 %copy-start.33 = (f32[512,256]{1,0:T(8,128)S(1)}, f32[512,256]{1,0:T(8,128)}, u32[]{:S(2)}) copy-start(f32[512,256]{1,0:T(8,128)} %param.37) | copy-start | bytes 1572868
  438.4 41.7 %copy-start.34 = (f32[512,256]{1,0:T(8,128)S(1)}, f32[512,256]{1,0:T(8,128)}, u32[]{:S(2)}) copy-start(f32[512,256]{1,0:T(8,128)} %param.31) | copy-start | bytes 1572868
  449.5 36.3 %collective-permute-start.21 = (bf16[128,2048]{1,0:T(8,128)(2,1)}, bf16[128,2048]{1,0:T(8,128)(2,1)S(1)}, u32[]{:S(2)}, u32[]{:S(2)}) collective-permute-start(bf16[128,2048]{1,0:T(8,128)(2,1)} %copy-done.26), channel_id=1, source_target_pairs={{0,4},{1,5},{2,6},{3,7},{4,0},{5,1},{6,2},{7,3},{8,12},{9,13},{10,... | collective-permute-start | bytes 1572872 | tf_op jit(solution)/shard_map/ppermute | solution.py:92
  478.0 3.5 copy-start.8
  480.0 2.6 copy-start.7
  487.0 5.2 copy-start.20
  487.0 7.3 %copy-start.24 = (bf16[128,2048]{1,0:T(8,128)(2,1)S(1)}, bf16[128,2048]{1,0:T(8,128)(2,1)}, u32[]{:S(2)}) copy-start(bf16[128,2048]{1,0:T(8,128)(2,1)} %get-tuple-element.197.refs_4_) | copy-start | bytes 1572868
  492.1 9.6 %collective-permute-start.28 = (bf16[1024,2048]{1,0:T(8,128)(2,1)}, bf16[1024,2048]{1,0:T(8,128)(2,1)}, u32[]{:S(2)}, u32[]{:S(2)}) collective-permute-start(bf16[1024,2048]{1,0:T(8,128)(2,1)} %pack_rows.2.refs_0_), channel_id=1, source_target_pairs={{0,1},{1,0},{2,3},{3,2},{4,5},{5,4},{6,7},{7,6},{8,9},{9,8},{10,11... | collective-permute-start | bytes 12582920 | tf_op jit(solution)/shard_map/ppermute | solution.py:92
  492.2 22.0 %collective-permute-start.29 = (bf16[144,2048]{1,0:T(8,128)(2,1)S(1)}, bf16[144,2048]{1,0:T(8,128)(2,1)S(1)}, u32[]{:S(2)}, u32[]{:S(2)}) collective-permute-start(bf16[144,2048]{1,0:T(8,128)(2,1)S(1)} %copy-done.20), channel_id=1, source_target_pairs={{0,2},{1,3},{2,0},{3,1},{4,6},{5,7},{6,4},{7,5},{8,10},{9,11},{10,... | collective-permute-start | bytes 1769480 | tf_op jit(solution)/shard_map/ppermute | solution.py:92
  493.6 26.9 %collective-permute-start.31 = (bf16[144,2048]{1,0:T(8,128)(2,1)S(1)}, bf16[144,2048]{1,0:T(8,128)(2,1)S(1)}, u32[]{:S(2)}, u32[]{:S(2)}) collective-permute-start(bf16[144,2048]{1,0:T(8,128)(2,1)S(1)} %collective-permute-done.26.refs_1_), channel_id=1, source_target_pairs={{0,2},{1,3},{2,0},{3,1},{4,6},{5,7},{6,4},{7,5},{8,10},{9,11},{10,... | collective-permute-start | bytes 1769480 | tf_op jit(solution)/shard_map/ppermute | solution.py:92
  494.3 19.9 %collective-permute-start.30 = (bf16[128,2048]{1,0:T(8,128)(2,1)S(1)}, bf16[128,2048]{1,0:T(8,128)(2,1)}, u32[]{:S(2)}, u32[]{:S(2)}) collective-permute-start(bf16[128,2048]{1,0:T(8,128)(2,1)S(1)} %copy-done.24), channel_id=1, source_target_pairs={{0,4},{1,5},{2,6},{3,7},{4,0},{5,1},{6,2},{7,3},{8,12},{9,13},{10,... | collective-permute-start | bytes 1572872 | tf_op jit(solution)/shard_map/ppermute | solution.py:92
  495.7 23.6 %collective-permute-start.32 = (bf16[128,2048]{1,0:T(8,128)(2,1)}, bf16[128,2048]{1,0:T(8,128)(2,1)}, u32[]{:S(2)}, u32[]{:S(2)}) collective-permute-start(bf16[128,2048]{1,0:T(8,128)(2,1)} %collective-permute-done.27.refs_5_), channel_id=1, source_target_pairs={{0,4},{1,5},{2,6},{3,7},{4,0},{5,1},{6,2},{7,3},{8,12},{9,13},{10,... | collective-permute-start | bytes 1572872 | tf_op jit(solution)/shard_map/ppermute | solution.py:92
  514.1 6.4 %copy-start.22 = (bf16[144,2048]{1,0:T(8,128)(2,1)}, bf16[144,2048]{1,0:T(8,128)(2,1)S(1)}, u32[]{:S(2)}) copy-start(bf16[144,2048]{1,0:T(8,128)(2,1)S(1)} %collective-permute-done.29.refs_2_) | copy-start | bytes 1769476
  526.5 7.9 %collective-permute-start.33 = (bf16[1088,2048]{1,0:T(8,128)(2,1)}, bf16[1088,2048]{1,0:T(8,128)(2,1)}, u32[]{:S(2)}, u32[]{:S(2)}) collective-permute-start(bf16[1088,2048]{1,0:T(8,128)(2,1)} %pack_rows.3.refs_0_.own_ref), channel_id=1, source_target_pairs={{0,1},{1,0},{2,3},{3,2},{4,5},{5,4},{6,7},{7,6},{8,9},{9,8},{10,11... | collective-permute-start | bytes 13369352 | tf_op jit(solution)/shard_map/ppermute | solution.py:92
  536.9 3.9 collective-permute-start.34
  540.8 8.3 %copy-start.41 = (f32[3,256]{1,0:T(4,128)S(1)}, f32[3,256]{1,0:T(4,128)}, u32[]{:S(2)}) copy-start(f32[3,256]{1,0:T(4,128)} %refs_5_.1) | copy-start | bytes 9220
  540.8 8.3 %copy-start.42 = (f32[3,256]{1,0:T(4,128)S(1)}, f32[3,256]{1,0:T(4,128)}, u32[]{:S(2)}) copy-start(f32[3,256]{1,0:T(4,128)} %param.41) | copy-start | bytes 9220
  540.8 8.3 %copy-start.43 = (f32[3,256]{1,0:T(4,128)S(1)}, f32[3,256]{1,0:T(4,128)}, u32[]{:S(2)}) copy-start(f32[3,256]{1,0:T(4,128)} %param.35) | copy-start | bytes 9220
  540.9 8.9 %copy-start.35 = (f32[2,2048]{1,0:T(2,128)S(1)}, f32[2,2048]{1,0:T(2,128)}, u32[]{:S(2)}) copy-start(f32[2,2048]{1,0:T(2,128)} %refs_6_.1) | copy-start | bytes 49156
  540.9 8.9 %copy-start.37 = (f32[2,2048]{1,0:T(2,128)S(1)}, f32[2,2048]{1,0:T(2,128)}, u32[]{:S(2)}) copy-start(f32[2,2048]{1,0:T(2,128)} %param.40) | copy-start | bytes 49156
  540.9 8.9 %copy-start.38 = (f32[2,2048]{1,0:T(2,128)S(1)}, f32[2,2048]{1,0:T(2,128)}, u32[]{:S(2)}) copy-start(f32[2,2048]{1,0:T(2,128)} %param.34) | copy-start | bytes 49156
  540.9 8.2 %collective-permute-start.35 = (f32[19,256]{1,0:T(8,128)S(1)}, f32[19,256]{1,0:T(8,128)S(1)}, u32[]{:S(2)}, u32[]{:S(2)}) collective-permute-start(f32[19,256]{1,0:T(8,128)S(1)} %add.150), channel_id=1, source_target_pairs={{0,16},{8,24},{16,0},{24,8},{1,17},{9,25},{17,1},{25,9},{2,18},{10... | collective-permute-start | bytes 58376 | tf_op jit(solution)/shard_map/ppermute | solution.py:92
  (20 other events, 29.4 us)
Sparse Core Ops, SparseCore 0:
  11.0 83.4 all-gather.3
  96.7 81.4 all-gather.5
  291.6 80.6 reduce-scatter.2
  377.6 101.3 reduce-scatter.4

commit v4 on v3

--- a/solution.py
+++ b/solution.py
@@ -256,31 +256,31 @@
 
 def put_part(split, info_ref, parts, value):
     if not split:
-        parts[0][...] = value
+        parts[0][...] = value.astype(low)
         return
     step = pl.program_id(0)
     sub = value.shape[0] // 4
     high = jnp.where(step % 2 == 0, info_ref[1], info_ref[2])
     small = jnp.where(step % 2 == 0, info_ref[2], info_ref[1])
-    for half in range(2):
-
-        @pl.when(step // 2 == half)
-        def _(half=half):
-            for i in range(4):
-                at = ((i // 2) ^ high) * 2 + ((i % 2) ^ small)
-                place = pl.ds(pl.multiple_of(at * sub, sub), sub)
-                parts[half][place, :] = value[i * sub : (i + 1) * sub]
+    first, second = value[: 2 * sub], value[2 * sub :]
+    near = jnp.where(high == 0, first, second).astype(low)
+    far = jnp.where(high == 0, second, first).astype(low)
+    for at in range(4):
+
+        @pl.when(step == at)
+        def _(at=at):
+            for ref, pair in ((parts[2 * at], near), (parts[2 * at + 1], far)):
+                for i in range(2):
+                    place = pl.ds(pl.multiple_of((i ^ small) * sub, sub), sub)
+                    ref[place, :] = pair[i * sub : (i + 1) * sub]
 
 
 def last_blocks(split, rows, width):
     if split:
         block, steps = rows // 4, 4
         place = lambda i, m: (m[0] ^ (1 - i // 2)) * 2 + i % 2
-        part_specs = [
-            pl.BlockSpec((block, width), lambda i, m: (jnp.minimum(i, 1), 0)),
-            pl.BlockSpec((block, width), lambda i, m: (jnp.maximum(i, 2) - 2, 0)),
-        ]
-        part_shapes = [shape((rows // 2, width), low)] * 2
+        part_specs = [pl.BlockSpec((block // 2, width), lambda i, m: (0, 0))] * 8
+        part_shapes = [shape((block // 2, width), low)] * 8
     else:
         block = min(256, rows)
         steps = rows // block
@@ -307,7 +307,7 @@
     _, upper, _, swish = swish_of(both)
     active = (swish * upper).astype(low)
     act_ref[...] = active
-    put_part(split, info_ref, parts, (early_ref[...].astype(full) + dot_tn(active, w_ref[2])).astype(low))
+    put_part(split, info_ref, parts, early_ref[...].astype(full) + dot_tn(active, w_ref[2]))
 
 
 def out_last(n, info, split, pieces, hidden, early):
@@ -343,7 +343,7 @@
     gates_grad = gates_grad_of(both_ref[...], dot_nt(w_ref[2], c_ref[...]))
     grad_ref[...] = gates_grad
     hid = early_ref[...].astype(full) + dot_tn(gates_grad, join_gates(w_ref))
-    put_part(split, info_ref, refs[:-1], hid.astype(low))
+    put_part(split, info_ref, refs[:-1], hid)
 
 
 def hid_last(info, split, weights, both, cot, early):
@@ -969,19 +969,19 @@
             else:
                 load = scatter_load(k - 1, attend_slots, *came)
             coming = scatter_hop(k - 1, *load)
-        beside = ()
+        meanwhile = ()
         if k == 1:
-            active, gates_grad, w_feed = beside = feed_chunk(n, me, [first_piece], hidden, cot)
+            active, gates_grad, w_feed = meanwhile = feed_chunk(n, me, [first_piece], hidden, cot)
         elif k == 2:
-            hid_early, out_early = beside = early_parts(
+            hid_early, out_early = meanwhile = early_parts(
                 active, gates_grad, w_feed, hid_early, out_early
             )
         elif k == 3:
-            first_grads = beside = feed_grads(n, hidden, cot, active, gates_grad)
+            first_grads = meanwhile = feed_grads(n, hidden, cot, active, gates_grad)
         if k > 1:
-            (right, left), came = after(((right, left), coming), beside)
+            (right, left), came = after(((right, left), coming), meanwhile)
         else:
-            right, left = after((right, left), beside)
+            right, left = after((right, left), meanwhile)
         rights.append(right)
         lefts.append(left)
     last_pieces = [last_shard] + rights[1:] + lefts[1:]
@@ -1007,11 +1007,14 @@
     states += [jnp.transpose(a) for a in (w_reduce, moment_reduce, average_reduce)]
 
     if fast:
-        e = rows // 8
-        s = e // 2
+        s = rows // 16
+
+        def swap_cores(parts):
+            came = {i: swap(parts[i], 1) for i in (1, 3, 0, 2)}
+            return [came[i] for i in range(4)]
 
         def sum_cores(own, came):
-            own = [own[i * e : (i + 1) * e].astype(full) + came[i * e : (i + 1) * e].astype(full) for i in range(4)]
+            own = [a.astype(full) + b.astype(full) for a, b in zip(own, came)]
             return own, (own[1].astype(low), own[3].astype(low))
 
         def sum_first(own, came):
@@ -1027,21 +1030,14 @@
             pieces = (one, first, second, third)
             return pack_rows(info, [p[0] for p in pieces] + [p[1] for p in pieces])
 
-        other_out, own_out, active, both, w_last = out_last(
-            n, info, True, last_pieces, hidden, out_early
-        )
-        came_out = swap(other_out, 1)
-        load = scatter_load(n - 1, after(attend_slots, other_out), *came)
-        came_out = after(came_out, load)
-        own_out, load_out = sum_cores(own_out, came_out)
+        *parts, active, both, w_last = out_last(n, info, True, last_pieces, hidden, out_early)
+        own_out, load_out = sum_cores(parts[4:], swap_cores(parts[:4]))
         one_out = both_ways(load_out, (2, 4))
-        other_hid, own_hid, gates_grad = hid_last(
-            info, True, w_last, after(both, load_out), cot, hid_early
-        )
-        came_hid = swap(other_hid, 1)
-        near_out, load_out = sum_first(own_out, after(one_out, other_hid))
+        *parts, gates_grad = hid_last(info, True, w_last, after(both, load_out), cot, hid_early)
+        came_hid = swap_cores(parts[:4])
+        near_out, load_out = sum_first(own_out, after(one_out, parts[0]))
         two_out = both_ways(load_out, (4, 2))
-        own_hid, load_hid = sum_cores(own_hid, after(came_hid, load_out))
+        own_hid, load_hid = sum_cores(parts[4:], after(came_hid, load_out))
         one_hid = both_ways(load_hid, (2, 4))
         last_grads = feed_grads(n, hidden, cot, after(active, load_hid), gates_grad)
         two_out = after(two_out, last_grads)
@@ -1051,24 +1047,22 @@
         out_two = both_ways(add, (2, 4))
         near_hid, load_hid = sum_first(own_hid, after(one_hid, add))
         two_hid = both_ways(load_hid, (4, 2))
-        came = scatter_hop(n - 1, *after(load, load_hid))
-        out_one = after(out_one, load_hid)
-        out_three = both_ways(out_one, (2, 4))
-        two_hid = after(two_hid, out_one)
         back = back_rows(info, tokens, near_hid, two_hid, norm_params)
         hid_one = both_ways(back, (4, 2))
         hid_two = both_ways(back, (2, 4))
-        begun = update_feed(0, after(first_grads, back), states, rates)
-        hid_one = after(hid_one, begun)
+        out_one, out_two = after((out_one, out_two), back)
+        out_three = both_ways(out_one, (2, 4))
+        begun = update_feed(0, after(first_grads, out_one), states, rates)
+        hid_one, hid_two = after((hid_one, hid_two), begun)
         hid_three = both_ways(hid_one, (2, 4))
-        attend_new = update_attend(after(came, hid_one))
-        out_two, out_three = after((out_two, out_three), attend_new)
+        out_three = after(out_three, hid_one)
         mine_out = join(add, out_one, out_two, out_three)
         other_out = swap(mine_out, 1)
         output = finish_rows(info, rows, 0, mine_out)
         output = finish_rows(info, rows, 1, after(other_out, output), begun=output)
         done = update_feed(cut, after(last_grads, output), states, rates, begun)
-        hid_two, hid_three = after((hid_two, hid_three), done)
+        came = scatter_hop(n - 1, *scatter_load(n - 1, after(attend_slots, done), *came))
+        hid_three = after(hid_three, done)
         mine_hid = join(back, hid_one, hid_two, hid_three)
         other_hid = swap(mine_hid, 1)
         input_grad = finish_rows(info, rows, 0, mine_hid, cot)
@@ -1076,6 +1070,7 @@
         norm_part = tail_sums(mine_hid, other_hid)
         sums = small_sum(join_sums(norm_part, bias_part), "dp")
         input_grad = finish_rows(info, rows, 1, after(other_hid, norm_part), cot, input_grad)
+        attend_new = update_attend(after(came, input_grad))
         norm_grad, bias_grad = split_sums(sums, norm_part, bias_part)
     else:
         out_part, active, both, w_last = out_last(n, info, False, last_pieces, hidden, out_early)

time: 568 us -> 555 us (0.977)
  waiting for transfers between devices: 170 us -> 146 us
  starting transfers between devices: 52.9 us -> 61.5 us
    ppermute x2, waiting for transfers between devices: 27.1 us -> 0.01 us  [scatter_hop(): lax.ppermute(to_left, 'dp', lefts)]
    ppermute x2, waiting for transfers between devices: 14.7 us -> 4.96 us  [scatter_hop(): lax.ppermute(to_right, 'dp', rights)]
    ppermute x26 -> x32, waiting for transfers between devices: 57.5 us -> 65.3 us  [swap(): return lax.ppermute(value, axis, [(a, a ^ mask) for a in range(n)])]
    ppermute x26 -> x32, starting transfers between devices: 22.6 us -> 30.1 us  [swap(): return lax.ppermute(value, axis, [(a, a ^ mask) for a in range(n)])]
  transfers between devices with their start and end apart: 40 -> 46, of which waited for: 18 -> 22; matrix products, arithmetic and copies ran while one was open for 7% -> 6% of each run, Pallas kernels for 43% -> 49%
where the time goes in v4:
time: 555 us; the launch traced here: 544 us
  Pallas kernels  272 us (49%)
  waiting for transfers between devices  146 us (26%)
  starting transfers between devices  61.5 us (11%)
  other arithmetic  39.4 us (7%)
  between operations  15 us (3%)
  local copies, waits for them, and re-layouts  10.8 us (2%)
    ppermute x32, waiting for transfers between devices, swap(): return lax.ppermute(value, axis, [(a, a ^ mask) for a in range(n)])  65.3 us
    all_gather x1, waiting for transfers between devices, body(): attend_pieces = [lax.all_gather(attend_shard, 'dp')]  62.9 us
    pallas_call x1, Pallas kernels, attend(): pl.pallas_call(functools.partial(attend_kernel, min(512, length)), grid=(...  34 us
    pallas_call x2, Pallas kernels, feed_grads(): pl.pallas_call(functools.partial(feed_grads_kernel, n, steps), grid=(step...  32.3 us
    ppermute x32, starting transfers between devices, swap(): return lax.ppermute(value, axis, [(a, a ^ mask) for a in range(n)])  30.1 us
    pallas_call x4, Pallas kernels, finish_rows(): pl.pallas_call(finish_kernel, grid_spec=pltpu.PrefetchScalarGridSpec(num_...  26.8 us
    pallas_call x1, Pallas kernels, out_last(): pl.pallas_call(functools.partial(out_last_kernel, n, count, split), grid_...  24.8 us
    pallas_call x1, Pallas kernels, hid_last(): pl.pallas_call(functools.partial(hid_last_kernel, split), grid_spec=pltpu...  22.2 us
  transfers between devices with their start and end apart: 46, of which 22 were waited for; matrix products, arithmetic and copies ran while one was open for 6% of the time, Pallas kernels for 49%

profile of v4, /device:TPU:0, one launch (start us, length us, event | category | flops | bytes accessed | tf_op | source)
XLA Modules:
  0.0 544.4 jit_solution(12812805156884028046)
XLA Ops:
  8.3 1.5 convert_bitcast_fusion
  11.0 1.6 bitcast_convert_fusion
  14.6 11.2 %layer_norm.1.refs_1_.h_ref.refs_7_ = bf16[2048,2048]{1,0:T(8,128)(2,1)} custom-call(bf16[2048,2048]{1,0:T(8,128)(2,1)} %bitcast.48, f32[2,2048]{1,0:T(2,128)} %refs_6_.1), custom_call_target="tpu_custom_call" | custom-call | flops 33554432 | bytes 16777216 | tf_op jit(solution)/shard_map/layer_norm/pallas_call | solution.py:126
  26.0 5.6 %fusion.4 = (f32[2048,128]{1,0:T(8,128)}, f32[2048,128]{1,0:T(8,128)}) fusion(f32[128]{0:T(128)S(1)} %fusion.9, f32[2048]{0:T(1024)S(1)} %bitcast.85, pred[128]{0:T(512)(128)(4,1)S(1)} %get-tuple-element.283, pred[128]{0:T(512)(128)(4,1)S(1)} %get-tuple-element.284), kind=kLoop, calls=%fused_computation.26 | loop fusion | flops 1310720 | bytes 2106112 | tf_op jit(solution)/shard_map/jit(_where)/select_n | solution.py:952
  31.6 62.9 %all-gather.4.cloned.1.call-done.refs_0_ = bf16[4,4,512,256]{3,2,1,0:T(8,128)(2,1)} async-done(((bf16[1,4,512,256]{3,2,1,0:T(8,128)(2,1)}), bf16[4,4,512,256]{3,2,1,0:T(8,128)(2,1)}) %all-gather.4.cloned.1.call-update) | async-done | bytes 4194320 | tf_op jit(solution)/shard_map/all_gather | solution.py:939
  94.5 17.4 %project.1 = (bf16[2048,256]{1,0:T(8,128)(2,1)}, bf16[2048,256]{1,0:T(8,128)(2,1)}, bf16[2048,256]{1,0:T(8,128)(2,1)}, bf16[2048,256]{1,0:T(8,128)(2,1)}, bf16[4,2048,256]{2,1,0:T(8,128)(2,1)}) custom-call(s32[1]{0:T(128)} %bitcast.3.me_ref, bf16[4,4,512,256]{3,2,1,0:T(8,128)(2,1)} %all-gather.4.cloned.1.call-done.refs_0_, ...), custom_call_target="tpu_custom_call" | custom-call | flops 8589934592 | bytes 25165824 | tf_op jit(solution)/shard_map/project/pallas_call | solution.py:450
  112.0 34.0 %attend.1 = (bf16[2048,256]{1,0:T(8,128)(2,1)}, bf16[3,2048,256]{2,1,0:T(8,128)(2,1)}, f32[3,256]{1,0:T(4,128)}) custom-call(bf16[2048,256]{1,0:T(8,128)(2,1)} %get-tuple-element.139.q_ref, bf16[2048,256]{1,0:T(8,128)(2,1)} %get-tuple-element.140.k_ref, bf16[2048,256]{1,0:T(8,128)(2,1)} %get-tuple-element.141.v_ref, ...), custom_call_target="tpu_custom_call" | custom-call | flops 21474836480 | bytes 10485760 | tf_op jit(solution)/shard_map/attend/pallas_call | solution.py:530
  145.9 16.9 %attend_grads.1 = (f32[4,512,256]{2,1,0:T(8,128)}, bf16[4,512,256]{2,1,0:T(8,128)(2,1)}, bf16[4,512,256]{2,1,0:T(8,128)(2,1)}, bf16[4,512,256]{2,1,0:T(8,128)(2,1)}, bf16[4,512,256]{2,1,0:T(8,128)(2,1)}) custom-call(s32[1]{0:T(128)} %bitcast.3.me_ref, bf16[2048,2048]{1,0:T(8,128)(2,1)} %layer_norm.1.refs_1_.h_ref.refs_7_, bf16[2048,2048]{1,0:T(8,128)(2,1)} %bitcast.56, ...), custom_call_target="tpu_custom_call" | custom-call | flops 8589934592 | bytes 25165824 | tf_op jit(solution)/shard_map/attend_grads/pallas_call | solution.py:589
  162.8 14.6 %heads_parts.1 = (bf16[2048,2048]{1,0:T(8,128)(2,1)}, bf16[2048,2048]{1,0:T(8,128)(2,1)}) custom-call(bf16[2048,256]{1,0:T(8,128)(2,1)} %get-tuple-element.144.ctx_ref, bf16[3,2048,256]{2,1,0:T(8,128)(2,1)} %get-tuple-element.143.mg_ref, bf16[4,2048,256]{2,1,0:T(8,128)(2,1)} %get-tuple-element.150.wa_ref), custom_call_target="tpu_custom_call" | custom-call | flops 8589934592 | bytes 25165824 | tf_op jit(solution)/shard_map/heads_parts/pallas_call | solution.py:621
  179.4 5.5 %collective-permute-start = (bf16[3,352,512]{2,1,0:T(8,128)(2,1)S(1)}, bf16[3,352,512]{2,1,0:T(8,128)(2,1)}, u32[]{:S(2)}, u32[]{:S(2)}) collective-permute-start(bf16[3,352,512]{2,1,0:T(8,128)(2,1)S(1)} %pad_maximum_fusion.refs_0_), channel_id=1, source_target_pairs={{0,8},{8,16},{16,24},{1,9},{9,17},{17,25},{2,10},{10,18},{18,26},{... | collective-permute-start | bytes 3244040 | tf_op jit(solution)/shard_map/ppermute | solution.py:68
  185.0 16.5 %feed_chunk.1 = (bf16[352,2048]{1,0:T(8,128)(2,1)}, bf16[704,2048]{1,0:T(8,128)(2,1)}, bf16[3,352,2048]{2,1,0:T(8,128)(2,1)}) custom-call(s32[1]{0:T(128)} %bitcast.3.me_ref, bf16[4,3,352,512]{3,2,1,0:T(8,128)(2,1)} %bitcast.86, bf16[2048,2048]{1,0:T(8,128)(2,1)} %layer_norm.1.refs_1_.h_ref.refs_7_, bf16[2048,2048]{1,0:T(8,128)(2,1)} %bitcast.57), custom_call_target="tpu_custom_call" | custom-call | flops 8858370048 | bytes 25427968 | tf_op jit(solution)/shard_map/feed_chunk/pallas_call | solution.py:231
  201.5 4.3 collective-permute-done.1.refs_4_
  208.9 7.6 %collective-permute-start.4 = (bf16[4,512,256]{2,1,0:T(8,128)(2,1)}, bf16[4,512,256]{2,1,0:T(8,128)(2,1)}, u32[]{:S(2)}, u32[]{:S(2)}) collective-permute-start(bf16[4,512,256]{2,1,0:T(8,128)(2,1)} %get-tuple-element.161), channel_id=1, source_target_pairs={{0,8},{24,16},{1,9},{25,17},{2,10},{26,18},{3,11},{27,19},{4,12},{... | collective-permute-start | bytes 3145736 | tf_op jit(solution)/shard_map/ppermute | solution.py:85
  216.5 19.7 %early_parts.1 = (bf16[2048,2048]{1,0:T(8,128)(2,1)}, bf16[2048,2048]{1,0:T(8,128)(2,1)}) custom-call(bf16[352,2048]{1,0:T(8,128)(2,1)} %get-tuple-element.155.act_ref, bf16[704,2048]{1,0:T(8,128)(2,1)} %get-tuple-element.156.grad_ref, bf16[3,352,2048]{2,1,0:T(8,128)(2,1)} %get-tuple-element.157.w_ref, bf16[2048,2048]{1,0:T(8,128)(2,1)} %get-tuple-element.162.hid_in_ref, ...), custom_call_target="tpu_custom_call" | custom-call | flops 8858370048 | bytes 42205184 | tf_op jit(solution)/shard_map/early_parts/pallas_call | solution.py:649
  237.2 4.1 fusion.1
  241.2 1.6 collective-permute-start.7
  242.9 5.1 collective-permute-start.6
  249.4 16.1 %feed_grads.2 = bf16[4,1056,512]{2,1,0:T(8,128)(2,1)} custom-call(bf16[2048,2048]{1,0:T(8,128)(2,1)} %layer_norm.1.refs_1_.h_ref.refs_7_, bf16[2048,2048]{1,0:T(8,128)(2,1)} %bitcast.58, bf16[352,2048]{1,0:T(8,128)(2,1)} %get-tuple-element.155.act_ref, bf16[704,2048]{1,0:T(8,128)(2,1)} %get-tuple-element.156.grad_ref), custom_call_target="tpu_custom_call" | custom-call | flops 8858370048 | bytes 25427968 | tf_op jit(solution)/shard_map/feed_grads/pallas_call | solution.py:387
  266.1 1.4 collective-permute-done.6
  267.6 5.7 %collective-permute-done.5.refs_3_.refs_6_ = bf16[3,352,512]{2,1,0:T(8,128)(2,1)S(1)} collective-permute-done((bf16[3,352,512]{2,1,0:T(8,128)(2,1)S(1)}, bf16[3,352,512]{2,1,0:T(8,128)(2,1)S(1)}, u32[]{:S(2)}, u32[]{:S(2)}) %collective-permute-start.5) | collective-permute-done | bytes 1081376 | tf_op jit(solution)/shard_map/ppermute | solution.py:66
  274.2 24.8 %out_last.1 = (bf16[256,2048]{1,0:T(8,128)(2,1)}, bf16[256,2048]{1,0:T(8,128)(2,1)}, bf16[256,2048]{1,0:T(8,128)(2,1)}, bf16[256,2048]{1,0:T(8,128)(2,1)}, bf16[...) custom-call(s32[4]{0:T(128)} %pad_add_fusion.info_ref, ...), custom_call_target="tpu_custom_call" | custom-call | flops 8858370048 | bytes 33554432 | tf_op jit(solution)/shard_map/out_last/pallas_call | solution.py:319
  299.6 2.4 collective-permute-done.9
  302.0 1.6 add_convert_fusion.9
  303.6 1.4 collective-permute-start.10
  305.5 1.5 collective-permute-start.12
  307.5 22.2 %hid_last.1 = (bf16[256,2048]{1,0:T(8,128)(2,1)}, bf16[256,2048]{1,0:T(8,128)(2,1)}, bf16[256,2048]{1,0:T(8,128)(2,1)}, bf16[256,2048]{1,0:T(8,128)(2,1)}, bf16[...) custom-call(s32[4]{0:T(128)} %pad_add_fusion.info_ref, ...), custom_call_target="tpu_custom_call" | custom-call | flops 8858370048 | bytes 33554432 | tf_op jit(solution)/shard_map/hid_last/pallas_call | solution.py:355
  331.1 2.1 add_convert_fusion.7
  334.6 2.1 add_convert_fusion.6
  338.5 1.5 collective-permute-start.25
  341.1 16.3 %feed_grads.3 = bf16[4,1056,512]{2,1,0:T(8,128)(2,1)} custom-call(bf16[2048,2048]{1,0:T(8,128)(2,1)} %layer_norm.1.refs_1_.h_ref.refs_7_, bf16[2048,2048]{1,0:T(8,128)(2,1)} %bitcast.60, bf16[352,2048]{1,0:T(8,128)(2,1)} %get-tuple-element.195.act_ref, bf16[704,2048]{1,0:T(8,128)(2,1)} %get-tuple-element.196.grad_ref), custom_call_target="tpu_custom_call" | custom-call | flops 8858370048 | bytes 25427968 | tf_op jit(solution)/shard_map/feed_grads/pallas_call | solution.py:387
  358.5 1.4 collective-permute-start.15
  359.9 14.9 %collective-permute-done.14.refs_4_ = bf16[128,2048]{1,0:T(8,128)(2,1)S(1)} collective-permute-done((bf16[128,2048]{1,0:T(8,128)(2,1)S(1)}, bf16[128,2048]{1,0:T(8,128)(2,1)S(1)}, u32[]{:S(2)}, u32[]{:S(2)}) %collective-permute-start.14) | collective-permute-done | bytes 524320 | tf_op jit(solution)/shard_map/ppermute | solution.py:92
  374.8 1.7 collective-permute-done.15.refs_5_
  377.3 3.8 add_rows.1
  381.2 2.1 add_convert_fusion.3
  385.0 1.8 add_convert_fusion.2
  389.6 1.4 collective-permute-start.22
  393.0 9.5 %collective-permute-done.27.refs_5_ = bf16[128,2048]{1,0:T(8,128)(2,1)S(1)} collective-permute-done((bf16[128,2048]{1,0:T(8,128)(2,1)S(1)}, bf16[128,2048]{1,0:T(8,128)(2,1)S(1)}, u32[]{:S(2)}, u32[]{:S(2)}) %collective-permute-start.27) | collective-permute-done | bytes 524320 | tf_op jit(solution)/shard_map/ppermute | solution.py:92
  404.0 5.5 %back_rows.1 = (bf16[144,2048]{1,0:T(8,128)(2,1)}, bf16[128,2048]{1,0:T(8,128)(2,1)}) custom-call(s32[4]{0:T(128)} %pad_add_fusion.info_ref, bf16[2048,2048]{1,0:T(8,128)(2,1)} %bitcast.51, bf16[2048,2048]{1,0:T(8,128)(2,1)} %bitcast.52, bf16[128,2048]{1,0:T(8,128)(2,1)} %get-tuple-element.272.refs_2_, bf16[128,2048]{1,0:T(8,128)(2,1)} %get-tuple-element.270.refs_3_, ...), custom_call_target="tpu_custom_call" | custom-call | flops 10485760 | bytes 4194304 | tf_op jit(solution)/shard_map/back_rows/pallas_call | solution.py:704
  410.8 2.9 collective-permute-done.22.refs_2_
  415.8 9.9 %collective-permute-done.23.refs_6_ = bf16[128,2048]{1,0:T(8,128)(2,1)S(1)} collective-permute-done((bf16[128,2048]{1,0:T(8,128)(2,1)S(1)}, bf16[128,2048]{1,0:T(8,128)(2,1)S(1)}, u32[]{:S(2)}, u32[]{:S(2)}) %collective-permute-start.23) | collective-permute-done | bytes 524320 | tf_op jit(solution)/shard_map/ppermute | solution.py:92
  425.7 1.4 collective-permute-start.31
  427.7 9.2 %collective-permute-done.33.refs_6_ = bf16[128,2048]{1,0:T(8,128)(2,1)S(1)} collective-permute-done((bf16[128,2048]{1,0:T(8,128)(2,1)}, bf16[128,2048]{1,0:T(8,128)(2,1)S(1)}, u32[]{:S(2)}, u32[]{:S(2)}) %collective-permute-start.33) | collective-permute-done | bytes 524320 | tf_op jit(solution)/shard_map/ppermute | solution.py:92
  438.2 7.0 %update_feed.2 = (f32[2,704,512]{2,1,0:T(8,128)}, f32[2,704,512]{2,1,0:T(8,128)}, f32[2,704,512]{2,1,0:T(8,128)}, f32[2,704,512]{2,1,0:T(8,128)}, f32[704,512]{1...) custom-call(bf16[3,352,512]{2,1,0:T(8,128)(2,1)} %bitcast.84, f32[2,704,512]{2,1,0:T(8,128)} %bitcast.63, ...), custom_call_target="tpu_custom_call" | custom-call | flops 5406720 | bytes 16220160 | tf_op jit(solution)/shard_map/update_feed/pallas_call | solution.py:881
  445.2 3.7 collective-permute-done.31.refs_5_
  449.5 8.5 %collective-permute-done.28.refs_3_ = bf16[128,2048]{1,0:T(8,128)(2,1)S(1)} collective-permute-done((bf16[128,2048]{1,0:T(8,128)(2,1)}, bf16[128,2048]{1,0:T(8,128)(2,1)S(1)}, u32[]{:S(2)}, u32[]{:S(2)}) %collective-permute-start.28) | collective-permute-done | bytes 524320 | tf_op jit(solution)/shard_map/ppermute | solution.py:92
  458.8 4.9 pack_rows.2.refs_0_
  464.9 1.6 collective-permute-start.36
  466.5 5.4 finish_rows.4.refs_1_
  471.9 5.4 finish_rows.5
  477.4 7.0 %update_feed.3 = (f32[2,704,512]{2,1,0:T(8,128)}, f32[2,704,512]{2,1,0:T(8,128)}, f32[2,704,512]{2,1,0:T(8,128)}, f32[2,704,512]{2,1,0:T(8,128)}, f32[704,512]{1...) custom-call(bf16[3,352,512]{2,1,0:T(8,128)(2,1)} %bitcast.83, ...), custom_call_target="tpu_custom_call", output_to_operand_aliasing={{0}: (7, {}), {1}: (8, {}), {2}: (9, {}), {3}: (10, {}), {4... | custom-call | flops 5406720 | bytes 16220160 | tf_op jit(solution)/shard_map/update_feed/pallas_call | solution.py:881
  485.4 5.2 pack_rows.3.refs_0_.own_ref
  490.7 1.5 add_convert_fusion
  493.6 2.5 add_convert_fusion.1
  496.1 5.5 %collective-permute-start.38 = (bf16[4,512,256]{2,1,0:T(8,128)(2,1)}, bf16[4,512,256]{2,1,0:T(8,128)(2,1)}, u32[]{:S(2)}, u32[]{:S(2)}) collective-permute-start(bf16[4,512,256]{2,1,0:T(8,128)(2,1)} %add_convert_fusion.1), channel_id=1, source_target_pairs={{0,8},{8,16},{16,24},{1,9},{9,17},{17,25},{2,10},{10,18},{18,26},{... | collective-permute-start | bytes 3145736 | tf_op jit(solution)/shard_map/ppermute | solution.py:87
  501.6 8.1 %finish_rows.6.refs_2_ = f32[2048,2048]{1,0:T(8,128)} custom-call(s32[4]{0:T(128)} %pad_add_fusion.info_ref, bf16[1088,2048]{1,0:T(8,128)(2,1)} %pack_rows.3.refs_0_.own_ref, bf16[2048,2048]{1,0:T(8,128)(2,1)} %bitcast.61), custom_call_target="tpu_custom_call" | custom-call | flops 4194304 | bytes 16777216 | tf_op jit(solution)/shard_map/finish_rows/pallas_call | solution.py:843
  509.7 1.7 tail_sums.1
  512.2 8.0 %finish_rows.7 = f32[2048,2048]{1,0:T(8,128)} custom-call(s32[4]{0:T(128)} %pad_add_fusion.info_ref, bf16[1088,2048]{1,0:T(8,128)(2,1)} %collective-permute-done.37.other_ref.refs_0_, bf16[2048,2048]{1,0:T(8,128)(2,1)} %bitcast.62, f32[2048,2048]{1,0:T(8,128)} %finish_rows.6.refs_2_), custom_call_target="tpu_custom_call", output_to_operand_aliasing={{}: (3, {})} | custom-call | flops 4194304 | bytes 16777216 | tf_op jit(solution)/shard_map/finish_rows/pallas_call | solution.py:843
  520.1 3.5 collective-permute-done.38
  523.7 2.6 collective-permute-start.40
  526.2 1.8 convert_add_fusion.2
  528.1 3.1 multiply_add_fusion
  531.3 2.3 collective-permute-start.41
  533.6 1.4 multiply_add_fusion.2
  (195 shorter events, 43.9 us)
Async XLA Ops:
  7.2 87.3 %all-gather.4.cloned.1.call-start = ((), (), s32[]{:S(2)}) async-start(), calls=%async_computation.2 | async-start | bytes 5242880 | tf_op jit(solution)/shard_map/all_gather | solution.py:939
  10.9 167.2 %all-gather.6.cloned.1.call-start = ((), (), s32[]{:S(2)}) async-start(), calls=%async_computation.5 | async-start | bytes 5406720 | tf_op jit(solution)/shard_map/all_gather | solution.py:941
  14.5 423.7 %reduce-scatter.3.cloned.1.call-start = ((), (), s32[]{:S(2)}) async-start(), calls=%async_computation.3 | async-start | bytes 5406720 | tf_op jit(solution)/shard_map/reduce_scatter | solution.py:990
  26.0 153.5 %copy-start.6 = (bf16[3,352,512]{2,1,0:T(8,128)(2,1)}, bf16[3,352,512]{2,1,0:T(8,128)(2,1)S(1)}, u32[]{:S(2)}) copy-start(bf16[3,352,512]{2,1,0:T(8,128)(2,1)S(1)} %pad_maximum_fusion.refs_0_) | copy-start | bytes 3244036
  178.1 27.6 %collective-permute-start.1 = (bf16[3,352,512]{2,1,0:T(8,128)(2,1)S(1)}, bf16[3,352,512]{2,1,0:T(8,128)(2,1)}, u32[]{:S(2)}, u32[]{:S(2)}) collective-permute-start(bf16[3,352,512]{2,1,0:T(8,128)(2,1)S(1)} %pad_maximum_fusion.refs_0_), channel_id=1, source_target_pairs={{8,0},{16,8},{24,16},{9,1},{17,9},{25,17},{10,2},{18,10},{26,18},{... | collective-permute-start | bytes 3244040 | tf_op jit(solution)/shard_map/ppermute | solution.py:68
  179.4 27.4 %collective-permute-start = (bf16[3,352,512]{2,1,0:T(8,128)(2,1)S(1)}, bf16[3,352,512]{2,1,0:T(8,128)(2,1)}, u32[]{:S(2)}, u32[]{:S(2)}) collective-permute-start(bf16[3,352,512]{2,1,0:T(8,128)(2,1)S(1)} %pad_maximum_fusion.refs_0_), channel_id=1, source_target_pairs={{0,8},{8,16},{16,24},{1,9},{9,17},{17,25},{2,10},{10,18},{18,26},{... | collective-permute-start | bytes 3244040 | tf_op jit(solution)/shard_map/ppermute | solution.py:68
  206.8 30.3 %collective-permute-start.2 = (bf16[3,352,512]{2,1,0:T(8,128)(2,1)}, bf16[3,352,512]{2,1,0:T(8,128)(2,1)S(1)}, u32[]{:S(2)}, u32[]{:S(2)}) collective-permute-start(bf16[3,352,512]{2,1,0:T(8,128)(2,1)} %collective-permute-done.refs_1_), channel_id=1, source_target_pairs={{8,16},{16,24},{9,17},{17,25},{10,18},{18,26},{11,19},{19,27},{12,... | collective-permute-start | bytes 3244040 | tf_op jit(solution)/shard_map/ppermute | solution.py:68
  207.6 29.6 %collective-permute-start.3 = (bf16[3,352,512]{2,1,0:T(8,128)(2,1)}, bf16[3,352,512]{2,1,0:T(8,128)(2,1)S(1)}, u32[]{:S(2)}, u32[]{:S(2)}) collective-permute-start(bf16[3,352,512]{2,1,0:T(8,128)(2,1)} %collective-permute-done.1.refs_4_), channel_id=1, source_target_pairs={{8,0},{16,8},{9,1},{17,9},{10,2},{18,10},{11,3},{19,11},{12,4},{20... | collective-permute-start | bytes 3244040 | tf_op jit(solution)/shard_map/ppermute | solution.py:68
  208.9 28.3 %collective-permute-start.4 = (bf16[4,512,256]{2,1,0:T(8,128)(2,1)}, bf16[4,512,256]{2,1,0:T(8,128)(2,1)}, u32[]{:S(2)}, u32[]{:S(2)}) collective-permute-start(bf16[4,512,256]{2,1,0:T(8,128)(2,1)} %get-tuple-element.161), channel_id=1, source_target_pairs={{0,8},{24,16},{1,9},{25,17},{2,10},{26,18},{3,11},{27,19},{4,12},{... | collective-permute-start | bytes 3145736 | tf_op jit(solution)/shard_map/ppermute | solution.py:85
  216.5 20.6 %copy-start.21 = (bf16[4,512,256]{2,1,0:T(8,128)(2,1)S(1)}, bf16[4,512,256]{2,1,0:T(8,128)(2,1)}, u32[]{:S(2)}) copy-start(bf16[4,512,256]{2,1,0:T(8,128)(2,1)} %get-tuple-element.168) | copy-start | bytes 3145732
  237.1 10.8 %copy-start.7 = (bf16[3,352,512]{2,1,0:T(8,128)(2,1)}, bf16[3,352,512]{2,1,0:T(8,128)(2,1)S(1)}, u32[]{:S(2)}) copy-start(bf16[3,352,512]{2,1,0:T(8,128)(2,1)S(1)} %collective-permute-done.2.refs_2_) | copy-start | bytes 3244036
  237.1 10.8 %copy-start.8 = (bf16[3,352,512]{2,1,0:T(8,128)(2,1)}, bf16[3,352,512]{2,1,0:T(8,128)(2,1)S(1)}, u32[]{:S(2)}) copy-start(bf16[3,352,512]{2,1,0:T(8,128)(2,1)S(1)} %collective-permute-done.3.refs_5_) | copy-start | bytes 3244036
  241.2 24.9 %collective-permute-start.7 = (bf16[4,512,256]{2,1,0:T(8,128)(2,1)}, bf16[4,512,256]{2,1,0:T(8,128)(2,1)}, u32[]{:S(2)}, u32[]{:S(2)}) collective-permute-start(bf16[4,512,256]{2,1,0:T(8,128)(2,1)} %get-tuple-element.277), channel_id=1, source_target_pairs={{24,16},{16,8},{25,17},{17,9},{26,18},{18,10},{27,19},{19,11},{28,... | collective-permute-start | bytes 3145736 | tf_op jit(solution)/shard_map/ppermute | solution.py:87
  242.9 24.7 %collective-permute-start.6 = (bf16[4,512,256]{2,1,0:T(8,128)(2,1)}, bf16[4,512,256]{2,1,0:T(8,128)(2,1)}, u32[]{:S(2)}, u32[]{:S(2)}) collective-permute-start(bf16[4,512,256]{2,1,0:T(8,128)(2,1)} %get-tuple-element.278), channel_id=1, source_target_pairs={{0,8},{8,16},{1,9},{9,17},{2,10},{10,18},{3,11},{11,19},{4,12},{12... | collective-permute-start | bytes 3145736 | tf_op jit(solution)/shard_map/ppermute | solution.py:87
  248.1 25.2 %collective-permute-start.5 = (bf16[3,352,512]{2,1,0:T(8,128)(2,1)S(1)}, bf16[3,352,512]{2,1,0:T(8,128)(2,1)S(1)}, u32[]{:S(2)}, u32[]{:S(2)}) collective-permute-start(bf16[3,352,512]{2,1,0:T(8,128)(2,1)S(1)} %broadcast_select_fusion), channel_id=1, source_target_pairs={{16,24},{8,0},{17,25},{9,1},{18,26},{10,2},{19,27},{11,3},{20,28},... | collective-permute-start | bytes 3244040 | tf_op jit(solution)/shard_map/ppermute | solution.py:66
  265.5 211.9 %reduce-scatter.5.cloned.1.call-start = ((), (), s32[]{:S(2)}) async-start(), calls=%async_computation.4 | async-start | bytes 5406720 | tf_op jit(solution)/shard_map/reduce_scatter | solution.py:990
  299.1 6.0 %copy-start.13 = (bf16[256,2048]{1,0:T(8,128)(2,1)S(1)}, bf16[256,2048]{1,0:T(8,128)(2,1)}, u32[]{:S(2)}) copy-start(bf16[256,2048]{1,0:T(8,128)(2,1)} %get-tuple-element.177) | copy-start | bytes 3145732
  299.1 2.9 collective-permute-start.9
  299.1 5.9 %collective-permute-start.11 = (bf16[256,2048]{1,0:T(8,128)(2,1)}, bf16[256,2048]{1,0:T(8,128)(2,1)S(1)}, u32[]{:S(2)}, u32[]{:S(2)}) collective-permute-start(bf16[256,2048]{1,0:T(8,128)(2,1)} %get-tuple-element.178), channel_id=1, source_target_pairs={{0,1},{1,0},{2,3},{3,2},{4,5},{5,4},{6,7},{7,6},{8,9},{9,8},{10,11... | collective-permute-start | bytes 3145736 | tf_op jit(solution)/shard_map/ppermute | solution.py:92
  303.6 26.1 %collective-permute-start.10 = (bf16[256,2048]{1,0:T(8,128)(2,1)S(1)}, bf16[256,2048]{1,0:T(8,128)(2,1)}, u32[]{:S(2)}, u32[]{:S(2)}) collective-permute-start(bf16[256,2048]{1,0:T(8,128)(2,1)S(1)} %add_convert_fusion.9), channel_id=1, source_target_pairs={{0,2},{1,3},{2,0},{3,1},{4,6},{5,7},{6,4},{7,5},{8,10},{9,11},{10,... | collective-permute-start | bytes 3145736 | tf_op jit(solution)/shard_map/ppermute | solution.py:92
  305.5 25.1 %collective-permute-start.12 = (bf16[256,2048]{1,0:T(8,128)(2,1)S(1)}, bf16[256,2048]{1,0:T(8,128)(2,1)}, u32[]{:S(2)}, u32[]{:S(2)}) collective-permute-start(bf16[256,2048]{1,0:T(8,128)(2,1)S(1)} %add_convert_fusion.8), channel_id=1, source_target_pairs={{0,4},{1,5},{2,6},{3,7},{4,0},{5,1},{6,2},{7,3},{8,12},{9,13},{10,... | collective-permute-start | bytes 3145736 | tf_op jit(solution)/shard_map/ppermute | solution.py:92
  307.0 23.6 %collective-permute-start.8 = (bf16[256,2048]{1,0:T(8,128)(2,1)}, bf16[256,2048]{1,0:T(8,128)(2,1)}, u32[]{:S(2)}, u32[]{:S(2)}) collective-permute-start(bf16[256,2048]{1,0:T(8,128)(2,1)} %get-tuple-element.174), channel_id=1, source_target_pairs={{0,1},{1,0},{2,3},{3,2},{4,5},{5,4},{6,7},{7,6},{8,9},{9,8},{10,11... | collective-permute-start | bytes 3145736 | tf_op jit(solution)/shard_map/ppermute | solution.py:92
  307.0 27.0 %collective-permute-start.13 = (bf16[256,2048]{1,0:T(8,128)(2,1)}, bf16[256,2048]{1,0:T(8,128)(2,1)}, u32[]{:S(2)}, u32[]{:S(2)}) collective-permute-start(bf16[256,2048]{1,0:T(8,128)(2,1)} %get-tuple-element.185), channel_id=1, source_target_pairs={{0,1},{1,0},{2,3},{3,2},{4,5},{5,4},{6,7},{7,6},{8,9},{9,8},{10,11... | collective-permute-start | bytes 3145736 | tf_op jit(solution)/shard_map/ppermute | solution.py:92
  307.5 23.6 %copy-start.20 = (bf16[256,2048]{1,0:T(8,128)(2,1)S(1)}, bf16[256,2048]{1,0:T(8,128)(2,1)}, u32[]{:S(2)}) copy-start(bf16[256,2048]{1,0:T(8,128)(2,1)} %get-tuple-element.173) | copy-start | bytes 3145732
  329.7 7.8 %collective-permute-start.17 = (bf16[256,2048]{1,0:T(8,128)(2,1)}, bf16[256,2048]{1,0:T(8,128)(2,1)S(1)}, u32[]{:S(2)}, u32[]{:S(2)}) collective-permute-start(bf16[256,2048]{1,0:T(8,128)(2,1)} %get-tuple-element.189), channel_id=1, source_target_pairs={{0,1},{1,0},{2,3},{3,2},{4,5},{5,4},{6,7},{7,6},{8,9},{9,8},{10,11... | collective-permute-start | bytes 3145736 | tf_op jit(solution)/shard_map/ppermute | solution.py:92
  329.7 7.8 %collective-permute-start.18 = (bf16[256,2048]{1,0:T(8,128)(2,1)}, bf16[256,2048]{1,0:T(8,128)(2,1)S(1)}, u32[]{:S(2)}, u32[]{:S(2)}) collective-permute-start(bf16[256,2048]{1,0:T(8,128)(2,1)} %get-tuple-element.190), channel_id=1, source_target_pairs={{0,1},{1,0},{2,3},{3,2},{4,5},{5,4},{6,7},{7,6},{8,9},{9,8},{10,11... | collective-permute-start | bytes 3145736 | tf_op jit(solution)/shard_map/ppermute | solution.py:92
  330.5 7.0 %collective-permute-start.16 = (bf16[256,2048]{1,0:T(8,128)(2,1)}, bf16[256,2048]{1,0:T(8,128)(2,1)S(1)}, u32[]{:S(2)}, u32[]{:S(2)}) collective-permute-start(bf16[256,2048]{1,0:T(8,128)(2,1)} %get-tuple-element.182), channel_id=1, source_target_pairs={{0,1},{1,0},{2,3},{3,2},{4,5},{5,4},{6,7},{7,6},{8,9},{9,8},{10,11... | collective-permute-start | bytes 3145736 | tf_op jit(solution)/shard_map/ppermute | solution.py:92
  330.6 7.0 %collective-permute-start.19 = (bf16[256,2048]{1,0:T(8,128)(2,1)}, bf16[256,2048]{1,0:T(8,128)(2,1)S(1)}, u32[]{:S(2)}, u32[]{:S(2)}) collective-permute-start(bf16[256,2048]{1,0:T(8,128)(2,1)} %get-tuple-element.191), channel_id=1, source_target_pairs={{0,1},{1,0},{2,3},{3,2},{4,5},{5,4},{6,7},{7,6},{8,9},{9,8},{10,11... | collective-permute-start | bytes 3145736 | tf_op jit(solution)/shard_map/ppermute | solution.py:92
  338.5 42.7 %collective-permute-start.25 = (bf16[256,2048]{1,0:T(8,128)(2,1)S(1)}, bf16[256,2048]{1,0:T(8,128)(2,1)}, u32[]{:S(2)}, u32[]{:S(2)}) collective-permute-start(bf16[256,2048]{1,0:T(8,128)(2,1)S(1)} %add_convert_fusion.4), channel_id=1, source_target_pairs={{0,4},{1,5},{2,6},{3,7},{4,0},{5,1},{6,2},{7,3},{8,12},{9,13},{10,... | collective-permute-start | bytes 3145736 | tf_op jit(solution)/shard_map/ppermute | solution.py:92
  340.4 40.7 %collective-permute-start.24 = (bf16[256,2048]{1,0:T(8,128)(2,1)S(1)}, bf16[256,2048]{1,0:T(8,128)(2,1)}, u32[]{:S(2)}, u32[]{:S(2)}) collective-permute-start(bf16[256,2048]{1,0:T(8,128)(2,1)S(1)} %add_convert_fusion.5), channel_id=1, source_target_pairs={{0,2},{1,3},{2,0},{3,1},{4,6},{5,7},{6,4},{7,5},{8,10},{9,11},{10,... | collective-permute-start | bytes 3145736 | tf_op jit(solution)/shard_map/ppermute | solution.py:92
  357.4 17.4 %collective-permute-start.14 = (bf16[128,2048]{1,0:T(8,128)(2,1)S(1)}, bf16[128,2048]{1,0:T(8,128)(2,1)S(1)}, u32[]{:S(2)}, u32[]{:S(2)}) collective-permute-start(bf16[128,2048]{1,0:T(8,128)(2,1)S(1)} %get-tuple-element.275), channel_id=1, source_target_pairs={{0,4},{1,5},{2,6},{3,7},{4,0},{5,1},{6,2},{7,3},{8,12},{9,13},{10,... | collective-permute-start | bytes 1572872 | tf_op jit(solution)/shard_map/ppermute | solution.py:92
  358.5 18.0 %collective-permute-start.15 = (bf16[128,2048]{1,0:T(8,128)(2,1)S(1)}, bf16[128,2048]{1,0:T(8,128)(2,1)S(1)}, u32[]{:S(2)}, u32[]{:S(2)}) collective-permute-start(bf16[128,2048]{1,0:T(8,128)(2,1)S(1)} %get-tuple-element.273), channel_id=1, source_target_pairs={{0,2},{1,3},{2,0},{3,1},{4,6},{5,7},{6,4},{7,5},{8,10},{9,11},{10,... | collective-permute-start | bytes 1572872 | tf_op jit(solution)/shard_map/ppermute | solution.py:92
  387.7 14.9 %collective-permute-start.27 = (bf16[128,2048]{1,0:T(8,128)(2,1)S(1)}, bf16[128,2048]{1,0:T(8,128)(2,1)S(1)}, u32[]{:S(2)}, u32[]{:S(2)}) collective-permute-start(bf16[128,2048]{1,0:T(8,128)(2,1)S(1)} %get-tuple-element.269), channel_id=1, source_target_pairs={{0,2},{1,3},{2,0},{3,1},{4,6},{5,7},{6,4},{7,5},{8,10},{9,11},{10,... | collective-permute-start | bytes 1572872 | tf_op jit(solution)/shard_map/ppermute | solution.py:92
  388.3 14.9 %collective-permute-start.26 = (bf16[128,2048]{1,0:T(8,128)(2,1)S(1)}, bf16[128,2048]{1,0:T(8,128)(2,1)S(1)}, u32[]{:S(2)}, u32[]{:S(2)}) collective-permute-start(bf16[128,2048]{1,0:T(8,128)(2,1)S(1)} %get-tuple-element.271), channel_id=1, source_target_pairs={{0,4},{1,5},{2,6},{3,7},{4,0},{5,1},{6,2},{7,3},{8,12},{9,13},{10,... | collective-permute-start | bytes 1572872 | tf_op jit(solution)/shard_map/ppermute | solution.py:92
  389.6 24.2 %collective-permute-start.22 = (bf16[128,2048]{1,0:T(8,128)(2,1)S(1)}, bf16[128,2048]{1,0:T(8,128)(2,1)S(1)}, u32[]{:S(2)}, u32[]{:S(2)}) collective-permute-start(bf16[128,2048]{1,0:T(8,128)(2,1)S(1)} %copy-done.25), channel_id=1, source_target_pairs={{0,2},{1,3},{2,0},{3,1},{4,6},{5,7},{6,4},{7,5},{8,10},{9,11},{10,... | collective-permute-start | bytes 1572872 | tf_op jit(solution)/shard_map/ppermute | solution.py:92
  391.0 23.5 %collective-permute-start.20 = (bf16[128,2048]{1,0:T(8,128)(2,1)S(1)}, bf16[128,2048]{1,0:T(8,128)(2,1)}, u32[]{:S(2)}, u32[]{:S(2)}) collective-permute-start(bf16[128,2048]{1,0:T(8,128)(2,1)S(1)} %copy-done.25), channel_id=1, source_target_pairs={{0,4},{1,5},{2,6},{3,7},{4,0},{5,1},{6,2},{7,3},{8,12},{9,13},{10,... | collective-permute-start | bytes 1572872 | tf_op jit(solution)/shard_map/ppermute | solution.py:92
  391.7 33.9 %collective-permute-start.23 = (bf16[128,2048]{1,0:T(8,128)(2,1)S(1)}, bf16[128,2048]{1,0:T(8,128)(2,1)S(1)}, u32[]{:S(2)}, u32[]{:S(2)}) collective-permute-start(bf16[128,2048]{1,0:T(8,128)(2,1)S(1)} %copy-done.26), channel_id=1, source_target_pairs={{0,4},{1,5},{2,6},{3,7},{4,0},{5,1},{6,2},{7,3},{8,12},{9,13},{10,... | collective-permute-start | bytes 1572872 | tf_op jit(solution)/shard_map/ppermute | solution.py:92
  402.6 24.5 %collective-permute-start.21 = (bf16[128,2048]{1,0:T(8,128)(2,1)S(1)}, bf16[128,2048]{1,0:T(8,128)(2,1)}, u32[]{:S(2)}, u32[]{:S(2)}) collective-permute-start(bf16[128,2048]{1,0:T(8,128)(2,1)S(1)} %copy-done.26), channel_id=1, source_target_pairs={{0,2},{1,3},{2,0},{3,1},{4,6},{5,7},{6,4},{7,5},{8,10},{9,11},{10,... | collective-permute-start | bytes 1572872 | tf_op jit(solution)/shard_map/ppermute | solution.py:92
  409.5 27.4 %collective-permute-start.33 = (bf16[128,2048]{1,0:T(8,128)(2,1)}, bf16[128,2048]{1,0:T(8,128)(2,1)S(1)}, u32[]{:S(2)}, u32[]{:S(2)}) collective-permute-start(bf16[128,2048]{1,0:T(8,128)(2,1)} %get-tuple-element.208.refs_4_), channel_id=1, source_target_pairs={{0,4},{1,5},{2,6},{3,7},{4,0},{5,1},{6,2},{7,3},{8,12},{9,13},{10,... | collective-permute-start | bytes 1572872 | tf_op jit(solution)/shard_map/ppermute | solution.py:92
  413.8 23.1 %copy-start.29 = (bf16[128,2048]{1,0:T(8,128)(2,1)}, bf16[128,2048]{1,0:T(8,128)(2,1)S(1)}, u32[]{:S(2)}) copy-start(bf16[128,2048]{1,0:T(8,128)(2,1)S(1)} %collective-permute-done.22.refs_2_) | copy-start | bytes 1572868
  413.8 35.1 %collective-permute-start.32 = (bf16[144,2048]{1,0:T(8,128)(2,1)}, bf16[144,2048]{1,0:T(8,128)(2,1)S(1)}, u32[]{:S(2)}, u32[]{:S(2)}) collective-permute-start(bf16[144,2048]{1,0:T(8,128)(2,1)} %get-tuple-element.207.refs_0_), channel_id=1, source_target_pairs={{0,2},{1,3},{2,0},{3,1},{4,6},{5,7},{6,4},{7,5},{8,10},{9,11},{10,... | collective-permute-start | bytes 1769480 | tf_op jit(solution)/shard_map/ppermute | solution.py:92
  414.5 35.0 %collective-permute-start.30 = (bf16[144,2048]{1,0:T(8,128)(2,1)}, bf16[144,2048]{1,0:T(8,128)(2,1)S(1)}, u32[]{:S(2)}, u32[]{:S(2)}) collective-permute-start(bf16[144,2048]{1,0:T(8,128)(2,1)} %get-tuple-element.207.refs_0_), channel_id=1, source_target_pairs={{0,4},{1,5},{2,6},{3,7},{4,0},{5,1},{6,2},{7,3},{8,12},{9,13},{10,... | collective-permute-start | bytes 1769480 | tf_op jit(solution)/shard_map/ppermute | solution.py:92
  425.7 11.2 %copy-start.30 = (bf16[128,2048]{1,0:T(8,128)(2,1)}, bf16[128,2048]{1,0:T(8,128)(2,1)S(1)}, u32[]{:S(2)}) copy-start(bf16[128,2048]{1,0:T(8,128)(2,1)S(1)} %collective-permute-done.23.refs_6_) | copy-start | bytes 1572868
  425.7 23.2 %collective-permute-start.31 = (bf16[128,2048]{1,0:T(8,128)(2,1)}, bf16[128,2048]{1,0:T(8,128)(2,1)S(1)}, u32[]{:S(2)}, u32[]{:S(2)}) collective-permute-start(bf16[128,2048]{1,0:T(8,128)(2,1)} %get-tuple-element.208.refs_4_), channel_id=1, source_target_pairs={{0,2},{1,3},{2,0},{3,1},{4,6},{5,7},{6,4},{7,5},{8,10},{9,11},{10,... | collective-permute-start | bytes 1572872 | tf_op jit(solution)/shard_map/ppermute | solution.py:92
  427.1 30.9 %collective-permute-start.28 = (bf16[128,2048]{1,0:T(8,128)(2,1)}, bf16[128,2048]{1,0:T(8,128)(2,1)S(1)}, u32[]{:S(2)}, u32[]{:S(2)}) collective-permute-start(bf16[128,2048]{1,0:T(8,128)(2,1)} %collective-permute-done.20.refs_1_), channel_id=1, source_target_pairs={{0,2},{1,3},{2,0},{3,1},{4,6},{5,7},{6,4},{7,5},{8,10},{9,11},{10,... | collective-permute-start | bytes 1572872 | tf_op jit(solution)/shard_map/ppermute | solution.py:92
  436.9 8.3 %copy-start.27 = (bf16[128,2048]{1,0:T(8,128)(2,1)}, bf16[128,2048]{1,0:T(8,128)(2,1)S(1)}, u32[]{:S(2)}) copy-start(bf16[128,2048]{1,0:T(8,128)(2,1)S(1)} %collective-permute-done.33.refs_6_) | copy-start | bytes 1572868
  436.9 21.6 %collective-permute-start.29 = (bf16[128,2048]{1,0:T(8,128)(2,1)}, bf16[128,2048]{1,0:T(8,128)(2,1)}, u32[]{:S(2)}, u32[]{:S(2)}) collective-permute-start(bf16[128,2048]{1,0:T(8,128)(2,1)} %collective-permute-done.21.refs_5_), channel_id=1, source_target_pairs={{0,4},{1,5},{2,6},{3,7},{4,0},{5,1},{6,2},{7,3},{8,12},{9,13},{10,... | collective-permute-start | bytes 1572872 | tf_op jit(solution)/shard_map/ppermute | solution.py:92
  448.9 16.0 %copy-start.28 = (bf16[128,2048]{1,0:T(8,128)(2,1)}, bf16[128,2048]{1,0:T(8,128)(2,1)S(1)}, u32[]{:S(2)}) copy-start(bf16[128,2048]{1,0:T(8,128)(2,1)S(1)} %collective-permute-done.31.refs_5_) | copy-start | bytes 1572868
  448.9 14.8 %copy-start.22 = (bf16[144,2048]{1,0:T(8,128)(2,1)}, bf16[144,2048]{1,0:T(8,128)(2,1)S(1)}, u32[]{:S(2)}) copy-start(bf16[144,2048]{1,0:T(8,128)(2,1)S(1)} %collective-permute-done.32.refs_2_) | copy-start | bytes 1769476
  449.5 14.3 %copy-start.23 = (bf16[144,2048]{1,0:T(8,128)(2,1)}, bf16[144,2048]{1,0:T(8,128)(2,1)S(1)}, u32[]{:S(2)}) copy-start(bf16[144,2048]{1,0:T(8,128)(2,1)S(1)} %collective-permute-done.30.refs_1_) | copy-start | bytes 1769476
  463.7 8.2 %collective-permute-start.34 = (bf16[1024,2048]{1,0:T(8,128)(2,1)}, bf16[1024,2048]{1,0:T(8,128)(2,1)}, u32[]{:S(2)}, u32[]{:S(2)}) collective-permute-start(bf16[1024,2048]{1,0:T(8,128)(2,1)} %pack_rows.2.refs_0_), channel_id=1, source_target_pairs={{0,1},{1,0},{2,3},{3,2},{4,5},{5,4},{6,7},{7,6},{8,9},{9,8},{10,11... | collective-permute-start | bytes 12582920 | tf_op jit(solution)/shard_map/ppermute | solution.py:92
  463.8 20.6 %collective-permute-start.35 = (bf16[144,2048]{1,0:T(8,128)(2,1)S(1)}, bf16[144,2048]{1,0:T(8,128)(2,1)S(1)}, u32[]{:S(2)}, u32[]{:S(2)}) collective-permute-start(bf16[144,2048]{1,0:T(8,128)(2,1)S(1)} %collective-permute-done.30.refs_1_), channel_id=1, source_target_pairs={{0,2},{1,3},{2,0},{3,1},{4,6},{5,7},{6,4},{7,5},{8,10},{9,11},{10,... | collective-permute-start | bytes 1769480 | tf_op jit(solution)/shard_map/ppermute | solution.py:92
  464.9 19.5 %collective-permute-start.36 = (bf16[128,2048]{1,0:T(8,128)(2,1)S(1)}, bf16[128,2048]{1,0:T(8,128)(2,1)S(1)}, u32[]{:S(2)}, u32[]{:S(2)}) collective-permute-start(bf16[128,2048]{1,0:T(8,128)(2,1)S(1)} %collective-permute-done.31.refs_5_), channel_id=1, source_target_pairs={{0,4},{1,5},{2,6},{3,7},{4,0},{5,1},{6,2},{7,3},{8,12},{9,13},{10,... | collective-permute-start | bytes 1572872 | tf_op jit(solution)/shard_map/ppermute | solution.py:92
  490.6 19.0 %collective-permute-start.37 = (bf16[1088,2048]{1,0:T(8,128)(2,1)}, bf16[1088,2048]{1,0:T(8,128)(2,1)}, u32[]{:S(2)}, u32[]{:S(2)}) collective-permute-start(bf16[1088,2048]{1,0:T(8,128)(2,1)} %pack_rows.3.refs_0_.own_ref), channel_id=1, source_target_pairs={{0,1},{1,0},{2,3},{3,2},{4,5},{5,4},{6,7},{7,6},{8,9},{9,8},{10,11... | collective-permute-start | bytes 13369352 | tf_op jit(solution)/shard_map/ppermute | solution.py:92
  492.3 27.9 %collective-permute-start.39 = (bf16[4,512,256]{2,1,0:T(8,128)(2,1)S(1)}, bf16[4,512,256]{2,1,0:T(8,128)(2,1)}, u32[]{:S(2)}, u32[]{:S(2)}) collective-permute-start(bf16[4,512,256]{2,1,0:T(8,128)(2,1)S(1)} %add_convert_fusion), channel_id=1, source_target_pairs={{24,16},{16,8},{8,0},{25,17},{17,9},{9,1},{26,18},{18,10},{10,2},{... | collective-permute-start | bytes 3145736 | tf_op jit(solution)/shard_map/ppermute | solution.py:87
  496.1 27.6 %collective-permute-start.38 = (bf16[4,512,256]{2,1,0:T(8,128)(2,1)}, bf16[4,512,256]{2,1,0:T(8,128)(2,1)}, u32[]{:S(2)}, u32[]{:S(2)}) collective-permute-start(bf16[4,512,256]{2,1,0:T(8,128)(2,1)} %add_convert_fusion.1), channel_id=1, source_target_pairs={{0,8},{8,16},{16,24},{1,9},{9,17},{17,25},{2,10},{10,18},{18,26},{... | collective-permute-start | bytes 3145736 | tf_op jit(solution)/shard_map/ppermute | solution.py:87
  512.1 11.5 %copy-start.44 = (f32[3,256]{1,0:T(4,128)S(1)}, f32[3,256]{1,0:T(4,128)}, u32[]{:S(2)}) copy-start(f32[3,256]{1,0:T(4,128)} %get-tuple-element.251) | copy-start | bytes 9220
  512.1 14.1 %copy-start.2 = (f32[4,512,256]{2,1,0:T(8,128)S(1)}, f32[4,512,256]{2,1,0:T(8,128)}, u32[]{:S(2)}) copy-start(f32[4,512,256]{2,1,0:T(8,128)} %get-tuple-element.242) | copy-start | bytes 6291460
  523.7 7.5 %collective-permute-start.40 = (f32[19,256]{1,0:T(8,128)S(1)}, f32[19,256]{1,0:T(8,128)S(1)}, u32[]{:S(2)}, u32[]{:S(2)}) collective-permute-start(f32[19,256]{1,0:T(8,128)S(1)} %constant_dynamic-update-slice_fusion), channel_id=1, source_target_pairs={{0,8},{8,0},{16,24},{24,16},{1,9},{9,1},{17,25},{25,17},{2,10},{10... | collective-permute-start | bytes 58376 | tf_op jit(solution)/shard_map/ppermute | solution.py:92
  528.1 5.5 %copy-start.3 = (f32[512,256]{1,0:T(8,128)S(1)}, f32[512,256]{1,0:T(8,128)}, u32[]{:S(2)}) copy-start(f32[512,256]{1,0:T(8,128)} %param.25) | copy-start | bytes 1572868
  531.2 5.5 %copy-start.39 = (f32[2,2048]{1,0:T(2,128)S(1)}, f32[2,2048]{1,0:T(2,128)}, u32[]{:S(2)}) copy-start(f32[2,2048]{1,0:T(2,128)} %refs_6_.1) | copy-start | bytes 49156
  531.3 5.5 %copy-start.41 = (f32[2,2048]{1,0:T(2,128)S(1)}, f32[2,2048]{1,0:T(2,128)}, u32[]{:S(2)}) copy-start(f32[2,2048]{1,0:T(2,128)} %param.40) | copy-start | bytes 49156
  531.3 5.5 %copy-start.42 = (f32[2,2048]{1,0:T(2,128)S(1)}, f32[2,2048]{1,0:T(2,128)}, u32[]{:S(2)}) copy-start(f32[2,2048]{1,0:T(2,128)} %param.34) | copy-start | bytes 49156
  531.3 4.8 collective-permute-start.41
  (31 other events, 86.9 us)
Sparse Core Ops, SparseCore 0:
  11.0 83.4 all-gather.3
  96.7 81.4 all-gather.5
  265.6 80.6 reduce-scatter.2
  357.5 78.7 reduce-scatter.4

commit v5 on v4

--- a/solution.py
+++ b/solution.py
@@ -1041,8 +1041,8 @@
         one_hid = both_ways(load_hid, (2, 4))
         last_grads = feed_grads(n, hidden, cot, after(active, load_hid), gates_grad)
         two_out = after(two_out, last_grads)
+        add = add_rows(info, tokens, near_out, two_out)
         last_grads = scatter(last_grads).reshape(3, units - cut, -1)
-        add = add_rows(info, tokens, near_out, two_out)
         out_one = both_ways(add, (4, 2))
         out_two = both_ways(add, (2, 4))
         near_hid, load_hid = sum_first(own_hid, after(one_hid, add))
@@ -1058,11 +1058,13 @@
         out_three = after(out_three, hid_one)
         mine_out = join(add, out_one, out_two, out_three)
         other_out = swap(mine_out, 1)
-        output = finish_rows(info, rows, 0, mine_out)
+        load = scatter_load(n - 1, after(attend_slots, mine_out), *came)
+        came = scatter_hop(n - 1, *load)
+        output = finish_rows(info, rows, 0, after(mine_out, load))
         output = finish_rows(info, rows, 1, after(other_out, output), begun=output)
         done = update_feed(cut, after(last_grads, output), states, rates, begun)
-        came = scatter_hop(n - 1, *scatter_load(n - 1, after(attend_slots, done), *came))
-        hid_three = after(hid_three, done)
+        attend_new = update_attend(after(came, done))
+        hid_three = after(hid_three, attend_new)
         mine_hid = join(back, hid_one, hid_two, hid_three)
         other_hid = swap(mine_hid, 1)
         input_grad = finish_rows(info, rows, 0, mine_hid, cot)
@@ -1070,7 +1072,6 @@
         norm_part = tail_sums(mine_hid, other_hid)
         sums = small_sum(join_sums(norm_part, bias_part), "dp")
         input_grad = finish_rows(info, rows, 1, after(other_hid, norm_part), cot, input_grad)
-        attend_new = update_attend(after(came, input_grad))
         norm_grad, bias_grad = split_sums(sums, norm_part, bias_part)
     else:
         out_part, active, both, w_last = out_last(n, info, False, last_pieces, hidden, out_early)

time: 555 us -> 555 us (level)
  transfers between devices with their start and end apart: 46 -> 46, of which waited for: 22 -> 21; matrix products, arithmetic and copies ran while one was open for 6% -> 6% of each run, Pallas kernels for 49% -> 49%
where the time goes in v5:
time: 555 us; the launch traced here: 545 us
  Pallas kernels  272 us (49%)
  waiting for transfers between devices  144 us (26%)
  starting transfers between devices  61.5 us (11%)
  other arithmetic  39.6 us (7%)
  between operations  15 us (3%)
  local copies, waits for them, and re-layouts  12.8 us (2%)
    ppermute x32, waiting for transfers between devices, swap(): return lax.ppermute(value, axis, [(a, a ^ mask) for a in range(n)])  65.9 us
    all_gather x1, waiting for transfers between devices, body(): attend_pieces = [lax.all_gather(attend_shard, 'dp')]  62.9 us
    pallas_call x1, Pallas kernels, attend(): pl.pallas_call(functools.partial(attend_kernel, min(512, length)), grid=(...  34 us
    pallas_call x2, Pallas kernels, feed_grads(): pl.pallas_call(functools.partial(feed_grads_kernel, n, steps), grid=(step...  32.3 us
    ppermute x32, starting transfers between devices, swap(): return lax.ppermute(value, axis, [(a, a ^ mask) for a in range(n)])  29.9 us
    pallas_call x4, Pallas kernels, finish_rows(): pl.pallas_call(finish_kernel, grid_spec=pltpu.PrefetchScalarGridSpec(num_...  26.7 us
    pallas_call x1, Pallas kernels, out_last(): pl.pallas_call(functools.partial(out_last_kernel, n, count, split), grid_...  24.8 us
    pallas_call x1, Pallas kernels, hid_last(): pl.pallas_call(functools.partial(hid_last_kernel, split), grid_spec=pltpu...  22.2 us
  transfers between devices with their start and end apart: 46, of which 21 were waited for; matrix products, arithmetic and copies ran while one was open for 6% of the time, Pallas kernels for 49%

profile of v5, /device:TPU:0, one launch (start us, length us, event | category | flops | bytes accessed | tf_op | source)
XLA Modules:
  0.0 544.8 jit_solution(11297499693139663738)
XLA Ops:
  8.3 1.5 convert_bitcast_fusion
  11.0 1.6 bitcast_convert_fusion
  14.6 11.2 %layer_norm.1.refs_1_.h_ref.refs_7_ = bf16[2048,2048]{1,0:T(8,128)(2,1)} custom-call(bf16[2048,2048]{1,0:T(8,128)(2,1)} %bitcast.48, f32[2,2048]{1,0:T(2,128)} %refs_6_.1), custom_call_target="tpu_custom_call" | custom-call | flops 33554432 | bytes 16777216 | tf_op jit(solution)/shard_map/layer_norm/pallas_call | solution.py:126
  26.0 5.6 %fusion.4 = (f32[2048,128]{1,0:T(8,128)}, f32[2048,128]{1,0:T(8,128)}) fusion(f32[128]{0:T(128)S(1)} %fusion.9, f32[2048]{0:T(1024)S(1)} %bitcast.85, pred[128]{0:T(512)(128)(4,1)S(1)} %get-tuple-element.285, pred[128]{0:T(512)(128)(4,1)S(1)} %get-tuple-element.286), kind=kLoop, calls=%fused_computation.26 | loop fusion | flops 1310720 | bytes 2106112 | tf_op jit(solution)/shard_map/jit(_where)/select_n | solution.py:952
  31.6 62.9 %all-gather.4.cloned.1.call-done.refs_0_ = bf16[4,4,512,256]{3,2,1,0:T(8,128)(2,1)} async-done(((bf16[1,4,512,256]{3,2,1,0:T(8,128)(2,1)}), bf16[4,4,512,256]{3,2,1,0:T(8,128)(2,1)}) %all-gather.4.cloned.1.call-update) | async-done | bytes 4194320 | tf_op jit(solution)/shard_map/all_gather | solution.py:939
  94.5 17.4 %project.1 = (bf16[2048,256]{1,0:T(8,128)(2,1)}, bf16[2048,256]{1,0:T(8,128)(2,1)}, bf16[2048,256]{1,0:T(8,128)(2,1)}, bf16[2048,256]{1,0:T(8,128)(2,1)}, bf16[4,2048,256]{2,1,0:T(8,128)(2,1)}) custom-call(s32[1]{0:T(128)} %bitcast.3.me_ref, bf16[4,4,512,256]{3,2,1,0:T(8,128)(2,1)} %all-gather.4.cloned.1.call-done.refs_0_, ...), custom_call_target="tpu_custom_call" | custom-call | flops 8589934592 | bytes 25165824 | tf_op jit(solution)/shard_map/project/pallas_call | solution.py:450
  112.0 34.0 %attend.1 = (bf16[2048,256]{1,0:T(8,128)(2,1)}, bf16[3,2048,256]{2,1,0:T(8,128)(2,1)}, f32[3,256]{1,0:T(4,128)}) custom-call(bf16[2048,256]{1,0:T(8,128)(2,1)} %get-tuple-element.140.q_ref, bf16[2048,256]{1,0:T(8,128)(2,1)} %get-tuple-element.141.k_ref, bf16[2048,256]{1,0:T(8,128)(2,1)} %get-tuple-element.142.v_ref, ...), custom_call_target="tpu_custom_call" | custom-call | flops 21474836480 | bytes 10485760 | tf_op jit(solution)/shard_map/attend/pallas_call | solution.py:530
  145.9 16.9 %attend_grads.1 = (f32[4,512,256]{2,1,0:T(8,128)}, bf16[4,512,256]{2,1,0:T(8,128)(2,1)}, bf16[4,512,256]{2,1,0:T(8,128)(2,1)}, bf16[4,512,256]{2,1,0:T(8,128)(2,1)}, bf16[4,512,256]{2,1,0:T(8,128)(2,1)}) custom-call(s32[1]{0:T(128)} %bitcast.3.me_ref, bf16[2048,2048]{1,0:T(8,128)(2,1)} %layer_norm.1.refs_1_.h_ref.refs_7_, bf16[2048,2048]{1,0:T(8,128)(2,1)} %bitcast.56, ...), custom_call_target="tpu_custom_call" | custom-call | flops 8589934592 | bytes 25165824 | tf_op jit(solution)/shard_map/attend_grads/pallas_call | solution.py:589
  162.8 14.6 %heads_parts.1 = (bf16[2048,2048]{1,0:T(8,128)(2,1)}, bf16[2048,2048]{1,0:T(8,128)(2,1)}) custom-call(bf16[2048,256]{1,0:T(8,128)(2,1)} %get-tuple-element.145.ctx_ref, bf16[3,2048,256]{2,1,0:T(8,128)(2,1)} %get-tuple-element.144.mg_ref, bf16[4,2048,256]{2,1,0:T(8,128)(2,1)} %get-tuple-element.151.wa_ref), custom_call_target="tpu_custom_call" | custom-call | flops 8589934592 | bytes 25165824 | tf_op jit(solution)/shard_map/heads_parts/pallas_call | solution.py:621
  179.4 5.6 %collective-permute-start = (bf16[3,352,512]{2,1,0:T(8,128)(2,1)S(1)}, bf16[3,352,512]{2,1,0:T(8,128)(2,1)}, u32[]{:S(2)}, u32[]{:S(2)}) collective-permute-start(bf16[3,352,512]{2,1,0:T(8,128)(2,1)S(1)} %pad_maximum_fusion.refs_0_), channel_id=1, source_target_pairs={{0,8},{8,16},{16,24},{1,9},{9,17},{17,25},{2,10},{10,18},{18,26},{... | collective-permute-start | bytes 3244040 | tf_op jit(solution)/shard_map/ppermute | solution.py:68
  185.0 16.5 %feed_chunk.1 = (bf16[352,2048]{1,0:T(8,128)(2,1)}, bf16[704,2048]{1,0:T(8,128)(2,1)}, bf16[3,352,2048]{2,1,0:T(8,128)(2,1)}) custom-call(s32[1]{0:T(128)} %bitcast.3.me_ref, bf16[4,3,352,512]{3,2,1,0:T(8,128)(2,1)} %bitcast.86, bf16[2048,2048]{1,0:T(8,128)(2,1)} %layer_norm.1.refs_1_.h_ref.refs_7_, bf16[2048,2048]{1,0:T(8,128)(2,1)} %bitcast.57), custom_call_target="tpu_custom_call" | custom-call | flops 8858370048 | bytes 25427968 | tf_op jit(solution)/shard_map/feed_chunk/pallas_call | solution.py:231
  201.5 4.3 collective-permute-done.1.refs_4_
  208.9 7.6 %collective-permute-start.4 = (bf16[4,512,256]{2,1,0:T(8,128)(2,1)}, bf16[4,512,256]{2,1,0:T(8,128)(2,1)}, u32[]{:S(2)}, u32[]{:S(2)}) collective-permute-start(bf16[4,512,256]{2,1,0:T(8,128)(2,1)} %get-tuple-element.162), channel_id=1, source_target_pairs={{0,8},{24,16},{1,9},{25,17},{2,10},{26,18},{3,11},{27,19},{4,12},{... | collective-permute-start | bytes 3145736 | tf_op jit(solution)/shard_map/ppermute | solution.py:85
  216.5 19.7 %early_parts.1 = (bf16[2048,2048]{1,0:T(8,128)(2,1)}, bf16[2048,2048]{1,0:T(8,128)(2,1)}) custom-call(bf16[352,2048]{1,0:T(8,128)(2,1)} %get-tuple-element.156.act_ref, bf16[704,2048]{1,0:T(8,128)(2,1)} %get-tuple-element.157.grad_ref, bf16[3,352,2048]{2,1,0:T(8,128)(2,1)} %get-tuple-element.158.w_ref, bf16[2048,2048]{1,0:T(8,128)(2,1)} %get-tuple-element.163.hid_in_ref, ...), custom_call_target="tpu_custom_call" | custom-call | flops 8858370048 | bytes 42205184 | tf_op jit(solution)/shard_map/early_parts/pallas_call | solution.py:649
  237.2 4.1 fusion.1
  241.2 1.6 collective-permute-start.7
  242.8 5.1 collective-permute-start.6
  249.4 16.1 %feed_grads.2 = bf16[4,1056,512]{2,1,0:T(8,128)(2,1)} custom-call(bf16[2048,2048]{1,0:T(8,128)(2,1)} %layer_norm.1.refs_1_.h_ref.refs_7_, bf16[2048,2048]{1,0:T(8,128)(2,1)} %bitcast.58, bf16[352,2048]{1,0:T(8,128)(2,1)} %get-tuple-element.156.act_ref, bf16[704,2048]{1,0:T(8,128)(2,1)} %get-tuple-element.157.grad_ref), custom_call_target="tpu_custom_call" | custom-call | flops 8858370048 | bytes 25427968 | tf_op jit(solution)/shard_map/feed_grads/pallas_call | solution.py:387
  266.1 1.4 collective-permute-done.6
  267.6 5.7 %collective-permute-done.5.refs_3_.refs_6_ = bf16[3,352,512]{2,1,0:T(8,128)(2,1)S(1)} collective-permute-done((bf16[3,352,512]{2,1,0:T(8,128)(2,1)S(1)}, bf16[3,352,512]{2,1,0:T(8,128)(2,1)S(1)}, u32[]{:S(2)}, u32[]{:S(2)}) %collective-permute-start.5) | collective-permute-done | bytes 1081376 | tf_op jit(solution)/shard_map/ppermute | solution.py:66
  274.2 24.8 %out_last.1 = (bf16[256,2048]{1,0:T(8,128)(2,1)}, bf16[256,2048]{1,0:T(8,128)(2,1)}, bf16[256,2048]{1,0:T(8,128)(2,1)}, bf16[256,2048]{1,0:T(8,128)(2,1)}, bf16[...) custom-call(s32[4]{0:T(128)} %pad_add_fusion.info_ref, ...), custom_call_target="tpu_custom_call" | custom-call | flops 8858370048 | bytes 33554432 | tf_op jit(solution)/shard_map/out_last/pallas_call | solution.py:319
  299.7 2.4 collective-permute-done.9
  302.0 1.6 add_convert_fusion.9
  303.6 1.4 collective-permute-start.10
  305.5 1.5 collective-permute-start.12
  307.5 22.2 %hid_last.1 = (bf16[256,2048]{1,0:T(8,128)(2,1)}, bf16[256,2048]{1,0:T(8,128)(2,1)}, bf16[256,2048]{1,0:T(8,128)(2,1)}, bf16[256,2048]{1,0:T(8,128)(2,1)}, bf16[...) custom-call(s32[4]{0:T(128)} %pad_add_fusion.info_ref, ...), custom_call_target="tpu_custom_call" | custom-call | flops 8858370048 | bytes 33554432 | tf_op jit(solution)/shard_map/hid_last/pallas_call | solution.py:355
  331.1 2.1 add_convert_fusion.7
  334.6 2.1 add_convert_fusion.6
  338.5 1.5 collective-permute-start.25
  341.1 16.3 %feed_grads.3 = bf16[4,1056,512]{2,1,0:T(8,128)(2,1)} custom-call(bf16[2048,2048]{1,0:T(8,128)(2,1)} %layer_norm.1.refs_1_.h_ref.refs_7_, bf16[2048,2048]{1,0:T(8,128)(2,1)} %bitcast.60, bf16[352,2048]{1,0:T(8,128)(2,1)} %get-tuple-element.196.act_ref, bf16[704,2048]{1,0:T(8,128)(2,1)} %get-tuple-element.197.grad_ref), custom_call_target="tpu_custom_call" | custom-call | flops 8858370048 | bytes 25427968 | tf_op jit(solution)/shard_map/feed_grads/pallas_call | solution.py:387
  358.5 1.4 collective-permute-start.15
  359.9 14.9 %collective-permute-done.14.refs_4_ = bf16[128,2048]{1,0:T(8,128)(2,1)S(1)} collective-permute-done((bf16[128,2048]{1,0:T(8,128)(2,1)S(1)}, bf16[128,2048]{1,0:T(8,128)(2,1)S(1)}, u32[]{:S(2)}, u32[]{:S(2)}) %collective-permute-start.14) | collective-permute-done | bytes 524320 | tf_op jit(solution)/shard_map/ppermute | solution.py:92
  374.8 1.7 collective-permute-done.15.refs_5_
  377.3 3.8 add_rows.1
  381.2 2.1 add_convert_fusion.3
  385.0 1.8 add_convert_fusion.2
  389.6 1.4 collective-permute-start.22
  393.1 9.5 %collective-permute-done.27.refs_5_ = bf16[128,2048]{1,0:T(8,128)(2,1)S(1)} collective-permute-done((bf16[128,2048]{1,0:T(8,128)(2,1)S(1)}, bf16[128,2048]{1,0:T(8,128)(2,1)S(1)}, u32[]{:S(2)}, u32[]{:S(2)}) %collective-permute-start.27) | collective-permute-done | bytes 524320 | tf_op jit(solution)/shard_map/ppermute | solution.py:92
  404.0 5.5 %back_rows.1 = (bf16[144,2048]{1,0:T(8,128)(2,1)}, bf16[128,2048]{1,0:T(8,128)(2,1)}) custom-call(s32[4]{0:T(128)} %pad_add_fusion.info_ref, bf16[2048,2048]{1,0:T(8,128)(2,1)} %bitcast.51, bf16[2048,2048]{1,0:T(8,128)(2,1)} %bitcast.52, bf16[128,2048]{1,0:T(8,128)(2,1)} %get-tuple-element.274.refs_2_, bf16[128,2048]{1,0:T(8,128)(2,1)} %get-tuple-element.272.refs_3_, ...), custom_call_target="tpu_custom_call" | custom-call | flops 10485760 | bytes 4194304 | tf_op jit(solution)/shard_map/back_rows/pallas_call | solution.py:704
  410.9 2.9 collective-permute-done.22.refs_2_
  415.7 10.0 %collective-permute-done.23.refs_6_ = bf16[128,2048]{1,0:T(8,128)(2,1)S(1)} collective-permute-done((bf16[128,2048]{1,0:T(8,128)(2,1)S(1)}, bf16[128,2048]{1,0:T(8,128)(2,1)S(1)}, u32[]{:S(2)}, u32[]{:S(2)}) %collective-permute-start.23) | collective-permute-done | bytes 524320 | tf_op jit(solution)/shard_map/ppermute | solution.py:92
  425.7 1.4 collective-permute-start.31
  427.9 9.2 %collective-permute-done.33.refs_6_ = bf16[128,2048]{1,0:T(8,128)(2,1)} collective-permute-done((bf16[128,2048]{1,0:T(8,128)(2,1)}, bf16[128,2048]{1,0:T(8,128)(2,1)}, u32[]{:S(2)}, u32[]{:S(2)}) %collective-permute-start.33) | collective-permute-done | bytes 524320 | tf_op jit(solution)/shard_map/ppermute | solution.py:92
  438.3 7.0 %update_feed.2 = (f32[2,704,512]{2,1,0:T(8,128)}, f32[2,704,512]{2,1,0:T(8,128)}, f32[2,704,512]{2,1,0:T(8,128)}, f32[2,704,512]{2,1,0:T(8,128)}, f32[704,512]{1...) custom-call(bf16[3,352,512]{2,1,0:T(8,128)(2,1)} %bitcast.84, f32[2,704,512]{2,1,0:T(8,128)} %bitcast.63, ...), custom_call_target="tpu_custom_call" | custom-call | flops 5406720 | bytes 16220160 | tf_op jit(solution)/shard_map/update_feed/pallas_call | solution.py:881
  445.3 3.7 collective-permute-done.31.refs_5_
  449.7 8.4 %collective-permute-done.28.refs_3_ = bf16[128,2048]{1,0:T(8,128)(2,1)S(1)} collective-permute-done((bf16[128,2048]{1,0:T(8,128)(2,1)S(1)}, bf16[128,2048]{1,0:T(8,128)(2,1)S(1)}, u32[]{:S(2)}, u32[]{:S(2)}) %collective-permute-start.28) | collective-permute-done | bytes 524320 | tf_op jit(solution)/shard_map/ppermute | solution.py:92
  459.6 4.9 pack_rows.2.refs_0_
  464.7 1.5 add_convert_fusion
  467.5 2.5 add_convert_fusion.1
  470.0 5.6 %collective-permute-start.37 = (bf16[4,512,256]{2,1,0:T(8,128)(2,1)}, bf16[4,512,256]{2,1,0:T(8,128)(2,1)}, u32[]{:S(2)}, u32[]{:S(2)}) collective-permute-start(bf16[4,512,256]{2,1,0:T(8,128)(2,1)} %add_convert_fusion.1), channel_id=1, source_target_pairs={{0,8},{8,16},{16,24},{1,9},{9,17},{17,25},{2,10},{10,18},{18,26},{... | collective-permute-start | bytes 3145736 | tf_op jit(solution)/shard_map/ppermute | solution.py:87
  475.6 1.6 collective-permute-start.36
  478.1 5.7 %finish_rows.4.refs_1_ = bf16[2048,2048]{1,0:T(8,128)(2,1)} custom-call(s32[4]{0:T(128)} %pad_add_fusion.info_ref, bf16[1024,2048]{1,0:T(8,128)(2,1)} %pack_rows.2.refs_0_), custom_call_target="tpu_custom_call" | custom-call | flops 4194304 | bytes 16777216 | tf_op jit(solution)/shard_map/finish_rows/pallas_call | solution.py:843
  483.8 5.4 finish_rows.5
  489.2 7.1 %update_feed.3 = (f32[2,704,512]{2,1,0:T(8,128)}, f32[2,704,512]{2,1,0:T(8,128)}, f32[2,704,512]{2,1,0:T(8,128)}, f32[2,704,512]{2,1,0:T(8,128)}, f32[704,512]{1...) custom-call(bf16[3,352,512]{2,1,0:T(8,128)(2,1)} %bitcast.83, ...), custom_call_target="tpu_custom_call", output_to_operand_aliasing={{0}: (7, {}), {1}: (8, {}), {2}: (9, {}), {3}: (10, {}), {4... | custom-call | flops 5406720 | bytes 16220160 | tf_op jit(solution)/shard_map/update_feed/pallas_call | solution.py:881
  497.6 2.0 convert_add_fusion.2
  499.6 1.5 multiply_add_fusion.2
  502.4 3.1 multiply_add_fusion
  506.3 5.1 pack_rows.3.refs_0_.own_ref
  511.5 7.8 %finish_rows.6.refs_2_ = f32[2048,2048]{1,0:T(8,128)} custom-call(s32[4]{0:T(128)} %pad_add_fusion.info_ref, bf16[1088,2048]{1,0:T(8,128)(2,1)} %pack_rows.3.refs_0_.own_ref, bf16[2048,2048]{1,0:T(8,128)(2,1)} %bitcast.61), custom_call_target="tpu_custom_call" | custom-call | flops 4194304 | bytes 16777216 | tf_op jit(solution)/shard_map/finish_rows/pallas_call | solution.py:843
  519.4 1.7 tail_sums.1
  521.9 2.5 collective-permute-start.40
  524.4 1.8 collective-permute-done.40
  526.3 2.3 collective-permute-start.41
  528.6 7.8 %finish_rows.7 = f32[2048,2048]{1,0:T(8,128)} custom-call(s32[4]{0:T(128)} %pad_add_fusion.info_ref, bf16[1088,2048]{1,0:T(8,128)(2,1)} %collective-permute-done.39.other_ref.refs_0_, bf16[2048,2048]{1,0:T(8,128)(2,1)} %bitcast.62, f32[2048,2048]{1,0:T(8,128)} %finish_rows.6.refs_2_), custom_call_target="tpu_custom_call", output_to_operand_aliasing={{}: (3, {})} | custom-call | flops 4194304 | bytes 16777216 | tf_op jit(solution)/shard_map/finish_rows/pallas_call | solution.py:843
  (191 shorter events, 45.8 us)
Async XLA Ops:
  7.2 87.3 %all-gather.4.cloned.1.call-start = ((), (), s32[]{:S(2)}) async-start(), calls=%async_computation.2 | async-start | bytes 5242880 | tf_op jit(solution)/shard_map/all_gather | solution.py:939
  10.9 167.2 %all-gather.6.cloned.1.call-start = ((), (), s32[]{:S(2)}) async-start(), calls=%async_computation.5 | async-start | bytes 5406720 | tf_op jit(solution)/shard_map/all_gather | solution.py:941
  14.5 423.8 %reduce-scatter.3.cloned.1.call-start = ((), (), s32[]{:S(2)}) async-start(), calls=%async_computation.3 | async-start | bytes 5406720 | tf_op jit(solution)/shard_map/reduce_scatter | solution.py:990
  26.0 153.5 %copy-start.6 = (bf16[3,352,512]{2,1,0:T(8,128)(2,1)}, bf16[3,352,512]{2,1,0:T(8,128)(2,1)S(1)}, u32[]{:S(2)}) copy-start(bf16[3,352,512]{2,1,0:T(8,128)(2,1)S(1)} %pad_maximum_fusion.refs_0_) | copy-start | bytes 3244036
  178.1 27.6 %collective-permute-start.1 = (bf16[3,352,512]{2,1,0:T(8,128)(2,1)S(1)}, bf16[3,352,512]{2,1,0:T(8,128)(2,1)}, u32[]{:S(2)}, u32[]{:S(2)}) collective-permute-start(bf16[3,352,512]{2,1,0:T(8,128)(2,1)S(1)} %pad_maximum_fusion.refs_0_), channel_id=1, source_target_pairs={{8,0},{16,8},{24,16},{9,1},{17,9},{25,17},{10,2},{18,10},{26,18},{... | collective-permute-start | bytes 3244040 | tf_op jit(solution)/shard_map/ppermute | solution.py:68
  179.4 27.4 %collective-permute-start = (bf16[3,352,512]{2,1,0:T(8,128)(2,1)S(1)}, bf16[3,352,512]{2,1,0:T(8,128)(2,1)}, u32[]{:S(2)}, u32[]{:S(2)}) collective-permute-start(bf16[3,352,512]{2,1,0:T(8,128)(2,1)S(1)} %pad_maximum_fusion.refs_0_), channel_id=1, source_target_pairs={{0,8},{8,16},{16,24},{1,9},{9,17},{17,25},{2,10},{10,18},{18,26},{... | collective-permute-start | bytes 3244040 | tf_op jit(solution)/shard_map/ppermute | solution.py:68
  206.8 30.3 %collective-permute-start.2 = (bf16[3,352,512]{2,1,0:T(8,128)(2,1)}, bf16[3,352,512]{2,1,0:T(8,128)(2,1)S(1)}, u32[]{:S(2)}, u32[]{:S(2)}) collective-permute-start(bf16[3,352,512]{2,1,0:T(8,128)(2,1)} %collective-permute-done.refs_1_), channel_id=1, source_target_pairs={{8,16},{16,24},{9,17},{17,25},{10,18},{18,26},{11,19},{19,27},{12,... | collective-permute-start | bytes 3244040 | tf_op jit(solution)/shard_map/ppermute | solution.py:68
  207.6 29.6 %collective-permute-start.3 = (bf16[3,352,512]{2,1,0:T(8,128)(2,1)}, bf16[3,352,512]{2,1,0:T(8,128)(2,1)S(1)}, u32[]{:S(2)}, u32[]{:S(2)}) collective-permute-start(bf16[3,352,512]{2,1,0:T(8,128)(2,1)} %collective-permute-done.1.refs_4_), channel_id=1, source_target_pairs={{8,0},{16,8},{9,1},{17,9},{10,2},{18,10},{11,3},{19,11},{12,4},{20... | collective-permute-start | bytes 3244040 | tf_op jit(solution)/shard_map/ppermute | solution.py:68
  208.9 28.3 %collective-permute-start.4 = (bf16[4,512,256]{2,1,0:T(8,128)(2,1)}, bf16[4,512,256]{2,1,0:T(8,128)(2,1)}, u32[]{:S(2)}, u32[]{:S(2)}) collective-permute-start(bf16[4,512,256]{2,1,0:T(8,128)(2,1)} %get-tuple-element.162), channel_id=1, source_target_pairs={{0,8},{24,16},{1,9},{25,17},{2,10},{26,18},{3,11},{27,19},{4,12},{... | collective-permute-start | bytes 3145736 | tf_op jit(solution)/shard_map/ppermute | solution.py:85
  216.5 20.7 %copy-start.21 = (bf16[4,512,256]{2,1,0:T(8,128)(2,1)S(1)}, bf16[4,512,256]{2,1,0:T(8,128)(2,1)}, u32[]{:S(2)}) copy-start(bf16[4,512,256]{2,1,0:T(8,128)(2,1)} %get-tuple-element.169) | copy-start | bytes 3145732
  237.1 10.8 %copy-start.7 = (bf16[3,352,512]{2,1,0:T(8,128)(2,1)}, bf16[3,352,512]{2,1,0:T(8,128)(2,1)S(1)}, u32[]{:S(2)}) copy-start(bf16[3,352,512]{2,1,0:T(8,128)(2,1)S(1)} %collective-permute-done.2.refs_2_) | copy-start | bytes 3244036
  237.1 10.8 %copy-start.8 = (bf16[3,352,512]{2,1,0:T(8,128)(2,1)}, bf16[3,352,512]{2,1,0:T(8,128)(2,1)S(1)}, u32[]{:S(2)}) copy-start(bf16[3,352,512]{2,1,0:T(8,128)(2,1)S(1)} %collective-permute-done.3.refs_5_) | copy-start | bytes 3244036
  241.2 24.9 %collective-permute-start.7 = (bf16[4,512,256]{2,1,0:T(8,128)(2,1)}, bf16[4,512,256]{2,1,0:T(8,128)(2,1)}, u32[]{:S(2)}, u32[]{:S(2)}) collective-permute-start(bf16[4,512,256]{2,1,0:T(8,128)(2,1)} %get-tuple-element.279), channel_id=1, source_target_pairs={{24,16},{16,8},{25,17},{17,9},{26,18},{18,10},{27,19},{19,11},{28,... | collective-permute-start | bytes 3145736 | tf_op jit(solution)/shard_map/ppermute | solution.py:87
  242.8 24.7 %collective-permute-start.6 = (bf16[4,512,256]{2,1,0:T(8,128)(2,1)}, bf16[4,512,256]{2,1,0:T(8,128)(2,1)}, u32[]{:S(2)}, u32[]{:S(2)}) collective-permute-start(bf16[4,512,256]{2,1,0:T(8,128)(2,1)} %get-tuple-element.280), channel_id=1, source_target_pairs={{0,8},{8,16},{1,9},{9,17},{2,10},{10,18},{3,11},{11,19},{4,12},{12... | collective-permute-start | bytes 3145736 | tf_op jit(solution)/shard_map/ppermute | solution.py:87
  248.1 25.2 %collective-permute-start.5 = (bf16[3,352,512]{2,1,0:T(8,128)(2,1)S(1)}, bf16[3,352,512]{2,1,0:T(8,128)(2,1)S(1)}, u32[]{:S(2)}, u32[]{:S(2)}) collective-permute-start(bf16[3,352,512]{2,1,0:T(8,128)(2,1)S(1)} %broadcast_select_fusion), channel_id=1, source_target_pairs={{16,24},{8,0},{17,25},{9,1},{18,26},{10,2},{19,27},{11,3},{20,28},... | collective-permute-start | bytes 3244040 | tf_op jit(solution)/shard_map/ppermute | solution.py:66
  265.5 223.7 %reduce-scatter.5.cloned.1.call-start = ((), (), s32[]{:S(2)}) async-start(), calls=%async_computation.4 | async-start | bytes 5406720 | tf_op jit(solution)/shard_map/reduce_scatter | solution.py:990
  299.1 6.0 %copy-start.13 = (bf16[256,2048]{1,0:T(8,128)(2,1)S(1)}, bf16[256,2048]{1,0:T(8,128)(2,1)}, u32[]{:S(2)}) copy-start(bf16[256,2048]{1,0:T(8,128)(2,1)} %get-tuple-element.178) | copy-start | bytes 3145732
  299.1 2.9 collective-permute-start.9
  299.2 5.9 %collective-permute-start.11 = (bf16[256,2048]{1,0:T(8,128)(2,1)}, bf16[256,2048]{1,0:T(8,128)(2,1)S(1)}, u32[]{:S(2)}, u32[]{:S(2)}) collective-permute-start(bf16[256,2048]{1,0:T(8,128)(2,1)} %get-tuple-element.179), channel_id=1, source_target_pairs={{0,1},{1,0},{2,3},{3,2},{4,5},{5,4},{6,7},{7,6},{8,9},{9,8},{10,11... | collective-permute-start | bytes 3145736 | tf_op jit(solution)/shard_map/ppermute | solution.py:92
  303.6 26.1 %collective-permute-start.10 = (bf16[256,2048]{1,0:T(8,128)(2,1)S(1)}, bf16[256,2048]{1,0:T(8,128)(2,1)}, u32[]{:S(2)}, u32[]{:S(2)}) collective-permute-start(bf16[256,2048]{1,0:T(8,128)(2,1)S(1)} %add_convert_fusion.9), channel_id=1, source_target_pairs={{0,2},{1,3},{2,0},{3,1},{4,6},{5,7},{6,4},{7,5},{8,10},{9,11},{10,... | collective-permute-start | bytes 3145736 | tf_op jit(solution)/shard_map/ppermute | solution.py:92
  305.5 25.1 %collective-permute-start.12 = (bf16[256,2048]{1,0:T(8,128)(2,1)S(1)}, bf16[256,2048]{1,0:T(8,128)(2,1)}, u32[]{:S(2)}, u32[]{:S(2)}) collective-permute-start(bf16[256,2048]{1,0:T(8,128)(2,1)S(1)} %add_convert_fusion.8), channel_id=1, source_target_pairs={{0,4},{1,5},{2,6},{3,7},{4,0},{5,1},{6,2},{7,3},{8,12},{9,13},{10,... | collective-permute-start | bytes 3145736 | tf_op jit(solution)/shard_map/ppermute | solution.py:92
  307.0 23.6 %collective-permute-start.8 = (bf16[256,2048]{1,0:T(8,128)(2,1)}, bf16[256,2048]{1,0:T(8,128)(2,1)}, u32[]{:S(2)}, u32[]{:S(2)}) collective-permute-start(bf16[256,2048]{1,0:T(8,128)(2,1)} %get-tuple-element.175), channel_id=1, source_target_pairs={{0,1},{1,0},{2,3},{3,2},{4,5},{5,4},{6,7},{7,6},{8,9},{9,8},{10,11... | collective-permute-start | bytes 3145736 | tf_op jit(solution)/shard_map/ppermute | solution.py:92
  307.0 27.0 %collective-permute-start.13 = (bf16[256,2048]{1,0:T(8,128)(2,1)}, bf16[256,2048]{1,0:T(8,128)(2,1)}, u32[]{:S(2)}, u32[]{:S(2)}) collective-permute-start(bf16[256,2048]{1,0:T(8,128)(2,1)} %get-tuple-element.186), channel_id=1, source_target_pairs={{0,1},{1,0},{2,3},{3,2},{4,5},{5,4},{6,7},{7,6},{8,9},{9,8},{10,11... | collective-permute-start | bytes 3145736 | tf_op jit(solution)/shard_map/ppermute | solution.py:92
  307.5 23.6 %copy-start.20 = (bf16[256,2048]{1,0:T(8,128)(2,1)S(1)}, bf16[256,2048]{1,0:T(8,128)(2,1)}, u32[]{:S(2)}) copy-start(bf16[256,2048]{1,0:T(8,128)(2,1)} %get-tuple-element.174) | copy-start | bytes 3145732
  329.7 7.8 %collective-permute-start.17 = (bf16[256,2048]{1,0:T(8,128)(2,1)}, bf16[256,2048]{1,0:T(8,128)(2,1)S(1)}, u32[]{:S(2)}, u32[]{:S(2)}) collective-permute-start(bf16[256,2048]{1,0:T(8,128)(2,1)} %get-tuple-element.190), channel_id=1, source_target_pairs={{0,1},{1,0},{2,3},{3,2},{4,5},{5,4},{6,7},{7,6},{8,9},{9,8},{10,11... | collective-permute-start | bytes 3145736 | tf_op jit(solution)/shard_map/ppermute | solution.py:92
  329.7 7.8 %collective-permute-start.18 = (bf16[256,2048]{1,0:T(8,128)(2,1)}, bf16[256,2048]{1,0:T(8,128)(2,1)S(1)}, u32[]{:S(2)}, u32[]{:S(2)}) collective-permute-start(bf16[256,2048]{1,0:T(8,128)(2,1)} %get-tuple-element.191), channel_id=1, source_target_pairs={{0,1},{1,0},{2,3},{3,2},{4,5},{5,4},{6,7},{7,6},{8,9},{9,8},{10,11... | collective-permute-start | bytes 3145736 | tf_op jit(solution)/shard_map/ppermute | solution.py:92
  330.6 7.0 %collective-permute-start.16 = (bf16[256,2048]{1,0:T(8,128)(2,1)}, bf16[256,2048]{1,0:T(8,128)(2,1)S(1)}, u32[]{:S(2)}, u32[]{:S(2)}) collective-permute-start(bf16[256,2048]{1,0:T(8,128)(2,1)} %get-tuple-element.183), channel_id=1, source_target_pairs={{0,1},{1,0},{2,3},{3,2},{4,5},{5,4},{6,7},{7,6},{8,9},{9,8},{10,11... | collective-permute-start | bytes 3145736 | tf_op jit(solution)/shard_map/ppermute | solution.py:92
  330.6 7.0 %collective-permute-start.19 = (bf16[256,2048]{1,0:T(8,128)(2,1)}, bf16[256,2048]{1,0:T(8,128)(2,1)S(1)}, u32[]{:S(2)}, u32[]{:S(2)}) collective-permute-start(bf16[256,2048]{1,0:T(8,128)(2,1)} %get-tuple-element.192), channel_id=1, source_target_pairs={{0,1},{1,0},{2,3},{3,2},{4,5},{5,4},{6,7},{7,6},{8,9},{9,8},{10,11... | collective-permute-start | bytes 3145736 | tf_op jit(solution)/shard_map/ppermute | solution.py:92
  338.5 42.7 %collective-permute-start.25 = (bf16[256,2048]{1,0:T(8,128)(2,1)S(1)}, bf16[256,2048]{1,0:T(8,128)(2,1)}, u32[]{:S(2)}, u32[]{:S(2)}) collective-permute-start(bf16[256,2048]{1,0:T(8,128)(2,1)S(1)} %add_convert_fusion.4), channel_id=1, source_target_pairs={{0,4},{1,5},{2,6},{3,7},{4,0},{5,1},{6,2},{7,3},{8,12},{9,13},{10,... | collective-permute-start | bytes 3145736 | tf_op jit(solution)/shard_map/ppermute | solution.py:92
  340.4 40.7 %collective-permute-start.24 = (bf16[256,2048]{1,0:T(8,128)(2,1)S(1)}, bf16[256,2048]{1,0:T(8,128)(2,1)}, u32[]{:S(2)}, u32[]{:S(2)}) collective-permute-start(bf16[256,2048]{1,0:T(8,128)(2,1)S(1)} %add_convert_fusion.5), channel_id=1, source_target_pairs={{0,2},{1,3},{2,0},{3,1},{4,6},{5,7},{6,4},{7,5},{8,10},{9,11},{10,... | collective-permute-start | bytes 3145736 | tf_op jit(solution)/shard_map/ppermute | solution.py:92
  357.4 17.4 %collective-permute-start.14 = (bf16[128,2048]{1,0:T(8,128)(2,1)S(1)}, bf16[128,2048]{1,0:T(8,128)(2,1)S(1)}, u32[]{:S(2)}, u32[]{:S(2)}) collective-permute-start(bf16[128,2048]{1,0:T(8,128)(2,1)S(1)} %get-tuple-element.277), channel_id=1, source_target_pairs={{0,4},{1,5},{2,6},{3,7},{4,0},{5,1},{6,2},{7,3},{8,12},{9,13},{10,... | collective-permute-start | bytes 1572872 | tf_op jit(solution)/shard_map/ppermute | solution.py:92
  358.5 18.0 %collective-permute-start.15 = (bf16[128,2048]{1,0:T(8,128)(2,1)S(1)}, bf16[128,2048]{1,0:T(8,128)(2,1)S(1)}, u32[]{:S(2)}, u32[]{:S(2)}) collective-permute-start(bf16[128,2048]{1,0:T(8,128)(2,1)S(1)} %get-tuple-element.275), channel_id=1, source_target_pairs={{0,2},{1,3},{2,0},{3,1},{4,6},{5,7},{6,4},{7,5},{8,10},{9,11},{10,... | collective-permute-start | bytes 1572872 | tf_op jit(solution)/shard_map/ppermute | solution.py:92
  386.8 5.0 copy-start.25
  387.7 14.9 %collective-permute-start.27 = (bf16[128,2048]{1,0:T(8,128)(2,1)S(1)}, bf16[128,2048]{1,0:T(8,128)(2,1)S(1)}, u32[]{:S(2)}, u32[]{:S(2)}) collective-permute-start(bf16[128,2048]{1,0:T(8,128)(2,1)S(1)} %get-tuple-element.271), channel_id=1, source_target_pairs={{0,2},{1,3},{2,0},{3,1},{4,6},{5,7},{6,4},{7,5},{8,10},{9,11},{10,... | collective-permute-start | bytes 1572872 | tf_op jit(solution)/shard_map/ppermute | solution.py:92
  388.3 14.9 %collective-permute-start.26 = (bf16[128,2048]{1,0:T(8,128)(2,1)S(1)}, bf16[128,2048]{1,0:T(8,128)(2,1)S(1)}, u32[]{:S(2)}, u32[]{:S(2)}) collective-permute-start(bf16[128,2048]{1,0:T(8,128)(2,1)S(1)} %get-tuple-element.273), channel_id=1, source_target_pairs={{0,4},{1,5},{2,6},{3,7},{4,0},{5,1},{6,2},{7,3},{8,12},{9,13},{10,... | collective-permute-start | bytes 1572872 | tf_op jit(solution)/shard_map/ppermute | solution.py:92
  389.6 24.2 %collective-permute-start.22 = (bf16[128,2048]{1,0:T(8,128)(2,1)S(1)}, bf16[128,2048]{1,0:T(8,128)(2,1)S(1)}, u32[]{:S(2)}, u32[]{:S(2)}) collective-permute-start(bf16[128,2048]{1,0:T(8,128)(2,1)S(1)} %copy-done.24), channel_id=1, source_target_pairs={{0,2},{1,3},{2,0},{3,1},{4,6},{5,7},{6,4},{7,5},{8,10},{9,11},{10,... | collective-permute-start | bytes 1572872 | tf_op jit(solution)/shard_map/ppermute | solution.py:92
  391.0 23.4 %collective-permute-start.20 = (bf16[128,2048]{1,0:T(8,128)(2,1)S(1)}, bf16[128,2048]{1,0:T(8,128)(2,1)S(1)}, u32[]{:S(2)}, u32[]{:S(2)}) collective-permute-start(bf16[128,2048]{1,0:T(8,128)(2,1)S(1)} %copy-done.24), channel_id=1, source_target_pairs={{0,4},{1,5},{2,6},{3,7},{4,0},{5,1},{6,2},{7,3},{8,12},{9,13},{10,... | collective-permute-start | bytes 1572872 | tf_op jit(solution)/shard_map/ppermute | solution.py:92
  391.8 33.9 %collective-permute-start.23 = (bf16[128,2048]{1,0:T(8,128)(2,1)S(1)}, bf16[128,2048]{1,0:T(8,128)(2,1)S(1)}, u32[]{:S(2)}, u32[]{:S(2)}) collective-permute-start(bf16[128,2048]{1,0:T(8,128)(2,1)S(1)} %copy-done.25), channel_id=1, source_target_pairs={{0,4},{1,5},{2,6},{3,7},{4,0},{5,1},{6,2},{7,3},{8,12},{9,13},{10,... | collective-permute-start | bytes 1572872 | tf_op jit(solution)/shard_map/ppermute | solution.py:92
  402.6 24.5 %collective-permute-start.21 = (bf16[128,2048]{1,0:T(8,128)(2,1)S(1)}, bf16[128,2048]{1,0:T(8,128)(2,1)}, u32[]{:S(2)}, u32[]{:S(2)}) collective-permute-start(bf16[128,2048]{1,0:T(8,128)(2,1)S(1)} %copy-done.25), channel_id=1, source_target_pairs={{0,2},{1,3},{2,0},{3,1},{4,6},{5,7},{6,4},{7,5},{8,10},{9,11},{10,... | collective-permute-start | bytes 1572872 | tf_op jit(solution)/shard_map/ppermute | solution.py:92
  409.5 27.5 %collective-permute-start.33 = (bf16[128,2048]{1,0:T(8,128)(2,1)}, bf16[128,2048]{1,0:T(8,128)(2,1)}, u32[]{:S(2)}, u32[]{:S(2)}) collective-permute-start(bf16[128,2048]{1,0:T(8,128)(2,1)} %get-tuple-element.209.refs_4_), channel_id=1, source_target_pairs={{0,4},{1,5},{2,6},{3,7},{4,0},{5,1},{6,2},{7,3},{8,12},{9,13},{10,... | collective-permute-start | bytes 1572872 | tf_op jit(solution)/shard_map/ppermute | solution.py:92
  413.8 31.5 %copy-start.26 = (bf16[128,2048]{1,0:T(8,128)(2,1)}, bf16[128,2048]{1,0:T(8,128)(2,1)S(1)}, u32[]{:S(2)}) copy-start(bf16[128,2048]{1,0:T(8,128)(2,1)S(1)} %collective-permute-done.22.refs_2_) | copy-start | bytes 1572868
  413.8 35.2 %collective-permute-start.32 = (bf16[144,2048]{1,0:T(8,128)(2,1)}, bf16[144,2048]{1,0:T(8,128)(2,1)S(1)}, u32[]{:S(2)}, u32[]{:S(2)}) collective-permute-start(bf16[144,2048]{1,0:T(8,128)(2,1)} %get-tuple-element.208.refs_0_), channel_id=1, source_target_pairs={{0,2},{1,3},{2,0},{3,1},{4,6},{5,7},{6,4},{7,5},{8,10},{9,11},{10,... | collective-permute-start | bytes 1769480 | tf_op jit(solution)/shard_map/ppermute | solution.py:92
  414.4 30.8 %copy-start.27 = (bf16[128,2048]{1,0:T(8,128)(2,1)}, bf16[128,2048]{1,0:T(8,128)(2,1)S(1)}, u32[]{:S(2)}) copy-start(bf16[128,2048]{1,0:T(8,128)(2,1)S(1)} %collective-permute-done.20.refs_1_) | copy-start | bytes 1572868
  414.5 35.2 %collective-permute-start.30 = (bf16[144,2048]{1,0:T(8,128)(2,1)}, bf16[144,2048]{1,0:T(8,128)(2,1)}, u32[]{:S(2)}, u32[]{:S(2)}) collective-permute-start(bf16[144,2048]{1,0:T(8,128)(2,1)} %get-tuple-element.208.refs_0_), channel_id=1, source_target_pairs={{0,4},{1,5},{2,6},{3,7},{4,0},{5,1},{6,2},{7,3},{8,12},{9,13},{10,... | collective-permute-start | bytes 1769480 | tf_op jit(solution)/shard_map/ppermute | solution.py:92
  425.7 23.3 %collective-permute-start.31 = (bf16[128,2048]{1,0:T(8,128)(2,1)}, bf16[128,2048]{1,0:T(8,128)(2,1)}, u32[]{:S(2)}, u32[]{:S(2)}) collective-permute-start(bf16[128,2048]{1,0:T(8,128)(2,1)} %get-tuple-element.209.refs_4_), channel_id=1, source_target_pairs={{0,2},{1,3},{2,0},{3,1},{4,6},{5,7},{6,4},{7,5},{8,10},{9,11},{10,... | collective-permute-start | bytes 1572872 | tf_op jit(solution)/shard_map/ppermute | solution.py:92
  427.1 30.9 %collective-permute-start.28 = (bf16[128,2048]{1,0:T(8,128)(2,1)S(1)}, bf16[128,2048]{1,0:T(8,128)(2,1)S(1)}, u32[]{:S(2)}, u32[]{:S(2)}) collective-permute-start(bf16[128,2048]{1,0:T(8,128)(2,1)S(1)} %collective-permute-done.20.refs_1_), channel_id=1, source_target_pairs={{0,2},{1,3},{2,0},{3,1},{4,6},{5,7},{6,4},{7,5},{8,10},{9,11},{10,... | collective-permute-start | bytes 1572872 | tf_op jit(solution)/shard_map/ppermute | solution.py:92
  437.0 21.4 %collective-permute-start.29 = (bf16[128,2048]{1,0:T(8,128)(2,1)}, bf16[128,2048]{1,0:T(8,128)(2,1)S(1)}, u32[]{:S(2)}, u32[]{:S(2)}) collective-permute-start(bf16[128,2048]{1,0:T(8,128)(2,1)} %collective-permute-done.21.refs_5_), channel_id=1, source_target_pairs={{0,4},{1,5},{2,6},{3,7},{4,0},{5,1},{6,2},{7,3},{8,12},{9,13},{10,... | collective-permute-start | bytes 1572872 | tf_op jit(solution)/shard_map/ppermute | solution.py:92
  449.0 15.5 %copy-start.22 = (bf16[144,2048]{1,0:T(8,128)(2,1)}, bf16[144,2048]{1,0:T(8,128)(2,1)S(1)}, u32[]{:S(2)}) copy-start(bf16[144,2048]{1,0:T(8,128)(2,1)S(1)} %collective-permute-done.32.refs_2_) | copy-start | bytes 1769476
  449.7 15.0 %copy-start.10 = (bf16[4,512,256]{2,1,0:T(8,128)(2,1)S(1)}, bf16[4,512,256]{2,1,0:T(8,128)(2,1)}, u32[]{:S(2)}) copy-start(bf16[4,512,256]{2,1,0:T(8,128)(2,1)} %get-tuple-element.232) | copy-start | bytes 3145732
  464.6 19.2 %collective-permute-start.34 = (bf16[1024,2048]{1,0:T(8,128)(2,1)}, bf16[1024,2048]{1,0:T(8,128)(2,1)}, u32[]{:S(2)}, u32[]{:S(2)}) collective-permute-start(bf16[1024,2048]{1,0:T(8,128)(2,1)} %pack_rows.2.refs_0_), channel_id=1, source_target_pairs={{0,1},{1,0},{2,3},{3,2},{4,5},{5,4},{6,7},{7,6},{8,9},{9,8},{10,11... | collective-permute-start | bytes 12582920 | tf_op jit(solution)/shard_map/ppermute | solution.py:92
  466.2 30.1 %collective-permute-start.38 = (bf16[4,512,256]{2,1,0:T(8,128)(2,1)S(1)}, bf16[4,512,256]{2,1,0:T(8,128)(2,1)}, u32[]{:S(2)}, u32[]{:S(2)}) collective-permute-start(bf16[4,512,256]{2,1,0:T(8,128)(2,1)S(1)} %add_convert_fusion), channel_id=1, source_target_pairs={{24,16},{16,8},{8,0},{25,17},{17,9},{9,1},{26,18},{18,10},{10,2},{... | collective-permute-start | bytes 3145736 | tf_op jit(solution)/shard_map/ppermute | solution.py:87
  470.0 27.6 %collective-permute-start.37 = (bf16[4,512,256]{2,1,0:T(8,128)(2,1)}, bf16[4,512,256]{2,1,0:T(8,128)(2,1)}, u32[]{:S(2)}, u32[]{:S(2)}) collective-permute-start(bf16[4,512,256]{2,1,0:T(8,128)(2,1)} %add_convert_fusion.1), channel_id=1, source_target_pairs={{0,8},{8,16},{16,24},{1,9},{9,17},{17,25},{2,10},{10,18},{18,26},{... | collective-permute-start | bytes 3145736 | tf_op jit(solution)/shard_map/ppermute | solution.py:87
  475.6 29.8 %collective-permute-start.36 = (bf16[128,2048]{1,0:T(8,128)(2,1)}, bf16[128,2048]{1,0:T(8,128)(2,1)}, u32[]{:S(2)}, u32[]{:S(2)}) collective-permute-start(bf16[128,2048]{1,0:T(8,128)(2,1)} %collective-permute-done.31.refs_5_), channel_id=1, source_target_pairs={{0,4},{1,5},{2,6},{3,7},{4,0},{5,1},{6,2},{7,3},{8,12},{9,13},{10,... | collective-permute-start | bytes 1572872 | tf_op jit(solution)/shard_map/ppermute | solution.py:92
  477.2 28.2 %collective-permute-start.35 = (bf16[144,2048]{1,0:T(8,128)(2,1)}, bf16[144,2048]{1,0:T(8,128)(2,1)S(1)}, u32[]{:S(2)}, u32[]{:S(2)}) collective-permute-start(bf16[144,2048]{1,0:T(8,128)(2,1)} %collective-permute-done.30.refs_1_), channel_id=1, source_target_pairs={{0,2},{1,3},{2,0},{3,1},{4,6},{5,7},{6,4},{7,5},{8,10},{9,11},{10,... | collective-permute-start | bytes 1769480 | tf_op jit(solution)/shard_map/ppermute | solution.py:92
  489.2 8.4 %copy-start.2 = (f32[4,512,256]{2,1,0:T(8,128)S(1)}, f32[4,512,256]{2,1,0:T(8,128)}, u32[]{:S(2)}) copy-start(f32[4,512,256]{2,1,0:T(8,128)} %get-tuple-element.227) | copy-start | bytes 6291460
  511.4 7.9 %collective-permute-start.39 = (bf16[1088,2048]{1,0:T(8,128)(2,1)}, bf16[1088,2048]{1,0:T(8,128)(2,1)}, u32[]{:S(2)}, u32[]{:S(2)}) collective-permute-start(bf16[1088,2048]{1,0:T(8,128)(2,1)} %pack_rows.3.refs_0_.own_ref), channel_id=1, source_target_pairs={{0,1},{1,0},{2,3},{3,2},{4,5},{5,4},{6,7},{7,6},{8,9},{9,8},{10,11... | collective-permute-start | bytes 13369352 | tf_op jit(solution)/shard_map/ppermute | solution.py:92
  521.9 4.4 collective-permute-start.40
  526.3 10.2 %copy-start.43 = (f32[3,256]{1,0:T(4,128)S(1)}, f32[3,256]{1,0:T(4,128)}, u32[]{:S(2)}) copy-start(f32[3,256]{1,0:T(4,128)} %refs_5_.1) | copy-start | bytes 9220
  526.3 10.2 %copy-start.44 = (f32[3,256]{1,0:T(4,128)S(1)}, f32[3,256]{1,0:T(4,128)}, u32[]{:S(2)}) copy-start(f32[3,256]{1,0:T(4,128)} %param.41) | copy-start | bytes 9220
  526.3 10.2 %copy-start.45 = (f32[3,256]{1,0:T(4,128)S(1)}, f32[3,256]{1,0:T(4,128)}, u32[]{:S(2)}) copy-start(f32[3,256]{1,0:T(4,128)} %param.35) | copy-start | bytes 9220
  526.3 10.8 %copy-start.37 = (f32[2,2048]{1,0:T(2,128)S(1)}, f32[2,2048]{1,0:T(2,128)}, u32[]{:S(2)}) copy-start(f32[2,2048]{1,0:T(2,128)} %refs_6_.1) | copy-start | bytes 49156
  526.3 10.8 %copy-start.39 = (f32[2,2048]{1,0:T(2,128)S(1)}, f32[2,2048]{1,0:T(2,128)}, u32[]{:S(2)}) copy-start(f32[2,2048]{1,0:T(2,128)} %param.40) | copy-start | bytes 49156
  526.3 10.8 %copy-start.40 = (f32[2,2048]{1,0:T(2,128)S(1)}, f32[2,2048]{1,0:T(2,128)}, u32[]{:S(2)}) copy-start(f32[2,2048]{1,0:T(2,128)} %param.34) | copy-start | bytes 49156
  526.3 10.1 %collective-permute-start.41 = (f32[19,256]{1,0:T(8,128)S(1)}, f32[19,256]{1,0:T(8,128)S(1)}, u32[]{:S(2)}, u32[]{:S(2)}) collective-permute-start(f32[19,256]{1,0:T(8,128)S(1)} %add.150), channel_id=1, source_target_pairs={{0,16},{8,24},{16,0},{24,8},{1,17},{9,25},{17,1},{25,9},{2,18},{10... | collective-permute-start | bytes 58376 | tf_op jit(solution)/shard_map/ppermute | solution.py:92
  (29 other events, 56.0 us)
Sparse Core Ops, SparseCore 0:
  11.0 83.4 all-gather.3
  96.7 81.4 all-gather.5
  265.6 80.6 reduce-scatter.2
  357.5 78.7 reduce-scatter.4

commit v6 on v5

--- a/solution.py
+++ b/solution.py
@@ -56,35 +56,6 @@
 
 def after(value, *others):
     return lax.optimization_barrier((value, others))[0]
-
-
-def gather_hop(k, right, left, me):
-    n = lax.axis_size("dp")
-    to_right = [(a, a + 1) for a in range(k - 1, n - 1)]
-    to_left = [(a, a - 1) for a in range(1, n - k + 1)]
-    if k == n - 1 and n != 3:
-        both = lax.ppermute(jnp.where(me == 1, left, right), "dp", to_right + to_left)
-        return both, both
-    return lax.ppermute(right, "dp", to_right), lax.ppermute(left, "dp", to_left)
-
-
-def scatter_load(k, slots, right, left):
-    n = lax.axis_size("dp")
-    to_right, to_left = slots[n - k], slots[k]
-    if k > 1:
-        to_right = (to_right.astype(full) + right.astype(full)).astype(low)
-        to_left = (to_left.astype(full) + left.astype(full)).astype(low)
-    return to_right, to_left
-
-
-def scatter_hop(k, to_right, to_left):
-    n = lax.axis_size("dp")
-    rights = [(a, a + 1) for a in range(k)]
-    lefts = [(a, a - 1) for a in range(n - 1, n - 1 - k, -1)]
-    if k == 1 and n != 3:
-        both = lax.ppermute(to_right, "dp", rights + lefts)
-        return both, both
-    return lax.ppermute(to_right, "dp", rights), lax.ppermute(to_left, "dp", lefts)
 
 
 def swap(value, mask, axis="mp"):
@@ -138,28 +109,14 @@
     )(rows, norm_params)
 
 
-def fetch(n, me, pieces, target_of, sems, action):
-    def run(source, index, sem):
-        copy = pltpu.make_async_copy(source, target_of(index), sem)
-        if action == "start":
-            copy.start()
-        else:
-            copy.wait()
-
-    if len(pieces) == 1:
-        for j in range(n):
-            run(pieces[0].at[j], j, sems.at[j])
-        return
-    run(pieces[0], me, sems.at[0])
-    for k in range(1, n):
-
-        @pl.when(me >= k)
-        def _(k=k):
-            run(pieces[k], me - k, sems.at[k])
-
-        @pl.when(me + k < n)
-        def _(k=k):
-            run(pieces[n - 1 + k], me + k, sems.at[n - 1 + k])
+def fetch(gathered, target_of, sems):
+    copies = [
+        pltpu.make_async_copy(gathered.at[j], target_of(j), sems.at[j]) for j in range(gathered.shape[0])
+    ]
+    for copy in copies:
+        copy.start()
+    for copy in copies:
+        copy.wait()
 
 
 def swish_of(both):
@@ -206,52 +163,43 @@
 
 
 def wide_target(w_ref, piece):
-    return lambda index: w_ref.at[:, :, pl.ds(pl.multiple_of(index * piece, piece), piece)]
-
-
-def feed_kernel(n, count, me_ref, *refs):
-    pieces = refs[:count]
-    h_ref, c_ref, act_ref, grad_ref, w_ref, sems = refs[count:]
-    target_of = wide_target(w_ref, w_ref.shape[2] // n)
-
+    return lambda index: w_ref.at[:, :, pl.ds(index * piece, piece)]
+
+
+def feed_kernel(shards_ref, h_ref, c_ref, act_ref, grad_ref, w_ref, sems):
     @pl.when(pl.program_id(0) == 0)
     def _():
-        fetch(n, me_ref[0], pieces, target_of, sems, "start")
-        fetch(n, me_ref[0], pieces, target_of, sems, "wait")
+        fetch(shards_ref, wide_target(w_ref, shards_ref.shape[3]), sems)
 
     act_ref[...], grad_ref[...] = gates_of(w_ref, h_ref[...], c_ref[...])
 
 
-def feed_chunk(n, me, pieces, hidden, cot):
+def feed_chunk(shards, hidden, cot):
     rows, width = hidden.shape
-    units = pieces[0].shape[-2]
-    count = len(pieces)
+    n, _, units, _ = shards.shape
     block = min(512, rows)
-    row_spec = pl.BlockSpec((block, width), lambda i, m: (i, 0))
-    return pl.pallas_call(
-        functools.partial(feed_kernel, n, count),
-        grid_spec=pltpu.PrefetchScalarGridSpec(
-            num_scalar_prefetch=1,
-            grid=(rows // block,),
-            in_specs=[pl.BlockSpec(memory_space=pl.ANY)] * count + [row_spec, row_spec],
-            out_specs=[
-                pl.BlockSpec((units, block), lambda i, m: (0, i)),
-                pl.BlockSpec((2 * units, block), lambda i, m: (0, i)),
-                pl.BlockSpec((3, units, width), lambda i, m: (0, 0, 0)),
-            ],
-            scratch_shapes=[pltpu.SemaphoreType.DMA((2 * n - 1,))],
-        ),
+    row_spec = pl.BlockSpec((block, width), lambda i: (i, 0))
+    return pl.pallas_call(
+        feed_kernel,
+        grid=(rows // block,),
+        in_specs=[pl.BlockSpec(memory_space=pl.ANY), row_spec, row_spec],
+        out_specs=[
+            pl.BlockSpec((units, block), lambda i: (0, i)),
+            pl.BlockSpec((2 * units, block), lambda i: (0, i)),
+            pl.BlockSpec((3, units, width), lambda i: (0, 0, 0)),
+        ],
         out_shape=[
             shape((units, rows), low),
             shape((2 * units, rows), low),
             shape((3, units, width), low),
         ],
+        scratch_shapes=[pltpu.SemaphoreType.DMA((n,))],
         compiler_params=params(),
         cost_estimate=cost(
             6 * rows * width * units, 4 * rows * width + 12 * units * width, rows * units
         ),
         name="feed_chunk",
-    )(me, *pieces, hidden, cot)
+    )(shards, hidden, cot)
 
 
 def put_part(split, info_ref, parts, value):
@@ -290,17 +238,13 @@
     return block, steps, place, part_specs, part_shapes
 
 
-def out_last_kernel(n, count, split, info_ref, *refs):
-    pieces = refs[:count]
-    h_ref, early_ref = refs[count : count + 2]
-    parts = refs[count + 2 : -4]
+def out_last_kernel(split, info_ref, shards_ref, h_ref, early_ref, *refs):
+    parts = refs[:-4]
     act_ref, both_ref, w_ref, sems = refs[-4:]
-    target_of = wide_target(w_ref, w_ref.shape[2] // n)
 
     @pl.when(pl.program_id(0) == 0)
     def _():
-        fetch(n, info_ref[3], pieces, target_of, sems, "start")
-        fetch(n, info_ref[3], pieces, target_of, sems, "wait")
+        fetch(shards_ref, wide_target(w_ref, shards_ref.shape[3]), sems)
 
     both = dot_nt(join_gates(w_ref), h_ref[...])
     both_ref[...] = both
@@ -310,32 +254,31 @@
     put_part(split, info_ref, parts, early_ref[...].astype(full) + dot_tn(active, w_ref[2]))
 
 
-def out_last(n, info, split, pieces, hidden, early):
+def out_last(info, split, shards, hidden, early):
     rows, width = hidden.shape
-    units = pieces[0].shape[-2]
-    count = len(pieces)
+    n, _, units, _ = shards.shape
     block, steps, place, part_specs, part_shapes = last_blocks(split, rows, width)
     row_spec = pl.BlockSpec((block, width), lambda i, m: (place(i, m), 0))
     return pl.pallas_call(
-        functools.partial(out_last_kernel, n, count, split),
+        functools.partial(out_last_kernel, split),
         grid_spec=pltpu.PrefetchScalarGridSpec(
             num_scalar_prefetch=1,
             grid=(steps,),
-            in_specs=[pl.BlockSpec(memory_space=pl.ANY)] * count + [row_spec] * 2,
+            in_specs=[pl.BlockSpec(memory_space=pl.ANY)] + [row_spec] * 2,
             out_specs=part_specs
             + [
                 pl.BlockSpec((units, block), lambda i, m: (0, place(i, m))),
                 pl.BlockSpec((2 * units, block), lambda i, m: (0, place(i, m))),
                 pl.BlockSpec((3, units, width), lambda i, m: (0, 0, 0)),
             ],
-            scratch_shapes=[pltpu.SemaphoreType.DMA((2 * n - 1,))],
+            scratch_shapes=[pltpu.SemaphoreType.DMA((n,))],
         ),
         out_shape=part_shapes
         + [shape((units, rows), low), shape((2 * units, rows), full), shape((3, units, width), low)],
         compiler_params=params(),
         cost_estimate=cost(6 * rows * width * units, 8 * rows * width, rows * units),
         name="out_last",
-    )(info, *pieces, hidden, early)
+    )(info, shards, hidden, early)
 
 
 def hid_last_kernel(split, info_ref, w_ref, both_ref, c_ref, early_ref, *refs):
@@ -415,20 +358,12 @@
     return values * cosine + other * sine
 
 
-def project_kernel(n, count, me_ref, *refs):
-    pieces = refs[:count]
-    h_ref, c_ref, cos_ref, sin_ref, bias_ref, q_ref, k_ref, v_ref, o_ref, w_ref, sems = refs[
-        count:
-    ]
-    piece = pieces[0].shape[-2]
-
-    def target_of(index):
-        return w_ref.at[:, pl.ds(pl.multiple_of(index * piece, piece), piece), :]
+def project_kernel(shards_ref, h_ref, c_ref, cos_ref, sin_ref, bias_ref, q_ref, k_ref, v_ref, o_ref, w_ref, sems):
+    piece = shards_ref.shape[2]
 
     @pl.when(pl.program_id(0) == 0)
     def _():
-        fetch(n, me_ref[0], pieces, target_of, sems, "start")
-        fetch(n, me_ref[0], pieces, target_of, sems, "wait")
+        fetch(shards_ref, lambda index: w_ref.at[:, pl.ds(index * piece, piece), :], sems)
 
     h = h_ref[...]
     cosine, sine = cos_ref[...], sin_ref[...]
@@ -439,30 +374,25 @@
     o_ref[...] = dot_nn(c_ref[...], w_ref[3]).astype(low)
 
 
-def project(n, me, pieces, hidden, cot, cosine, sine, bias):
+def project(shards, hidden, cot, cosine, sine, bias):
     rows, width = hidden.shape
-    piece, cols = pieces[0].shape[-2:]
-    count = len(pieces)
+    n, _, _, cols = shards.shape
     block = min(512, rows)
-    row_spec = pl.BlockSpec((block, width), lambda i, m: (i, 0))
-    angle_spec = pl.BlockSpec((block, 128), lambda i, m: (i, 0))
-    out_spec = pl.BlockSpec((block, cols), lambda i, m: (i, 0))
-    return pl.pallas_call(
-        functools.partial(project_kernel, n, count),
-        grid_spec=pltpu.PrefetchScalarGridSpec(
-            num_scalar_prefetch=1,
-            grid=(rows // block,),
-            in_specs=[pl.BlockSpec(memory_space=pl.ANY)] * count
-            + [row_spec, row_spec, angle_spec, angle_spec]
-            + [pl.BlockSpec((3, cols), lambda i, m: (0, 0))],
-            out_specs=[out_spec] * 4 + [pl.BlockSpec((4, width, cols), lambda i, m: (0, 0, 0))],
-            scratch_shapes=[pltpu.SemaphoreType.DMA((2 * n - 1,))],
-        ),
+    row_spec = pl.BlockSpec((block, width), lambda i: (i, 0))
+    angle_spec = pl.BlockSpec((block, 128), lambda i: (i, 0))
+    out_spec = pl.BlockSpec((block, cols), lambda i: (i, 0))
+    return pl.pallas_call(
+        project_kernel,
+        grid=(rows // block,),
+        in_specs=[pl.BlockSpec(memory_space=pl.ANY), row_spec, row_spec, angle_spec, angle_spec]
+        + [pl.BlockSpec((3, cols), lambda i: (0, 0))],
+        out_specs=[out_spec] * 4 + [pl.BlockSpec((4, width, cols), lambda i: (0, 0, 0))],
         out_shape=[shape((rows, cols), low)] * 4 + [shape((4, width, cols), low)],
+        scratch_shapes=[pltpu.SemaphoreType.DMA((n,))],
         compiler_params=params(),
         cost_estimate=cost(8 * rows * width * cols, 4 * rows * width + 16 * width * cols),
         name="project",
-    )(me, *pieces, hidden, cot, cosine, sine, bias)
+    )(shards, hidden, cot, cosine, sine, bias)
 
 
 def attend_kernel(block, q_ref, k_ref, v_ref, o_ref, cos_ref, sin_ref, ctx_ref, mg_ref, bias_ref, dq, dk, dv):
@@ -550,61 +480,41 @@
     )(q, k, v, o, cosine, sine)
 
 
-def attend_grads_kernel(n, me_ref, h_ref, c_ref, mg_ref, ctx_ref, *refs):
-    own_ref, *slot_refs = refs[:n]
-    edge_ref, wide = refs[n:]
-    step = pl.program_id(0)
+def attend_grads_kernel(h_ref, c_ref, mg_ref, ctx_ref, out_ref, wide):
     cols = ctx_ref.shape[1]
 
-    @pl.when(step == 0)
+    @pl.when(pl.program_id(0) == 0)
     def _():
         for part in range(3):
             wide[:, part * cols : (part + 1) * cols] = mg_ref[part]
 
     grad = dot_tn(h_ref[...], wide[...])
-    grads = [grad[:, part * cols : (part + 1) * cols] for part in range(3)]
-    grads.append(dot_tn(c_ref[...], ctx_ref[...]))
-    for j in range(n):
-
-        @pl.when(step == j)
-        def _(j=j):
-            for part in range(4):
-                if j == 0:
-                    own_ref[part] = grads[part]
-                else:
-                    slot_refs[j - 1][part] = grads[part].astype(low)
-
-    @pl.when(lax.rem(me_ref[0] + step, n) == n - 1 - me_ref[0])
-    def _():
-        for part in range(4):
-            edge_ref[part] = grads[part].astype(low)
-
-
-def attend_grads(n, me, hidden, cot, mixed_grad, context):
+    for part in range(3):
+        out_ref[0, part] = grad[:, part * cols : (part + 1) * cols].astype(low)
+    out_ref[0, 3] = dot_tn(c_ref[...], ctx_ref[...]).astype(low)
+
+
+def attend_grads(n, hidden, cot, mixed_grad, context):
     rows, width = hidden.shape
     cols = context.shape[1]
     piece = width // n
-    whole3 = pl.BlockSpec((4, piece, cols), lambda i, m: (0, 0, 0))
-    cut_spec = pl.BlockSpec((rows, piece), lambda i, m: (0, lax.rem(m[0] + i, n)))
-    return pl.pallas_call(
-        functools.partial(attend_grads_kernel, n),
-        grid_spec=pltpu.PrefetchScalarGridSpec(
-            num_scalar_prefetch=1,
-            grid=(n,),
-            in_specs=[
-                cut_spec,
-                cut_spec,
-                pl.BlockSpec((3, rows, cols), lambda i, m: (0, 0, 0)),
-                pl.BlockSpec((rows, cols), lambda i, m: (0, 0)),
-            ],
-            out_specs=[whole3] * (n + 1),
-            scratch_shapes=[pltpu.VMEM((rows, 3 * cols), low)],
-        ),
-        out_shape=[shape((4, piece, cols), full)] + [shape((4, piece, cols), low)] * n,
+    cut_spec = pl.BlockSpec((rows, piece), lambda i: (0, i))
+    return pl.pallas_call(
+        attend_grads_kernel,
+        grid=(n,),
+        in_specs=[
+            cut_spec,
+            cut_spec,
+            pl.BlockSpec((3, rows, cols), lambda i: (0, 0, 0)),
+            pl.BlockSpec((rows, cols), lambda i: (0, 0)),
+        ],
+        out_specs=pl.BlockSpec((1, 4, piece, cols), lambda i: (i, 0, 0, 0)),
+        out_shape=shape((n, 4, piece, cols), low),
+        scratch_shapes=[pltpu.VMEM((rows, 3 * cols), low)],
         compiler_params=params(),
         cost_estimate=cost(8 * rows * width * cols, 4 * rows * width + 16 * width * cols),
         name="attend_grads",
-    )(me, hidden, cot, mixed_grad, context)
+    )(hidden, cot, mixed_grad, context)
 
 
 def heads_kernel(ctx_ref, mg_ref, wa_ref, hid_ref, out_ref):
@@ -793,65 +703,70 @@
     )(info, *pieces)
 
 
-def tail_kernel(own_ref, other_ref, out_ref):
-    def total(ref):
-        values = ref[...].astype(full)
-        sums = 0.0
-        for i in range(4):
-            at = i * tail_rows
-            sums += values[at : at + 2] + values[at + 2 : at + 4] + values[at + 4 : at + 6]
-        return sums
-
-    out_ref[...] = total(own_ref) + total(other_ref)
-
-
-def tail_sums(own, other):
-    count, width = own.shape
-    size = 4 * tail_rows
-    spec = pl.BlockSpec((size, width), lambda i: (count // size - 1, 0))
-    return pl.pallas_call(
-        tail_kernel,
-        grid=(1,),
-        in_specs=[spec, spec],
-        out_specs=pl.BlockSpec((2, width), lambda i: (0, 0)),
-        out_shape=shape((2, width), full),
-        compiler_params=params(),
-        cost_estimate=cost(20 * width, 512 * width),
-        name="tail_sums",
-    )(own, other)
+def tail_total(ref):
+    values = ref[...].astype(full)
+    sums = 0.0
+    for i in range(4):
+        at = i * tail_rows
+        sums += values[at : at + 2] + values[at + 2 : at + 4] + values[at + 4 : at + 6]
+    return sums
 
 
 def finish_kernel(info_ref, *refs):
-    out_ref = refs[-1]
-    value = refs[0][...]
-    if len(refs) > 2 and refs[1].shape == out_ref.shape:
-        value = refs[1][...].astype(full) + value.astype(full)
-    out_ref[...] = value
-
-
-def finish_rows(info, rows, half, part, cot=None, begun=None):
-    width = part.shape[1]
+    mine = (pl.program_id(0) // 4) == info_ref[0]
+    own_ref, other_ref = refs[:2]
+    summed = len(refs) > 3
+    out_ref = refs[5] if summed else refs[2]
+
+    def store(value):
+        if summed:
+            value = refs[2][...].astype(full) + value.astype(full)
+        out_ref[...] = value
+
+    @pl.when(mine)
+    def _():
+        store(own_ref[...])
+
+    @pl.when(jnp.logical_not(mine))
+    def _():
+        store(other_ref[...])
+
+    if summed:
+
+        @pl.when(pl.program_id(0) == 0)
+        def _():
+            refs[6][...] = tail_total(refs[3]) + tail_total(refs[4])
+
+
+def finish_rows(info, rows, own, other, cot=None):
+    width = own.shape[1]
     block = rows // 8
-    place = lambda i, m: ((m[0] ^ half) * 4 + i, 0)
-    ins, specs = [part], [pl.BlockSpec((block, width), lambda i, m: (i, 0))]
+    spec = pl.BlockSpec((block, width), lambda i, m: (i, 0))
+    edge = lambda i: jnp.where(i < 4, 0, 3)
+    ins = [own, other]
+    specs = [
+        pl.BlockSpec((block, width), lambda i, m: (jnp.where(i // 4 == m[0], i % 4, edge(i)), 0)),
+        pl.BlockSpec((block, width), lambda i, m: (jnp.where(i // 4 == m[0], edge(i), i % 4), 0)),
+    ]
+    out_specs, out_shape = [spec], [shape((rows, width), low if cot is None else full)]
     if cot is not None:
-        ins.append(cot)
-        specs.append(pl.BlockSpec((block, width), place))
-    if begun is not None:
-        ins.append(begun)
-        specs.append(pl.BlockSpec(memory_space=pl.ANY))
+        size = 4 * tail_rows
+        last = own.shape[0] // size - 1
+        ins += [cot, own, other]
+        specs += [spec] + [pl.BlockSpec((size, width), lambda i, m: (last, 0))] * 2
+        out_specs.append(pl.BlockSpec((2, width), lambda i, m: (0, 0)))
+        out_shape.append(shape((2, width), full))
     return pl.pallas_call(
         finish_kernel,
         grid_spec=pltpu.PrefetchScalarGridSpec(
             num_scalar_prefetch=1,
-            grid=(4,),
+            grid=(8,),
             in_specs=specs,
-            out_specs=pl.BlockSpec((block, width), place),
+            out_specs=out_specs,
         ),
-        out_shape=shape((rows, width), low if cot is None else full),
-        input_output_aliases={} if begun is None else {len(ins): 0},
-        compiler_params=params(),
-        cost_estimate=cost(rows * width, 4 * rows * width),
+        out_shape=out_shape,
+        compiler_params=params(),
+        cost_estimate=cost(2 * rows * width, 8 * rows * width),
         name="finish_rows",
     )(info, *ins)
 
@@ -922,9 +837,8 @@
     units = w_expand.shape[2]
     n = lax.axis_size("dp")
     group = lax.axis_size("mp")
-    me = lax.axis_index("dp").astype(jnp.int32).reshape(1)
     spot = lax.axis_index("mp").astype(jnp.int32)
-    info = jnp.stack([spot & 1, (spot >> 1) & 1, (spot >> 2) & 1, me[0]])
+    info = jnp.stack([spot & 1, (spot >> 1) & 1, (spot >> 2) & 1])
     fast = group == 8
 
     expand_t = jnp.transpose(w_expand, (1, 2, 0))
@@ -936,9 +850,9 @@
         for a, b in ((0, cut), (cut, units))
     ]
     attend_shard = jnp.concatenate([in_t, w_attend_out[None]], axis=0).astype(low)
-    attend_pieces = [lax.all_gather(attend_shard, "dp")]
-    first_shard, _ = lax.optimization_barrier((shards[0], attend_shard))
-    first_pieces = [lax.all_gather(first_shard, "dp")]
+    attend_all = lax.all_gather(attend_shard, "dp")
+    first_all = lax.all_gather(after(shards[0], attend_shard), "dp")
+    last_all = lax.all_gather(after(shards[1], shards[0]), "dp")
 
     tokens = inputs.reshape(rows, width)
     cot = cotangent.reshape(rows, width)
@@ -951,50 +865,25 @@
     cosine = jnp.where(lane < ROT, jnp.cos(angles), 1.0)
     sine = jnp.where(lane < half, -jnp.sin(angles), jnp.where(lane < ROT, jnp.sin(angles), 0.0))
 
-    q, k, v, o, w_attend = project(n, me, attend_pieces, hidden, cot, cosine, sine, attend_bias)
-    context, mixed_grad, bias_part = attend(batch, q, k, v, o, cosine, sine)
-    *attend_slots, edge = attend_grads(n, me, hidden, cot, mixed_grad, context)
-    hid_early, out_early = heads_parts(context, mixed_grad, w_attend)
-    last_shard, first_piece, attend_slots, edge, hid_early, out_early = lax.optimization_barrier(
-        (shards[1], first_pieces[0], attend_slots, edge, hid_early, out_early)
-    )
-
-    rights, lefts = [last_shard], [last_shard]
-    came = (None, None)
-    for k in range(1, n):
-        right, left = gather_hop(k, rights[-1], lefts[-1], me[0])
-        if k > 1:
-            if k == 2:
-                load = (after(edge, (rights[-1], lefts[-1])),) * 2
-            else:
-                load = scatter_load(k - 1, attend_slots, *came)
-            coming = scatter_hop(k - 1, *load)
-        meanwhile = ()
-        if k == 1:
-            active, gates_grad, w_feed = meanwhile = feed_chunk(n, me, [first_piece], hidden, cot)
-        elif k == 2:
-            hid_early, out_early = meanwhile = early_parts(
-                active, gates_grad, w_feed, hid_early, out_early
-            )
-        elif k == 3:
-            first_grads = meanwhile = feed_grads(n, hidden, cot, active, gates_grad)
-        if k > 1:
-            (right, left), came = after(((right, left), coming), meanwhile)
-        else:
-            right, left = after((right, left), meanwhile)
-        rights.append(right)
-        lefts.append(left)
-    last_pieces = [last_shard] + rights[1:] + lefts[1:]
-
     def scatter(grads):
         return lax.psum_scatter(grads, "dp", scatter_dimension=0, tiled=False)
 
-    first_grads = scatter(first_grads).reshape(3, cut, -1)
+    q, k, v, o, w_attend = project(attend_all, hidden, cot, cosine, sine, attend_bias)
+    context, mixed_grad, bias_part = attend(batch, q, k, v, o, cosine, sine)
+    attend_grad = attend_grads(n, hidden, cot, mixed_grad, context)
+    hid_early, out_early = heads_parts(context, mixed_grad, w_attend)
+    first_all = after(first_all, attend_grad, hid_early, out_early)
+    active, gates_grad, w_feed = feed_chunk(first_all, hidden, cot)
+    hid_early, out_early = early_parts(active, gates_grad, w_feed, hid_early, out_early)
+    first_grads = feed_grads(n, hidden, cot, active, gates_grad)
+    last_all = after(last_all, first_grads, hid_early, out_early)
+    attend_grad = scatter(after(attend_grad, last_all))
+    first_grads = scatter(after(first_grads, last_all)).reshape(3, cut, -1)
 
     total_tokens = rows * n
 
-    def update_attend(came):
-        grad = attend_slots[0] + came[0].astype(full) + came[1].astype(full)
+    def update_attend(grad):
+        grad = grad.astype(full)
         grad_in, grad_out = jnp.transpose(grad[:3], (1, 0, 2)), grad[3]
         rate_in = 0.5 / math.sqrt(width * total_tokens)
         rate_out = 1.8 / math.sqrt(width * batch * n)
@@ -1030,7 +919,7 @@
             pieces = (one, first, second, third)
             return pack_rows(info, [p[0] for p in pieces] + [p[1] for p in pieces])
 
-        *parts, active, both, w_last = out_last(n, info, True, last_pieces, hidden, out_early)
+        *parts, active, both, w_last = out_last(info, True, last_all, hidden, out_early)
         own_out, load_out = sum_cores(parts[4:], swap_cores(parts[:4]))
         one_out = both_ways(load_out, (2, 4))
         *parts, gates_grad = hid_last(info, True, w_last, after(both, load_out), cot, hid_early)
@@ -1052,32 +941,25 @@
         hid_two = both_ways(back, (2, 4))
         out_one, out_two = after((out_one, out_two), back)
         out_three = both_ways(out_one, (2, 4))
-        begun = update_feed(0, after(first_grads, out_one), states, rates)
-        hid_one, hid_two = after((hid_one, hid_two), begun)
+        attend_new = update_attend(after(attend_grad, out_one))
+        hid_one, hid_two = after((hid_one, hid_two), attend_new)
         hid_three = both_ways(hid_one, (2, 4))
-        out_three = after(out_three, hid_one)
+        begun = update_feed(0, after(first_grads, hid_one), states, rates)
+        out_three = after(out_three, begun)
         mine_out = join(add, out_one, out_two, out_three)
         other_out = swap(mine_out, 1)
-        load = scatter_load(n - 1, after(attend_slots, mine_out), *came)
-        came = scatter_hop(n - 1, *load)
-        output = finish_rows(info, rows, 0, after(mine_out, load))
-        output = finish_rows(info, rows, 1, after(other_out, output), begun=output)
-        done = update_feed(cut, after(last_grads, output), states, rates, begun)
-        attend_new = update_attend(after(came, done))
-        hid_three = after(hid_three, attend_new)
+        hid_three = after(hid_three, other_out)
         mine_hid = join(back, hid_one, hid_two, hid_three)
         other_hid = swap(mine_hid, 1)
-        input_grad = finish_rows(info, rows, 0, mine_hid, cot)
-        other_hid = after(other_hid, input_grad)
-        norm_part = tail_sums(mine_hid, other_hid)
+        (output,) = finish_rows(info, rows, after(mine_out, mine_hid), other_out)
+        input_grad, norm_part = finish_rows(info, rows, mine_hid, after(other_hid, output), cot)
         sums = small_sum(join_sums(norm_part, bias_part), "dp")
-        input_grad = finish_rows(info, rows, 1, after(other_hid, norm_part), cot, input_grad)
+        done = update_feed(cut, after(last_grads, input_grad), states, rates, begun)
         norm_grad, bias_grad = split_sums(sums, norm_part, bias_part)
     else:
-        out_part, active, both, w_last = out_last(n, info, False, last_pieces, hidden, out_early)
+        out_part, active, both, w_last = out_last(info, False, last_all, hidden, out_early)
         hid_part, gates_grad = hid_last(info, False, w_last, both, cot, hid_early)
-        came = scatter_hop(n - 1, *scatter_load(n - 1, attend_slots, *came))
-        attend_new = update_attend(came)
+        attend_new = update_attend(attend_grad)
         last_grads = scatter(feed_grads(n, hidden, cot, active, gates_grad)).reshape(3, units - cut, -1)
         hidden_grad = lax.psum(hid_part, "mp").astype(full)
         summed = lax.psum(out_part, "mp").astype(full)

time: 555 us -> 571 us (1.029)
  waiting for transfers between devices: 144 us -> 200 us
  starting transfers between devices: 61.5 us -> 25.9 us
  other arithmetic: 39.6 us -> 31.8 us
  Pallas kernels: 272 us -> 278 us
    all_gather x2 -> x3, waiting for transfers between devices: 63.7 us -> 95.9 us  [the longest x1 62 us: body(): attend_all = lax.all_gather(attend_shard, 'dp')]
    ppermute x10 -> x0, starting transfers between devices: 31.4 us -> none  [the longest x2 10.7 us: scatter_hop(): lax.ppermute(to_right, 'dp', rights)]
    reduce_scatter x2 -> x3, waiting for transfers between devices: 0.01 us -> 24.6 us  [scatter(): return lax.psum_scatter(grads, 'dp', scatter_dimension=0, tiled=False)]
    ppermute x10 -> x0, waiting for transfers between devices: 14.6 us -> none  [the longest x1 5.69 us: gather_hop(): lax.ppermute(jnp.where(me == 1, left, right), 'dp', to_right + to_left)]
    ppermute x32, waiting for transfers between devices: 65.9 us -> 79.1 us  [swap(): return lax.ppermute(value, axis, [(a, a ^ mask) for a in range(n)])]
    pallas_call x5 -> x4, Pallas kernels: 77.4 us -> 84.3 us  [the longest x1 35.5 us: out_last(): pl.pallas_call(functools.partial(out_last_kernel, split), grid_spec=pltpu...]
    convert_element_type x3 -> x1, other arithmetic: 8.09 us -> 1.49 us  [update_attend(): grad = grad.astype(full)]
    pallas_call x4 -> x2, Pallas kernels: 26.7 us -> 25.1 us  [finish_rows(): pl.pallas_call(finish_kernel, grid_spec=pltpu.PrefetchScalarGridSpec(num_...]
  transfers between devices with their start and end apart: 46 -> 38, of which waited for: 21 -> 17; matrix products, arithmetic and copies ran while one was open for 6% -> 6% of each run, Pallas kernels for 49% -> 49%
where the time goes in v6:
time: 571 us; the launch traced here: 560 us
  Pallas kernels  278 us (49%)
  waiting for transfers between devices  200 us (35%)
  other arithmetic  31.8 us (6%)
  starting transfers between devices  25.9 us (5%)
  between operations  15.1 us (3%)
  local copies, waits for them, and re-layouts  9.93 us (2%)
    ppermute x32, waiting for transfers between devices, swap(): return lax.ppermute(value, axis, [(a, a ^ mask) for a in range(n)])  79.1 us
    all_gather x1, waiting for transfers between devices, body(): attend_all = lax.all_gather(attend_shard, 'dp')  62 us
    pallas_call x1, Pallas kernels, out_last(): pl.pallas_call(functools.partial(out_last_kernel, split), grid_spec=pltpu...  35.5 us
    pallas_call x1, Pallas kernels, attend(): pl.pallas_call(functools.partial(attend_kernel, min(512, length)), grid=(...  34 us
    pallas_call x2, Pallas kernels, feed_grads(): pl.pallas_call(functools.partial(feed_grads_kernel, n, steps), grid=(step...  32.4 us
    all_gather x1, waiting for transfers between devices, body(): last_all = lax.all_gather(after(shards[1], shards[0]), 'dp')  31.1 us
    ppermute x32, starting transfers between devices, swap(): return lax.ppermute(value, axis, [(a, a ^ mask) for a in range(n)])  25.6 us
    pallas_call x2, Pallas kernels, finish_rows(): pl.pallas_call(finish_kernel, grid_spec=pltpu.PrefetchScalarGridSpec(num_...  25.1 us
  transfers between devices with their start and end apart: 38, of which 17 were waited for; matrix products, arithmetic and copies ran while one was open for 6% of the time, Pallas kernels for 49%

profile of v6, /device:TPU:0, one launch (start us, length us, event | category | flops | bytes accessed | tf_op | source)
XLA Modules:
  0.0 560.2 jit_solution(7378055737146587174)
XLA Ops:
  7.2 1.1 convert_bitcast_fusion.1
  8.3 1.5 convert_bitcast_fusion
  9.8 1.1 pad_maximum_fusion.2
  11.0 1.6 bitcast_convert_fusion
  13.4 1.1 pad_maximum_fusion.1
  14.6 1.1 pad_maximum_fusion
  15.8 11.2 %layer_norm.1.h_ref = bf16[2048,2048]{1,0:T(8,128)(2,1)} custom-call(bf16[2048,2048]{1,0:T(8,128)(2,1)} %bitcast.49, f32[2,2048]{1,0:T(2,128)} %refs_6_.1), custom_call_target="tpu_custom_call" | custom-call | flops 33554432 | bytes 16777216 | tf_op jit(solution)/shard_map/layer_norm/pallas_call | solution.py:97
  27.0 5.6 fusion.2
  32.5 62.0 %all-gather.6.cloned.1.call-done.shards_ref = bf16[4,4,512,256]{3,2,1,0:T(8,128)(2,1)} async-done(((bf16[1,4,512,256]{3,2,1,0:T(8,128)(2,1)}), bf16[4,4,512,256]{3,2,1,0:T(8,128)(2,1)}) %all-gather.6.cloned.1.call-update) | async-done | bytes 4194320 | tf_op jit(solution)/shard_map/all_gather | solution.py:853
  94.5 17.4 %project.1 = (bf16[2048,256]{1,0:T(8,128)(2,1)}, bf16[2048,256]{1,0:T(8,128)(2,1)}, bf16[2048,256]{1,0:T(8,128)(2,1)}, bf16[2048,256]{1,0:T(8,128)(2,1)}, bf16[4,2048,256]{2,1,0:T(8,128)(2,1)}) custom-call(bf16[4,4,512,256]{3,2,1,0:T(8,128)(2,1)} %all-gather.6.cloned.1.call-done.shards_ref, bf16[2048,2048]{1,0:T(8,128)(2,1)} %layer_norm.1.h_ref, ...), custom_call_target="tpu_custom_call" | custom-call | flops 8589934592 | bytes 25165824 | tf_op jit(solution)/shard_map/project/pallas_call | solution.py:384
  111.9 34.0 %attend.1 = (bf16[2048,256]{1,0:T(8,128)(2,1)}, bf16[3,2048,256]{2,1,0:T(8,128)(2,1)}, f32[3,256]{1,0:T(4,128)}) custom-call(bf16[2048,256]{1,0:T(8,128)(2,1)} %get-tuple-element.118.q_ref, bf16[2048,256]{1,0:T(8,128)(2,1)} %get-tuple-element.119.k_ref, bf16[2048,256]{1,0:T(8,128)(2,1)} %get-tuple-element.120.v_ref, ...), custom_call_target="tpu_custom_call" | custom-call | flops 21474836480 | bytes 10485760 | tf_op jit(solution)/shard_map/attend/pallas_call | solution.py:460
  145.9 14.8 %attend_grads.1 = bf16[4,4,512,256]{3,2,1,0:T(8,128)(2,1)} custom-call(bf16[2048,2048]{1,0:T(8,128)(2,1)} %layer_norm.1.h_ref, bf16[2048,2048]{1,0:T(8,128)(2,1)} %bitcast.64, bf16[3,2048,256]{2,1,0:T(8,128)(2,1)} %get-tuple-element.122.mg_ref, bf16[2048,256]{1,0:T(8,128)(2,1)} %get-tuple-element.123.ctx_ref), custom_call_target="tpu_custom_call" | custom-call | flops 8589934592 | bytes 25165824 | tf_op jit(solution)/shard_map/attend_grads/pallas_call | solution.py:502
  160.7 14.6 %heads_parts.1 = (bf16[2048,2048]{1,0:T(8,128)(2,1)}, bf16[2048,2048]{1,0:T(8,128)(2,1)}) custom-call(bf16[2048,256]{1,0:T(8,128)(2,1)} %get-tuple-element.123.ctx_ref, bf16[3,2048,256]{2,1,0:T(8,128)(2,1)} %get-tuple-element.122.mg_ref, bf16[4,2048,256]{2,1,0:T(8,128)(2,1)} %get-tuple-element.124.wa_ref), custom_call_target="tpu_custom_call" | custom-call | flops 8589934592 | bytes 25165824 | tf_op jit(solution)/shard_map/heads_parts/pallas_call | solution.py:531
  175.3 2.8 all-gather.10.cloned.1.call-done
  178.1 16.6 %feed_chunk.1 = (bf16[352,2048]{1,0:T(8,128)(2,1)}, bf16[704,2048]{1,0:T(8,128)(2,1)}, bf16[3,352,2048]{2,1,0:T(8,128)(2,1)}) custom-call(bf16[4,3,352,512]{3,2,1,0:T(8,128)(2,1)} %bitcast.88, bf16[2048,2048]{1,0:T(8,128)(2,1)} %layer_norm.1.h_ref, bf16[2048,2048]{1,0:T(8,128)(2,1)} %bitcast.65), custom_call_target="tpu_custom_call" | custom-call | flops 8858370048 | bytes 25427968 | tf_op jit(solution)/shard_map/feed_chunk/pallas_call | solution.py:182
  194.7 16.1 %feed_grads.2 = bf16[4,1056,512]{2,1,0:T(8,128)(2,1)} custom-call(bf16[2048,2048]{1,0:T(8,128)(2,1)} %layer_norm.1.h_ref, bf16[2048,2048]{1,0:T(8,128)(2,1)} %bitcast.66, bf16[352,2048]{1,0:T(8,128)(2,1)} %get-tuple-element.128.act_ref, bf16[704,2048]{1,0:T(8,128)(2,1)} %get-tuple-element.129.grad_ref), custom_call_target="tpu_custom_call" | custom-call | flops 8858370048 | bytes 25427968 | tf_op jit(solution)/shard_map/feed_grads/pallas_call | solution.py:330
  210.9 19.8 %early_parts.1 = (bf16[2048,2048]{1,0:T(8,128)(2,1)}, bf16[2048,2048]{1,0:T(8,128)(2,1)}) custom-call(bf16[352,2048]{1,0:T(8,128)(2,1)} %get-tuple-element.128.act_ref, bf16[704,2048]{1,0:T(8,128)(2,1)} %get-tuple-element.129.grad_ref, bf16[3,352,2048]{2,1,0:T(8,128)(2,1)} %get-tuple-element.130.w_ref, bf16[2048,2048]{1,0:T(8,128)(2,1)} %get-tuple-element.125.hid_in_ref, ...), custom_call_target="tpu_custom_call" | custom-call | flops 8858370048 | bytes 42205184 | tf_op jit(solution)/shard_map/early_parts/pallas_call | solution.py:559
  230.7 31.1 %all-gather.8.cloned.1.call-done = bf16[12,352,512]{2,1,0:T(8,128)(2,1)} async-done(((bf16[3,352,512]{2,1,0:T(8,128)(2,1)}), bf16[12,352,512]{2,1,0:T(8,128)(2,1)}) %all-gather.8.cloned.1.call-update) | async-done | bytes 4325392 | tf_op jit(solution)/shard_map/all_gather | solution.py:855
  262.4 35.5 %out_last.1 = (bf16[256,2048]{1,0:T(8,128)(2,1)}, bf16[256,2048]{1,0:T(8,128)(2,1)}, bf16[256,2048]{1,0:T(8,128)(2,1)}, bf16[256,2048]{1,0:T(8,128)(2,1)}, bf16[...) custom-call(s32[3]{0:T(128)} %pad_add_fusion.info_ref, ...), custom_call_target="tpu_custom_call" | custom-call | flops 8858370048 | bytes 33554432 | tf_op jit(solution)/shard_map/out_last/pallas_call | solution.py:262
  298.5 2.4 collective-permute-done.1
  300.9 1.6 add_convert_fusion.7
  302.5 1.6 collective-permute-start.2
  304.6 1.5 collective-permute-start.4
  306.7 22.2 %hid_last.1 = (bf16[256,2048]{1,0:T(8,128)(2,1)}, bf16[256,2048]{1,0:T(8,128)(2,1)}, bf16[256,2048]{1,0:T(8,128)(2,1)}, bf16[256,2048]{1,0:T(8,128)(2,1)}, bf16[...) custom-call(s32[3]{0:T(128)} %pad_add_fusion.info_ref, ...), custom_call_target="tpu_custom_call" | custom-call | flops 8858370048 | bytes 33554432 | tf_op jit(solution)/shard_map/hid_last/pallas_call | solution.py:298
  330.2 2.1 add_convert_fusion.5
  333.9 2.1 add_convert_fusion.4
  337.9 1.5 collective-permute-start.17
  341.6 1.4 collective-permute-start.7
  343.0 16.3 %feed_grads.3 = bf16[4,1056,512]{2,1,0:T(8,128)(2,1)} custom-call(bf16[2048,2048]{1,0:T(8,128)(2,1)} %layer_norm.1.h_ref, bf16[2048,2048]{1,0:T(8,128)(2,1)} %bitcast.68, bf16[352,2048]{1,0:T(8,128)(2,1)} %get-tuple-element.156.act_ref, bf16[704,2048]{1,0:T(8,128)(2,1)} %get-tuple-element.157.grad_ref), custom_call_target="tpu_custom_call" | custom-call | flops 8858370048 | bytes 25427968 | tf_op jit(solution)/shard_map/feed_grads/pallas_call | solution.py:330
  359.3 15.0 %collective-permute-done.6.refs_4_ = bf16[128,2048]{1,0:T(8,128)(2,1)S(1)} collective-permute-done((bf16[128,2048]{1,0:T(8,128)(2,1)}, bf16[128,2048]{1,0:T(8,128)(2,1)S(1)}, u32[]{:S(2)}, u32[]{:S(2)}) %collective-permute-start.6) | collective-permute-done | bytes 524320 | tf_op jit(solution)/shard_map/ppermute | solution.py:63
  374.3 1.7 collective-permute-done.7.refs_5_
  376.8 3.9 add_rows.1
  380.7 2.1 add_convert_fusion
  384.6 1.8 add_convert_fusion.1
  387.2 1.3 collective-permute-start.18
  388.5 1.2 collective-permute-start.14
  390.4 1.3 collective-permute-start.15
  391.7 6.8 %collective-permute-done.19.refs_5_ = bf16[128,2048]{1,0:T(8,128)(2,1)S(1)} collective-permute-done((bf16[128,2048]{1,0:T(8,128)(2,1)S(1)}, bf16[128,2048]{1,0:T(8,128)(2,1)S(1)}, u32[]{:S(2)}, u32[]{:S(2)}) %collective-permute-start.19) | collective-permute-done | bytes 524320 | tf_op jit(solution)/shard_map/ppermute | solution.py:63
  399.1 3.0 collective-permute-done.18.refs_4_
  402.9 5.6 %back_rows.1 = (bf16[144,2048]{1,0:T(8,128)(2,1)}, bf16[128,2048]{1,0:T(8,128)(2,1)}) custom-call(s32[3]{0:T(128)} %pad_add_fusion.info_ref, bf16[2048,2048]{1,0:T(8,128)(2,1)} %bitcast.52, bf16[2048,2048]{1,0:T(8,128)(2,1)} %bitcast.53, bf16[128,2048]{1,0:T(8,128)(2,1)} %get-tuple-element.228.refs_2_, bf16[128,2048]{1,0:T(8,128)(2,1)} %get-tuple-element.226.refs_3_, ...), custom_call_target="tpu_custom_call" | custom-call | flops 10485760 | bytes 4194304 | tf_op jit(solution)/shard_map/back_rows/pallas_call | solution.py:614
  408.5 1.3 collective-permute-start.25
  410.6 1.2 collective-permute-start.24
  411.8 1.6 collective-permute-done.12.refs_1_
  413.4 1.3 collective-permute-start.22
  414.7 9.9 %collective-permute-done.15.refs_6_ = bf16[128,2048]{1,0:T(8,128)(2,1)} collective-permute-done((bf16[128,2048]{1,0:T(8,128)(2,1)}, bf16[128,2048]{1,0:T(8,128)(2,1)}, u32[]{:S(2)}, u32[]{:S(2)}) %collective-permute-start.15) | collective-permute-done | bytes 524320 | tf_op jit(solution)/shard_map/ppermute | solution.py:63
  424.6 1.1 collective-permute-start.20
  425.8 1.3 collective-permute-start.21
  427.1 1.5 convert_element_type.137
  428.7 1.4 multiply_add_fusion.2
  430.1 5.8 %collective-permute-done.25.refs_6_ = bf16[128,2048]{1,0:T(8,128)(2,1)} collective-permute-done((bf16[128,2048]{1,0:T(8,128)(2,1)}, bf16[128,2048]{1,0:T(8,128)(2,1)}, u32[]{:S(2)}, u32[]{:S(2)}) %collective-permute-start.25) | collective-permute-done | bytes 524320 | tf_op jit(solution)/shard_map/ppermute | solution.py:63
  435.9 1.1 collective-permute-start.23
  437.0 3.1 multiply_add_fusion
  440.1 13.9 %collective-permute-done.23.refs_5_ = bf16[128,2048]{1,0:T(8,128)(2,1)S(1)} collective-permute-done((bf16[128,2048]{1,0:T(8,128)(2,1)S(1)}, bf16[128,2048]{1,0:T(8,128)(2,1)S(1)}, u32[]{:S(2)}, u32[]{:S(2)}) %collective-permute-start.23) | collective-permute-done | bytes 524320 | tf_op jit(solution)/shard_map/ppermute | solution.py:63
  454.1 7.5 %update_feed.2 = (f32[2,704,512]{2,1,0:T(8,128)}, f32[2,704,512]{2,1,0:T(8,128)}, f32[2,704,512]{2,1,0:T(8,128)}, f32[2,704,512]{2,1,0:T(8,128)}, f32[704,512]{1...) custom-call(bf16[3,352,512]{2,1,0:T(8,128)(2,1)} %bitcast.83, f32[2,704,512]{2,1,0:T(8,128)} %bitcast.54, ...), custom_call_target="tpu_custom_call" | custom-call | flops 5406720 | bytes 16220160 | tf_op jit(solution)/shard_map/update_feed/pallas_call | solution.py:796
  461.6 4.9 pack_rows.2.refs_0_
  467.2 1.6 collective-permute-start.27
  468.8 12.4 %collective-permute-done.27.refs_7_ = bf16[128,2048]{1,0:T(8,128)(2,1)S(1)} collective-permute-done((bf16[128,2048]{1,0:T(8,128)(2,1)S(1)}, bf16[128,2048]{1,0:T(8,128)(2,1)S(1)}, u32[]{:S(2)}, u32[]{:S(2)}) %collective-permute-start.27) | collective-permute-done | bytes 524320 | tf_op jit(solution)/shard_map/ppermute | solution.py:63
  481.3 1.2 collective-permute-done.26.refs_3_
  483.3 5.1 pack_rows.3.refs_0_.refs_3_
  488.5 10.2 %finish_rows.2 = bf16[2048,2048]{1,0:T(8,128)(2,1)} custom-call(s32[3]{0:T(128)} %pad_add_fusion.info_ref, bf16[1024,2048]{1,0:T(8,128)(2,1)} %pack_rows.2.refs_0_, bf16[1024,2048]{1,0:T(8,128)(2,1)} %collective-permute-done.28.refs_1_), custom_call_target="tpu_custom_call" | custom-call | flops 8388608 | bytes 33554432 | tf_op jit(solution)/shard_map/finish_rows/pallas_call | solution.py:759
  498.7 14.9 %finish_rows.3 = (f32[2048,2048]{1,0:T(8,128)}, f32[2,2048]{1,0:T(2,128)}) custom-call(s32[3]{0:T(128)} %pad_add_fusion.info_ref, bf16[1088,2048]{1,0:T(8,128)(2,1)} %pack_rows.3.refs_0_.refs_3_, bf16[1088,2048]{1,0:T(8,128)(2,1)} %collective-permute-done.29.refs_1_.refs_4_, bf16[2048,2048]{1,0:T(8,128)(2,1)} %bitcast.69, ...), custom_call_target="tpu_custom_call" | custom-call | flops 8388608 | bytes 33554432 | tf_op jit(solution)/shard_map/finish_rows/pallas_call | solution.py:759
  514.4 5.1 collective-permute-done.30
  519.9 24.6 %reduce-scatter.8.cloned.1.call-done = bf16[1,1056,512]{2,1,0:T(8,128)(2,1)} async-done(((bf16[4,1056,512]{2,1,0:T(8,128)(2,1)}), bf16[1,1056,512]{2,1,0:T(8,128)(2,1)}) %reduce-scatter.8.cloned.1.call-update) | async-done | bytes 1081360 | tf_op jit(solution)/shard_map/reduce_scatter | solution.py:869
  544.5 7.0 %update_feed.3 = (f32[2,704,512]{2,1,0:T(8,128)}, f32[2,704,512]{2,1,0:T(8,128)}, f32[2,704,512]{2,1,0:T(8,128)}, f32[2,704,512]{2,1,0:T(8,128)}, f32[704,512]{1...) custom-call(bf16[3,352,512]{2,1,0:T(8,128)(2,1)} %bitcast.82, ...), custom_call_target="tpu_custom_call", output_to_operand_aliasing={{0}: (7, {}), {1}: (8, {}), {2}: (9, {}), {3}: (10, {}), {4... | custom-call | flops 5406720 | bytes 16220160 | tf_op jit(solution)/shard_map/update_feed/pallas_call | solution.py:796
  (152 shorter events, 20.7 us)
Async XLA Ops:
  7.2 87.3 %all-gather.6.cloned.1.call-start = ((), (), s32[]{:S(2)}) async-start(), calls=%async_computation.3 | async-start | bytes 5242880 | tf_op jit(solution)/shard_map/all_gather | solution.py:853
  10.9 2.2 copy-start
  10.9 167.2 %all-gather.10.cloned.1.call-start = ((), (), s32[]{:S(2)}) async-start(), calls=%async_computation.8 | async-start | bytes 5406720 | tf_op jit(solution)/shard_map/all_gather | solution.py:854
  14.5 247.2 %all-gather.8.cloned.1.call-start = ((), (), s32[]{:S(2)}) async-start(), calls=%async_computation.7 | async-start | bytes 5406720 | tf_op jit(solution)/shard_map/all_gather | solution.py:855
  15.7 411.5 %reduce-scatter.6.cloned.1.call-start = ((), (), s32[]{:S(2)}) async-start(), calls=%async_computation.5 | async-start | bytes 5242880 | tf_op jit(solution)/shard_map/reduce_scatter | solution.py:869
  261.8 192.3 %reduce-scatter.4.cloned.1.call-start = ((), (), s32[]{:S(2)}) async-start(), calls=%async_computation.4 | async-start | bytes 5406720 | tf_op jit(solution)/shard_map/reduce_scatter | solution.py:869
  297.9 6.2 %copy-start.7 = (bf16[256,2048]{1,0:T(8,128)(2,1)S(1)}, bf16[256,2048]{1,0:T(8,128)(2,1)}, u32[]{:S(2)}) copy-start(bf16[256,2048]{1,0:T(8,128)(2,1)} %get-tuple-element.138) | copy-start | bytes 3145732
  298.0 2.9 collective-permute-start.1
  298.0 6.1 %collective-permute-start.3 = (bf16[256,2048]{1,0:T(8,128)(2,1)}, bf16[256,2048]{1,0:T(8,128)(2,1)S(1)}, u32[]{:S(2)}, u32[]{:S(2)}) collective-permute-start(bf16[256,2048]{1,0:T(8,128)(2,1)} %get-tuple-element.139), channel_id=1, source_target_pairs={{0,1},{1,0},{2,3},{3,2},{4,5},{5,4},{6,7},{7,6},{8,9},{9,8},{10,11... | collective-permute-start | bytes 3145736 | tf_op jit(solution)/shard_map/ppermute | solution.py:63
  302.5 26.4 %collective-permute-start.2 = (bf16[256,2048]{1,0:T(8,128)(2,1)S(1)}, bf16[256,2048]{1,0:T(8,128)(2,1)}, u32[]{:S(2)}, u32[]{:S(2)}) collective-permute-start(bf16[256,2048]{1,0:T(8,128)(2,1)S(1)} %add_convert_fusion.7), channel_id=1, source_target_pairs={{0,2},{1,3},{2,0},{3,1},{4,6},{5,7},{6,4},{7,5},{8,10},{9,11},{10,... | collective-permute-start | bytes 3145736 | tf_op jit(solution)/shard_map/ppermute | solution.py:63
  304.6 25.1 %collective-permute-start.4 = (bf16[256,2048]{1,0:T(8,128)(2,1)S(1)}, bf16[256,2048]{1,0:T(8,128)(2,1)}, u32[]{:S(2)}, u32[]{:S(2)}) collective-permute-start(bf16[256,2048]{1,0:T(8,128)(2,1)S(1)} %add_convert_fusion.6), channel_id=1, source_target_pairs={{0,4},{1,5},{2,6},{3,7},{4,0},{5,1},{6,2},{7,3},{8,12},{9,13},{10,... | collective-permute-start | bytes 3145736 | tf_op jit(solution)/shard_map/ppermute | solution.py:63
  306.1 23.6 %collective-permute-start = (bf16[256,2048]{1,0:T(8,128)(2,1)}, bf16[256,2048]{1,0:T(8,128)(2,1)}, u32[]{:S(2)}, u32[]{:S(2)}) collective-permute-start(bf16[256,2048]{1,0:T(8,128)(2,1)} %get-tuple-element.135), channel_id=1, source_target_pairs={{0,1},{1,0},{2,3},{3,2},{4,5},{5,4},{6,7},{7,6},{8,9},{9,8},{10,11... | collective-permute-start | bytes 3145736 | tf_op jit(solution)/shard_map/ppermute | solution.py:63
  306.1 27.2 %collective-permute-start.5 = (bf16[256,2048]{1,0:T(8,128)(2,1)}, bf16[256,2048]{1,0:T(8,128)(2,1)}, u32[]{:S(2)}, u32[]{:S(2)}) collective-permute-start(bf16[256,2048]{1,0:T(8,128)(2,1)} %get-tuple-element.146), channel_id=1, source_target_pairs={{0,1},{1,0},{2,3},{3,2},{4,5},{5,4},{6,7},{7,6},{8,9},{9,8},{10,11... | collective-permute-start | bytes 3145736 | tf_op jit(solution)/shard_map/ppermute | solution.py:63
  306.7 237.8 %reduce-scatter.8.cloned.1.call-start = ((), (), s32[]{:S(2)}) async-start(), calls=%async_computation.6 | async-start | bytes 5406720 | tf_op jit(solution)/shard_map/reduce_scatter | solution.py:869
  306.7 23.5 %copy-start.14 = (bf16[256,2048]{1,0:T(8,128)(2,1)S(1)}, bf16[256,2048]{1,0:T(8,128)(2,1)}, u32[]{:S(2)}) copy-start(bf16[256,2048]{1,0:T(8,128)(2,1)} %get-tuple-element.134) | copy-start | bytes 3145732
  328.9 8.1 %collective-permute-start.9 = (bf16[256,2048]{1,0:T(8,128)(2,1)}, bf16[256,2048]{1,0:T(8,128)(2,1)S(1)}, u32[]{:S(2)}, u32[]{:S(2)}) collective-permute-start(bf16[256,2048]{1,0:T(8,128)(2,1)} %get-tuple-element.150), channel_id=1, source_target_pairs={{0,1},{1,0},{2,3},{3,2},{4,5},{5,4},{6,7},{7,6},{8,9},{9,8},{10,11... | collective-permute-start | bytes 3145736 | tf_op jit(solution)/shard_map/ppermute | solution.py:63
  328.9 8.0 %collective-permute-start.10 = (bf16[256,2048]{1,0:T(8,128)(2,1)}, bf16[256,2048]{1,0:T(8,128)(2,1)S(1)}, u32[]{:S(2)}, u32[]{:S(2)}) collective-permute-start(bf16[256,2048]{1,0:T(8,128)(2,1)} %get-tuple-element.151), channel_id=1, source_target_pairs={{0,1},{1,0},{2,3},{3,2},{4,5},{5,4},{6,7},{7,6},{8,9},{9,8},{10,11... | collective-permute-start | bytes 3145736 | tf_op jit(solution)/shard_map/ppermute | solution.py:63
  329.7 7.3 %collective-permute-start.8 = (bf16[256,2048]{1,0:T(8,128)(2,1)}, bf16[256,2048]{1,0:T(8,128)(2,1)S(1)}, u32[]{:S(2)}, u32[]{:S(2)}) collective-permute-start(bf16[256,2048]{1,0:T(8,128)(2,1)} %get-tuple-element.143), channel_id=1, source_target_pairs={{0,1},{1,0},{2,3},{3,2},{4,5},{5,4},{6,7},{7,6},{8,9},{9,8},{10,11... | collective-permute-start | bytes 3145736 | tf_op jit(solution)/shard_map/ppermute | solution.py:63
  329.7 7.3 %collective-permute-start.11 = (bf16[256,2048]{1,0:T(8,128)(2,1)}, bf16[256,2048]{1,0:T(8,128)(2,1)S(1)}, u32[]{:S(2)}, u32[]{:S(2)}) collective-permute-start(bf16[256,2048]{1,0:T(8,128)(2,1)} %get-tuple-element.152), channel_id=1, source_target_pairs={{0,1},{1,0},{2,3},{3,2},{4,5},{5,4},{6,7},{7,6},{8,9},{9,8},{10,11... | collective-permute-start | bytes 3145736 | tf_op jit(solution)/shard_map/ppermute | solution.py:63
  337.0 2.5 copy-start.5
  337.0 2.9 copy-start.12
  337.0 2.9 copy-start.10
  337.9 42.8 %collective-permute-start.17 = (bf16[256,2048]{1,0:T(8,128)(2,1)S(1)}, bf16[256,2048]{1,0:T(8,128)(2,1)}, u32[]{:S(2)}, u32[]{:S(2)}) collective-permute-start(bf16[256,2048]{1,0:T(8,128)(2,1)S(1)} %add_convert_fusion.2), channel_id=1, source_target_pairs={{0,4},{1,5},{2,6},{3,7},{4,0},{5,1},{6,2},{7,3},{8,12},{9,13},{10,... | collective-permute-start | bytes 3145736 | tf_op jit(solution)/shard_map/ppermute | solution.py:63
  339.9 40.8 %collective-permute-start.16 = (bf16[256,2048]{1,0:T(8,128)(2,1)S(1)}, bf16[256,2048]{1,0:T(8,128)(2,1)}, u32[]{:S(2)}, u32[]{:S(2)}) collective-permute-start(bf16[256,2048]{1,0:T(8,128)(2,1)S(1)} %add_convert_fusion.3), channel_id=1, source_target_pairs={{0,2},{1,3},{2,0},{3,1},{4,6},{5,7},{6,4},{7,5},{8,10},{9,11},{10,... | collective-permute-start | bytes 3145736 | tf_op jit(solution)/shard_map/ppermute | solution.py:63
  340.6 33.7 %collective-permute-start.6 = (bf16[128,2048]{1,0:T(8,128)(2,1)}, bf16[128,2048]{1,0:T(8,128)(2,1)S(1)}, u32[]{:S(2)}, u32[]{:S(2)}) collective-permute-start(bf16[128,2048]{1,0:T(8,128)(2,1)} %get-tuple-element.231), channel_id=1, source_target_pairs={{0,4},{1,5},{2,6},{3,7},{4,0},{5,1},{6,2},{7,3},{8,12},{9,13},{10,... | collective-permute-start | bytes 1572872 | tf_op jit(solution)/shard_map/ppermute | solution.py:63
  341.6 34.4 %collective-permute-start.7 = (bf16[128,2048]{1,0:T(8,128)(2,1)}, bf16[128,2048]{1,0:T(8,128)(2,1)S(1)}, u32[]{:S(2)}, u32[]{:S(2)}) collective-permute-start(bf16[128,2048]{1,0:T(8,128)(2,1)} %get-tuple-element.229), channel_id=1, source_target_pairs={{0,2},{1,3},{2,0},{3,1},{4,6},{5,7},{6,4},{7,5},{8,10},{9,11},{10,... | collective-permute-start | bytes 1572872 | tf_op jit(solution)/shard_map/ppermute | solution.py:63
  374.3 1.7 copy-start.24
  376.8 3.9 copy-start.9
  382.8 1.8 copy-start.11
  383.7 14.9 %collective-permute-start.19 = (bf16[128,2048]{1,0:T(8,128)(2,1)S(1)}, bf16[128,2048]{1,0:T(8,128)(2,1)S(1)}, u32[]{:S(2)}, u32[]{:S(2)}) collective-permute-start(bf16[128,2048]{1,0:T(8,128)(2,1)S(1)} %get-tuple-element.225), channel_id=1, source_target_pairs={{0,2},{1,3},{2,0},{3,1},{4,6},{5,7},{6,4},{7,5},{8,10},{9,11},{10,... | collective-permute-start | bytes 1572872 | tf_op jit(solution)/shard_map/ppermute | solution.py:63
  386.3 2.2 copy-start.18
  387.2 14.9 %collective-permute-start.18 = (bf16[128,2048]{1,0:T(8,128)(2,1)S(1)}, bf16[128,2048]{1,0:T(8,128)(2,1)S(1)}, u32[]{:S(2)}, u32[]{:S(2)}) collective-permute-start(bf16[128,2048]{1,0:T(8,128)(2,1)S(1)} %get-tuple-element.227), channel_id=1, source_target_pairs={{0,4},{1,5},{2,6},{3,7},{4,0},{5,1},{6,2},{7,3},{8,12},{9,13},{10,... | collective-permute-start | bytes 1572872 | tf_op jit(solution)/shard_map/ppermute | solution.py:63
  388.5 21.3 %collective-permute-start.14 = (bf16[128,2048]{1,0:T(8,128)(2,1)S(1)}, bf16[128,2048]{1,0:T(8,128)(2,1)S(1)}, u32[]{:S(2)}, u32[]{:S(2)}) collective-permute-start(bf16[128,2048]{1,0:T(8,128)(2,1)S(1)} %copy-done.18), channel_id=1, source_target_pairs={{0,2},{1,3},{2,0},{3,1},{4,6},{5,7},{6,4},{7,5},{8,10},{9,11},{10,... | collective-permute-start | bytes 1572872 | tf_op jit(solution)/shard_map/ppermute | solution.py:63
  389.7 23.7 %collective-permute-start.12 = (bf16[128,2048]{1,0:T(8,128)(2,1)S(1)}, bf16[128,2048]{1,0:T(8,128)(2,1)}, u32[]{:S(2)}, u32[]{:S(2)}) collective-permute-start(bf16[128,2048]{1,0:T(8,128)(2,1)S(1)} %copy-done.18), channel_id=1, source_target_pairs={{0,4},{1,5},{2,6},{3,7},{4,0},{5,1},{6,2},{7,3},{8,12},{9,13},{10,... | collective-permute-start | bytes 1572872 | tf_op jit(solution)/shard_map/ppermute | solution.py:63
  390.4 34.3 %collective-permute-start.15 = (bf16[128,2048]{1,0:T(8,128)(2,1)}, bf16[128,2048]{1,0:T(8,128)(2,1)}, u32[]{:S(2)}, u32[]{:S(2)}) collective-permute-start(bf16[128,2048]{1,0:T(8,128)(2,1)} %get-tuple-element.161.refs_4_), channel_id=1, source_target_pairs={{0,4},{1,5},{2,6},{3,7},{4,0},{5,1},{6,2},{7,3},{8,12},{9,13},{10,... | collective-permute-start | bytes 1572872 | tf_op jit(solution)/shard_map/ppermute | solution.py:63
  398.5 3.5 copy-start.22
  398.5 26.1 %collective-permute-start.13 = (bf16[128,2048]{1,0:T(8,128)(2,1)}, bf16[128,2048]{1,0:T(8,128)(2,1)}, u32[]{:S(2)}, u32[]{:S(2)}) collective-permute-start(bf16[128,2048]{1,0:T(8,128)(2,1)} %get-tuple-element.161.refs_4_), channel_id=1, source_target_pairs={{0,2},{1,3},{2,0},{3,1},{4,6},{5,7},{6,4},{7,5},{8,10},{9,11},{10,... | collective-permute-start | bytes 1572872 | tf_op jit(solution)/shard_map/ppermute | solution.py:63
  402.9 34.2 %copy-start.4 = (f32[512,3,256]{2,0,1:T(8,128)S(1)}, f32[512,3,256]{2,0,1:T(8,128)}, u32[]{:S(2)}) copy-start(f32[512,3,256]{2,0,1:T(8,128)} %param.30) | copy-start | bytes 4718596
  408.5 20.1 %copy-start.2 = (f32[512,256]{1,0:T(8,128)S(1)}, f32[512,256]{1,0:T(8,128)}, u32[]{:S(2)}) copy-start(f32[512,256]{1,0:T(8,128)} %param.25) | copy-start | bytes 1572868
  408.5 27.4 %collective-permute-start.25 = (bf16[128,2048]{1,0:T(8,128)(2,1)}, bf16[128,2048]{1,0:T(8,128)(2,1)}, u32[]{:S(2)}, u32[]{:S(2)}) collective-permute-start(bf16[128,2048]{1,0:T(8,128)(2,1)} %get-tuple-element.169.refs_4_), channel_id=1, source_target_pairs={{0,4},{1,5},{2,6},{3,7},{4,0},{5,1},{6,2},{7,3},{8,12},{9,13},{10,... | collective-permute-start | bytes 1572872 | tf_op jit(solution)/shard_map/ppermute | solution.py:63
  410.6 43.4 %collective-permute-start.24 = (bf16[144,2048]{1,0:T(8,128)(2,1)}, bf16[144,2048]{1,0:T(8,128)(2,1)S(1)}, u32[]{:S(2)}, u32[]{:S(2)}) collective-permute-start(bf16[144,2048]{1,0:T(8,128)(2,1)} %get-tuple-element.168.refs_0_), channel_id=1, source_target_pairs={{0,2},{1,3},{2,0},{3,1},{4,6},{5,7},{6,4},{7,5},{8,10},{9,11},{10,... | collective-permute-start | bytes 1769480 | tf_op jit(solution)/shard_map/ppermute | solution.py:63
  413.4 40.6 %collective-permute-start.22 = (bf16[144,2048]{1,0:T(8,128)(2,1)}, bf16[144,2048]{1,0:T(8,128)(2,1)S(1)}, u32[]{:S(2)}, u32[]{:S(2)}) collective-permute-start(bf16[144,2048]{1,0:T(8,128)(2,1)} %get-tuple-element.168.refs_0_), channel_id=1, source_target_pairs={{0,4},{1,5},{2,6},{3,7},{4,0},{5,1},{6,2},{7,3},{8,12},{9,13},{10,... | collective-permute-start | bytes 1769480 | tf_op jit(solution)/shard_map/ppermute | solution.py:63
  424.6 37.0 %collective-permute-start.20 = (bf16[128,2048]{1,0:T(8,128)(2,1)}, bf16[128,2048]{1,0:T(8,128)(2,1)}, u32[]{:S(2)}, u32[]{:S(2)}) collective-permute-start(bf16[128,2048]{1,0:T(8,128)(2,1)} %collective-permute-done.12.refs_1_), channel_id=1, source_target_pairs={{0,2},{1,3},{2,0},{3,1},{4,6},{5,7},{6,4},{7,5},{8,10},{9,11},{10,... | collective-permute-start | bytes 1572872 | tf_op jit(solution)/shard_map/ppermute | solution.py:63
  425.8 35.8 %collective-permute-start.21 = (bf16[128,2048]{1,0:T(8,128)(2,1)}, bf16[128,2048]{1,0:T(8,128)(2,1)}, u32[]{:S(2)}, u32[]{:S(2)}) collective-permute-start(bf16[128,2048]{1,0:T(8,128)(2,1)} %collective-permute-done.13.refs_5_), channel_id=1, source_target_pairs={{0,4},{1,5},{2,6},{3,7},{4,0},{5,1},{6,2},{7,3},{8,12},{9,13},{10,... | collective-permute-start | bytes 1572872 | tf_op jit(solution)/shard_map/ppermute | solution.py:63
  428.7 7.2 %copy-start.19 = (bf16[128,2048]{1,0:T(8,128)(2,1)S(1)}, bf16[128,2048]{1,0:T(8,128)(2,1)}, u32[]{:S(2)}) copy-start(bf16[128,2048]{1,0:T(8,128)(2,1)} %get-tuple-element.169.refs_4_) | copy-start | bytes 1572868
  428.7 8.4 %copy-start.1 = (f32[512,3,256]{2,0,1:T(8,128)S(1)}, f32[512,3,256]{2,0,1:T(8,128)}, u32[]{:S(2)}) copy-start(f32[512,3,256]{2,0,1:T(8,128)} %param.24) | copy-start | bytes 4718596
  428.7 8.3 %copy-start.3 = (f32[512,3,256]{2,0,1:T(8,128)S(1)}, f32[512,3,256]{2,0,1:T(8,128)}, u32[]{:S(2)}) copy-start(f32[512,3,256]{2,0,1:T(8,128)} %param.36) | copy-start | bytes 4718596
  435.9 18.1 %collective-permute-start.23 = (bf16[128,2048]{1,0:T(8,128)(2,1)S(1)}, bf16[128,2048]{1,0:T(8,128)(2,1)S(1)}, u32[]{:S(2)}, u32[]{:S(2)}) collective-permute-start(bf16[128,2048]{1,0:T(8,128)(2,1)S(1)} %copy-done.19), channel_id=1, source_target_pairs={{0,2},{1,3},{2,0},{3,1},{4,6},{5,7},{6,4},{7,5},{8,10},{9,11},{10,... | collective-permute-start | bytes 1572872 | tf_op jit(solution)/shard_map/ppermute | solution.py:63
  454.0 13.2 %copy-start.21 = (bf16[128,2048]{1,0:T(8,128)(2,1)}, bf16[128,2048]{1,0:T(8,128)(2,1)S(1)}, u32[]{:S(2)}) copy-start(bf16[128,2048]{1,0:T(8,128)(2,1)S(1)} %collective-permute-done.23.refs_5_) | copy-start | bytes 1572868
  454.0 7.6 %copy-start.15 = (bf16[144,2048]{1,0:T(8,128)(2,1)}, bf16[144,2048]{1,0:T(8,128)(2,1)S(1)}, u32[]{:S(2)}) copy-start(bf16[144,2048]{1,0:T(8,128)(2,1)S(1)} %collective-permute-done.24.refs_2_) | copy-start | bytes 1769476
  454.0 12.6 %copy-start.16 = (bf16[144,2048]{1,0:T(8,128)(2,1)}, bf16[144,2048]{1,0:T(8,128)(2,1)S(1)}, u32[]{:S(2)}) copy-start(bf16[144,2048]{1,0:T(8,128)(2,1)S(1)} %collective-permute-done.22.refs_1_) | copy-start | bytes 1769476
  466.6 15.9 %collective-permute-start.28 = (bf16[1024,2048]{1,0:T(8,128)(2,1)}, bf16[1024,2048]{1,0:T(8,128)(2,1)}, u32[]{:S(2)}, u32[]{:S(2)}) collective-permute-start(bf16[1024,2048]{1,0:T(8,128)(2,1)} %pack_rows.2.refs_0_), channel_id=1, source_target_pairs={{0,1},{1,0},{2,3},{3,2},{4,5},{5,4},{6,7},{7,6},{8,9},{9,8},{10,11... | collective-permute-start | bytes 12582920 | tf_op jit(solution)/shard_map/ppermute | solution.py:63
  466.7 15.8 %collective-permute-start.26 = (bf16[144,2048]{1,0:T(8,128)(2,1)S(1)}, bf16[144,2048]{1,0:T(8,128)(2,1)S(1)}, u32[]{:S(2)}, u32[]{:S(2)}) collective-permute-start(bf16[144,2048]{1,0:T(8,128)(2,1)S(1)} %collective-permute-done.22.refs_1_), channel_id=1, source_target_pairs={{0,2},{1,3},{2,0},{3,1},{4,6},{5,7},{6,4},{7,5},{8,10},{9,11},{10,... | collective-permute-start | bytes 1769480 | tf_op jit(solution)/shard_map/ppermute | solution.py:63
  467.2 14.0 %collective-permute-start.27 = (bf16[128,2048]{1,0:T(8,128)(2,1)S(1)}, bf16[128,2048]{1,0:T(8,128)(2,1)S(1)}, u32[]{:S(2)}, u32[]{:S(2)}) collective-permute-start(bf16[128,2048]{1,0:T(8,128)(2,1)S(1)} %collective-permute-done.23.refs_5_), channel_id=1, source_target_pairs={{0,4},{1,5},{2,6},{3,7},{4,0},{5,1},{6,2},{7,3},{8,12},{9,13},{10,... | collective-permute-start | bytes 1572872 | tf_op jit(solution)/shard_map/ppermute | solution.py:63
  488.4 10.3 %collective-permute-start.29 = (bf16[1088,2048]{1,0:T(8,128)(2,1)}, bf16[1088,2048]{1,0:T(8,128)(2,1)}, u32[]{:S(2)}, u32[]{:S(2)}) collective-permute-start(bf16[1088,2048]{1,0:T(8,128)(2,1)} %pack_rows.3.refs_0_.refs_3_), channel_id=1, source_target_pairs={{0,1},{1,0},{2,3},{3,2},{4,5},{5,4},{6,7},{7,6},{8,9},{9,8},{10,11... | collective-permute-start | bytes 13369352 | tf_op jit(solution)/shard_map/ppermute | solution.py:63
  498.6 15.6 %copy-start.34 = (f32[3,256]{1,0:T(4,128)S(1)}, f32[3,256]{1,0:T(4,128)}, u32[]{:S(2)}) copy-start(f32[3,256]{1,0:T(4,128)} %get-tuple-element.201) | copy-start | bytes 9220
  514.3 5.2 collective-permute-start.30
  519.5 32.1 %collective-permute-start.31 = (f32[19,256]{1,0:T(8,128)S(1)}, f32[19,256]{1,0:T(8,128)S(1)}, u32[]{:S(2)}, u32[]{:S(2)}) collective-permute-start(f32[19,256]{1,0:T(8,128)S(1)} %add.128), channel_id=1, source_target_pairs={{0,16},{8,24},{16,0},{24,8},{1,17},{9,25},{17,1},{25,9},{2,18},{10... | collective-permute-start | bytes 58376 | tf_op jit(solution)/shard_map/ppermute | solution.py:63
  544.5 7.1 %copy-start.35 = (f32[3,256]{1,0:T(4,128)S(1)}, f32[3,256]{1,0:T(4,128)}, u32[]{:S(2)}) copy-start(f32[3,256]{1,0:T(4,128)} %bias_ref.1) | copy-start | bytes 9220
  544.5 7.1 %copy-start.36 = (f32[3,256]{1,0:T(4,128)S(1)}, f32[3,256]{1,0:T(4,128)}, u32[]{:S(2)}) copy-start(f32[3,256]{1,0:T(4,128)} %param.41) | copy-start | bytes 9220
  544.5 7.1 %copy-start.37 = (f32[3,256]{1,0:T(4,128)S(1)}, f32[3,256]{1,0:T(4,128)}, u32[]{:S(2)}) copy-start(f32[3,256]{1,0:T(4,128)} %param.35) | copy-start | bytes 9220
  544.5 7.8 %copy-start.29 = (f32[2,2048]{1,0:T(2,128)S(1)}, f32[2,2048]{1,0:T(2,128)}, u32[]{:S(2)}) copy-start(f32[2,2048]{1,0:T(2,128)} %refs_6_.1) | copy-start | bytes 49156
  544.5 7.8 %copy-start.31 = (f32[2,2048]{1,0:T(2,128)S(1)}, f32[2,2048]{1,0:T(2,128)}, u32[]{:S(2)}) copy-start(f32[2,2048]{1,0:T(2,128)} %param.40) | copy-start | bytes 49156
  544.5 7.8 %copy-start.32 = (f32[2,2048]{1,0:T(2,128)S(1)}, f32[2,2048]{1,0:T(2,128)}, u32[]{:S(2)}) copy-start(f32[2,2048]{1,0:T(2,128)} %param.34) | copy-start | bytes 49156
  (12 other events, 14.6 us)
Sparse Core Ops, SparseCore 0:
  11.0 83.4 all-gather.5
  96.7 81.4 all-gather.9
  180.3 81.4 all-gather.7
  263.9 75.2 reduce-scatter.5
  341.5 79.3 reduce-scatter.3
  466.8 77.6 reduce-scatter.7

commit v7 on v6

--- a/solution.py
+++ b/solution.py
@@ -877,7 +877,6 @@
     hid_early, out_early = early_parts(active, gates_grad, w_feed, hid_early, out_early)
     first_grads = feed_grads(n, hidden, cot, active, gates_grad)
     last_all = after(last_all, first_grads, hid_early, out_early)
-    attend_grad = scatter(after(attend_grad, last_all))
     first_grads = scatter(after(first_grads, last_all)).reshape(3, cut, -1)
 
     total_tokens = rows * n
@@ -922,6 +921,7 @@
         *parts, active, both, w_last = out_last(info, True, last_all, hidden, out_early)
         own_out, load_out = sum_cores(parts[4:], swap_cores(parts[:4]))
         one_out = both_ways(load_out, (2, 4))
+        attend_grad = scatter(after(attend_grad, load_out))
         *parts, gates_grad = hid_last(info, True, w_last, after(both, load_out), cot, hid_early)
         came_hid = swap_cores(parts[:4])
         near_out, load_out = sum_first(own_out, after(one_out, parts[0]))
@@ -941,17 +941,17 @@
         hid_two = both_ways(back, (2, 4))
         out_one, out_two = after((out_one, out_two), back)
         out_three = both_ways(out_one, (2, 4))
-        attend_new = update_attend(after(attend_grad, out_one))
-        hid_one, hid_two = after((hid_one, hid_two), attend_new)
+        begun = update_feed(0, after(first_grads, out_one), states, rates)
+        hid_one, hid_two = after((hid_one, hid_two), begun)
         hid_three = both_ways(hid_one, (2, 4))
-        begun = update_feed(0, after(first_grads, hid_one), states, rates)
-        out_three = after(out_three, begun)
+        out_three = after(out_three, hid_one)
         mine_out = join(add, out_one, out_two, out_three)
         other_out = swap(mine_out, 1)
-        hid_three = after(hid_three, other_out)
+        hid_three = after(hid_three, mine_out)
         mine_hid = join(back, hid_one, hid_two, hid_three)
         other_hid = swap(mine_hid, 1)
-        (output,) = finish_rows(info, rows, after(mine_out, mine_hid), other_out)
+        attend_new = update_attend(after(attend_grad, mine_hid))
+        (output,) = finish_rows(info, rows, mine_out, after(other_out, attend_new))
         input_grad, norm_part = finish_rows(info, rows, mine_hid, after(other_hid, output), cot)
         sums = small_sum(join_sums(norm_part, bias_part), "dp")
         done = update_feed(cut, after(last_grads, input_grad), states, rates, begun)
@@ -959,7 +959,7 @@
     else:
         out_part, active, both, w_last = out_last(info, False, last_all, hidden, out_early)
         hid_part, gates_grad = hid_last(info, False, w_last, both, cot, hid_early)
-        attend_new = update_attend(attend_grad)
+        attend_new = update_attend(scatter(attend_grad))
         last_grads = scatter(feed_grads(n, hidden, cot, active, gates_grad)).reshape(3, units - cut, -1)
         hidden_grad = lax.psum(hid_part, "mp").astype(full)
         summed = lax.psum(out_part, "mp").astype(full)

time: 571 us -> 554 us (0.970)
  waiting for transfers between devices: 200 us -> 181 us
    reduce_scatter x3, waiting for transfers between devices: 24.6 us -> 0.01 us  [scatter(): return lax.psum_scatter(grads, 'dp', scatter_dimension=0, tiled=False)]
    ppermute x32, waiting for transfers between devices: 79.1 us -> 84.9 us  [swap(): return lax.ppermute(value, axis, [(a, a ^ mask) for a in range(n)])]
  transfers between devices with their start and end apart: 38 -> 38, of which waited for: 17 -> 16; matrix products, arithmetic and copies ran while one was open for 6% -> 6% of each run, Pallas kernels for 49% -> 51%
where the time goes in v7:
time: 554 us; the launch traced here: 544 us
  Pallas kernels  277 us (50%)
  waiting for transfers between devices  181 us (33%)
  other arithmetic  31.8 us (6%)
  starting transfers between devices  26.9 us (5%)
  between operations  15.2 us (3%)
  local copies, waits for them, and re-layouts  11.7 us (2%)
    ppermute x32, waiting for transfers between devices, swap(): return lax.ppermute(value, axis, [(a, a ^ mask) for a in range(n)])  84.9 us
    all_gather x1, waiting for transfers between devices, body(): attend_all = lax.all_gather(attend_shard, 'dp')  62 us
    pallas_call x1, Pallas kernels, out_last(): pl.pallas_call(functools.partial(out_last_kernel, split), grid_spec=pltpu...  35.5 us
    pallas_call x1, Pallas kernels, attend(): pl.pallas_call(functools.partial(attend_kernel, min(512, length)), grid=(...  33.9 us
    pallas_call x2, Pallas kernels, feed_grads(): pl.pallas_call(functools.partial(feed_grads_kernel, n, steps), grid=(step...  32.9 us
    all_gather x1, waiting for transfers between devices, body(): last_all = lax.all_gather(after(shards[1], shards[0]), 'dp')  31.1 us
    ppermute x32, starting transfers between devices, swap(): return lax.ppermute(value, axis, [(a, a ^ mask) for a in range(n)])  26.6 us
    pallas_call x2, Pallas kernels, finish_rows(): pl.pallas_call(finish_kernel, grid_spec=pltpu.PrefetchScalarGridSpec(num_...  25 us
  transfers between devices with their start and end apart: 38, of which 16 were waited for; matrix products, arithmetic and copies ran while one was open for 6% of the time, Pallas kernels for 51%

profile of v7, /device:TPU:0, one launch (start us, length us, event | category | flops | bytes accessed | tf_op | source)
XLA Modules:
  0.0 543.9 jit_solution(14039348416186643576)
XLA Ops:
  7.2 1.1 convert_bitcast_fusion.1
  8.3 1.5 convert_bitcast_fusion
  9.8 1.1 pad_maximum_fusion.2
  11.0 1.6 bitcast_convert_fusion
  13.4 1.1 pad_maximum_fusion.1
  14.6 1.1 pad_maximum_fusion
  15.8 11.2 %layer_norm.1.h_ref = bf16[2048,2048]{1,0:T(8,128)(2,1)} custom-call(bf16[2048,2048]{1,0:T(8,128)(2,1)} %bitcast.49, f32[2,2048]{1,0:T(2,128)} %refs_6_.1), custom_call_target="tpu_custom_call" | custom-call | flops 33554432 | bytes 16777216 | tf_op jit(solution)/shard_map/layer_norm/pallas_call | solution.py:97
  27.0 5.6 %fusion.2 = (f32[2048,128]{1,0:T(8,128)}, f32[2048,128]{1,0:T(8,128)}) fusion(f32[128]{0:T(128)S(1)} %fusion.7, f32[2048]{0:T(1024)S(1)} %bitcast.85, pred[128]{0:T(512)(128)(4,1)S(1)} %get-tuple-element.237, pred[128]{0:T(512)(128)(4,1)S(1)} %get-tuple-element.238), kind=kLoop, calls=%fused_computation.18 | loop fusion | flops 1310720 | bytes 2106112 | tf_op jit(solution)/shard_map/jit(_where)/select_n | solution.py:866
  32.5 62.0 %all-gather.6.cloned.1.call-done.shards_ref = bf16[4,4,512,256]{3,2,1,0:T(8,128)(2,1)} async-done(((bf16[1,4,512,256]{3,2,1,0:T(8,128)(2,1)}), bf16[4,4,512,256]{3,2,1,0:T(8,128)(2,1)}) %all-gather.6.cloned.1.call-update) | async-done | bytes 4194320 | tf_op jit(solution)/shard_map/all_gather | solution.py:853
  94.5 17.4 %project.1 = (bf16[2048,256]{1,0:T(8,128)(2,1)}, bf16[2048,256]{1,0:T(8,128)(2,1)}, bf16[2048,256]{1,0:T(8,128)(2,1)}, bf16[2048,256]{1,0:T(8,128)(2,1)}, bf16[4,2048,256]{2,1,0:T(8,128)(2,1)}) custom-call(bf16[4,4,512,256]{3,2,1,0:T(8,128)(2,1)} %all-gather.6.cloned.1.call-done.shards_ref, bf16[2048,2048]{1,0:T(8,128)(2,1)} %layer_norm.1.h_ref, ...), custom_call_target="tpu_custom_call" | custom-call | flops 8589934592 | bytes 25165824 | tf_op jit(solution)/shard_map/project/pallas_call | solution.py:384
  111.9 33.9 %attend.1 = (bf16[2048,256]{1,0:T(8,128)(2,1)}, bf16[3,2048,256]{2,1,0:T(8,128)(2,1)}, f32[3,256]{1,0:T(4,128)}) custom-call(bf16[2048,256]{1,0:T(8,128)(2,1)} %get-tuple-element.118.q_ref, bf16[2048,256]{1,0:T(8,128)(2,1)} %get-tuple-element.119.k_ref, bf16[2048,256]{1,0:T(8,128)(2,1)} %get-tuple-element.120.v_ref, ...), custom_call_target="tpu_custom_call" | custom-call | flops 21474836480 | bytes 10485760 | tf_op jit(solution)/shard_map/attend/pallas_call | solution.py:460
  145.9 14.8 %attend_grads.1 = bf16[4,4,512,256]{3,2,1,0:T(8,128)(2,1)} custom-call(bf16[2048,2048]{1,0:T(8,128)(2,1)} %layer_norm.1.h_ref, bf16[2048,2048]{1,0:T(8,128)(2,1)} %bitcast.64, bf16[3,2048,256]{2,1,0:T(8,128)(2,1)} %get-tuple-element.122.mg_ref, bf16[2048,256]{1,0:T(8,128)(2,1)} %get-tuple-element.123.ctx_ref), custom_call_target="tpu_custom_call" | custom-call | flops 8589934592 | bytes 25165824 | tf_op jit(solution)/shard_map/attend_grads/pallas_call | solution.py:502
  160.7 14.6 %heads_parts.1 = (bf16[2048,2048]{1,0:T(8,128)(2,1)}, bf16[2048,2048]{1,0:T(8,128)(2,1)}) custom-call(bf16[2048,256]{1,0:T(8,128)(2,1)} %get-tuple-element.123.ctx_ref, bf16[3,2048,256]{2,1,0:T(8,128)(2,1)} %get-tuple-element.122.mg_ref, bf16[4,2048,256]{2,1,0:T(8,128)(2,1)} %get-tuple-element.124.wa_ref), custom_call_target="tpu_custom_call" | custom-call | flops 8589934592 | bytes 25165824 | tf_op jit(solution)/shard_map/heads_parts/pallas_call | solution.py:531
  175.3 2.8 all-gather.10.cloned.1.call-done
  178.1 16.6 %feed_chunk.1 = (bf16[352,2048]{1,0:T(8,128)(2,1)}, bf16[704,2048]{1,0:T(8,128)(2,1)}, bf16[3,352,2048]{2,1,0:T(8,128)(2,1)}) custom-call(bf16[4,3,352,512]{3,2,1,0:T(8,128)(2,1)} %bitcast.88, bf16[2048,2048]{1,0:T(8,128)(2,1)} %layer_norm.1.h_ref, bf16[2048,2048]{1,0:T(8,128)(2,1)} %bitcast.65), custom_call_target="tpu_custom_call" | custom-call | flops 8858370048 | bytes 25427968 | tf_op jit(solution)/shard_map/feed_chunk/pallas_call | solution.py:182
  194.7 16.2 %feed_grads.2 = bf16[4,1056,512]{2,1,0:T(8,128)(2,1)} custom-call(bf16[2048,2048]{1,0:T(8,128)(2,1)} %layer_norm.1.h_ref, bf16[2048,2048]{1,0:T(8,128)(2,1)} %bitcast.66, bf16[352,2048]{1,0:T(8,128)(2,1)} %get-tuple-element.128.act_ref, bf16[704,2048]{1,0:T(8,128)(2,1)} %get-tuple-element.129.grad_ref), custom_call_target="tpu_custom_call" | custom-call | flops 8858370048 | bytes 25427968 | tf_op jit(solution)/shard_map/feed_grads/pallas_call | solution.py:330
  210.9 19.8 %early_parts.1 = (bf16[2048,2048]{1,0:T(8,128)(2,1)}, bf16[2048,2048]{1,0:T(8,128)(2,1)}) custom-call(bf16[352,2048]{1,0:T(8,128)(2,1)} %get-tuple-element.128.act_ref, bf16[704,2048]{1,0:T(8,128)(2,1)} %get-tuple-element.129.grad_ref, bf16[3,352,2048]{2,1,0:T(8,128)(2,1)} %get-tuple-element.130.w_ref, bf16[2048,2048]{1,0:T(8,128)(2,1)} %get-tuple-element.125.hid_in_ref, ...), custom_call_target="tpu_custom_call" | custom-call | flops 8858370048 | bytes 42205184 | tf_op jit(solution)/shard_map/early_parts/pallas_call | solution.py:559
  230.7 31.1 %all-gather.8.cloned.1.call-done = bf16[12,352,512]{2,1,0:T(8,128)(2,1)} async-done(((bf16[3,352,512]{2,1,0:T(8,128)(2,1)}), bf16[12,352,512]{2,1,0:T(8,128)(2,1)}) %all-gather.8.cloned.1.call-update) | async-done | bytes 4325392 | tf_op jit(solution)/shard_map/all_gather | solution.py:855
  262.4 35.5 %out_last.1 = (bf16[256,2048]{1,0:T(8,128)(2,1)}, bf16[256,2048]{1,0:T(8,128)(2,1)}, bf16[256,2048]{1,0:T(8,128)(2,1)}, bf16[256,2048]{1,0:T(8,128)(2,1)}, bf16[...) custom-call(s32[3]{0:T(128)} %pad_add_fusion.info_ref, ...), custom_call_target="tpu_custom_call" | custom-call | flops 8858370048 | bytes 33554432 | tf_op jit(solution)/shard_map/out_last/pallas_call | solution.py:262
  298.5 2.4 collective-permute-done.1
  300.9 1.6 add_convert_fusion.7
  303.1 1.6 collective-permute-start.2
  304.7 1.5 collective-permute-start.4
  306.7 22.2 %hid_last.1 = (bf16[256,2048]{1,0:T(8,128)(2,1)}, bf16[256,2048]{1,0:T(8,128)(2,1)}, bf16[256,2048]{1,0:T(8,128)(2,1)}, bf16[256,2048]{1,0:T(8,128)(2,1)}, bf16[...) custom-call(s32[3]{0:T(128)} %pad_add_fusion.info_ref, ...), custom_call_target="tpu_custom_call" | custom-call | flops 8858370048 | bytes 33554432 | tf_op jit(solution)/shard_map/hid_last/pallas_call | solution.py:298
  330.2 2.1 add_convert_fusion.5
  333.9 2.1 add_convert_fusion.4
  337.9 1.5 collective-permute-start.17
  341.6 1.4 collective-permute-start.7
  343.0 16.7 %feed_grads.3 = bf16[4,1056,512]{2,1,0:T(8,128)(2,1)} custom-call(bf16[2048,2048]{1,0:T(8,128)(2,1)} %layer_norm.1.h_ref, bf16[2048,2048]{1,0:T(8,128)(2,1)} %bitcast.68, bf16[352,2048]{1,0:T(8,128)(2,1)} %get-tuple-element.156.act_ref, bf16[704,2048]{1,0:T(8,128)(2,1)} %get-tuple-element.157.grad_ref), custom_call_target="tpu_custom_call" | custom-call | flops 8858370048 | bytes 25427968 | tf_op jit(solution)/shard_map/feed_grads/pallas_call | solution.py:330
  359.8 14.6 %collective-permute-done.6.refs_4_ = bf16[128,2048]{1,0:T(8,128)(2,1)S(1)} collective-permute-done((bf16[128,2048]{1,0:T(8,128)(2,1)}, bf16[128,2048]{1,0:T(8,128)(2,1)S(1)}, u32[]{:S(2)}, u32[]{:S(2)}) %collective-permute-start.6) | collective-permute-done | bytes 524320 | tf_op jit(solution)/shard_map/ppermute | solution.py:63
  374.3 1.7 collective-permute-done.7.refs_5_
  376.8 3.8 add_rows.1
  380.7 2.1 add_convert_fusion
  384.5 1.8 add_convert_fusion.1
  387.2 1.2 collective-permute-start.18
  388.4 1.2 collective-permute-start.14
  390.4 1.2 collective-permute-start.15
  391.6 6.9 %collective-permute-done.19.refs_5_ = bf16[128,2048]{1,0:T(8,128)(2,1)S(1)} collective-permute-done((bf16[128,2048]{1,0:T(8,128)(2,1)S(1)}, bf16[128,2048]{1,0:T(8,128)(2,1)S(1)}, u32[]{:S(2)}, u32[]{:S(2)}) %collective-permute-start.19) | collective-permute-done | bytes 524320 | tf_op jit(solution)/shard_map/ppermute | solution.py:63
  398.5 3.5 collective-permute-done.18.refs_4_
  402.8 5.5 %back_rows.1 = (bf16[144,2048]{1,0:T(8,128)(2,1)}, bf16[128,2048]{1,0:T(8,128)(2,1)}) custom-call(s32[3]{0:T(128)} %pad_add_fusion.info_ref, bf16[2048,2048]{1,0:T(8,128)(2,1)} %bitcast.52, bf16[2048,2048]{1,0:T(8,128)(2,1)} %bitcast.53, bf16[128,2048]{1,0:T(8,128)(2,1)} %get-tuple-element.228.refs_2_, bf16[128,2048]{1,0:T(8,128)(2,1)} %get-tuple-element.226.refs_3_, ...), custom_call_target="tpu_custom_call" | custom-call | flops 10485760 | bytes 4194304 | tf_op jit(solution)/shard_map/back_rows/pallas_call | solution.py:614
  408.3 1.2 collective-permute-start.24
  409.6 1.2 collective-permute-start.22
  411.6 1.6 collective-permute-done.12.refs_1_
  413.3 1.2 collective-permute-start.25
  414.5 10.0 %collective-permute-done.15.refs_6_ = bf16[128,2048]{1,0:T(8,128)(2,1)S(1)} collective-permute-done((bf16[128,2048]{1,0:T(8,128)(2,1)S(1)}, bf16[128,2048]{1,0:T(8,128)(2,1)S(1)}, u32[]{:S(2)}, u32[]{:S(2)}) %collective-permute-start.15) | collective-permute-done | bytes 524320 | tf_op jit(solution)/shard_map/ppermute | solution.py:63
  424.5 1.2 collective-permute-start.23
  425.7 10.5 %collective-permute-done.13.refs_5_ = bf16[128,2048]{1,0:T(8,128)(2,1)} collective-permute-done((bf16[128,2048]{1,0:T(8,128)(2,1)S(1)}, bf16[128,2048]{1,0:T(8,128)(2,1)}, u32[]{:S(2)}, u32[]{:S(2)}) %collective-permute-start.13) | collective-permute-done | bytes 524320 | tf_op jit(solution)/shard_map/ppermute | solution.py:63
  436.2 7.1 %update_feed.2 = (f32[2,704,512]{2,1,0:T(8,128)}, f32[2,704,512]{2,1,0:T(8,128)}, f32[2,704,512]{2,1,0:T(8,128)}, f32[2,704,512]{2,1,0:T(8,128)}, f32[704,512]{1...) custom-call(bf16[3,352,512]{2,1,0:T(8,128)(2,1)} %bitcast.83, f32[2,704,512]{2,1,0:T(8,128)} %bitcast.54, ...), custom_call_target="tpu_custom_call" | custom-call | flops 5406720 | bytes 16220160 | tf_op jit(solution)/shard_map/update_feed/pallas_call | solution.py:796
  443.3 2.9 collective-permute-done.25.refs_6_
  446.3 1.0 collective-permute-start.27
  447.3 1.1 collective-permute-start.20
  448.4 1.6 collective-permute-start.21
  450.4 20.5 %collective-permute-done.20.refs_3_ = bf16[128,2048]{1,0:T(8,128)(2,1)S(1)} collective-permute-done((bf16[128,2048]{1,0:T(8,128)(2,1)S(1)}, bf16[128,2048]{1,0:T(8,128)(2,1)S(1)}, u32[]{:S(2)}, u32[]{:S(2)}) %collective-permute-start.20) | collective-permute-done | bytes 524320 | tf_op jit(solution)/shard_map/ppermute | solution.py:63
  471.6 4.9 pack_rows.2.refs_0_
  478.2 5.2 pack_rows.3.refs_0_.refs_3_
  484.0 1.4 convert_element_type.137
  485.5 1.5 multiply_add_fusion.2
  488.1 3.1 multiply_add_fusion
  491.2 6.2 %collective-permute-done.26.refs_1_ = bf16[1024,2048]{1,0:T(8,128)(2,1)} collective-permute-done((bf16[1024,2048]{1,0:T(8,128)(2,1)}, bf16[1024,2048]{1,0:T(8,128)(2,1)}, u32[]{:S(2)}, u32[]{:S(2)}) %collective-permute-start.26) | collective-permute-done | bytes 4194336 | tf_op jit(solution)/shard_map/ppermute | solution.py:63
  497.4 10.2 %finish_rows.2 = bf16[2048,2048]{1,0:T(8,128)(2,1)} custom-call(s32[3]{0:T(128)} %pad_add_fusion.info_ref, bf16[1024,2048]{1,0:T(8,128)(2,1)} %pack_rows.2.refs_0_, bf16[1024,2048]{1,0:T(8,128)(2,1)} %collective-permute-done.26.refs_1_), custom_call_target="tpu_custom_call" | custom-call | flops 8388608 | bytes 33554432 | tf_op jit(solution)/shard_map/finish_rows/pallas_call | solution.py:759
  507.6 14.8 %finish_rows.3 = (f32[2048,2048]{1,0:T(8,128)}, f32[2,2048]{1,0:T(2,128)}) custom-call(s32[3]{0:T(128)} %pad_add_fusion.info_ref, bf16[1088,2048]{1,0:T(8,128)(2,1)} %pack_rows.3.refs_0_.refs_3_, bf16[1088,2048]{1,0:T(8,128)(2,1)} %collective-permute-done.29.refs_1_.refs_4_, bf16[2048,2048]{1,0:T(8,128)(2,1)} %bitcast.69, ...), custom_call_target="tpu_custom_call" | custom-call | flops 8388608 | bytes 33554432 | tf_op jit(solution)/shard_map/finish_rows/pallas_call | solution.py:759
  523.2 3.8 collective-permute-done.30
  527.0 1.2 collective-permute-start.31
  528.3 7.0 %update_feed.3 = (f32[2,704,512]{2,1,0:T(8,128)}, f32[2,704,512]{2,1,0:T(8,128)}, f32[2,704,512]{2,1,0:T(8,128)}, f32[2,704,512]{2,1,0:T(8,128)}, f32[704,512]{1...) custom-call(bf16[3,352,512]{2,1,0:T(8,128)(2,1)} %bitcast.82, ...), custom_call_target="tpu_custom_call", output_to_operand_aliasing={{0}: (7, {}), {1}: (8, {}), {2}: (9, {}), {3}: (10, {}), {4... | custom-call | flops 5406720 | bytes 16220160 | tf_op jit(solution)/shard_map/update_feed/pallas_call | solution.py:796
  (160 shorter events, 23.0 us)
Async XLA Ops:
  7.2 87.3 %all-gather.6.cloned.1.call-start = ((), (), s32[]{:S(2)}) async-start(), calls=%async_computation.3 | async-start | bytes 5242880 | tf_op jit(solution)/shard_map/all_gather | solution.py:853
  10.9 2.2 copy-start
  10.9 167.2 %all-gather.10.cloned.1.call-start = ((), (), s32[]{:S(2)}) async-start(), calls=%async_computation.8 | async-start | bytes 5406720 | tf_op jit(solution)/shard_map/all_gather | solution.py:854
  14.5 247.2 %all-gather.8.cloned.1.call-start = ((), (), s32[]{:S(2)}) async-start(), calls=%async_computation.7 | async-start | bytes 5406720 | tf_op jit(solution)/shard_map/all_gather | solution.py:855
  15.7 420.5 %reduce-scatter.4.cloned.1.call-start = ((), (), s32[]{:S(2)}) async-start(), calls=%async_computation.4 | async-start | bytes 5406720 | tf_op jit(solution)/shard_map/reduce_scatter | solution.py:869
  261.8 222.2 %reduce-scatter.6.cloned.1.call-start = ((), (), s32[]{:S(2)}) async-start(), calls=%async_computation.5 | async-start | bytes 5242880 | tf_op jit(solution)/shard_map/reduce_scatter | solution.py:869
  297.9 4.6 copy-start.7
  298.0 2.9 collective-permute-start.1
  298.0 4.5 collective-permute-start.3
  303.0 225.2 %reduce-scatter.8.cloned.1.call-start = ((), (), s32[]{:S(2)}) async-start(), calls=%async_computation.6 | async-start | bytes 5406720 | tf_op jit(solution)/shard_map/reduce_scatter | solution.py:869
  303.1 25.8 %collective-permute-start.2 = (bf16[256,2048]{1,0:T(8,128)(2,1)S(1)}, bf16[256,2048]{1,0:T(8,128)(2,1)}, u32[]{:S(2)}, u32[]{:S(2)}) collective-permute-start(bf16[256,2048]{1,0:T(8,128)(2,1)S(1)} %add_convert_fusion.7), channel_id=1, source_target_pairs={{0,2},{1,3},{2,0},{3,1},{4,6},{5,7},{6,4},{7,5},{8,10},{9,11},{10,... | collective-permute-start | bytes 3145736 | tf_op jit(solution)/shard_map/ppermute | solution.py:63
  304.7 25.0 %collective-permute-start.4 = (bf16[256,2048]{1,0:T(8,128)(2,1)S(1)}, bf16[256,2048]{1,0:T(8,128)(2,1)}, u32[]{:S(2)}, u32[]{:S(2)}) collective-permute-start(bf16[256,2048]{1,0:T(8,128)(2,1)S(1)} %add_convert_fusion.6), channel_id=1, source_target_pairs={{0,4},{1,5},{2,6},{3,7},{4,0},{5,1},{6,2},{7,3},{8,12},{9,13},{10,... | collective-permute-start | bytes 3145736 | tf_op jit(solution)/shard_map/ppermute | solution.py:63
  306.1 23.6 %collective-permute-start = (bf16[256,2048]{1,0:T(8,128)(2,1)}, bf16[256,2048]{1,0:T(8,128)(2,1)}, u32[]{:S(2)}, u32[]{:S(2)}) collective-permute-start(bf16[256,2048]{1,0:T(8,128)(2,1)} %get-tuple-element.135), channel_id=1, source_target_pairs={{0,1},{1,0},{2,3},{3,2},{4,5},{5,4},{6,7},{7,6},{8,9},{9,8},{10,11... | collective-permute-start | bytes 3145736 | tf_op jit(solution)/shard_map/ppermute | solution.py:63
  306.1 27.2 %collective-permute-start.5 = (bf16[256,2048]{1,0:T(8,128)(2,1)}, bf16[256,2048]{1,0:T(8,128)(2,1)}, u32[]{:S(2)}, u32[]{:S(2)}) collective-permute-start(bf16[256,2048]{1,0:T(8,128)(2,1)} %get-tuple-element.146), channel_id=1, source_target_pairs={{0,1},{1,0},{2,3},{3,2},{4,5},{5,4},{6,7},{7,6},{8,9},{9,8},{10,11... | collective-permute-start | bytes 3145736 | tf_op jit(solution)/shard_map/ppermute | solution.py:63
  306.7 23.6 %copy-start.14 = (bf16[256,2048]{1,0:T(8,128)(2,1)S(1)}, bf16[256,2048]{1,0:T(8,128)(2,1)}, u32[]{:S(2)}) copy-start(bf16[256,2048]{1,0:T(8,128)(2,1)} %get-tuple-element.134) | copy-start | bytes 3145732
  328.9 8.1 %collective-permute-start.9 = (bf16[256,2048]{1,0:T(8,128)(2,1)}, bf16[256,2048]{1,0:T(8,128)(2,1)S(1)}, u32[]{:S(2)}, u32[]{:S(2)}) collective-permute-start(bf16[256,2048]{1,0:T(8,128)(2,1)} %get-tuple-element.150), channel_id=1, source_target_pairs={{0,1},{1,0},{2,3},{3,2},{4,5},{5,4},{6,7},{7,6},{8,9},{9,8},{10,11... | collective-permute-start | bytes 3145736 | tf_op jit(solution)/shard_map/ppermute | solution.py:63
  328.9 8.1 %collective-permute-start.10 = (bf16[256,2048]{1,0:T(8,128)(2,1)}, bf16[256,2048]{1,0:T(8,128)(2,1)S(1)}, u32[]{:S(2)}, u32[]{:S(2)}) collective-permute-start(bf16[256,2048]{1,0:T(8,128)(2,1)} %get-tuple-element.151), channel_id=1, source_target_pairs={{0,1},{1,0},{2,3},{3,2},{4,5},{5,4},{6,7},{7,6},{8,9},{9,8},{10,11... | collective-permute-start | bytes 3145736 | tf_op jit(solution)/shard_map/ppermute | solution.py:63
  329.7 7.3 %collective-permute-start.8 = (bf16[256,2048]{1,0:T(8,128)(2,1)}, bf16[256,2048]{1,0:T(8,128)(2,1)S(1)}, u32[]{:S(2)}, u32[]{:S(2)}) collective-permute-start(bf16[256,2048]{1,0:T(8,128)(2,1)} %get-tuple-element.143), channel_id=1, source_target_pairs={{0,1},{1,0},{2,3},{3,2},{4,5},{5,4},{6,7},{7,6},{8,9},{9,8},{10,11... | collective-permute-start | bytes 3145736 | tf_op jit(solution)/shard_map/ppermute | solution.py:63
  329.7 7.3 %collective-permute-start.11 = (bf16[256,2048]{1,0:T(8,128)(2,1)}, bf16[256,2048]{1,0:T(8,128)(2,1)S(1)}, u32[]{:S(2)}, u32[]{:S(2)}) collective-permute-start(bf16[256,2048]{1,0:T(8,128)(2,1)} %get-tuple-element.152), channel_id=1, source_target_pairs={{0,1},{1,0},{2,3},{3,2},{4,5},{5,4},{6,7},{7,6},{8,9},{9,8},{10,11... | collective-permute-start | bytes 3145736 | tf_op jit(solution)/shard_map/ppermute | solution.py:63
  337.0 2.5 copy-start.5
  337.0 2.9 copy-start.12
  337.0 2.9 copy-start.10
  337.9 42.7 %collective-permute-start.17 = (bf16[256,2048]{1,0:T(8,128)(2,1)S(1)}, bf16[256,2048]{1,0:T(8,128)(2,1)}, u32[]{:S(2)}, u32[]{:S(2)}) collective-permute-start(bf16[256,2048]{1,0:T(8,128)(2,1)S(1)} %add_convert_fusion.2), channel_id=1, source_target_pairs={{0,4},{1,5},{2,6},{3,7},{4,0},{5,1},{6,2},{7,3},{8,12},{9,13},{10,... | collective-permute-start | bytes 3145736 | tf_op jit(solution)/shard_map/ppermute | solution.py:63
  339.9 40.7 %collective-permute-start.16 = (bf16[256,2048]{1,0:T(8,128)(2,1)S(1)}, bf16[256,2048]{1,0:T(8,128)(2,1)}, u32[]{:S(2)}, u32[]{:S(2)}) collective-permute-start(bf16[256,2048]{1,0:T(8,128)(2,1)S(1)} %add_convert_fusion.3), channel_id=1, source_target_pairs={{0,2},{1,3},{2,0},{3,1},{4,6},{5,7},{6,4},{7,5},{8,10},{9,11},{10,... | collective-permute-start | bytes 3145736 | tf_op jit(solution)/shard_map/ppermute | solution.py:63
  340.6 33.7 %collective-permute-start.6 = (bf16[128,2048]{1,0:T(8,128)(2,1)}, bf16[128,2048]{1,0:T(8,128)(2,1)S(1)}, u32[]{:S(2)}, u32[]{:S(2)}) collective-permute-start(bf16[128,2048]{1,0:T(8,128)(2,1)} %get-tuple-element.231), channel_id=1, source_target_pairs={{0,4},{1,5},{2,6},{3,7},{4,0},{5,1},{6,2},{7,3},{8,12},{9,13},{10,... | collective-permute-start | bytes 1572872 | tf_op jit(solution)/shard_map/ppermute | solution.py:63
  341.6 34.4 %collective-permute-start.7 = (bf16[128,2048]{1,0:T(8,128)(2,1)}, bf16[128,2048]{1,0:T(8,128)(2,1)S(1)}, u32[]{:S(2)}, u32[]{:S(2)}) collective-permute-start(bf16[128,2048]{1,0:T(8,128)(2,1)} %get-tuple-element.229), channel_id=1, source_target_pairs={{0,2},{1,3},{2,0},{3,1},{4,6},{5,7},{6,4},{7,5},{8,10},{9,11},{10,... | collective-permute-start | bytes 1572872 | tf_op jit(solution)/shard_map/ppermute | solution.py:63
  376.8 3.8 copy-start.9
  383.6 14.9 %collective-permute-start.19 = (bf16[128,2048]{1,0:T(8,128)(2,1)S(1)}, bf16[128,2048]{1,0:T(8,128)(2,1)S(1)}, u32[]{:S(2)}, u32[]{:S(2)}) collective-permute-start(bf16[128,2048]{1,0:T(8,128)(2,1)S(1)} %get-tuple-element.225), channel_id=1, source_target_pairs={{0,2},{1,3},{2,0},{3,1},{4,6},{5,7},{6,4},{7,5},{8,10},{9,11},{10,... | collective-permute-start | bytes 1572872 | tf_op jit(solution)/shard_map/ppermute | solution.py:63
  386.3 2.1 copy-start.18
  386.3 4.1 copy-start.19
  387.2 14.9 %collective-permute-start.18 = (bf16[128,2048]{1,0:T(8,128)(2,1)S(1)}, bf16[128,2048]{1,0:T(8,128)(2,1)S(1)}, u32[]{:S(2)}, u32[]{:S(2)}) collective-permute-start(bf16[128,2048]{1,0:T(8,128)(2,1)S(1)} %get-tuple-element.227), channel_id=1, source_target_pairs={{0,4},{1,5},{2,6},{3,7},{4,0},{5,1},{6,2},{7,3},{8,12},{9,13},{10,... | collective-permute-start | bytes 1572872 | tf_op jit(solution)/shard_map/ppermute | solution.py:63
  388.4 22.4 %collective-permute-start.14 = (bf16[128,2048]{1,0:T(8,128)(2,1)S(1)}, bf16[128,2048]{1,0:T(8,128)(2,1)S(1)}, u32[]{:S(2)}, u32[]{:S(2)}) collective-permute-start(bf16[128,2048]{1,0:T(8,128)(2,1)S(1)} %copy-done.18), channel_id=1, source_target_pairs={{0,2},{1,3},{2,0},{3,1},{4,6},{5,7},{6,4},{7,5},{8,10},{9,11},{10,... | collective-permute-start | bytes 1572872 | tf_op jit(solution)/shard_map/ppermute | solution.py:63
  389.6 23.7 %collective-permute-start.12 = (bf16[128,2048]{1,0:T(8,128)(2,1)S(1)}, bf16[128,2048]{1,0:T(8,128)(2,1)S(1)}, u32[]{:S(2)}, u32[]{:S(2)}) collective-permute-start(bf16[128,2048]{1,0:T(8,128)(2,1)S(1)} %copy-done.18), channel_id=1, source_target_pairs={{0,4},{1,5},{2,6},{3,7},{4,0},{5,1},{6,2},{7,3},{8,12},{9,13},{10,... | collective-permute-start | bytes 1572872 | tf_op jit(solution)/shard_map/ppermute | solution.py:63
  390.4 34.1 %collective-permute-start.15 = (bf16[128,2048]{1,0:T(8,128)(2,1)S(1)}, bf16[128,2048]{1,0:T(8,128)(2,1)S(1)}, u32[]{:S(2)}, u32[]{:S(2)}) collective-permute-start(bf16[128,2048]{1,0:T(8,128)(2,1)S(1)} %copy-done.19), channel_id=1, source_target_pairs={{0,4},{1,5},{2,6},{3,7},{4,0},{5,1},{6,2},{7,3},{8,12},{9,13},{10,... | collective-permute-start | bytes 1572872 | tf_op jit(solution)/shard_map/ppermute | solution.py:63
  398.5 3.5 copy-start.25
  408.3 37.9 %collective-permute-start.24 = (bf16[144,2048]{1,0:T(8,128)(2,1)}, bf16[144,2048]{1,0:T(8,128)(2,1)S(1)}, u32[]{:S(2)}, u32[]{:S(2)}) collective-permute-start(bf16[144,2048]{1,0:T(8,128)(2,1)} %get-tuple-element.168.refs_0_), channel_id=1, source_target_pairs={{0,2},{1,3},{2,0},{3,1},{4,6},{5,7},{6,4},{7,5},{8,10},{9,11},{10,... | collective-permute-start | bytes 1769480 | tf_op jit(solution)/shard_map/ppermute | solution.py:63
  409.6 36.7 %collective-permute-start.22 = (bf16[144,2048]{1,0:T(8,128)(2,1)}, bf16[144,2048]{1,0:T(8,128)(2,1)S(1)}, u32[]{:S(2)}, u32[]{:S(2)}) collective-permute-start(bf16[144,2048]{1,0:T(8,128)(2,1)} %get-tuple-element.168.refs_0_), channel_id=1, source_target_pairs={{0,4},{1,5},{2,6},{3,7},{4,0},{5,1},{6,2},{7,3},{8,12},{9,13},{10,... | collective-permute-start | bytes 1769480 | tf_op jit(solution)/shard_map/ppermute | solution.py:63
  410.8 32.5 %copy-start.20 = (bf16[128,2048]{1,0:T(8,128)(2,1)}, bf16[128,2048]{1,0:T(8,128)(2,1)S(1)}, u32[]{:S(2)}) copy-start(bf16[128,2048]{1,0:T(8,128)(2,1)S(1)} %collective-permute-done.14.refs_2_) | copy-start | bytes 1572868
  410.8 25.4 %collective-permute-start.13 = (bf16[128,2048]{1,0:T(8,128)(2,1)S(1)}, bf16[128,2048]{1,0:T(8,128)(2,1)}, u32[]{:S(2)}, u32[]{:S(2)}) collective-permute-start(bf16[128,2048]{1,0:T(8,128)(2,1)S(1)} %copy-done.19), channel_id=1, source_target_pairs={{0,2},{1,3},{2,0},{3,1},{4,6},{5,7},{6,4},{7,5},{8,10},{9,11},{10,... | collective-permute-start | bytes 1572872 | tf_op jit(solution)/shard_map/ppermute | solution.py:63
  413.3 11.2 %copy-start.21 = (bf16[128,2048]{1,0:T(8,128)(2,1)}, bf16[128,2048]{1,0:T(8,128)(2,1)S(1)}, u32[]{:S(2)}) copy-start(bf16[128,2048]{1,0:T(8,128)(2,1)S(1)} %collective-permute-done.12.refs_1_) | copy-start | bytes 1572868
  413.3 33.0 %collective-permute-start.25 = (bf16[128,2048]{1,0:T(8,128)(2,1)}, bf16[128,2048]{1,0:T(8,128)(2,1)S(1)}, u32[]{:S(2)}, u32[]{:S(2)}) collective-permute-start(bf16[128,2048]{1,0:T(8,128)(2,1)} %get-tuple-element.169.refs_4_), channel_id=1, source_target_pairs={{0,4},{1,5},{2,6},{3,7},{4,0},{5,1},{6,2},{7,3},{8,12},{9,13},{10,... | collective-permute-start | bytes 1572872 | tf_op jit(solution)/shard_map/ppermute | solution.py:63
  424.5 18.8 %copy-start.23 = (bf16[128,2048]{1,0:T(8,128)(2,1)}, bf16[128,2048]{1,0:T(8,128)(2,1)S(1)}, u32[]{:S(2)}) copy-start(bf16[128,2048]{1,0:T(8,128)(2,1)S(1)} %collective-permute-done.15.refs_6_) | copy-start | bytes 1572868
  424.5 21.7 %collective-permute-start.23 = (bf16[128,2048]{1,0:T(8,128)(2,1)}, bf16[128,2048]{1,0:T(8,128)(2,1)}, u32[]{:S(2)}, u32[]{:S(2)}) collective-permute-start(bf16[128,2048]{1,0:T(8,128)(2,1)} %get-tuple-element.169.refs_4_), channel_id=1, source_target_pairs={{0,2},{1,3},{2,0},{3,1},{4,6},{5,7},{6,4},{7,5},{8,10},{9,11},{10,... | collective-permute-start | bytes 1572872 | tf_op jit(solution)/shard_map/ppermute | solution.py:63
  436.2 11.1 %copy-start.22 = (bf16[128,2048]{1,0:T(8,128)(2,1)S(1)}, bf16[128,2048]{1,0:T(8,128)(2,1)}, u32[]{:S(2)}) copy-start(bf16[128,2048]{1,0:T(8,128)(2,1)} %copy-done.21) | copy-start | bytes 1572868
  446.2 30.4 %copy-start.24 = (bf16[128,2048]{1,0:T(8,128)(2,1)}, bf16[128,2048]{1,0:T(8,128)(2,1)S(1)}, u32[]{:S(2)}) copy-start(bf16[128,2048]{1,0:T(8,128)(2,1)S(1)} %collective-permute-done.25.refs_6_) | copy-start | bytes 1572868
  446.2 30.4 %copy-start.15 = (bf16[144,2048]{1,0:T(8,128)(2,1)}, bf16[144,2048]{1,0:T(8,128)(2,1)S(1)}, u32[]{:S(2)}) copy-start(bf16[144,2048]{1,0:T(8,128)(2,1)S(1)} %collective-permute-done.24.refs_2_) | copy-start | bytes 1769476
  446.2 30.3 %copy-start.16 = (bf16[144,2048]{1,0:T(8,128)(2,1)}, bf16[144,2048]{1,0:T(8,128)(2,1)S(1)}, u32[]{:S(2)}) copy-start(bf16[144,2048]{1,0:T(8,128)(2,1)S(1)} %collective-permute-done.22.refs_1_) | copy-start | bytes 1769476
  446.3 31.1 %collective-permute-start.27 = (bf16[144,2048]{1,0:T(8,128)(2,1)S(1)}, bf16[144,2048]{1,0:T(8,128)(2,1)S(1)}, u32[]{:S(2)}, u32[]{:S(2)}) collective-permute-start(bf16[144,2048]{1,0:T(8,128)(2,1)S(1)} %collective-permute-done.22.refs_1_), channel_id=1, source_target_pairs={{0,2},{1,3},{2,0},{3,1},{4,6},{5,7},{6,4},{7,5},{8,10},{9,11},{10,... | collective-permute-start | bytes 1769480 | tf_op jit(solution)/shard_map/ppermute | solution.py:63
  447.3 23.6 %collective-permute-start.20 = (bf16[128,2048]{1,0:T(8,128)(2,1)S(1)}, bf16[128,2048]{1,0:T(8,128)(2,1)S(1)}, u32[]{:S(2)}, u32[]{:S(2)}) collective-permute-start(bf16[128,2048]{1,0:T(8,128)(2,1)S(1)} %copy-done.22), channel_id=1, source_target_pairs={{0,2},{1,3},{2,0},{3,1},{4,6},{5,7},{6,4},{7,5},{8,10},{9,11},{10,... | collective-permute-start | bytes 1572872 | tf_op jit(solution)/shard_map/ppermute | solution.py:63
  448.4 22.5 %collective-permute-start.21 = (bf16[128,2048]{1,0:T(8,128)(2,1)}, bf16[128,2048]{1,0:T(8,128)(2,1)}, u32[]{:S(2)}, u32[]{:S(2)}) collective-permute-start(bf16[128,2048]{1,0:T(8,128)(2,1)} %collective-permute-done.13.refs_5_), channel_id=1, source_target_pairs={{0,4},{1,5},{2,6},{3,7},{4,0},{5,1},{6,2},{7,3},{8,12},{9,13},{10,... | collective-permute-start | bytes 1572872 | tf_op jit(solution)/shard_map/ppermute | solution.py:63
  449.9 26.7 %collective-permute-start.28 = (bf16[128,2048]{1,0:T(8,128)(2,1)}, bf16[128,2048]{1,0:T(8,128)(2,1)S(1)}, u32[]{:S(2)}, u32[]{:S(2)}) collective-permute-start(bf16[128,2048]{1,0:T(8,128)(2,1)} %collective-permute-done.23.refs_5_), channel_id=1, source_target_pairs={{0,4},{1,5},{2,6},{3,7},{4,0},{5,1},{6,2},{7,3},{8,12},{9,13},{10,... | collective-permute-start | bytes 1572872 | tf_op jit(solution)/shard_map/ppermute | solution.py:63
  478.2 8.7 %copy-start.4 = (f32[512,3,256]{2,0,1:T(8,128)S(1)}, f32[512,3,256]{2,0,1:T(8,128)}, u32[]{:S(2)}) copy-start(f32[512,3,256]{2,0,1:T(8,128)} %param.30) | copy-start | bytes 4718596
  483.5 24.1 %collective-permute-start.29 = (bf16[1088,2048]{1,0:T(8,128)(2,1)}, bf16[1088,2048]{1,0:T(8,128)(2,1)}, u32[]{:S(2)}, u32[]{:S(2)}) collective-permute-start(bf16[1088,2048]{1,0:T(8,128)(2,1)} %pack_rows.3.refs_0_.refs_3_), channel_id=1, source_target_pairs={{0,1},{1,0},{2,3},{3,2},{4,5},{5,4},{6,7},{7,6},{8,9},{9,8},{10,11... | collective-permute-start | bytes 13369352 | tf_op jit(solution)/shard_map/ppermute | solution.py:63
  483.5 13.9 %collective-permute-start.26 = (bf16[1024,2048]{1,0:T(8,128)(2,1)}, bf16[1024,2048]{1,0:T(8,128)(2,1)}, u32[]{:S(2)}, u32[]{:S(2)}) collective-permute-start(bf16[1024,2048]{1,0:T(8,128)(2,1)} %pack_rows.2.refs_0_), channel_id=1, source_target_pairs={{0,1},{1,0},{2,3},{3,2},{4,5},{5,4},{6,7},{7,6},{8,9},{9,8},{10,11... | collective-permute-start | bytes 12582920 | tf_op jit(solution)/shard_map/ppermute | solution.py:63
  485.5 2.6 copy-start.3
  507.6 15.6 %copy-start.38 = (f32[3,256]{1,0:T(4,128)S(1)}, f32[3,256]{1,0:T(4,128)}, u32[]{:S(2)}) copy-start(f32[3,256]{1,0:T(4,128)} %get-tuple-element.201) | copy-start | bytes 9220
  523.1 3.9 collective-permute-start.30
  527.0 8.3 %collective-permute-start.31 = (f32[19,256]{1,0:T(8,128)S(1)}, f32[19,256]{1,0:T(8,128)S(1)}, u32[]{:S(2)}, u32[]{:S(2)}) collective-permute-start(f32[19,256]{1,0:T(8,128)S(1)} %add.128), channel_id=1, source_target_pairs={{0,16},{8,24},{16,0},{24,8},{1,17},{9,25},{17,1},{25,9},{2,18},{10... | collective-permute-start | bytes 58376 | tf_op jit(solution)/shard_map/ppermute | solution.py:63
  528.2 7.1 %copy-start.39 = (f32[3,256]{1,0:T(4,128)S(1)}, f32[3,256]{1,0:T(4,128)}, u32[]{:S(2)}) copy-start(f32[3,256]{1,0:T(4,128)} %bias_ref.1) | copy-start | bytes 9220
  528.2 7.1 %copy-start.40 = (f32[3,256]{1,0:T(4,128)S(1)}, f32[3,256]{1,0:T(4,128)}, u32[]{:S(2)}) copy-start(f32[3,256]{1,0:T(4,128)} %param.41) | copy-start | bytes 9220
  528.2 7.2 %copy-start.41 = (f32[3,256]{1,0:T(4,128)S(1)}, f32[3,256]{1,0:T(4,128)}, u32[]{:S(2)}) copy-start(f32[3,256]{1,0:T(4,128)} %param.35) | copy-start | bytes 9220
  528.2 7.8 %copy-start.33 = (f32[2,2048]{1,0:T(2,128)S(1)}, f32[2,2048]{1,0:T(2,128)}, u32[]{:S(2)}) copy-start(f32[2,2048]{1,0:T(2,128)} %refs_6_.1) | copy-start | bytes 49156
  528.3 7.8 %copy-start.35 = (f32[2,2048]{1,0:T(2,128)S(1)}, f32[2,2048]{1,0:T(2,128)}, u32[]{:S(2)}) copy-start(f32[2,2048]{1,0:T(2,128)} %param.40) | copy-start | bytes 49156
  528.3 7.8 %copy-start.36 = (f32[2,2048]{1,0:T(2,128)S(1)}, f32[2,2048]{1,0:T(2,128)}, u32[]{:S(2)}) copy-start(f32[2,2048]{1,0:T(2,128)} %param.34) | copy-start | bytes 49156
  (16 other events, 23.0 us)
Sparse Core Ops, SparseCore 0:
  11.0 83.4 all-gather.5
  96.7 81.4 all-gather.9
  180.3 81.4 all-gather.7
  263.9 77.3 reduce-scatter.3
  343.5 77.2 reduce-scatter.5
  423.1 79.3 reduce-scatter.7

commit v8 on v7

--- a/solution.py
+++ b/solution.py
@@ -844,7 +844,7 @@
     expand_t = jnp.transpose(w_expand, (1, 2, 0))
     reduce_t = jnp.transpose(w_reduce)
     in_t = jnp.transpose(w_attend_in, (1, 0, 2))
-    cut = units // 2 // 16 * 16
+    cut = units * 7 // 11 // 16 * 16
     shards = [
         jnp.concatenate([expand_t[:, a:b], reduce_t[None, a:b]], axis=0).astype(low)
         for a, b in ((0, cut), (cut, units))
@@ -942,19 +942,19 @@
         out_one, out_two = after((out_one, out_two), back)
         out_three = both_ways(out_one, (2, 4))
         begun = update_feed(0, after(first_grads, out_one), states, rates)
-        hid_one, hid_two = after((hid_one, hid_two), begun)
-        hid_three = both_ways(hid_one, (2, 4))
-        out_three = after(out_three, hid_one)
+        out_two, out_three = after((out_two, out_three), begun)
         mine_out = join(add, out_one, out_two, out_three)
         other_out = swap(mine_out, 1)
-        hid_three = after(hid_three, mine_out)
+        hid_one, hid_two = after((hid_one, hid_two), mine_out)
+        hid_three = both_ways(hid_one, (2, 4))
         mine_hid = join(back, hid_one, hid_two, hid_three)
         other_hid = swap(mine_hid, 1)
         attend_new = update_attend(after(attend_grad, mine_hid))
         (output,) = finish_rows(info, rows, mine_out, after(other_out, attend_new))
         input_grad, norm_part = finish_rows(info, rows, mine_hid, after(other_hid, output), cot)
-        sums = small_sum(join_sums(norm_part, bias_part), "dp")
-        done = update_feed(cut, after(last_grads, input_grad), states, rates, begun)
+        sums = join_sums(norm_part, bias_part)
+        done = update_feed(cut, after(last_grads, sums), states, rates, begun)
+        sums = small_sum(sums, "dp")
         norm_grad, bias_grad = split_sums(sums, norm_part, bias_part)
     else:
         out_part, active, both, w_last = out_last(info, False, last_all, hidden, out_early)

time: 554 us -> 540 us (0.975)
  waiting for transfers between devices: 181 us -> 170 us
    all_gather x1, waiting for transfers between devices: 31.1 us -> 0.01 us  [body(): last_all = lax.all_gather(after(shards[1], shards[0]), 'dp')]
    all_gather x1, waiting for transfers between devices: 2.83 us -> 22 us  [body(): first_all = lax.all_gather(after(shards[0], attend_shard), 'dp')]
    pallas_call x1, Pallas kernels: 35.5 us -> 20.9 us  [out_last(): pl.pallas_call(functools.partial(out_last_kernel, split), grid_spec=pltpu...]
    pallas_call x1, Pallas kernels: 19.8 us -> 30.8 us  [early_parts(): pl.pallas_call(early_kernel, grid=(rows // block,), in_specs=[pl.BlockSpe...]
  transfers between devices with their start and end apart: 38 -> 38, of which waited for: 16 -> 18; matrix products, arithmetic and copies ran while one was open for 6% -> 6% of each run, Pallas kernels for 51% -> 52%
where the time goes in v8:
time: 540 us; the launch traced here: 529 us
  Pallas kernels  273 us (51%)
  waiting for transfers between devices  170 us (31%)
  other arithmetic  30.8 us (6%)
  starting transfers between devices  24.8 us (5%)
  local copies, waits for them, and re-layouts  15.2 us (3%)
  between operations  15.2 us (3%)
    ppermute x32, waiting for transfers between devices, swap(): return lax.ppermute(value, axis, [(a, a ^ mask) for a in range(n)])  87.2 us
    all_gather x1, waiting for transfers between devices, body(): attend_all = lax.all_gather(attend_shard, 'dp')  60.3 us
    pallas_call x1, Pallas kernels, attend(): pl.pallas_call(functools.partial(attend_kernel, min(512, length)), grid=(...  34 us
    pallas_call x2, Pallas kernels, feed_grads(): pl.pallas_call(functools.partial(feed_grads_kernel, n, steps), grid=(step...  32.7 us
    pallas_call x1, Pallas kernels, early_parts(): pl.pallas_call(early_kernel, grid=(rows // block,), in_specs=[pl.BlockSpe...  30.8 us
    pallas_call x2, Pallas kernels, finish_rows(): pl.pallas_call(finish_kernel, grid_spec=pltpu.PrefetchScalarGridSpec(num_...  24.9 us
    ppermute x32, starting transfers between devices, swap(): return lax.ppermute(value, axis, [(a, a ^ mask) for a in range(n)])  24.6 us
    all_gather x1, waiting for transfers between devices, body(): first_all = lax.all_gather(after(shards[0], attend_shard), 'dp')  22 us
  transfers between devices with their start and end apart: 38, of which 18 were waited for; matrix products, arithmetic and copies ran while one was open for 6% of the time, Pallas kernels for 52%

profile of v8, /device:TPU:0, one launch (start us, length us, event | category | flops | bytes accessed | tf_op | source)
XLA Modules:
  0.0 529.1 jit_solution(10888174257029315096)
XLA Ops:
  7.2 1.1 convert_bitcast_fusion.1
  8.3 1.5 convert_bitcast_fusion
  9.8 1.1 pad_maximum_fusion.1
  11.0 1.0 copy-done
  12.3 1.6 copy-done.1
  14.0 1.2 pad_maximum_fusion
  17.4 11.3 %layer_norm.1.h_ref = bf16[2048,2048]{1,0:T(8,128)(2,1)} custom-call(bf16[2048,2048]{1,0:T(8,128)(2,1)} %bitcast.49, f32[2,2048]{1,0:T(2,128)} %refs_6_.1), custom_call_target="tpu_custom_call" | custom-call | flops 33554432 | bytes 16777216 | tf_op jit(solution)/shard_map/layer_norm/pallas_call | solution.py:97
  28.6 5.6 %fusion.2 = (f32[2048,128]{1,0:T(8,128)}, f32[2048,128]{1,0:T(8,128)}) fusion(f32[128]{0:T(128)S(1)} %fusion.7, f32[2048]{0:T(1024)S(1)} %bitcast.85, pred[128]{0:T(512)(128)(4,1)S(1)} %get-tuple-element.233, pred[128]{0:T(512)(128)(4,1)S(1)} %get-tuple-element.234), kind=kLoop, calls=%fused_computation.17 | loop fusion | flops 1310720 | bytes 2106112 | tf_op jit(solution)/shard_map/jit(_where)/select_n | solution.py:866
  34.2 60.3 %all-gather.6.cloned.1.call-done.shards_ref = bf16[4,4,512,256]{3,2,1,0:T(8,128)(2,1)} async-done(((bf16[1,4,512,256]{3,2,1,0:T(8,128)(2,1)}), bf16[4,4,512,256]{3,2,1,0:T(8,128)(2,1)}) %all-gather.6.cloned.1.call-update) | async-done | bytes 4194320 | tf_op jit(solution)/shard_map/all_gather | solution.py:853
  94.5 17.6 %project.1 = (bf16[2048,256]{1,0:T(8,128)(2,1)}, bf16[2048,256]{1,0:T(8,128)(2,1)}, bf16[2048,256]{1,0:T(8,128)(2,1)}, bf16[2048,256]{1,0:T(8,128)(2,1)}, bf16[4,2048,256]{2,1,0:T(8,128)(2,1)}) custom-call(bf16[4,4,512,256]{3,2,1,0:T(8,128)(2,1)} %all-gather.6.cloned.1.call-done.shards_ref, bf16[2048,2048]{1,0:T(8,128)(2,1)} %layer_norm.1.h_ref, ...), custom_call_target="tpu_custom_call" | custom-call | flops 8589934592 | bytes 25165824 | tf_op jit(solution)/shard_map/project/pallas_call | solution.py:384
  112.1 34.0 %attend.1 = (bf16[2048,256]{1,0:T(8,128)(2,1)}, bf16[3,2048,256]{2,1,0:T(8,128)(2,1)}, f32[3,256]{1,0:T(4,128)}) custom-call(bf16[2048,256]{1,0:T(8,128)(2,1)} %get-tuple-element.118.q_ref, bf16[2048,256]{1,0:T(8,128)(2,1)} %get-tuple-element.119.k_ref, bf16[2048,256]{1,0:T(8,128)(2,1)} %get-tuple-element.120.v_ref, ...), custom_call_target="tpu_custom_call" | custom-call | flops 21474836480 | bytes 10485760 | tf_op jit(solution)/shard_map/attend/pallas_call | solution.py:460
  146.1 14.9 %attend_grads.1 = bf16[4,4,512,256]{3,2,1,0:T(8,128)(2,1)} custom-call(bf16[2048,2048]{1,0:T(8,128)(2,1)} %layer_norm.1.h_ref, bf16[2048,2048]{1,0:T(8,128)(2,1)} %bitcast.55, bf16[3,2048,256]{2,1,0:T(8,128)(2,1)} %get-tuple-element.122.mg_ref, bf16[2048,256]{1,0:T(8,128)(2,1)} %get-tuple-element.123.ctx_ref), custom_call_target="tpu_custom_call" | custom-call | flops 8589934592 | bytes 25165824 | tf_op jit(solution)/shard_map/attend_grads/pallas_call | solution.py:502
  161.0 14.7 %heads_parts.1 = (bf16[2048,2048]{1,0:T(8,128)(2,1)}, bf16[2048,2048]{1,0:T(8,128)(2,1)}) custom-call(bf16[2048,256]{1,0:T(8,128)(2,1)} %get-tuple-element.123.ctx_ref, bf16[3,2048,256]{2,1,0:T(8,128)(2,1)} %get-tuple-element.122.mg_ref, bf16[4,2048,256]{2,1,0:T(8,128)(2,1)} %get-tuple-element.124.wa_ref), custom_call_target="tpu_custom_call" | custom-call | flops 8589934592 | bytes 25165824 | tf_op jit(solution)/shard_map/heads_parts/pallas_call | solution.py:531
  175.6 22.0 %all-gather.10.cloned.1.call-done = bf16[12,448,512]{2,1,0:T(8,128)(2,1)} async-done(((bf16[3,448,512]{2,1,0:T(8,128)(2,1)}), bf16[12,448,512]{2,1,0:T(8,128)(2,1)}) %all-gather.10.cloned.1.call-update) | async-done | bytes 5505040 | tf_op jit(solution)/shard_map/all_gather | solution.py:854
  197.6 19.2 %feed_chunk.1 = (bf16[448,2048]{1,0:T(8,128)(2,1)}, bf16[896,2048]{1,0:T(8,128)(2,1)}, bf16[3,448,2048]{2,1,0:T(8,128)(2,1)}) custom-call(bf16[4,3,448,512]{3,2,1,0:T(8,128)(2,1)} %bitcast.87, bf16[2048,2048]{1,0:T(8,128)(2,1)} %layer_norm.1.h_ref, bf16[2048,2048]{1,0:T(8,128)(2,1)} %bitcast.56), custom_call_target="tpu_custom_call" | custom-call | flops 11274289152 | bytes 27787264 | tf_op jit(solution)/shard_map/feed_chunk/pallas_call | solution.py:182
  216.8 19.2 %feed_grads.2 = bf16[4,1344,512]{2,1,0:T(8,128)(2,1)} custom-call(bf16[2048,2048]{1,0:T(8,128)(2,1)} %layer_norm.1.h_ref, bf16[2048,2048]{1,0:T(8,128)(2,1)} %bitcast.57, bf16[448,2048]{1,0:T(8,128)(2,1)} %get-tuple-element.128.act_ref, bf16[896,2048]{1,0:T(8,128)(2,1)} %get-tuple-element.129.grad_ref), custom_call_target="tpu_custom_call" | custom-call | flops 11274289152 | bytes 27787264 | tf_op jit(solution)/shard_map/feed_grads/pallas_call | solution.py:330
  236.1 30.8 %early_parts.1 = (bf16[2048,2048]{1,0:T(8,128)(2,1)}, bf16[2048,2048]{1,0:T(8,128)(2,1)}) custom-call(bf16[448,2048]{1,0:T(8,128)(2,1)} %get-tuple-element.128.act_ref, bf16[896,2048]{1,0:T(8,128)(2,1)} %get-tuple-element.129.grad_ref, bf16[3,448,2048]{2,1,0:T(8,128)(2,1)} %get-tuple-element.130.w_ref, bf16[2048,2048]{1,0:T(8,128)(2,1)} %get-tuple-element.125.hid_in_ref, ...), custom_call_target="tpu_custom_call" | custom-call | flops 11274289152 | bytes 44564480 | tf_op jit(solution)/shard_map/early_parts/pallas_call | solution.py:559
  267.5 20.9 %out_last.1 = (bf16[256,2048]{1,0:T(8,128)(2,1)}, bf16[256,2048]{1,0:T(8,128)(2,1)}, bf16[256,2048]{1,0:T(8,128)(2,1)}, bf16[256,2048]{1,0:T(8,128)(2,1)}, bf16[...) custom-call(s32[3]{0:T(128)} %pad_add_fusion.info_ref, ...), custom_call_target="tpu_custom_call" | custom-call | flops 6442450944 | bytes 33554432 | tf_op jit(solution)/shard_map/out_last/pallas_call | solution.py:262
  289.0 2.4 collective-permute-done.1
  291.4 1.6 add_convert_fusion.7
  293.6 1.5 collective-permute-start.2
  295.1 1.5 collective-permute-start.4
  297.1 18.8 %hid_last.1 = (bf16[256,2048]{1,0:T(8,128)(2,1)}, bf16[256,2048]{1,0:T(8,128)(2,1)}, bf16[256,2048]{1,0:T(8,128)(2,1)}, bf16[256,2048]{1,0:T(8,128)(2,1)}, bf16[...) custom-call(s32[3]{0:T(128)} %pad_add_fusion.info_ref, ...), custom_call_target="tpu_custom_call" | custom-call | flops 6442450944 | bytes 33554432 | tf_op jit(solution)/shard_map/hid_last/pallas_call | solution.py:298
  315.9 3.1 collective-permute-done.2
  319.0 1.1 collective-permute-done.4
  320.6 2.1 add_convert_fusion.5
  324.3 2.1 add_convert_fusion.4
  328.4 1.6 collective-permute-start.17
  332.0 1.4 collective-permute-start.7
  333.4 13.5 %feed_grads.3 = bf16[4,768,512]{2,1,0:T(8,128)(2,1)} custom-call(bf16[2048,2048]{1,0:T(8,128)(2,1)} %layer_norm.1.h_ref, bf16[2048,2048]{1,0:T(8,128)(2,1)} %bitcast.59, bf16[256,2048]{1,0:T(8,128)(2,1)} %get-tuple-element.156.act_ref, bf16[512,2048]{1,0:T(8,128)(2,1)} %get-tuple-element.157.grad_ref), custom_call_target="tpu_custom_call" | custom-call | flops 6442450944 | bytes 23068672 | tf_op jit(solution)/shard_map/feed_grads/pallas_call | solution.py:330
  346.9 17.8 %collective-permute-done.6.refs_4_ = bf16[128,2048]{1,0:T(8,128)(2,1)S(1)} collective-permute-done((bf16[128,2048]{1,0:T(8,128)(2,1)}, bf16[128,2048]{1,0:T(8,128)(2,1)S(1)}, u32[]{:S(2)}, u32[]{:S(2)}) %collective-permute-start.6) | collective-permute-done | bytes 524320 | tf_op jit(solution)/shard_map/ppermute | solution.py:63
  364.7 1.7 collective-permute-done.7.refs_5_
  367.2 3.8 add_rows.1
  371.0 2.6 add_convert_fusion
  375.4 1.8 add_convert_fusion.1
  378.9 1.2 collective-permute-start.14
  380.1 1.2 collective-permute-start.12
  382.1 7.3 %collective-permute-done.19.refs_5_ = bf16[128,2048]{1,0:T(8,128)(2,1)S(1)} collective-permute-done((bf16[128,2048]{1,0:T(8,128)(2,1)S(1)}, bf16[128,2048]{1,0:T(8,128)(2,1)S(1)}, u32[]{:S(2)}, u32[]{:S(2)}) %collective-permute-start.19) | collective-permute-done | bytes 524320 | tf_op jit(solution)/shard_map/ppermute | solution.py:63
  389.7 3.2 collective-permute-done.18.refs_4_
  393.7 5.5 %back_rows.1 = (bf16[144,2048]{1,0:T(8,128)(2,1)}, bf16[128,2048]{1,0:T(8,128)(2,1)}) custom-call(s32[3]{0:T(128)} %pad_add_fusion.info_ref, bf16[2048,2048]{1,0:T(8,128)(2,1)} %bitcast.52, bf16[2048,2048]{1,0:T(8,128)(2,1)} %bitcast.53, bf16[128,2048]{1,0:T(8,128)(2,1)} %get-tuple-element.226.refs_2_, bf16[128,2048]{1,0:T(8,128)(2,1)} %get-tuple-element.224.refs_3_, ...), custom_call_target="tpu_custom_call" | custom-call | flops 10485760 | bytes 4194304 | tf_op jit(solution)/shard_map/back_rows/pallas_call | solution.py:614
  399.2 1.5 collective-permute-done.14.refs_2_
  400.7 3.6 collective-permute-done.12.refs_1_
  404.3 8.7 %collective-permute-done.15.refs_6_ = bf16[128,2048]{1,0:T(8,128)(2,1)S(1)} collective-permute-done((bf16[128,2048]{1,0:T(8,128)(2,1)S(1)}, bf16[128,2048]{1,0:T(8,128)(2,1)S(1)}, u32[]{:S(2)}, u32[]{:S(2)}) %collective-permute-start.15) | collective-permute-done | bytes 524320 | tf_op jit(solution)/shard_map/ppermute | solution.py:63
  413.8 1.3 collective-permute-start.20
  415.9 1.6 collective-permute-start.23
  417.9 1.6 collective-permute-start.26
  419.6 9.4 %collective-permute-done.20.refs_3_ = bf16[128,2048]{1,0:T(8,128)(2,1)} collective-permute-done((bf16[128,2048]{1,0:T(8,128)(2,1)}, bf16[128,2048]{1,0:T(8,128)(2,1)}, u32[]{:S(2)}, u32[]{:S(2)}) %collective-permute-start.20) | collective-permute-done | bytes 524320 | tf_op jit(solution)/shard_map/ppermute | solution.py:63
  429.0 1.3 collective-permute-start.24
  430.3 8.3 %update_feed.2 = (f32[2,704,512]{2,1,0:T(8,128)}, f32[2,704,512]{2,1,0:T(8,128)}, f32[2,704,512]{2,1,0:T(8,128)}, f32[2,704,512]{2,1,0:T(8,128)}, f32[704,512]{1...) custom-call(bf16[3,448,512]{2,1,0:T(8,128)(2,1)} %bitcast.82, f32[2,704,512]{2,1,0:T(8,128)} %bitcast.61, ...), custom_call_target="tpu_custom_call" | custom-call | flops 6881280 | bytes 20643840 | tf_op jit(solution)/shard_map/update_feed/pallas_call | solution.py:796
  438.6 5.0 collective-permute-done.21.refs_7_
  443.5 4.9 pack_rows.2.refs_0_
  448.4 3.1 collective-permute-done.26.refs_6_
  451.6 1.4 collective-permute-start.27
  453.0 1.7 collective-permute-start.28
  454.8 9.3 %collective-permute-done.28.refs_7_ = bf16[128,2048]{1,0:T(8,128)(2,1)S(1)} collective-permute-done((bf16[128,2048]{1,0:T(8,128)(2,1)}, bf16[128,2048]{1,0:T(8,128)(2,1)S(1)}, u32[]{:S(2)}, u32[]{:S(2)}) %collective-permute-start.28) | collective-permute-done | bytes 524320 | tf_op jit(solution)/shard_map/ppermute | solution.py:63
  465.7 5.3 pack_rows.3.refs_0_.refs_3_
  471.6 1.4 convert_element_type.137
  473.1 1.5 multiply_add_fusion.2
  475.7 3.1 multiply_add_fusion
  478.8 6.2 %collective-permute-done.22.refs_1_ = bf16[1024,2048]{1,0:T(8,128)(2,1)} collective-permute-done((bf16[1024,2048]{1,0:T(8,128)(2,1)}, bf16[1024,2048]{1,0:T(8,128)(2,1)}, u32[]{:S(2)}, u32[]{:S(2)}) %collective-permute-start.22) | collective-permute-done | bytes 4194336 | tf_op jit(solution)/shard_map/ppermute | solution.py:63
  485.0 10.2 %finish_rows.2 = bf16[2048,2048]{1,0:T(8,128)(2,1)} custom-call(s32[3]{0:T(128)} %pad_add_fusion.info_ref, bf16[1024,2048]{1,0:T(8,128)(2,1)} %pack_rows.2.refs_0_, bf16[1024,2048]{1,0:T(8,128)(2,1)} %collective-permute-done.22.refs_1_), custom_call_target="tpu_custom_call" | custom-call | flops 8388608 | bytes 33554432 | tf_op jit(solution)/shard_map/finish_rows/pallas_call | solution.py:759
  495.2 14.6 %finish_rows.3 = (f32[2048,2048]{1,0:T(8,128)}, f32[2,2048]{1,0:T(2,128)}) custom-call(s32[3]{0:T(128)} %pad_add_fusion.info_ref, bf16[1088,2048]{1,0:T(8,128)(2,1)} %pack_rows.3.refs_0_.refs_3_, bf16[1088,2048]{1,0:T(8,128)(2,1)} %collective-permute-done.29.refs_1_.refs_4_, bf16[2048,2048]{1,0:T(8,128)(2,1)} %bitcast.60, ...), custom_call_target="tpu_custom_call" | custom-call | flops 8388608 | bytes 33554432 | tf_op jit(solution)/shard_map/finish_rows/pallas_call | solution.py:759
  510.7 3.8 collective-permute-done.30
  514.6 5.8 %update_feed.3 = (f32[2,704,512]{2,1,0:T(8,128)}, f32[2,704,512]{2,1,0:T(8,128)}, f32[2,704,512]{2,1,0:T(8,128)}, f32[2,704,512]{2,1,0:T(8,128)}, f32[704,512]{1...) custom-call(bf16[3,256,512]{2,1,0:T(8,128)(2,1)} %bitcast.84, ...), custom_call_target="tpu_custom_call", output_to_operand_aliasing={{0}: (7, {}), {1}: (8, {}), {2}: (9, {}), {3}: (10, {}), {4... | custom-call | flops 3932160 | bytes 11796480 | tf_op jit(solution)/shard_map/update_feed/pallas_call | solution.py:796
  (167 shorter events, 24.6 us)
Async XLA Ops:
  7.2 87.3 %all-gather.6.cloned.1.call-start = ((), (), s32[]{:S(2)}) async-start(), calls=%async_computation.3 | async-start | bytes 5242880 | tf_op jit(solution)/shard_map/all_gather | solution.py:853
  9.8 2.2 copy-start
  10.9 186.7 %all-gather.10.cloned.1.call-start = ((), (), s32[]{:S(2)}) async-start(), calls=%async_computation.8 | async-start | bytes 6881280 | tf_op jit(solution)/shard_map/all_gather | solution.py:854
  15.3 251.6 %all-gather.8.cloned.1.call-start = ((), (), s32[]{:S(2)}) async-start(), calls=%async_computation.7 | async-start | bytes 3932160 | tf_op jit(solution)/shard_map/all_gather | solution.py:855
  17.3 413.0 %reduce-scatter.4.cloned.1.call-start = ((), (), s32[]{:S(2)}) async-start(), calls=%async_computation.4 | async-start | bytes 6881280 | tf_op jit(solution)/shard_map/reduce_scatter | solution.py:869
  266.9 204.8 %reduce-scatter.6.cloned.1.call-start = ((), (), s32[]{:S(2)}) async-start(), calls=%async_computation.5 | async-start | bytes 5242880 | tf_op jit(solution)/shard_map/reduce_scatter | solution.py:869
  288.4 4.6 copy-start.9
  288.4 2.9 collective-permute-start.1
  288.5 4.5 collective-permute-start.3
  293.5 221.0 %reduce-scatter.8.cloned.1.call-start = ((), (), s32[]{:S(2)}) async-start(), calls=%async_computation.6 | async-start | bytes 3932160 | tf_op jit(solution)/shard_map/reduce_scatter | solution.py:869
  293.6 25.4 %collective-permute-start.2 = (bf16[256,2048]{1,0:T(8,128)(2,1)S(1)}, bf16[256,2048]{1,0:T(8,128)(2,1)}, u32[]{:S(2)}, u32[]{:S(2)}) collective-permute-start(bf16[256,2048]{1,0:T(8,128)(2,1)S(1)} %add_convert_fusion.7), channel_id=1, source_target_pairs={{0,2},{1,3},{2,0},{3,1},{4,6},{5,7},{6,4},{7,5},{8,10},{9,11},{10,... | collective-permute-start | bytes 3145736 | tf_op jit(solution)/shard_map/ppermute | solution.py:63
  295.1 25.0 %collective-permute-start.4 = (bf16[256,2048]{1,0:T(8,128)(2,1)S(1)}, bf16[256,2048]{1,0:T(8,128)(2,1)}, u32[]{:S(2)}, u32[]{:S(2)}) collective-permute-start(bf16[256,2048]{1,0:T(8,128)(2,1)S(1)} %add_convert_fusion.6), channel_id=1, source_target_pairs={{0,4},{1,5},{2,6},{3,7},{4,0},{5,1},{6,2},{7,3},{8,12},{9,13},{10,... | collective-permute-start | bytes 3145736 | tf_op jit(solution)/shard_map/ppermute | solution.py:63
  296.5 23.6 %collective-permute-start = (bf16[256,2048]{1,0:T(8,128)(2,1)}, bf16[256,2048]{1,0:T(8,128)(2,1)}, u32[]{:S(2)}, u32[]{:S(2)}) collective-permute-start(bf16[256,2048]{1,0:T(8,128)(2,1)} %get-tuple-element.135), channel_id=1, source_target_pairs={{0,1},{1,0},{2,3},{3,2},{4,5},{5,4},{6,7},{7,6},{8,9},{9,8},{10,11... | collective-permute-start | bytes 3145736 | tf_op jit(solution)/shard_map/ppermute | solution.py:63
  296.5 27.2 %collective-permute-start.5 = (bf16[256,2048]{1,0:T(8,128)(2,1)}, bf16[256,2048]{1,0:T(8,128)(2,1)}, u32[]{:S(2)}, u32[]{:S(2)}) collective-permute-start(bf16[256,2048]{1,0:T(8,128)(2,1)} %get-tuple-element.146), channel_id=1, source_target_pairs={{0,1},{1,0},{2,3},{3,2},{4,5},{5,4},{6,7},{7,6},{8,9},{9,8},{10,11... | collective-permute-start | bytes 3145736 | tf_op jit(solution)/shard_map/ppermute | solution.py:63
  297.1 23.6 %copy-start.16 = (bf16[256,2048]{1,0:T(8,128)(2,1)S(1)}, bf16[256,2048]{1,0:T(8,128)(2,1)}, u32[]{:S(2)}) copy-start(bf16[256,2048]{1,0:T(8,128)(2,1)} %get-tuple-element.134) | copy-start | bytes 3145732
  315.9 11.5 %collective-permute-start.9 = (bf16[256,2048]{1,0:T(8,128)(2,1)}, bf16[256,2048]{1,0:T(8,128)(2,1)S(1)}, u32[]{:S(2)}, u32[]{:S(2)}) collective-permute-start(bf16[256,2048]{1,0:T(8,128)(2,1)} %get-tuple-element.150), channel_id=1, source_target_pairs={{0,1},{1,0},{2,3},{3,2},{4,5},{5,4},{6,7},{7,6},{8,9},{9,8},{10,11... | collective-permute-start | bytes 3145736 | tf_op jit(solution)/shard_map/ppermute | solution.py:63
  319.0 8.5 %collective-permute-start.10 = (bf16[256,2048]{1,0:T(8,128)(2,1)}, bf16[256,2048]{1,0:T(8,128)(2,1)S(1)}, u32[]{:S(2)}, u32[]{:S(2)}) collective-permute-start(bf16[256,2048]{1,0:T(8,128)(2,1)} %get-tuple-element.151), channel_id=1, source_target_pairs={{0,1},{1,0},{2,3},{3,2},{4,5},{5,4},{6,7},{7,6},{8,9},{9,8},{10,11... | collective-permute-start | bytes 3145736 | tf_op jit(solution)/shard_map/ppermute | solution.py:63
  320.1 7.3 %collective-permute-start.8 = (bf16[256,2048]{1,0:T(8,128)(2,1)}, bf16[256,2048]{1,0:T(8,128)(2,1)S(1)}, u32[]{:S(2)}, u32[]{:S(2)}) collective-permute-start(bf16[256,2048]{1,0:T(8,128)(2,1)} %get-tuple-element.143), channel_id=1, source_target_pairs={{0,1},{1,0},{2,3},{3,2},{4,5},{5,4},{6,7},{7,6},{8,9},{9,8},{10,11... | collective-permute-start | bytes 3145736 | tf_op jit(solution)/shard_map/ppermute | solution.py:63
  320.1 7.3 %collective-permute-start.11 = (bf16[256,2048]{1,0:T(8,128)(2,1)}, bf16[256,2048]{1,0:T(8,128)(2,1)S(1)}, u32[]{:S(2)}, u32[]{:S(2)}) collective-permute-start(bf16[256,2048]{1,0:T(8,128)(2,1)} %get-tuple-element.152), channel_id=1, source_target_pairs={{0,1},{1,0},{2,3},{3,2},{4,5},{5,4},{6,7},{7,6},{8,9},{9,8},{10,11... | collective-permute-start | bytes 3145736 | tf_op jit(solution)/shard_map/ppermute | solution.py:63
  327.4 2.5 copy-start.7
  327.4 2.9 copy-start.14
  327.5 2.9 copy-start.12
  328.4 42.7 %collective-permute-start.17 = (bf16[256,2048]{1,0:T(8,128)(2,1)S(1)}, bf16[256,2048]{1,0:T(8,128)(2,1)}, u32[]{:S(2)}, u32[]{:S(2)}) collective-permute-start(bf16[256,2048]{1,0:T(8,128)(2,1)S(1)} %add_convert_fusion.2), channel_id=1, source_target_pairs={{0,4},{1,5},{2,6},{3,7},{4,0},{5,1},{6,2},{7,3},{8,12},{9,13},{10,... | collective-permute-start | bytes 3145736 | tf_op jit(solution)/shard_map/ppermute | solution.py:63
  330.4 40.7 %collective-permute-start.16 = (bf16[256,2048]{1,0:T(8,128)(2,1)S(1)}, bf16[256,2048]{1,0:T(8,128)(2,1)}, u32[]{:S(2)}, u32[]{:S(2)}) collective-permute-start(bf16[256,2048]{1,0:T(8,128)(2,1)S(1)} %add_convert_fusion.3), channel_id=1, source_target_pairs={{0,2},{1,3},{2,0},{3,1},{4,6},{5,7},{6,4},{7,5},{8,10},{9,11},{10,... | collective-permute-start | bytes 3145736 | tf_op jit(solution)/shard_map/ppermute | solution.py:63
  331.0 33.7 %collective-permute-start.6 = (bf16[128,2048]{1,0:T(8,128)(2,1)}, bf16[128,2048]{1,0:T(8,128)(2,1)S(1)}, u32[]{:S(2)}, u32[]{:S(2)}) collective-permute-start(bf16[128,2048]{1,0:T(8,128)(2,1)} %get-tuple-element.229), channel_id=1, source_target_pairs={{0,4},{1,5},{2,6},{3,7},{4,0},{5,1},{6,2},{7,3},{8,12},{9,13},{10,... | collective-permute-start | bytes 1572872 | tf_op jit(solution)/shard_map/ppermute | solution.py:63
  332.0 34.4 %collective-permute-start.7 = (bf16[128,2048]{1,0:T(8,128)(2,1)}, bf16[128,2048]{1,0:T(8,128)(2,1)S(1)}, u32[]{:S(2)}, u32[]{:S(2)}) collective-permute-start(bf16[128,2048]{1,0:T(8,128)(2,1)} %get-tuple-element.227), channel_id=1, source_target_pairs={{0,2},{1,3},{2,0},{3,1},{4,6},{5,7},{6,4},{7,5},{8,10},{9,11},{10,... | collective-permute-start | bytes 1572872 | tf_op jit(solution)/shard_map/ppermute | solution.py:63
  367.2 3.8 copy-start.11
  374.6 14.9 %collective-permute-start.19 = (bf16[128,2048]{1,0:T(8,128)(2,1)S(1)}, bf16[128,2048]{1,0:T(8,128)(2,1)S(1)}, u32[]{:S(2)}, u32[]{:S(2)}) collective-permute-start(bf16[128,2048]{1,0:T(8,128)(2,1)S(1)} %get-tuple-element.223), channel_id=1, source_target_pairs={{0,2},{1,3},{2,0},{3,1},{4,6},{5,7},{6,4},{7,5},{8,10},{9,11},{10,... | collective-permute-start | bytes 1572872 | tf_op jit(solution)/shard_map/ppermute | solution.py:63
  377.2 4.1 copy-start.22
  378.1 14.9 %collective-permute-start.18 = (bf16[128,2048]{1,0:T(8,128)(2,1)S(1)}, bf16[128,2048]{1,0:T(8,128)(2,1)S(1)}, u32[]{:S(2)}, u32[]{:S(2)}) collective-permute-start(bf16[128,2048]{1,0:T(8,128)(2,1)S(1)} %get-tuple-element.225), channel_id=1, source_target_pairs={{0,4},{1,5},{2,6},{3,7},{4,0},{5,1},{6,2},{7,3},{8,12},{9,13},{10,... | collective-permute-start | bytes 1572872 | tf_op jit(solution)/shard_map/ppermute | solution.py:63
  378.9 21.8 %collective-permute-start.14 = (bf16[128,2048]{1,0:T(8,128)(2,1)S(1)}, bf16[128,2048]{1,0:T(8,128)(2,1)S(1)}, u32[]{:S(2)}, u32[]{:S(2)}) collective-permute-start(bf16[128,2048]{1,0:T(8,128)(2,1)S(1)} %copy-done.21), channel_id=1, source_target_pairs={{0,2},{1,3},{2,0},{3,1},{4,6},{5,7},{6,4},{7,5},{8,10},{9,11},{10,... | collective-permute-start | bytes 1572872 | tf_op jit(solution)/shard_map/ppermute | solution.py:63
  380.1 24.2 %collective-permute-start.12 = (bf16[128,2048]{1,0:T(8,128)(2,1)S(1)}, bf16[128,2048]{1,0:T(8,128)(2,1)}, u32[]{:S(2)}, u32[]{:S(2)}) collective-permute-start(bf16[128,2048]{1,0:T(8,128)(2,1)S(1)} %copy-done.21), channel_id=1, source_target_pairs={{0,4},{1,5},{2,6},{3,7},{4,0},{5,1},{6,2},{7,3},{8,12},{9,13},{10,... | collective-permute-start | bytes 1572872 | tf_op jit(solution)/shard_map/ppermute | solution.py:63
  381.3 31.7 %collective-permute-start.15 = (bf16[128,2048]{1,0:T(8,128)(2,1)S(1)}, bf16[128,2048]{1,0:T(8,128)(2,1)S(1)}, u32[]{:S(2)}, u32[]{:S(2)}) collective-permute-start(bf16[128,2048]{1,0:T(8,128)(2,1)S(1)} %copy-done.22), channel_id=1, source_target_pairs={{0,4},{1,5},{2,6},{3,7},{4,0},{5,1},{6,2},{7,3},{8,12},{9,13},{10,... | collective-permute-start | bytes 1572872 | tf_op jit(solution)/shard_map/ppermute | solution.py:63
  389.4 3.5 copy-start.28
  389.4 23.6 %collective-permute-start.13 = (bf16[128,2048]{1,0:T(8,128)(2,1)S(1)}, bf16[128,2048]{1,0:T(8,128)(2,1)S(1)}, u32[]{:S(2)}, u32[]{:S(2)}) collective-permute-start(bf16[128,2048]{1,0:T(8,128)(2,1)S(1)} %copy-done.22), channel_id=1, source_target_pairs={{0,2},{1,3},{2,0},{3,1},{4,6},{5,7},{6,4},{7,5},{8,10},{9,11},{10,... | collective-permute-start | bytes 1572872 | tf_op jit(solution)/shard_map/ppermute | solution.py:63
  399.2 15.9 %copy-start.17 = (bf16[144,2048]{1,0:T(8,128)(2,1)S(1)}, bf16[144,2048]{1,0:T(8,128)(2,1)}, u32[]{:S(2)}) copy-start(bf16[144,2048]{1,0:T(8,128)(2,1)} %get-tuple-element.168.refs_0_) | copy-start | bytes 1769476
  400.7 12.3 %copy-start.24 = (bf16[128,2048]{1,0:T(8,128)(2,1)}, bf16[128,2048]{1,0:T(8,128)(2,1)S(1)}, u32[]{:S(2)}) copy-start(bf16[128,2048]{1,0:T(8,128)(2,1)S(1)} %collective-permute-done.14.refs_2_) | copy-start | bytes 1572868
  404.3 13.7 %copy-start.23 = (bf16[128,2048]{1,0:T(8,128)(2,1)S(1)}, bf16[128,2048]{1,0:T(8,128)(2,1)}, u32[]{:S(2)}) copy-start(bf16[128,2048]{1,0:T(8,128)(2,1)} %get-tuple-element.169.refs_4_) | copy-start | bytes 1572868
  413.0 2.1 copy-start.26
  413.8 15.2 %collective-permute-start.20 = (bf16[128,2048]{1,0:T(8,128)(2,1)}, bf16[128,2048]{1,0:T(8,128)(2,1)}, u32[]{:S(2)}, u32[]{:S(2)}) collective-permute-start(bf16[128,2048]{1,0:T(8,128)(2,1)} %collective-permute-done.12.refs_1_), channel_id=1, source_target_pairs={{0,2},{1,3},{2,0},{3,1},{4,6},{5,7},{6,4},{7,5},{8,10},{9,11},{10,... | collective-permute-start | bytes 1572872 | tf_op jit(solution)/shard_map/ppermute | solution.py:63
  415.1 36.5 %collective-permute-start.25 = (bf16[144,2048]{1,0:T(8,128)(2,1)S(1)}, bf16[144,2048]{1,0:T(8,128)(2,1)S(1)}, u32[]{:S(2)}, u32[]{:S(2)}) collective-permute-start(bf16[144,2048]{1,0:T(8,128)(2,1)S(1)} %copy-done.17), channel_id=1, source_target_pairs={{0,2},{1,3},{2,0},{3,1},{4,6},{5,7},{6,4},{7,5},{8,10},{9,11},{10,... | collective-permute-start | bytes 1769480 | tf_op jit(solution)/shard_map/ppermute | solution.py:63
  415.9 35.7 %collective-permute-start.23 = (bf16[144,2048]{1,0:T(8,128)(2,1)S(1)}, bf16[144,2048]{1,0:T(8,128)(2,1)S(1)}, u32[]{:S(2)}, u32[]{:S(2)}) collective-permute-start(bf16[144,2048]{1,0:T(8,128)(2,1)S(1)} %copy-done.17), channel_id=1, source_target_pairs={{0,4},{1,5},{2,6},{3,7},{4,0},{5,1},{6,2},{7,3},{8,12},{9,13},{10,... | collective-permute-start | bytes 1769480 | tf_op jit(solution)/shard_map/ppermute | solution.py:63
  417.6 26.0 %collective-permute-start.21 = (bf16[128,2048]{1,0:T(8,128)(2,1)}, bf16[128,2048]{1,0:T(8,128)(2,1)}, u32[]{:S(2)}, u32[]{:S(2)}) collective-permute-start(bf16[128,2048]{1,0:T(8,128)(2,1)} %copy-done.26), channel_id=1, source_target_pairs={{0,4},{1,5},{2,6},{3,7},{4,0},{5,1},{6,2},{7,3},{8,12},{9,13},{10,... | collective-permute-start | bytes 1572872 | tf_op jit(solution)/shard_map/ppermute | solution.py:63
  417.9 33.6 %collective-permute-start.26 = (bf16[128,2048]{1,0:T(8,128)(2,1)S(1)}, bf16[128,2048]{1,0:T(8,128)(2,1)S(1)}, u32[]{:S(2)}, u32[]{:S(2)}) collective-permute-start(bf16[128,2048]{1,0:T(8,128)(2,1)S(1)} %copy-done.23), channel_id=1, source_target_pairs={{0,4},{1,5},{2,6},{3,7},{4,0},{5,1},{6,2},{7,3},{8,12},{9,13},{10,... | collective-permute-start | bytes 1572872 | tf_op jit(solution)/shard_map/ppermute | solution.py:63
  429.0 22.6 %collective-permute-start.24 = (bf16[128,2048]{1,0:T(8,128)(2,1)S(1)}, bf16[128,2048]{1,0:T(8,128)(2,1)}, u32[]{:S(2)}, u32[]{:S(2)}) collective-permute-start(bf16[128,2048]{1,0:T(8,128)(2,1)S(1)} %copy-done.23), channel_id=1, source_target_pairs={{0,2},{1,3},{2,0},{3,1},{4,6},{5,7},{6,4},{7,5},{8,10},{9,11},{10,... | collective-permute-start | bytes 1572872 | tf_op jit(solution)/shard_map/ppermute | solution.py:63
  451.6 12.5 %copy-start.27 = (bf16[128,2048]{1,0:T(8,128)(2,1)}, bf16[128,2048]{1,0:T(8,128)(2,1)S(1)}, u32[]{:S(2)}) copy-start(bf16[128,2048]{1,0:T(8,128)(2,1)S(1)} %collective-permute-done.26.refs_6_) | copy-start | bytes 1572868
  451.6 12.5 %copy-start.18 = (bf16[144,2048]{1,0:T(8,128)(2,1)}, bf16[144,2048]{1,0:T(8,128)(2,1)S(1)}, u32[]{:S(2)}) copy-start(bf16[144,2048]{1,0:T(8,128)(2,1)S(1)} %collective-permute-done.25.refs_2_) | copy-start | bytes 1769476
  451.6 12.5 %copy-start.19 = (bf16[144,2048]{1,0:T(8,128)(2,1)}, bf16[144,2048]{1,0:T(8,128)(2,1)S(1)}, u32[]{:S(2)}) copy-start(bf16[144,2048]{1,0:T(8,128)(2,1)S(1)} %collective-permute-done.23.refs_1_) | copy-start | bytes 1769476
  451.6 12.5 %collective-permute-start.27 = (bf16[144,2048]{1,0:T(8,128)(2,1)S(1)}, bf16[144,2048]{1,0:T(8,128)(2,1)S(1)}, u32[]{:S(2)}, u32[]{:S(2)}) collective-permute-start(bf16[144,2048]{1,0:T(8,128)(2,1)S(1)} %collective-permute-done.23.refs_1_), channel_id=1, source_target_pairs={{0,2},{1,3},{2,0},{3,1},{4,6},{5,7},{6,4},{7,5},{8,10},{9,11},{10,... | collective-permute-start | bytes 1769480 | tf_op jit(solution)/shard_map/ppermute | solution.py:63
  453.0 11.1 %collective-permute-start.28 = (bf16[128,2048]{1,0:T(8,128)(2,1)}, bf16[128,2048]{1,0:T(8,128)(2,1)S(1)}, u32[]{:S(2)}, u32[]{:S(2)}) collective-permute-start(bf16[128,2048]{1,0:T(8,128)(2,1)} %collective-permute-done.24.refs_5_), channel_id=1, source_target_pairs={{0,4},{1,5},{2,6},{3,7},{4,0},{5,1},{6,2},{7,3},{8,12},{9,13},{10,... | collective-permute-start | bytes 1572872 | tf_op jit(solution)/shard_map/ppermute | solution.py:63
  465.7 8.8 %copy-start.6 = (f32[512,3,256]{2,0,1:T(8,128)S(1)}, f32[512,3,256]{2,0,1:T(8,128)}, u32[]{:S(2)}) copy-start(f32[512,3,256]{2,0,1:T(8,128)} %param.30) | copy-start | bytes 4718596
  471.1 24.2 %collective-permute-start.29 = (bf16[1088,2048]{1,0:T(8,128)(2,1)}, bf16[1088,2048]{1,0:T(8,128)(2,1)}, u32[]{:S(2)}, u32[]{:S(2)}) collective-permute-start(bf16[1088,2048]{1,0:T(8,128)(2,1)} %pack_rows.3.refs_0_.refs_3_), channel_id=1, source_target_pairs={{0,1},{1,0},{2,3},{3,2},{4,5},{5,4},{6,7},{7,6},{8,9},{9,8},{10,11... | collective-permute-start | bytes 13369352 | tf_op jit(solution)/shard_map/ppermute | solution.py:63
  471.1 13.9 %collective-permute-start.22 = (bf16[1024,2048]{1,0:T(8,128)(2,1)}, bf16[1024,2048]{1,0:T(8,128)(2,1)}, u32[]{:S(2)}, u32[]{:S(2)}) collective-permute-start(bf16[1024,2048]{1,0:T(8,128)(2,1)} %pack_rows.2.refs_0_), channel_id=1, source_target_pairs={{0,1},{1,0},{2,3},{3,2},{4,5},{5,4},{6,7},{7,6},{8,9},{9,8},{10,11... | collective-permute-start | bytes 12582920 | tf_op jit(solution)/shard_map/ppermute | solution.py:63
  473.1 2.2 copy-start.2
  473.1 2.6 copy-start.5
  495.2 15.4 %copy-start.40 = (f32[3,256]{1,0:T(4,128)S(1)}, f32[3,256]{1,0:T(4,128)}, u32[]{:S(2)}) copy-start(f32[3,256]{1,0:T(4,128)} %get-tuple-element.198) | copy-start | bytes 9220
  510.6 3.9 collective-permute-start.30
  514.5 5.9 %collective-permute-start.31 = (f32[19,256]{1,0:T(8,128)S(1)}, f32[19,256]{1,0:T(8,128)S(1)}, u32[]{:S(2)}, u32[]{:S(2)}) collective-permute-start(f32[19,256]{1,0:T(8,128)S(1)} %add.128), channel_id=1, source_target_pairs={{0,16},{8,24},{16,0},{24,8},{1,17},{9,25},{17,1},{25,9},{2,18},{10... | collective-permute-start | bytes 58376 | tf_op jit(solution)/shard_map/ppermute | solution.py:63
  514.6 6.0 %copy-start.41 = (f32[3,256]{1,0:T(4,128)S(1)}, f32[3,256]{1,0:T(4,128)}, u32[]{:S(2)}) copy-start(f32[3,256]{1,0:T(4,128)} %bias_ref.1) | copy-start | bytes 9220
  514.6 5.9 %copy-start.42 = (f32[3,256]{1,0:T(4,128)S(1)}, f32[3,256]{1,0:T(4,128)}, u32[]{:S(2)}) copy-start(f32[3,256]{1,0:T(4,128)} %param.41) | copy-start | bytes 9220
  514.6 5.9 %copy-start.43 = (f32[3,256]{1,0:T(4,128)S(1)}, f32[3,256]{1,0:T(4,128)}, u32[]{:S(2)}) copy-start(f32[3,256]{1,0:T(4,128)} %param.35) | copy-start | bytes 9220
  514.6 6.6 %copy-start.35 = (f32[2,2048]{1,0:T(2,128)S(1)}, f32[2,2048]{1,0:T(2,128)}, u32[]{:S(2)}) copy-start(f32[2,2048]{1,0:T(2,128)} %refs_6_.1) | copy-start | bytes 49156
  514.6 6.6 %copy-start.37 = (f32[2,2048]{1,0:T(2,128)S(1)}, f32[2,2048]{1,0:T(2,128)}, u32[]{:S(2)}) copy-start(f32[2,2048]{1,0:T(2,128)} %param.40) | copy-start | bytes 49156
  514.6 6.5 %copy-start.38 = (f32[2,2048]{1,0:T(2,128)S(1)}, f32[2,2048]{1,0:T(2,128)}, u32[]{:S(2)}) copy-start(f32[2,2048]{1,0:T(2,128)} %param.34) | copy-start | bytes 49156
  (19 other events, 27.9 us)
Sparse Core Ops, SparseCore 0:
  11.0 83.4 all-gather.5
  96.7 100.9 all-gather.9
  199.8 61.8 all-gather.7
  267.0 96.3 reduce-scatter.3
  365.5 77.2 reduce-scatter.5
  445.1 60.7 reduce-scatter.7
